TPU v7x, 32 devices: a whole 2x2x4 slice. The times are simulated.
32 devices in a mesh: seq: 16 (over z, y, x), tp: 2 (over core).
Axes of the slice: x: 2, y: 2, z: 4, core: 2. Of those that a mesh axis runs over, the one named last changes fastest.
Arguments:
- hidden_in: bfloat16 [4096, 2048], P('seq', 'tp'), may hold values from -6 to 6
- w_query: bfloat16 [2048, 2048], P(None, 'tp'), may hold values from -0.375 to 0.375
- w_keyval: bfloat16 [2048, 2, 2048], P(None, None, 'tp'), may hold values from -0.125 to 0.125
- w_out: bfloat16 [2048, 2048], P('tp'), may hold values from -0.125 to 0.125
- prompt_cache: bfloat16 [2048, 2, 2048], P('seq', None, 'tp'), may hold values from -160 to 160
- tail_cache: bfloat16 [32, 128, 2, 2048], P('seq', None, None, 'tp'), may hold values from -6 to 6
- tail_table: int32 [8, 4], replicated, may hold values from 0 to 31, as said below
- tail_len: int32 [8], replicated, may hold values from 1 to 512
- shared_len: int32 [1], replicated, may hold values from 1024 to 2048
Outputs:
- hidden_out: bfloat16 [4096, 2048], P('seq', 'tp')
- new_cache: bfloat16 [4096, 2, 2048], P('seq', None, 'tp')
Inputs may be any that keep to these rules, and one draw needn't show every extreme that they name: Row r lists each of the slots r * 4 to (r + 1) * 4 - 1 once; block j of request r's tail is held in slot tail_table[r, j].
All inputs are finite; a program needn't handle non-finite values.
Results may differ from a plain program's by a relative error of at most 0.013.
Values may be sent and summed in bfloat16 or wider, within the bound.
No kernel may reach another device: no remote copies, remote signals or barrier semaphores. Data moves between devices by JAX's collectives and lax.ppermute only.
A program may use at most 128 MiB of HBM per device.

v0:
```python
import jax
import jax.numpy as jnp
from jax import lax
from jax.sharding import PartitionSpec as P

HD = 128
REQ = 8


NEGATIVE = -1e30


def swapped(value, axis, stride):
    mask = 2**stride
    pairs = [(source, source ^ mask) for source in range(lax.axis_size(axis))]
    return lax.ppermute(value, axis, pairs)


def layer_norm(inputs):
    values = inputs.astype(jnp.float32)
    mean = jnp.mean(values, axis=-1, keepdims=True)
    centred = values - mean
    spread = jnp.mean(centred * centred, axis=-1, keepdims=True)
    return (centred * lax.rsqrt(spread + 1e-05)).astype(jnp.bfloat16)


def rotate(vectors, positions):
    half = vectors.shape[-1] // 2
    freqs = 10000.0 ** (-jnp.arange(half, dtype=jnp.float32) / half)
    angles = positions.astype(jnp.float32)[:, None, None] * freqs
    cosine = jnp.cos(angles)
    sine = jnp.sin(angles)
    first = vectors[..., :half]
    second = vectors[..., half:]
    return jnp.concatenate(
        [first * cosine - second * sine, second * cosine + first * sine], axis=-1
    )


def start_state(heads, queries, width):
    return (
        jnp.full((heads, queries), NEGATIVE, jnp.float32),
        jnp.zeros((heads, queries), jnp.float32),
        jnp.zeros((heads, queries, width), jnp.float32),
    )


def absorb(state, queries, keys, values, allowed):
    scores = jnp.einsum("hqd,khd->hqk", queries, keys, preferred_element_type=jnp.float32) * HD ** (
        -0.5
    )
    scores = jnp.where(allowed[None], scores, -jnp.inf)
    old_top, old_total, old_mixed = state
    new_top = jnp.maximum(old_top, jnp.max(scores, axis=2))
    factor = jnp.exp(old_top - new_top)
    weights = jnp.exp(scores - new_top[:, :, None])
    total = old_total * factor + jnp.sum(weights, axis=2)
    mixed = old_mixed * factor[:, :, None] + jnp.einsum(
        "hqk,khd->hqd", weights.astype(jnp.bfloat16), values, preferred_element_type=jnp.float32
    )
    return (new_top, total, mixed)


def combine(first, second):
    top = jnp.maximum(first[0], second[0])
    left = jnp.exp(first[0] - top)
    right = jnp.exp(second[0] - top)
    return (
        top,
        first[1] * left + second[1] * right,
        first[2] * left[:, :, None] + second[2] * right[:, :, None],
    )


def block_numbers(table_row, slot_ids):
    matches = table_row[None, :] == slot_ids[:, None]
    return jnp.sum(
        jnp.where(matches, jnp.arange(table_row.shape[0], dtype=jnp.int32)[None, :], 0), axis=1
    )


def local(
    hidden_in, w_query, w_keyval, w_out, prompt_cache, tail_cache, tail_table, tail_len, shared_len
):
    local_rows = hidden_in.shape[0]
    heads_here = w_query.shape[1] // HD
    group = lax.axis_size("seq") // REQ
    levels = group.bit_length() - 1
    seq_index = lax.axis_index("seq")
    request = seq_index // group
    member = seq_index % group
    offset = member * local_rows
    prompt_length = shared_len[0]
    own_length = lax.dynamic_index_in_dim(tail_len, request, 0, keepdims=False)
    table_row = lax.dynamic_index_in_dim(tail_table, request, 0, keepdims=False)
    slot_rows = tail_cache.shape[0]
    block_size = tail_cache.shape[1]
    whole = lax.all_gather(hidden_in, "tp", axis=1, tiled=True)
    normed = layer_norm(whole)
    query = jnp.dot(normed, w_query, preferred_element_type=jnp.float32).reshape(
        local_rows, heads_here, HD
    )
    projected = jnp.dot(
        normed, w_keyval.reshape(w_keyval.shape[0], -1), preferred_element_type=jnp.float32
    )
    projected = projected.reshape(local_rows, 2, heads_here, HD)
    positions = prompt_length + own_length + offset + jnp.arange(local_rows, dtype=jnp.int32)
    query = rotate(query, positions).astype(jnp.bfloat16)
    new_keys = rotate(projected[:, 0], positions).astype(jnp.bfloat16)
    new_values = projected[:, 1].astype(jnp.bfloat16)
    new_cache = jnp.stack(
        [new_keys.reshape(local_rows, -1), new_values.reshape(local_rows, -1)], axis=1
    )
    head_query = query.transpose(1, 0, 2)
    piece = lax.all_gather(prompt_cache, "seq", axis=0, tiled=True)
    length = piece.shape[0]
    allowed = (jnp.arange(length, dtype=jnp.int32) < prompt_length)[None, :]
    split = piece.reshape(length, 2, heads_here, HD)
    prompt_state = absorb(
        start_state(heads_here, local_rows, HD), head_query, split[:, 0], split[:, 1], allowed
    )
    packed = jnp.concatenate(
        [tail_cache.reshape(slot_rows * block_size, 2, tail_cache.shape[3]), new_cache], axis=0
    )
    per_member = packed.shape[0]
    for level in range(levels):
        other = swapped(packed, "seq", level)
        upper_half = seq_index // 2**level % 2 == 1
        packed = jnp.where(
            upper_half,
            jnp.concatenate([other, packed], axis=0),
            jnp.concatenate([packed, other], axis=0),
        )
    packed = packed.reshape(group, per_member, 2, heads_here, HD)
    tail_part = packed[:, : slot_rows * block_size].reshape(
        group * slot_rows * block_size, 2, heads_here, HD
    )
    fresh_part = packed[:, slot_rows * block_size :].reshape(group * local_rows, 2, heads_here, HD)
    slot_ids = request * group * slot_rows + jnp.arange(group * slot_rows, dtype=jnp.int32)
    tail_positions = (
        block_numbers(table_row, slot_ids)[:, None] * block_size
        + jnp.arange(block_size, dtype=jnp.int32)[None, :]
    ).reshape(-1)
    tail_allowed = (tail_positions < own_length)[None, :]
    fresh_allowed = (
        jnp.arange(group * local_rows, dtype=jnp.int32)[None, :]
        <= offset + jnp.arange(local_rows, dtype=jnp.int32)[:, None]
    )
    group_state = absorb(
        start_state(heads_here, local_rows, HD),
        head_query,
        tail_part[:, 0],
        tail_part[:, 1],
        tail_allowed,
    )
    group_state = absorb(group_state, head_query, fresh_part[:, 0], fresh_part[:, 1], fresh_allowed)
    final = combine(prompt_state, group_state)
    attended = (
        (final[2] / final[1][:, :, None])
        .astype(jnp.bfloat16)
        .transpose(1, 0, 2)
        .reshape(local_rows, -1)
    )
    summed = lax.psum_scatter(
        lax.dot_general(
            w_out, attended, (((0,), (1,)), ((), ())), preferred_element_type=jnp.float32
        ).astype(jnp.bfloat16),
        "tp",
        scatter_dimension=0,
        tiled=True,
    ).astype(jnp.float32)
    hidden_out = (hidden_in.astype(jnp.float32) + summed.T).astype(jnp.bfloat16)
    return (hidden_out, new_cache)


def solution(mesh):
    return jax.shard_map(
        local,
        mesh=mesh,
        in_specs=(
            P("seq", "tp"),
            P(None, "tp"),
            P(None, None, "tp"),
            P("tp", None),
            P("seq", None, "tp"),
            P("seq", None, None, "tp"),
            P(),
            P(),
            P(),
        ),
        out_specs=(P("seq", "tp"), P("seq", None, "tp")),
        check_vma=False,
    )
```

profile of v0, /device:TPU:0, one launch (start us, length us, event | category | flops | bytes accessed | tf_op | source)
XLA Modules:
  0.0 222.3 jit_solution(16281709333979913240)
XLA Ops:
  8.0 2.0 copy.36
  10.7 2.4 %copy.50 = bf16[256,2,1024]{0,2,1:T(8,128)(2,1)S(1)} copy(bf16[256,2,1024]{2,1,0:T(2,128)(2,1)} %bitcast.192) | data formatting | bytes 2097152 | tf_op jit(solution)/shard_map/reshape | solution.py:123
  13.1 10.1 %copy.58 = bf16[256,8,2,1024]{3,1,2,0:T(8,128)(2,1)} copy(bf16[256,8,2,1024]{3,2,1,0:T(2,128)(2,1)} %bitcast.178) | data formatting | bytes 16777216
  23.3 12.4 %copy.39 = bf16[2048,2048]{1,0:T(8,128)(2,1)} copy(bf16[2048,2048]{0,1:T(8,128)(2,1)} %bitcast.175) | data formatting | bytes 16777216 | tf_op jit(solution)/shard_map/dot_general | solution.py:103
  37.1 1.3 multiply_cosine_fusion
  38.3 1.4 convert_reduce_fusion
  39.8 1.6 fusion.16
  41.4 6.5 %fusion.62 = f32[256,2,8,128]{0,3,2,1:T(8,128)S(1)} fusion(bf16[2,8,128,2048]{3,2,1,0:T(8,128)(2,1)} %bitcast.179, bf16[256,2048]{1,0:T(8,128)(2,1)} %all-gather.3.cloned.1.call-done, f32[256]{0:T(256)S(1)} %add_rsqrt_fusion, f32[256]{0:T(256)S(1)} %broadcast_multiply_fusion), kind=kOutput, calls=%fused_computation.59 | convolution fusion | flops 2149580800 | bytes 11536384 | tf_op jit(solution)/shard_map/dot_general | solution.py:103
  49.9 1.3 convolution_bitcast_fusion
  51.4 1.6 copy.54
  53.4 1.9 subtract_convert_fusion
  57.6 2.8 %maximum_maximum_fusion = bf16[512,2,1024]{0,2,1:T(8,128)(2,1)} fusion(bf16[256,1,1024]{0,2,1:T(8,128)(2,1)} %bitcast.180, bf16[256,1,1024]{0,2,1:T(8,128)(2,1)S(1)} %bitcast.183, bf16[256,2,1024]{0,2,1:T(8,128)(2,1)S(1)} %copy.50), kind=kLoop, calls=%fused_computation.31 | loop fusion | flops 6291456 | bytes 4194304 | tf_op jit(solution)/shard_map/concatenate | solution.py:122
  60.3 2.9 %collective-permute-start = (bf16[512,2,1024]{0,2,1:T(8,128)(2,1)}, bf16[512,2,1024]{0,2,1:T(8,128)(2,1)}, u32[]{:S(2)}, u32[]{:S(2)}) collective-permute-start(bf16[512,2,1024]{0,2,1:T(8,128)(2,1)} %maximum_maximum_fusion), channel_id=1, source_target_pairs={{0,2},{2,0},{4,6},{6,4},{8,10},{10,8},{12,14},{14,12},{16,18},{18,... | collective-permute-start | bytes 6291464 | tf_op jit(solution)/shard_map/ppermute | solution.py:16
  64.6 58.7 %collective-permute-done = bf16[512,2,1024]{0,2,1:T(8,128)(2,1)} collective-permute-done((bf16[512,2,1024]{0,2,1:T(8,128)(2,1)}, bf16[512,2,1024]{0,2,1:T(8,128)(2,1)}, u32[]{:S(2)}, u32[]{:S(2)}) %collective-permute-start) | collective-permute-done | bytes 2097184 | tf_op jit(solution)/shard_map/ppermute | solution.py:16
  123.3 5.6 %maximum_select_fusion = bf16[1024,2,1024]{0,2,1:T(8,128)(2,1)} fusion(bf16[256,1,1024]{0,2,1:T(8,128)(2,1)S(1)} %bitcast.181, bf16[256,1,1024]{0,2,1:T(8,128)(2,1)S(1)} %bitcast.184, bf16[256,2,1024]{0,2,1:T(8,128)(2,1)S(1)} %copy.50, bf16[512,2,1024]{0,2,1:T(8,128)(2,1)} %collective-permute-done, pred[]{:T(512)S(6)} %eq.25), kind=kLoop, calls=%fused_computation.10 | loop fusion | flops 35651584 | bytes 8388609 | tf_op jit(solution)/shard_map/jit(_where)/select_n | solution.py:129
  128.9 7.9 %select_n.55 = bf16[2,512,2,8,128]{1,0,4,3,2:T(2,128)(2,1)} reshape(bf16[1024,2,1024]{0,2,1:T(8,128)(2,1)} %maximum_select_fusion) | data formatting | bytes 8388608 | tf_op jit(solution)/shard_map/jit(_where)/select_n | solution.py:129
  136.8 5.7 %fusion.88 = (bf16[2,256,2,8,128]{1,0,4,3,2:T(2,128)(2,1)}, bf16[2,256,2,8,128]{1,0,4,3,2:T(2,128)(2,1)S(1)}) fusion(bf16[2,512,2,8,128]{1,0,4,3,2:T(2,128)(2,1)} %select_n.55), kind=kLoop, calls=%fused_computation.114 | loop fusion | bytes 8388608 | tf_op jit(solution)/shard_map/slice | solution.py:135
  142.5 6.0 %copy.55 = bf16[2,256,2,8,128]{4,1,0,3,2:T(8,128)(2,1)} copy(bf16[2,256,2,8,128]{1,0,4,3,2:T(2,128)(2,1)} %get-tuple-element.6) | data formatting | bytes 4194304
  148.5 3.7 %copy.56 = bf16[2,256,2,8,128]{4,1,0,3,2:T(8,128)(2,1)} copy(bf16[2,256,2,8,128]{1,0,4,3,2:T(2,128)(2,1)S(1)} %get-tuple-element.7) | data formatting | bytes 4194304
  152.2 2.3 %fusion.7 = (f32[8,256]{1,0:T(8,128)S(1)}, f32[8,256,512]{2,1,0:T(8,128)S(1)}) fusion(pred[512]{0:T(512)(128)(4,1)S(1)} %fusion.78, bf16[512,2,8,128]{3,0,2,1:T(8,128)(2,1)} %bitcast.190, bf16[256,8,64]{2,0,1:T(8,128)(2,1)S(1)} %get-tuple-element.14, bf16[256,8,64]{2,0,1:T(8,128)(2,1)S(1)} %get-tuple-element.15), kind=kOutput, calls=%fused_computation.15 | convolution fusion | flops 272627712 | bytes 5775872 | tf_op jit(solution)/shard_map/hqd,khd->hqk/dot_general | solution.py:49
  156.4 1.4 copy-done.2
  157.8 2.8 %fusion.9 = (f32[8,256]{1,0:T(8,128)}, f32[8,256]{1,0:T(8,128)}) fusion(f32[8,256,512]{2,1,0:T(8,128)S(1)} %get-tuple-element.31, f32[8,256]{1,0:T(8,128)S(1)} %get-tuple-element.23, pred[512]{0:T(512)(128)(4,1)S(1)} %fusion.78, f32[8,256]{1,0:T(8,128)S(1)} %get-tuple-element.22, f32[8,256,512]{2,1,0:T(8,128)S(1)} %get-tuple-element.29, ...), kind=kLoop, calls=%fused_computation.17 | loop fusion | flops 8384512 | bytes 8552960 | tf_op jit(solution)/shard_map/reduce_sum | solution.py:57
  160.6 20.6 %all-gather.5.cloned.1.call-done = bf16[2048,2,1024]{0,2,1:T(8,128)(2,1)} async-done(((bf16[128,2,1024]{0,2,1:T(8,128)(2,1)}), bf16[2048,2,1024]{0,2,1:T(8,128)(2,1)}) %all-gather.5.cloned.1.call-update) | async-done | bytes 8388624 | tf_op jit(solution)/shard_map/all_gather | solution.py:115
  181.2 4.7 %fusion = (f32[8,256]{1,0:T(8,128)S(1)}, f32[8,256,2048]{2,1,0:T(8,128)S(1)}) fusion(pred[2048]{0:T(1024)(128)(4,1)S(1)} %iota_compare_fusion.1, bf16[2048,2,8,128]{0,3,2,1:T(8,128)(2,1)} %bitcast.186, bf16[256,8,64]{2,0,1:T(8,128)(2,1)S(1)} %get-tuple-element.14, bf16[256,8,64]{2,0,1:T(8,128)(2,1)S(1)} %get-tuple-element.15), kind=kOutput, calls=%fused_computation.2 | convolution fusion | flops 1087371264 | bytes 21506048 | tf_op jit(solution)/shard_map/hqd,khd->hqk/dot_general | solution.py:49
  186.0 3.8 %fusion.1 = f32[8,256]{1,0:T(8,128)S(1)} fusion(f32[8,256,2048]{2,1,0:T(8,128)S(1)} %get-tuple-element.27, f32[8,256]{1,0:T(8,128)S(1)} %broadcast_maximum_fusion.1, pred[2048]{0:T(1024)(128)(4,1)S(1)} %iota_compare_fusion.1), kind=kLoop, calls=%fused_computation.3 | loop fusion | flops 16775168 | bytes 16795648 | tf_op jit(solution)/shard_map/reduce_sum | solution.py:57
  189.9 2.4 %fusion.51 = f32[256,8,128]{0,2,1:T(8,128)} fusion(f32[8,256,512]{2,1,0:T(8,128)S(1)} %copy-done.4, f32[8,256]{1,0:T(8,128)S(1)} %copy-done.22, pred[512]{0:T(512)(128)(4,1)S(1)} %copy-done.24, bf16[512,2,8,128]{3,0,2,1:T(8,128)(2,1)S(1)} %bitcast.191, f32[256,8]{0,1:T(8,128)S(1)} %get-tuple-element.19, f32[256,8]{0,1:T(8,128)S(1)} %get-tuple-element.20), kind=kOutput, calls=%fused_computation.48 | convolution fusion | flops 273154048 | bytes 6316544 | tf_op jit(solution)/shard_map/hqk,khd->hqd/dot_general | solution.py:58
  192.3 6.4 %fusion.45 = f32[256,8,128]{0,2,1:T(8,128)} fusion(bf16[2048,2,8,128]{0,3,2,1:T(8,128)(2,1)} %bitcast.187, f32[8,256,2048]{2,1,0:T(8,128)S(1)} %get-tuple-element.27, f32[8,256]{1,0:T(8,128)S(1)} %broadcast_maximum_fusion.1, pred[2048]{0:T(1024)(128)(4,1)S(1)} %iota_compare_fusion.1, f32[256,8]{0,1:T(8,128)S(1)} %get-tuple-element.18, ...), kind=kOutput, calls=%fused_computation.46 | convolution fusion | flops 1091043328 | bytes 22046720 | tf_op jit(solution)/shard_map/hqk,khd->hqd/dot_general | solution.py:58
  198.7 4.7 %divide_convert_fusion = bf16[256,8,128]{0,2,1:T(8,128)(2,1)S(1)} fusion(f32[256,8,128]{0,2,1:T(8,128)} %fusion.45, f32[256,8,128]{0,2,1:T(8,128)} %fusion.51, bf16[512,2,8,128]{3,0,2,1:T(8,128)(2,1)} %bitcast.188, f32[8,256,512]{2,1,0:T(8,128)} %copy-done.2, f32[8,256]{1,0:T(8,128)S(1)} %copy-done.20, pred[256,512]{1,0:T(8,128)(4,1)S(1)} %copy-done.14, ...), kind=kOutput, calls=%fused_computation.63 | convolution fusion | flops 273940480 | bytes 8019968 | tf_op jit(solution)/shard_map/hqk,khd->hqd/dot_general | solution.py:58
  203.5 2.3 %fusion.15 = bf16[2048,256]{0,1:T(8,128)(2,1)} fusion(bf16[256,1024]{0,1:T(8,128)(2,1)S(1)} %bitcast.193, bf16[1024,2048]{1,0:T(8,128)(2,1)S(1)} %copy-done.26), kind=kOutput, calls=%fused_computation.26 | convolution fusion | flops 1074266112 | bytes 5767168 | tf_op jit(solution)/shard_map/dot_general | solution.py:165
  205.9 2.1 copy.46
  208.0 5.7 %reduce-scatter.2.cloned.1.call-done = bf16[1024,256]{0,1:T(8,128)(2,1)} async-done(((bf16[2048,256]{0,1:T(8,128)(2,1)}), bf16[1024,256]{0,1:T(8,128)(2,1)}) %reduce-scatter.2.cloned.1.call-update) | async-done | bytes 524304 | tf_op jit(solution)/shard_map/reduce_scatter | solution.py:164
  213.7 2.0 fusion.64
  (86 shorter events, 9.7 us)
Async XLA Ops:
  7.2 56.1 %copy-start = (s32[8,4]{0,1:T(4,128)S(1)}, s32[8,4]{0,1:T(4,128)}, u32[]{:S(2)}) copy-start(s32[8,4]{0,1:T(4,128)} %param.15) | copy-start | bytes 388
  7.2 31.1 %all-gather.3.cloned.1.call-start = ((), (), s32[]{:S(2)}) async-start(), calls=%async_computation.1 | async-start | bytes 1572864 | tf_op jit(solution)/shard_map/all_gather | solution.py:98
  7.9 173.3 %all-gather.5.cloned.1.call-start = ((), (), s32[]{:S(2)}) async-start(), calls=%async_computation.2 | async-start | bytes 8912896 | tf_op jit(solution)/shard_map/all_gather | solution.py:115
  10.0 203.7 %reduce-scatter.2.cloned.1.call-start = ((), (), s32[]{:S(2)}) async-start(), calls=%async_computation.3 | async-start | bytes 1572864 | tf_op jit(solution)/shard_map/reduce_scatter | solution.py:164
  23.3 12.4 %copy-start.27 = (s32[8]{0:T(128)S(1)}, s32[8]{0:T(128)}, u32[]{:S(2)}) copy-start(s32[8]{0:T(128)} %param.16) | copy-start | bytes 100
  41.4 8.4 %copy-start.11 = (bf16[256,2048]{1,0:T(8,128)(2,1)S(1)}, bf16[256,2048]{1,0:T(8,128)(2,1)}, u32[]{:S(2)}) copy-start(bf16[256,2048]{1,0:T(8,128)(2,1)} %all-gather.3.cloned.1.call-done) | copy-start | bytes 3145732
  41.4 8.4 %copy-start.25 = (bf16[2048,1024]{1,0:T(8,128)(2,1)S(1)}, bf16[2048,1024]{1,0:T(8,128)(2,1)}, u32[]{:S(2)}) copy-start(bf16[2048,1024]{1,0:T(8,128)(2,1)} %param.10) | copy-start | bytes 12582916
  55.2 68.1 %copy-start.5 = (bf16[256,1,8,128]{0,3,2,1:T(8,128)(2,1)S(1)}, bf16[256,1,8,128]{0,3,2,1:T(8,128)(2,1)}, u32[]{:S(2)}) copy-start(bf16[256,1,8,128]{0,3,2,1:T(8,128)(2,1)} %slice.96) | copy-start | bytes 1572868
  57.6 71.4 %copy-start.7 = (bf16[256,8,128]{0,2,1:T(8,128)(2,1)}, bf16[256,8,128]{0,2,1:T(8,128)(2,1)S(1)}, u32[]{:S(2)}) copy-start(bf16[256,8,128]{0,2,1:T(8,128)(2,1)S(1)} %copy.41) | copy-start | bytes 1572868
  60.3 62.9 %collective-permute-start = (bf16[512,2,1024]{0,2,1:T(8,128)(2,1)}, bf16[512,2,1024]{0,2,1:T(8,128)(2,1)}, u32[]{:S(2)}, u32[]{:S(2)}) collective-permute-start(bf16[512,2,1024]{0,2,1:T(8,128)(2,1)} %maximum_maximum_fusion), channel_id=1, source_target_pairs={{0,2},{2,0},{4,6},{6,4},{8,10},{10,8},{12,14},{14,12},{16,18},{18,... | collective-permute-start | bytes 6291464 | tf_op jit(solution)/shard_map/ppermute | solution.py:16
  64.4 91.2 %copy-start.23 = (pred[512]{0:T(512)(128)(4,1)}, pred[512]{0:T(512)(128)(4,1)S(1)}, u32[]{:S(2)}) copy-start(pred[512]{0:T(512)(128)(4,1)S(1)} %fusion.78) | copy-start | bytes 1540
  64.6 91.1 %copy-start.13 = (pred[256,512]{1,0:T(8,128)(4,1)}, pred[256,512]{1,0:T(8,128)(4,1)S(1)}, u32[]{:S(2)}) copy-start(pred[256,512]{1,0:T(8,128)(4,1)S(1)} %iota_compare_fusion) | copy-start | bytes 393220
  152.2 2.3 %copy-start.9 = (bf16[2,256,2,8,128]{4,1,0,3,2:T(8,128)(2,1)S(1)}, bf16[2,256,2,8,128]{4,1,0,3,2:T(8,128)(2,1)}, u32[]{:S(2)}) copy-start(bf16[2,256,2,8,128]{4,1,0,3,2:T(8,128)(2,1)} %copy.56) | copy-start | bytes 6291460
  154.5 1.9 copy-start.3
  155.6 2.2 copy-start.2
  155.6 5.0 %copy-start.15 = (f32[8,256]{1,0:T(8,128)}, f32[8,256]{1,0:T(8,128)S(1)}, u32[]{:S(2)}) copy-start(f32[8,256]{1,0:T(8,128)S(1)} %get-tuple-element.28) | copy-start | bytes 24580
  155.6 5.0 %copy-start.19 = (f32[8,256]{1,0:T(8,128)}, f32[8,256]{1,0:T(8,128)S(1)}, u32[]{:S(2)}) copy-start(f32[8,256]{1,0:T(8,128)S(1)} %get-tuple-element.22) | copy-start | bytes 24580
  155.7 5.0 %copy-start.21 = (f32[8,256]{1,0:T(8,128)}, f32[8,256]{1,0:T(8,128)S(1)}, u32[]{:S(2)}) copy-start(f32[8,256]{1,0:T(8,128)S(1)} %get-tuple-element.23) | copy-start | bytes 24580
  185.9 3.8 %copy-start.16 = (f32[8,256]{1,0:T(8,128)S(1)}, f32[8,256]{1,0:T(8,128)}, u32[]{:S(2)}) copy-start(f32[8,256]{1,0:T(8,128)} %copy-done.15) | copy-start | bytes 24580
  185.9 3.8 %copy-start.17 = (f32[8,256]{1,0:T(8,128)S(1)}, f32[8,256]{1,0:T(8,128)}, u32[]{:S(2)}) copy-start(f32[8,256]{1,0:T(8,128)} %get-tuple-element.32) | copy-start | bytes 24580
  186.0 3.8 %copy-start.18 = (f32[8,256]{1,0:T(8,128)S(1)}, f32[8,256]{1,0:T(8,128)}, u32[]{:S(2)}) copy-start(f32[8,256]{1,0:T(8,128)} %get-tuple-element.33) | copy-start | bytes 24580
  186.0 3.9 %copy-start.4 = (f32[8,256,512]{2,1,0:T(8,128)S(1)}, f32[8,256,512]{2,1,0:T(8,128)}, u32[]{:S(2)}) copy-start(f32[8,256,512]{2,1,0:T(8,128)} %copy-done.3) | copy-start | bytes 12582916
  186.0 3.9 %copy-start.10 = (bf16[2,256,2,8,128]{4,1,0,3,2:T(8,128)(2,1)S(1)}, bf16[2,256,2,8,128]{4,1,0,3,2:T(8,128)(2,1)}, u32[]{:S(2)}) copy-start(bf16[2,256,2,8,128]{4,1,0,3,2:T(8,128)(2,1)} %copy.55) | copy-start | bytes 6291460
  186.0 3.9 %copy-start.22 = (f32[8,256]{1,0:T(8,128)S(1)}, f32[8,256]{1,0:T(8,128)}, u32[]{:S(2)}) copy-start(f32[8,256]{1,0:T(8,128)} %copy-done.21) | copy-start | bytes 24580
  186.0 3.9 %copy-start.24 = (pred[512]{0:T(512)(128)(4,1)S(1)}, pred[512]{0:T(512)(128)(4,1)}, u32[]{:S(2)}) copy-start(pred[512]{0:T(512)(128)(4,1)} %copy-done.23) | copy-start | bytes 1540
  192.3 6.4 %copy-start.14 = (pred[256,512]{1,0:T(8,128)(4,1)S(1)}, pred[256,512]{1,0:T(8,128)(4,1)}, u32[]{:S(2)}) copy-start(pred[256,512]{1,0:T(8,128)(4,1)} %copy-done.13) | copy-start | bytes 393220
  192.3 6.4 %copy-start.20 = (f32[8,256]{1,0:T(8,128)S(1)}, f32[8,256]{1,0:T(8,128)}, u32[]{:S(2)}) copy-start(f32[8,256]{1,0:T(8,128)} %copy-done.19) | copy-start | bytes 24580
  198.7 4.7 %copy-start.26 = (bf16[1024,2048]{1,0:T(8,128)(2,1)S(1)}, bf16[1024,2048]{1,0:T(8,128)(2,1)}, u32[]{:S(2)}) copy-start(bf16[1024,2048]{1,0:T(8,128)(2,1)} %param.12) | copy-start | bytes 12582916
  203.4 2.3 %copy-start.6 = (bf16[256,1,8,128]{0,3,2,1:T(8,128)(2,1)S(1)}, bf16[256,1,8,128]{0,3,2,1:T(8,128)(2,1)}, u32[]{:S(2)}) copy-start(bf16[256,1,8,128]{0,3,2,1:T(8,128)(2,1)} %slice.96) | copy-start | bytes 1572868
  203.4 2.3 %copy-start.8 = (bf16[256,8,128]{0,2,1:T(8,128)(2,1)S(1)}, bf16[256,8,128]{0,2,1:T(8,128)(2,1)}, u32[]{:S(2)}) copy-start(bf16[256,8,128]{0,2,1:T(8,128)(2,1)} %copy-done.7) | copy-start | bytes 1572868
  203.5 12.3 %copy-start.1 = (s32[8,4]{0,1:T(4,128)S(1)}, s32[8,4]{0,1:T(4,128)}, u32[]{:S(2)}) copy-start(s32[8,4]{0,1:T(4,128)} %param.15) | copy-start | bytes 388
  205.7 8.0 %copy-start.12 = (bf16[256,1024]{1,0:T(8,128)(2,1)S(1)}, bf16[256,1024]{1,0:T(8,128)(2,1)}, u32[]{:S(2)}) copy-start(bf16[256,1024]{1,0:T(8,128)(2,1)} %param.9) | copy-start | bytes 1572868
Sparse Core Ops, SparseCore 0:
  9.6 11.7 all-gather.2
  24.6 156.5 all-gather.4
  205.9 7.7 reduce-scatter.1
where the time goes:
time: 223 us; the launch traced here: 222 us
  waiting for transfers between devices  85.7 us (38%)
  local copies, waits for them, and re-layouts  60.7 us (27%)
  matrix products  31.7 us (14%)
  other arithmetic  25.5 us (11%)
  between operations  15.5 us (7%)
  starting transfers between devices  3.03 us (1%)
    ppermute x1, waiting for transfers between devices, swapped(): return lax.ppermute(value, axis, pairs)  58.7 us
    unnamed x63, local copies, waits for them, and re-layouts  28 us
    all_gather x1, waiting for transfers between devices, local(): piece = lax.all_gather(prompt_cache, 'seq', axis=0, tiled=True)  20.6 us
    dot_general x3, matrix products, absorb(): jnp.einsum('hqk,khd->hqd', weights.astype(jnp.bfloat16), values, preferre...  13.5 us
    dot_general x1, local copies, waits for them, and re-layouts, local(): jnp.dot(normed, w_keyval.reshape(w_keyval.shape[0], -1), preferred_elemen...  12.4 us
    dot_general x3, matrix products, absorb(): jnp.einsum('hqd,khd->hqk', queries, keys, preferred_element_type=jnp.floa...  8.1 us
    select_n x1, local copies, waits for them, and re-layouts, local(): jnp.where(upper_half, jnp.concatenate([other, packed], axis=0), jnp.conca...  7.86 us
    reduce_sum x2, other arithmetic, absorb(): total = old_total * factor + jnp.sum(weights, axis=2)  6.57 us
  transfers between devices with their start and end apart: 4, of which 3 were waited for; matrix products, arithmetic and copies ran while one was open for 40% of the time, Pallas kernels for 0%

commit v1 on v0

v1 whole, which is shorter than its diff:
```python
import functools

import jax
import jax.numpy as jnp
import numpy as np
from jax import lax
from jax.experimental import pallas as pl
from jax.experimental.pallas import tpu as pltpu
from jax.sharding import PartitionSpec as P

HD = 128
REQ = 8
NEGATIVE = -1e30
SCALE = float(HD**-0.5 * np.log2(np.e))
STAT_ROWS = 16


def params(mib=48):
    return pltpu.CompilerParams(vmem_limit_bytes=mib * 2**20)


def cost(flops, moved, exps=0):
    return pl.CostEstimate(flops=int(flops), bytes_accessed=int(moved), transcendentals=int(exps))


def cycle_of(group):
    if group == 2:
        return [0, 2, 4, 6, 7, 5, 3, 1]
    return list(range(REQ))


def pick(table, index):
    result = jnp.int32(table[0])
    for place, value in enumerate(table):
        result = jnp.where(index == place, jnp.int32(value), result)
    return result


def swap(value, axis, mask):
    pairs = [(source, source ^ mask) for source in range(lax.axis_size(axis))]
    return lax.ppermute(value, axis, pairs)


def turn(value, cycle, group, way):
    count = len(cycle)
    pairs = []
    for place in range(count):
        source, target = cycle[place], cycle[(place + way) % count]
        pairs += [(source * group + m, target * group + m) for m in range(group)]
    return lax.ppermute(value, "seq", pairs)


def rotated(vectors, cosine, sine):
    return vectors * cosine + pltpu.roll(vectors, HD // 2, 1) * sine


def angles(positions):
    half = HD // 2
    freqs = 10000.0 ** (-jnp.arange(half, dtype=jnp.float32) / half)
    angle = positions.astype(jnp.float32)[:, None] * freqs
    cosine, sine = jnp.cos(angle), jnp.sin(angle)
    return (
        jnp.concatenate([cosine, cosine], axis=1),
        jnp.concatenate([-sine, sine], axis=1),
    )


def query_kernel(count, *refs):
    pieces = refs[:count]
    weight, cosine, sine, query, normed = refs[count:]
    columns = pieces[0].shape[1]

    @pl.when(pl.program_id(0) == 0)
    def _():
        index = lax.axis_index("tp")
        values = [piece[...].astype(jnp.float32) for piece in pieces]
        features = columns * count
        mean = sum(jnp.sum(v, axis=1, keepdims=True) for v in values) / features
        values = [v - mean for v in values]
        spread = sum(jnp.sum(v * v, axis=1, keepdims=True) for v in values) / features
        inverse = lax.rsqrt(spread + 1e-05)
        for shift, v in enumerate(values):
            start = pl.multiple_of((index ^ shift) * columns, columns)
            normed[:, pl.ds(start, columns)] = (v * inverse).astype(jnp.bfloat16)

    product = jnp.dot(normed[...], weight[...], preferred_element_type=jnp.float32)
    for start in range(0, product.shape[1], HD):
        query[:, start : start + HD] = rotated(
            product[:, start : start + HD], cosine[...], sine[...]
        ).astype(jnp.bfloat16)


def project_query(pieces, w_query, cosine, sine):
    rows, columns = pieces[0].shape
    depth, width = w_query.shape
    wide = min(width, 2 * HD)
    whole = lambda shape: pl.BlockSpec(shape, lambda i: (0, 0))
    return pl.pallas_call(
        functools.partial(query_kernel, len(pieces)),
        grid=(width // wide,),
        in_specs=[whole((rows, columns))] * len(pieces)
        + [pl.BlockSpec((depth, wide), lambda i: (0, i)), whole((rows, HD)), whole((rows, HD))],
        out_specs=[pl.BlockSpec((rows, wide), lambda i: (0, i)), whole((rows, depth))],
        out_shape=[
            jax.ShapeDtypeStruct((rows, width), jnp.bfloat16),
            jax.ShapeDtypeStruct((rows, depth), jnp.bfloat16),
        ],
        compiler_params=params(),
        cost_estimate=cost(2 * rows * depth * width, 2 * depth * width),
        name="project_query",
    )(*pieces, w_query, cosine, sine)


def keyval_kernel(normed, weight, cosine, sine, keys, values, cache, apart, woven):
    rows, depth = normed.shape
    chunk = apart.shape[0] // 2
    flat = weight.reshape(2 * depth, HD)
    total = jnp.zeros((rows, 2 * HD), jnp.float32)
    for start in range(0, depth, chunk):
        apart[...] = flat[2 * start : 2 * (start + chunk), :].astype(jnp.float32)
        both = jnp.concatenate(
            [apart[pl.ds(0, chunk, stride=2), :], apart[pl.ds(1, chunk, stride=2), :]], axis=1
        ).astype(jnp.bfloat16)
        total += jnp.dot(
            normed[:, start : start + chunk], both, preferred_element_type=jnp.float32
        )
    key = rotated(total[:, :HD], cosine[...], sine[...]).astype(jnp.bfloat16)
    value = total[:, HD:].astype(jnp.bfloat16)
    keys[...] = key
    values[...] = value
    woven[pl.ds(0, rows, stride=2), :] = key.astype(jnp.float32)
    woven[pl.ds(1, rows, stride=2), :] = value.astype(jnp.float32)
    cache.reshape(2 * rows, HD)[...] = woven[...].astype(jnp.bfloat16)


def project_keyval(normed, w_keyval, cosine, sine):
    rows, depth = normed.shape
    width = w_keyval.shape[2]
    chunk = min(depth, 512)
    whole = lambda shape: pl.BlockSpec(shape, lambda i: (0, 0))
    column = pl.BlockSpec((rows, HD), lambda i: (0, i))
    return pl.pallas_call(
        keyval_kernel,
        grid=(width // HD,),
        in_specs=[
            whole((rows, depth)),
            pl.BlockSpec((depth, 2, HD), lambda i: (0, 0, i)),
            whole((rows, HD)),
            whole((rows, HD)),
        ],
        out_specs=[column, column, pl.BlockSpec((rows, 2, HD), lambda i: (0, 0, i))],
        out_shape=[
            jax.ShapeDtypeStruct((rows, width), jnp.bfloat16),
            jax.ShapeDtypeStruct((rows, width), jnp.bfloat16),
            jax.ShapeDtypeStruct((rows, 2, width), jnp.bfloat16),
        ],
        scratch_shapes=[
            pltpu.VMEM((2 * chunk, HD), jnp.float32),
            pltpu.VMEM((2 * rows, HD), jnp.float32),
        ],
        compiler_params=params(),
        cost_estimate=cost(4 * rows * depth * width, 4 * depth * width),
        name="project_keyval",
    )(normed, w_keyval, cosine, sine)


def part_apart(block, apart, keys, values, start):
    count = block.shape[0]
    apart[: 2 * count, :] = block.reshape(2 * count, HD)[...].astype(jnp.float32)
    keys[start : start + count, :] = apart[pl.ds(0, count, stride=2), :].astype(jnp.bfloat16)
    values[start : start + count, :HD] = apart[pl.ds(1, count, stride=2), :].astype(jnp.bfloat16)


def column_of(stats, lane):
    place = lax.broadcasted_iota(jnp.int32, stats.shape, 1)
    return jnp.sum(jnp.where(place == lane, stats, 0.0), axis=1, keepdims=True)


def with_column(stats, lane, column):
    place = lax.broadcasted_iota(jnp.int32, stats.shape, 1)
    return jnp.where(place == lane, column, stats)


def row_of(column):
    count = column.shape[0]
    eye = lax.broadcasted_iota(jnp.int32, (HD, HD), 0) == lax.broadcasted_iota(
        jnp.int32, (HD, HD), 1
    )
    return [
        jnp.sum(jnp.where(eye, column[start : start + HD], 0.0), axis=0, keepdims=True)
        for start in range(0, count, HD)
    ]


def column_from(rows):
    eye = lax.broadcasted_iota(jnp.int32, (HD, HD), 0) == lax.broadcasted_iota(
        jnp.int32, (HD, HD), 1
    )
    return jnp.concatenate(
        [jnp.sum(jnp.where(eye, row, 0.0), axis=1, keepdims=True) for row in rows], axis=0
    )


def attend_kernel(spec, *refs):
    group, steps, piece, own, first, last = spec
    refs = list(refs)
    take = lambda count: [refs.pop(0) for _ in range(count)]
    lengths, shared, table = take(3)
    queries = take(group)
    blocks = take(len(steps))
    if own:
        tail, fresh_keys, fresh_values = take(3)
    if not first:
        old_total, old_stats = take(2)
    if last:
        result, result_stats = take(2)
        parts = take(group - 1)
    else:
        new_total, new_stats = take(2)
    keys, values, bias, apart = take(4)
    head = pl.program_id(0)
    rows = queries[0].shape[0]
    cycle = cycle_of(group)
    seq = lax.axis_index("seq")
    request, member = seq // group, seq % group
    place = pick(list(np.argsort(cycle)), request)
    count = 0
    edges = []
    if own:
        block_size = 128
        slots = tail.shape[0] // block_size
        for i in range(slots):
            wanted = seq * slots + i
            number = jnp.int32(0)
            for j in range(table.shape[1]):
                number = jnp.where(table[request, j] == wanted, jnp.int32(j), number)
            edges.append((count + i * block_size, block_size, number * block_size, lengths[request]))
        part_apart(tail, apart, keys, values, count)
        count += tail.shape[0]
    for (step, begin), block in zip(steps, blocks):
        origin = pick(cycle, lax.rem(place + step + REQ, REQ))
        size = block.shape[0]
        start = (origin * group + member) * piece + begin
        edges.append((count, size, start, shared[0]))
        part_apart(block, apart, keys, values, count)
        count += size
    plain = count
    if own:
        keys[count : count + rows, :] = fresh_keys[...]
        values[count : count + rows, :HD] = fresh_values[...]
        count += rows

    @pl.when(head == 0)
    def _():
        values[:, HD:] = jnp.ones((values.shape[0], HD), jnp.bfloat16)
        for begin, size, start, length in edges:
            positions = start + lax.broadcasted_iota(jnp.int32, (1, size), 1)
            bias[:, begin : begin + size] = jnp.broadcast_to(
                jnp.where(positions < length, 0.0, NEGATIVE), (8, size)
            )
        if last:
            result_stats[...] = jnp.zeros_like(result_stats)
        else:
            new_stats[...] = jnp.zeros_like(new_stats)

    across = (((1,), (1,)), ((), ()))
    for shift in range(group):
        scores = lax.dot_general(
            queries[shift][...], keys[...], across, preferred_element_type=jnp.float32
        )
        seen = scores[:, :plain] + bias[0:1, :]
        if own:
            mine = (member ^ shift) * rows + lax.broadcasted_iota(jnp.int32, (rows, rows), 0)
            theirs = member * rows + lax.broadcasted_iota(jnp.int32, (rows, rows), 1)
            causal = jnp.where(theirs <= mine, scores[:, plain:], NEGATIVE)
            seen = jnp.concatenate([seen, causal], axis=1)
        top = jnp.max(seen, axis=1, keepdims=True)
        span = slice(shift * rows, (shift + 1) * rows)
        if not first:
            stats = old_stats[span, :]
            old_top = column_of(stats, head)
            top = jnp.maximum(top, old_top)
        weights = jnp.exp2((seen - top) * SCALE).astype(jnp.bfloat16)
        mixed = jnp.dot(weights, values[...], preferred_element_type=jnp.float32)
        total, summed = mixed[:, :HD], mixed[:, HD:]
        if not first:
            factor = jnp.exp2((old_top - top) * SCALE)
            total = total + old_total[shift] * factor
            summed = summed + column_of(stats, head + 64) * factor
        if last:
            even = total / summed
            extent = top * SCALE + jnp.log2(summed)
            if shift == 0:
                result[...] = even
                result_stats[...] = with_column(result_stats[...], head, extent)
            else:
                part = parts[shift - 1]
                part[:rows, :] = even.astype(jnp.bfloat16)
                lines = row_of(extent)
                packed = []
                for _ in range(3):
                    rounded = [line.astype(jnp.bfloat16).astype(jnp.float32) for line in lines]
                    packed += rounded
                    lines = [line - r for line, r in zip(lines, rounded)]
                line_number = lax.broadcasted_iota(jnp.int32, (STAT_ROWS, HD), 0)
                tile = jnp.zeros((STAT_ROWS, HD), jnp.float32)
                for i, line in enumerate(packed):
                    tile = jnp.where(line_number == i, line, tile)
                part[rows:, :] = tile.astype(jnp.bfloat16)
        else:
            new_total[shift] = total
            marked = with_column(new_stats[span, :], head, top)
            new_stats[span, :] = with_column(marked, head + 64, summed)


def attend(tail_len, shared_len, tail_table, queries, steps, blocks, own, old, last, name):
    group = len(queries)
    rows, width = queries[0].shape
    column = pl.BlockSpec((rows, HD), lambda i: (0, i))
    smem = pl.BlockSpec(memory_space=pltpu.SMEM)
    triple = lambda value: pl.BlockSpec((value.shape[0], 2, HD), lambda i: (0, 0, i))
    total_spec = pl.BlockSpec((group, rows, HD), lambda i: (0, 0, i))
    stats_spec = pl.BlockSpec((group * rows, HD), lambda i: (0, 0))
    in_specs = [smem] * 3 + [column] * group + [triple(block) for block in blocks]
    operands = [tail_len, shared_len, tail_table, *queries, *blocks]
    plain = sum(block.shape[0] for block in blocks)
    longest = max(block.shape[0] for block in blocks)
    count = plain
    if own:
        in_specs += [triple(own[0]), column, column]
        operands += own
        plain += own[0].shape[0]
        longest = max(longest, own[0].shape[0])
        count = plain + rows
    if old:
        in_specs += [total_spec, stats_spec]
        operands += old
    if last:
        out_specs = [column, pl.BlockSpec((rows, HD), lambda i: (0, 0))]
        out_shape = [
            jax.ShapeDtypeStruct((rows, width), jnp.float32),
            jax.ShapeDtypeStruct((rows, HD), jnp.float32),
        ]
        out_specs += [pl.BlockSpec((rows + STAT_ROWS, HD), lambda i: (0, i))] * (group - 1)
        out_shape += [jax.ShapeDtypeStruct((rows + STAT_ROWS, width), jnp.bfloat16)] * (group - 1)
    else:
        out_specs = [total_spec, stats_spec]
        out_shape = [
            jax.ShapeDtypeStruct((group, rows, width), jnp.float32),
            jax.ShapeDtypeStruct((group * rows, HD), jnp.float32),
        ]
    scores = group * rows * count * (width // HD)
    return pl.pallas_call(
        functools.partial(attend_kernel, (group, steps, blocks[0].shape[0], bool(own), not old, last)),
        grid=(width // HD,),
        in_specs=in_specs,
        out_specs=out_specs,
        out_shape=out_shape,
        scratch_shapes=[
            pltpu.VMEM((count, HD), jnp.bfloat16),
            pltpu.VMEM((count, 2 * HD), jnp.bfloat16),
            pltpu.VMEM((8, plain), jnp.float32),
            pltpu.VMEM((2 * longest, HD), jnp.float32),
        ],
        compiler_params=params(),
        cost_estimate=cost(4 * scores * HD, 4 * count * width, scores),
        name=name,
    )(*operands)


def output_kernel(group, heads, *refs):
    refs = list(refs)
    result, result_stats = refs[:2]
    parts = refs[2 : 1 + group]
    weight, hidden = refs[1 + group : 3 + group]
    kept = refs[3 + group]
    sent = refs[4 + group : -1]
    attended = refs[-1]
    rows = result.shape[0]
    lines = rows // HD
    for head in range(heads):
        span = slice(head * HD, (head + 1) * HD)
        extents = [result_stats[:, head : head + 1]]
        mixes = [result[:, span]]
        for part in parts:
            tile = part[rows:, span].astype(jnp.float32)
            extents.append(
                column_from(
                    [
                        tile[i : i + 1] + tile[lines + i : lines + i + 1]
                        + tile[2 * lines + i : 2 * lines + i + 1]
                        for i in range(lines)
                    ]
                )
            )
            mixes.append(part[:rows, span].astype(jnp.float32))
        top = functools.reduce(jnp.maximum, extents)
        shares = [jnp.exp2(extent - top) for extent in extents]
        mixed = sum(mix * share for mix, share in zip(mixes, shares)) / sum(shares)
        attended[:, span] = mixed.astype(jnp.bfloat16)
    index = lax.axis_index("tp")
    columns = hidden.shape[1]
    wide = min(columns, 256)
    for shift in range(len(sent), -1, -1):
        for start in range(0, columns, wide):
            place = pl.multiple_of((index ^ shift) * columns + start, wide)
            product = jnp.dot(
                attended[...], weight[:, pl.ds(place, wide)], preferred_element_type=jnp.float32
            )
            if shift:
                sent[shift - 1][:, start : start + wide] = product.astype(jnp.bfloat16)
            else:
                kept[:, start : start + wide] = product + hidden[:, start : start + wide].astype(
                    jnp.float32
                )


def project_output(result, stats, parts, w_out, hidden, ways):
    rows, width = result.shape
    columns = hidden.shape[1]
    vmem = pl.BlockSpec(memory_space=pltpu.VMEM)
    return pl.pallas_call(
        functools.partial(output_kernel, 1 + len(parts), width // HD),
        in_specs=[vmem] * (4 + len(parts)),
        out_specs=[vmem] * ways,
        out_shape=[jax.ShapeDtypeStruct((rows, columns), jnp.float32)]
        + [jax.ShapeDtypeStruct((rows, columns), jnp.bfloat16)] * (ways - 1),
        scratch_shapes=[pltpu.VMEM((rows, width), jnp.bfloat16)],
        compiler_params=params(),
        cost_estimate=cost(2 * rows * width * columns * ways, 2 * width * columns * ways),
        name="project_output",
    )(result, stats, *parts, w_out, hidden)


def local(
    hidden_in, w_query, w_keyval, w_out, prompt_cache, tail_cache, tail_table, tail_len, shared_len
):
    rows = hidden_in.shape[0]
    group = lax.axis_size("seq") // REQ
    ways = lax.axis_size("tp")
    cycle = cycle_of(group)
    seq = lax.axis_index("seq")
    request = seq // group
    member = seq % group

    pieces = [hidden_in] + [swap(hidden_in, "tp", shift) for shift in range(1, ways)]
    ahead, behind = [prompt_cache], [prompt_cache]
    half = REQ // 2
    for _ in range(half - 1):
        ahead.append(turn(ahead[-1], cycle, group, 1))
        behind.append(turn(behind[-1], cycle, group, -1))
    middle = prompt_cache.shape[0] // 2
    far_low = turn(ahead[-1][:middle], cycle, group, 1)
    far_high = turn(behind[-1][middle:], cycle, group, -1)

    own_length = lax.dynamic_index_in_dim(tail_len, request, 0, keepdims=False)
    positions = (
        shared_len[0] + own_length + member * rows + jnp.arange(rows, dtype=jnp.int32)
    )
    cosine, sine = angles(positions)
    query, normed = project_query(pieces, w_query, cosine, sine)
    queries = [query] + [swap(query, "seq", shift) for shift in range(1, group)]
    fresh_keys, fresh_values, new_cache = project_keyval(normed, w_keyval, cosine, sine)

    tail = tail_cache.reshape(-1, 2, tail_cache.shape[3])
    numbers = (tail_len, shared_len, tail_table, queries)
    near = [(0, 0)] + [(way * step, 0) for step in (1, 2) for way in (-1, 1)]
    near_blocks = [prompt_cache, ahead[1], behind[1], ahead[2], behind[2]]
    state = attend(
        *numbers, near, near_blocks, [tail, fresh_keys, fresh_values], None, False, "attend_near"
    )
    far = [(-3, 0), (3, 0), (-half, 0), (half, middle)]
    far_blocks = [ahead[3], behind[3], far_low, far_high]
    result, stats, *parts = attend(*numbers, far, far_blocks, None, state, True, "attend_far")
    parts = [swap(part, "seq", shift + 1) for shift, part in enumerate(parts)]
    kept, *sent = project_output(result, stats, parts, w_out, hidden_in, ways)
    total = kept
    for shift, part in enumerate(sent):
        total = total + swap(part, "tp", shift + 1).astype(jnp.float32)
    return (total.astype(jnp.bfloat16), new_cache)


def solution(mesh):
    return jax.shard_map(
        local,
        mesh=mesh,
        in_specs=(
            P("seq", "tp"),
            P(None, "tp"),
            P(None, None, "tp"),
            P("tp", None),
            P("seq", None, "tp"),
            P("seq", None, None, "tp"),
            P(),
            P(),
            P(),
        ),
        out_specs=(P("seq", "tp"), P("seq", None, "tp")),
        check_vma=False,
    )
```

time: 223 us -> 105 us (0.47)
  local copies, waits for them, and re-layouts: 60.7 us -> 4.35 us
  waiting for transfers between devices: 85.7 us -> 33.6 us
  Pallas kernels: 0 us -> 50.5 us
  matrix products: 31.7 us -> 0 us
  other arithmetic: 25.5 us -> 1.62 us
  between operations: 15.5 us -> 2.1 us
  starting transfers between devices: 3.03 us -> 11.9 us
    pallas_call x0 -> x5, Pallas kernels: none -> 50.5 us  [the longest x2 26.7 us: attend(): pl.pallas_call(functools.partial(attend_kernel, (group, steps, blocks[0]....]
    dot_general x9 -> x0, matrix products: 31.7 us -> none  [the longest x3 13.5 us: absorb(): jnp.einsum('hqk,khd->hqd', weights.astype(jnp.bfloat16), values, preferre...]
    unnamed x63 -> x21, local copies, waits for them, and re-layouts: 28 us -> 2.75 us
    ppermute x1 -> x12, waiting for transfers between devices: 58.7 us -> 33.6 us  [the longest x8 21.6 us: turn(): return lax.ppermute(value, 'seq', pairs)]
    all_gather x2 -> x0, waiting for transfers between devices: 20.6 us -> none  [the longest x1 20.6 us: local(): piece = lax.all_gather(prompt_cache, 'seq', axis=0, tiled=True)]
    dot_general x1 -> x0, local copies, waits for them, and re-layouts: 12.4 us -> none  [local(): jnp.dot(normed, w_keyval.reshape(w_keyval.shape[0], -1), preferred_elemen...]
    reduce_sum x5 -> x0, other arithmetic: 9.84 us -> none  [the longest x2 6.57 us: absorb(): total = old_total * factor + jnp.sum(weights, axis=2)]
    ppermute x1 -> x12, starting transfers between devices: 2.92 us -> 11.9 us  [the longest x8 9.02 us: turn(): return lax.ppermute(value, 'seq', pairs)]
  transfers between devices with their start and end apart: 4 -> 12, of which waited for: 3 -> 7; matrix products, arithmetic and copies ran while one was open for 40% -> 2% of each run, Pallas kernels for 0% -> 33%
where the time goes in v1:
time: 105 us; the launch traced here: 104 us
  Pallas kernels  50.5 us (48%)
  waiting for transfers between devices  33.6 us (32%)
  starting transfers between devices  11.9 us (11%)
  local copies, waits for them, and re-layouts  4.35 us (4%)
  between operations  2.1 us (2%)
  other arithmetic  1.62 us (2%)
    pallas_call x2, Pallas kernels, attend(): pl.pallas_call(functools.partial(attend_kernel, (group, steps, blocks[0]....  26.7 us
    ppermute x8, waiting for transfers between devices, turn(): return lax.ppermute(value, 'seq', pairs)  21.6 us
    pallas_call x1, Pallas kernels, project_keyval(): pl.pallas_call(keyval_kernel, grid=(width // HD,), in_specs=[whole((rows,...  12.2 us
    ppermute x4, waiting for transfers between devices, swap(): return lax.ppermute(value, axis, pairs)  12 us
    ppermute x8, starting transfers between devices, turn(): return lax.ppermute(value, 'seq', pairs)  9.02 us
    pallas_call x1, Pallas kernels, project_output(): pl.pallas_call(functools.partial(output_kernel, 1 + len(parts), width //...  6.82 us
    pallas_call x1, Pallas kernels, project_query(): pl.pallas_call(functools.partial(query_kernel, len(pieces)), grid=(width...  4.77 us
    ppermute x4, starting transfers between devices, swap(): return lax.ppermute(value, axis, pairs)  2.91 us
  transfers between devices with their start and end apart: 12, of which 7 were waited for; matrix products, arithmetic and copies ran while one was open for 2% of the time, Pallas kernels for 33%

profile of v1, /device:TPU:0, one launch (start us, length us, event | category | flops | bytes accessed | tf_op | source)
XLA Modules:
  0.0 104.2 jit_solution(11818204118846913339)
XLA Ops:
  0.6 3.1 %collective-permute-start.2 = (bf16[128,2,1024]{2,1,0:T(2,128)(2,1)}, bf16[128,2,1024]{2,1,0:T(2,128)(2,1)S(1)}, u32[]{:S(2)}, u32[]{:S(2)}) collective-permute-start(bf16[128,2,1024]{2,1,0:T(2,128)(2,1)} %refs_5_.1), channel_id=1, source_target_pairs={{0,8},{2,10},{8,16},{10,18},{16,24},{18,26},{24,28},{26,30},{28,20... | collective-permute-start | bytes 1572872 | tf_op jit(solution)/shard_map/ppermute | solution.py:50
  3.7 12.1 %collective-permute-done.2.refs_6_ = bf16[128,2,1024]{2,1,0:T(2,128)(2,1)S(1)} collective-permute-done((bf16[128,2,1024]{2,1,0:T(2,128)(2,1)}, bf16[128,2,1024]{2,1,0:T(2,128)(2,1)S(1)}, u32[]{:S(2)}, u32[]{:S(2)}) %collective-permute-start.2) | collective-permute-done | bytes 524320 | tf_op jit(solution)/shard_map/ppermute | solution.py:50
  15.8 1.8 %collective-permute-start.3 = (bf16[128,2,1024]{2,1,0:T(2,128)(2,1)S(1)}, bf16[128,2,1024]{2,1,0:T(2,128)(2,1)}, u32[]{:S(2)}, u32[]{:S(2)}) collective-permute-start(bf16[128,2,1024]{2,1,0:T(2,128)(2,1)S(1)} %collective-permute-done.2.refs_6_), channel_id=1, source_target_pairs={{0,8},{2,10},{8,16},{10,18},{16,24},{18,26},{24,28},{26,30},{28,20... | collective-permute-start | bytes 1572872 | tf_op jit(solution)/shard_map/ppermute | solution.py:50
  17.6 0.8 copy-done.5
  18.4 0.2 collective-permute-start.6
  18.6 0.8 copy-done.7
  20.1 1.2 %dynamic_slice.4 = s32[1]{0:T(128)} dynamic-slice(s32[8]{0:T(128)} %refs_0_.5, s32[]{:T(128)S(6)} %select_n.16), dynamic_slice_sizes={1} | dynamic-slice | bytes 12 | tf_op jit(solution)/shard_map/jit(dynamic_index_in_dim)/dynamic_slice | solution.py:456
  22.0 0.5 fusion
  22.6 6.5 %collective-permute-done.3.refs_8_ = bf16[128,2,1024]{2,1,0:T(2,128)(2,1)} collective-permute-done((bf16[128,2,1024]{2,1,0:T(2,128)(2,1)S(1)}, bf16[128,2,1024]{2,1,0:T(2,128)(2,1)}, u32[]{:S(2)}, u32[]{:S(2)}) %collective-permute-start.3) | collective-permute-done | bytes 524320 | tf_op jit(solution)/shard_map/ppermute | solution.py:50
  29.0 1.5 %collective-permute-start.4 = (bf16[128,2,1024]{2,1,0:T(2,128)(2,1)}, bf16[128,2,1024]{2,1,0:T(2,128)(2,1)S(1)}, u32[]{:S(2)}, u32[]{:S(2)}) collective-permute-start(bf16[128,2,1024]{2,1,0:T(2,128)(2,1)} %collective-permute-done.3.refs_8_), channel_id=1, source_target_pairs={{0,8},{2,10},{8,16},{10,18},{16,24},{18,26},{24,28},{26,30},{28,20... | collective-permute-start | bytes 1572872 | tf_op jit(solution)/shard_map/ppermute | solution.py:50
  30.5 0.5 collective-permute-done.6.refs_9_
  31.0 0.5 collective-permute-start.7
  31.6 0.1 pad_maximum_fusion
  31.7 1.0 copy-done
  32.8 4.8 %project_query.1 = (bf16[256,1024]{1,0:T(8,128)(2,1)S(1)}, bf16[256,2048]{1,0:T(8,128)(2,1)S(1)}) custom-call(bf16[256,1024]{1,0:T(8,128)(2,1)S(1)} %copy-done, bf16[256,1024]{1,0:T(8,128)(2,1)S(1)} %collective-permute-done.refs_1_, bf16[2048,1024]{1,0:T(8,128)(2,1)} %refs_2_.3, f32[256,128]{1,0:T(8,128)S(1)} %get-tuple-element.29.refs_3_.cosine, ...), custom_call_target="tpu_custom_call" | custom-call | flops 1073741824 | bytes 4194304 | tf_op jit(solution)/shard_map/project_query/pallas_call | solution.py:98
  37.5 1.5 %collective-permute-start.1 = (bf16[256,1024]{1,0:T(8,128)(2,1)S(1)}, bf16[256,1024]{1,0:T(8,128)(2,1)S(1)}, u32[]{:S(2)}, u32[]{:S(2)}) collective-permute-start(bf16[256,1024]{1,0:T(8,128)(2,1)S(1)} %get-tuple-element.14.refs_3_), channel_id=1, source_target_pairs={{0,2},{2,0},{4,6},{6,4},{8,10},{10,8},{12,14},{14,12},{16,18},{18,... | collective-permute-start | bytes 1572872 | tf_op jit(solution)/shard_map/ppermute | solution.py:41
  39.0 0.1 copy.12.refs_2_
  39.1 2.3 %collective-permute-done.4.refs_5_ = bf16[128,2,1024]{2,1,0:T(2,128)(2,1)S(1)} collective-permute-done((bf16[128,2,1024]{2,1,0:T(2,128)(2,1)}, bf16[128,2,1024]{2,1,0:T(2,128)(2,1)S(1)}, u32[]{:S(2)}, u32[]{:S(2)}) %collective-permute-start.4) | collective-permute-done | bytes 524320 | tf_op jit(solution)/shard_map/ppermute | solution.py:50
  41.4 0.2 slice.8
  41.6 1.2 %collective-permute-start.8 = (bf16[64,2,1024]{2,1,0:T(2,128)(2,1)S(1)}, bf16[64,2,1024]{2,1,0:T(2,128)(2,1)S(1)}, u32[]{:S(2)}, u32[]{:S(2)}) collective-permute-start(bf16[64,2,1024]{2,1,0:T(2,128)(2,1)S(1)} %slice.8), channel_id=1, source_target_pairs={{0,8},{2,10},{8,16},{10,18},{16,24},{18,26},{24,28},{26,30},{28,20... | collective-permute-start | bytes 786440 | tf_op jit(solution)/shard_map/ppermute | solution.py:50
  42.8 0.3 collective-permute-done.7.refs_6_
  43.1 0.2 slice.9
  43.2 0.7 collective-permute-start.9
  43.9 12.2 %project_keyval.1 = (bf16[256,1024]{1,0:T(8,128)(2,1)S(1)}, bf16[256,1024]{1,0:T(8,128)(2,1)S(1)}, bf16[256,2,1024]{2,1,0:T(2,128)(2,1)}) custom-call(bf16[256,2048]{1,0:T(8,128)(2,1)S(1)} %get-tuple-element.15.normed, bf16[2048,2,1024]{2,1,0:T(2,128)(2,1)} %weight.1, f32[256,128]{1,0:T(8,128)S(1)} %get-tuple-element.29.refs_3_.cosine, ...), custom_call_target="tpu_custom_call" | custom-call | flops 2147483648 | bytes 8388608 | tf_op jit(solution)/shard_map/project_keyval/pallas_call | solution.py:142
  56.2 17.1 %attend_near.1 = (f32[2,256,1024]{2,1,0:T(8,128)}, f32[512,128]{1,0:T(8,128)S(1)}) custom-call(s32[8]{0:T(128)S(1)} %copy-done.2, s32[1]{0:T(128)S(6)} %copy.13.refs_1_, s32[8,4]{1,0:T(8,128)S(1)} %copy.12.refs_2_, bf16[256,1024]{1,0:T(8,128)(2,1)S(1)} %get-tuple-element.14.refs_3_, bf16[256,1024]{1,0:T(8,128)(2,1)S(1)} %collective-permute-done.1.refs_4_, ...), custom_call_target="tpu_custom_call" | custom-call | flops 2415919104 | bytes 4718592 | tf_op jit(solution)/shard_map/attend_near/pallas_call | solution.py:353
  73.3 9.6 %attend_far.1 = (f32[256,1024]{1,0:T(8,128)S(1)}, f32[256,128]{1,0:T(8,128)S(1)}, bf16[272,1024]{1,0:T(8,128)(2,1)S(1)}) custom-call(s32[8]{0:T(128)S(1)} %copy-done.2, s32[1]{0:T(128)S(6)} %copy.13.refs_1_, s32[8,4]{1,0:T(8,128)S(1)} %copy.12.refs_2_, bf16[256,1024]{1,0:T(8,128)(2,1)S(1)} %get-tuple-element.14.refs_3_, ...), custom_call_target="tpu_custom_call" | custom-call | flops 805306368 | bytes 1572864 | tf_op jit(solution)/shard_map/attend_far/pallas_call | solution.py:353
  83.0 1.4 %collective-permute-start.10 = (bf16[272,1024]{1,0:T(8,128)(2,1)S(1)}, bf16[272,1024]{1,0:T(8,128)(2,1)S(1)}, u32[]{:S(2)}, u32[]{:S(2)}) collective-permute-start(bf16[272,1024]{1,0:T(8,128)(2,1)S(1)} %get-tuple-element.22), channel_id=1, source_target_pairs={{0,2},{2,0},{4,6},{6,4},{8,10},{10,8},{12,14},{14,12},{16,18},{18,... | collective-permute-start | bytes 1671176 | tf_op jit(solution)/shard_map/ppermute | solution.py:41
  84.3 10.1 %collective-permute-done.10.refs_2_ = bf16[272,1024]{1,0:T(8,128)(2,1)S(1)} collective-permute-done((bf16[272,1024]{1,0:T(8,128)(2,1)S(1)}, bf16[272,1024]{1,0:T(8,128)(2,1)S(1)}, u32[]{:S(2)}, u32[]{:S(2)}) %collective-permute-start.10) | collective-permute-done | bytes 557088 | tf_op jit(solution)/shard_map/ppermute | solution.py:41
  94.4 6.8 %project_output.1 = (f32[256,1024]{1,0:T(8,128)S(1)}, bf16[256,1024]{1,0:T(8,128)(2,1)S(1)}) custom-call(f32[256,1024]{1,0:T(8,128)S(1)} %get-tuple-element.20.refs_0_, f32[256,128]{1,0:T(8,128)S(1)} %get-tuple-element.21.refs_1_, bf16[272,1024]{1,0:T(8,128)(2,1)S(1)} %collective-permute-done.10.refs_2_, bf16[1024,2048]{1,0:T(8,128)(2,1)} %refs_3_.1, ...), custom_call_target="tpu_custom_call" | custom-call | flops 1073741824 | bytes 4194304 | tf_op jit(solution)/shard_map/project_output/pallas_call | solution.py:422
  101.3 0.1 collective-permute-start.11
  101.3 1.9 %collective-permute-done.11 = bf16[256,1024]{1,0:T(8,128)(2,1)S(1)} collective-permute-done((bf16[256,1024]{1,0:T(8,128)(2,1)S(1)}, bf16[256,1024]{1,0:T(8,128)(2,1)S(1)}, u32[]{:S(2)}, u32[]{:S(2)}) %collective-permute-start.11) | collective-permute-done | bytes 524320 | tf_op jit(solution)/shard_map/ppermute | solution.py:41
  103.2 0.9 add_convert_fusion
  (26 shorter events, 0.1 us)
Async XLA Ops:
  0.6 38.4 %copy-start.9 = (s32[8,4]{0,1:T(4,128)S(1)}, s32[8,4]{0,1:T(4,128)}, u32[]{:S(2)}) copy-start(s32[8,4]{0,1:T(4,128)} %param.15) | copy-start | bytes 388
  0.6 15.2 %collective-permute-start.2 = (bf16[128,2,1024]{2,1,0:T(2,128)(2,1)}, bf16[128,2,1024]{2,1,0:T(2,128)(2,1)S(1)}, u32[]{:S(2)}, u32[]{:S(2)}) collective-permute-start(bf16[128,2,1024]{2,1,0:T(2,128)(2,1)} %refs_5_.1), channel_id=1, source_target_pairs={{0,8},{2,10},{8,16},{10,18},{16,24},{18,26},{24,28},{26,30},{28,20... | collective-permute-start | bytes 1572872 | tf_op jit(solution)/shard_map/ppermute | solution.py:50
  3.7 14.7 %collective-permute-start.5 = (bf16[128,2,1024]{2,1,0:T(2,128)(2,1)}, bf16[128,2,1024]{2,1,0:T(2,128)(2,1)S(1)}, u32[]{:S(2)}, u32[]{:S(2)}) collective-permute-start(bf16[128,2,1024]{2,1,0:T(2,128)(2,1)} %refs_5_.1), channel_id=1, source_target_pairs={{0,4},{2,6},{8,0},{10,2},{16,8},{18,10},{24,16},{26,18},{28,24},{3... | collective-permute-start | bytes 1572872 | tf_op jit(solution)/shard_map/ppermute | solution.py:50
  15.8 13.2 %collective-permute-start.3 = (bf16[128,2,1024]{2,1,0:T(2,128)(2,1)S(1)}, bf16[128,2,1024]{2,1,0:T(2,128)(2,1)}, u32[]{:S(2)}, u32[]{:S(2)}) collective-permute-start(bf16[128,2,1024]{2,1,0:T(2,128)(2,1)S(1)} %collective-permute-done.2.refs_6_), channel_id=1, source_target_pairs={{0,8},{2,10},{8,16},{10,18},{16,24},{18,26},{24,28},{26,30},{28,20... | collective-permute-start | bytes 1572872 | tf_op jit(solution)/shard_map/ppermute | solution.py:50
  17.6 0.8 copy-start.5
  18.4 12.6 %collective-permute-start.6 = (bf16[128,2,1024]{2,1,0:T(2,128)(2,1)S(1)}, bf16[128,2,1024]{2,1,0:T(2,128)(2,1)}, u32[]{:S(2)}, u32[]{:S(2)}) collective-permute-start(bf16[128,2,1024]{2,1,0:T(2,128)(2,1)S(1)} %collective-permute-done.5.refs_7_), channel_id=1, source_target_pairs={{0,4},{2,6},{8,0},{10,2},{16,8},{18,10},{24,16},{26,18},{28,24},{3... | collective-permute-start | bytes 1572872 | tf_op jit(solution)/shard_map/ppermute | solution.py:50
  18.6 0.8 copy-start.7
  19.4 12.3 %collective-permute-start = (bf16[256,1024]{1,0:T(8,128)(2,1)}, bf16[256,1024]{1,0:T(8,128)(2,1)S(1)}, u32[]{:S(2)}, u32[]{:S(2)}) collective-permute-start(bf16[256,1024]{1,0:T(8,128)(2,1)} %refs_4_.1), channel_id=1, source_target_pairs={{0,1},{1,0},{2,3},{3,2},{4,5},{5,4},{6,7},{7,6},{8,9},{9,8},{10,11... | collective-permute-start | bytes 1572872 | tf_op jit(solution)/shard_map/ppermute | solution.py:41
  29.0 12.4 %collective-permute-start.4 = (bf16[128,2,1024]{2,1,0:T(2,128)(2,1)}, bf16[128,2,1024]{2,1,0:T(2,128)(2,1)S(1)}, u32[]{:S(2)}, u32[]{:S(2)}) collective-permute-start(bf16[128,2,1024]{2,1,0:T(2,128)(2,1)} %collective-permute-done.3.refs_8_), channel_id=1, source_target_pairs={{0,8},{2,10},{8,16},{10,18},{16,24},{18,26},{24,28},{26,30},{28,20... | collective-permute-start | bytes 1572872 | tf_op jit(solution)/shard_map/ppermute | solution.py:50
  31.0 12.1 %collective-permute-start.7 = (bf16[128,2,1024]{2,1,0:T(2,128)(2,1)}, bf16[128,2,1024]{2,1,0:T(2,128)(2,1)S(1)}, u32[]{:S(2)}, u32[]{:S(2)}) collective-permute-start(bf16[128,2,1024]{2,1,0:T(2,128)(2,1)} %collective-permute-done.6.refs_9_), channel_id=1, source_target_pairs={{0,4},{2,6},{8,0},{10,2},{16,8},{18,10},{24,16},{26,18},{28,24},{3... | collective-permute-start | bytes 1572872 | tf_op jit(solution)/shard_map/ppermute | solution.py:50
  31.7 1.0 %copy-start = (bf16[256,1024]{1,0:T(8,128)(2,1)S(1)}, bf16[256,1024]{1,0:T(8,128)(2,1)}, u32[]{:S(2)}) copy-start(bf16[256,1024]{1,0:T(8,128)(2,1)} %refs_4_.1) | copy-start | bytes 1572868
  37.5 18.6 %collective-permute-start.1 = (bf16[256,1024]{1,0:T(8,128)(2,1)S(1)}, bf16[256,1024]{1,0:T(8,128)(2,1)S(1)}, u32[]{:S(2)}, u32[]{:S(2)}) collective-permute-start(bf16[256,1024]{1,0:T(8,128)(2,1)S(1)} %get-tuple-element.14.refs_3_), channel_id=1, source_target_pairs={{0,2},{2,0},{4,6},{6,4},{8,10},{10,8},{12,14},{14,12},{16,18},{18,... | collective-permute-start | bytes 1572872 | tf_op jit(solution)/shard_map/ppermute | solution.py:41
  41.6 31.7 %collective-permute-start.8 = (bf16[64,2,1024]{2,1,0:T(2,128)(2,1)S(1)}, bf16[64,2,1024]{2,1,0:T(2,128)(2,1)S(1)}, u32[]{:S(2)}, u32[]{:S(2)}) collective-permute-start(bf16[64,2,1024]{2,1,0:T(2,128)(2,1)S(1)} %slice.8), channel_id=1, source_target_pairs={{0,8},{2,10},{8,16},{10,18},{16,24},{18,26},{24,28},{26,30},{28,20... | collective-permute-start | bytes 786440 | tf_op jit(solution)/shard_map/ppermute | solution.py:50
  43.2 30.1 %collective-permute-start.9 = (bf16[64,2,1024]{2,1,0:T(2,128)(2,1)S(1)}, bf16[64,2,1024]{2,1,0:T(2,128)(2,1)S(1)}, u32[]{:S(2)}, u32[]{:S(2)}) collective-permute-start(bf16[64,2,1024]{2,1,0:T(2,128)(2,1)S(1)} %slice.9), channel_id=1, source_target_pairs={{0,4},{2,6},{8,0},{10,2},{16,8},{18,10},{24,16},{26,18},{28,24},{3... | collective-permute-start | bytes 786440 | tf_op jit(solution)/shard_map/ppermute | solution.py:50
  43.9 12.2 %copy-start.2 = (s32[8]{0:T(128)S(1)}, s32[8]{0:T(128)}, u32[]{:S(2)}) copy-start(s32[8]{0:T(128)} %refs_0_.5) | copy-start | bytes 100
  43.9 12.2 %copy-start.3 = (bf16[2,128,2,1024]{3,2,1,0:T(2,128)(2,1)S(1)}, bf16[2,128,2,1024]{3,2,1,0:T(2,128)(2,1)}, u32[]{:S(2)}) copy-start(bf16[2,128,2,1024]{3,2,1,0:T(2,128)(2,1)} %param.14) | copy-start | bytes 3145732
  43.9 12.2 %copy-start.4 = (bf16[128,2,1024]{2,1,0:T(2,128)(2,1)S(1)}, bf16[128,2,1024]{2,1,0:T(2,128)(2,1)}, u32[]{:S(2)}) copy-start(bf16[128,2,1024]{2,1,0:T(2,128)(2,1)} %refs_5_.1) | copy-start | bytes 1572868
  43.9 12.3 %copy-start.6 = (bf16[128,2,1024]{2,1,0:T(2,128)(2,1)S(1)}, bf16[128,2,1024]{2,1,0:T(2,128)(2,1)}, u32[]{:S(2)}) copy-start(bf16[128,2,1024]{2,1,0:T(2,128)(2,1)} %copy-done.5) | copy-start | bytes 1572868
  43.9 12.3 %copy-start.8 = (bf16[128,2,1024]{2,1,0:T(2,128)(2,1)S(1)}, bf16[128,2,1024]{2,1,0:T(2,128)(2,1)}, u32[]{:S(2)}) copy-start(bf16[128,2,1024]{2,1,0:T(2,128)(2,1)} %copy-done.7) | copy-start | bytes 1572868
  73.3 21.1 %copy-start.1 = (bf16[256,1024]{1,0:T(8,128)(2,1)S(1)}, bf16[256,1024]{1,0:T(8,128)(2,1)}, u32[]{:S(2)}) copy-start(bf16[256,1024]{1,0:T(8,128)(2,1)} %refs_4_.1) | copy-start | bytes 1572868
  83.0 11.5 %collective-permute-start.10 = (bf16[272,1024]{1,0:T(8,128)(2,1)S(1)}, bf16[272,1024]{1,0:T(8,128)(2,1)S(1)}, u32[]{:S(2)}, u32[]{:S(2)}) collective-permute-start(bf16[272,1024]{1,0:T(8,128)(2,1)S(1)} %get-tuple-element.22), channel_id=1, source_target_pairs={{0,2},{2,0},{4,6},{6,4},{8,10},{10,8},{12,14},{14,12},{16,18},{18,... | collective-permute-start | bytes 1671176 | tf_op jit(solution)/shard_map/ppermute | solution.py:41
  101.3 2.0 %collective-permute-start.11 = (bf16[256,1024]{1,0:T(8,128)(2,1)S(1)}, bf16[256,1024]{1,0:T(8,128)(2,1)S(1)}, u32[]{:S(2)}, u32[]{:S(2)}) collective-permute-start(bf16[256,1024]{1,0:T(8,128)(2,1)S(1)} %get-tuple-element.24), channel_id=1, source_target_pairs={{0,1},{1,0},{2,3},{3,2},{4,5},{5,4},{6,7},{7,6},{8,9},{9,8},{10,11... | collective-permute-start | bytes 1572872 | tf_op jit(solution)/shard_map/ppermute | solution.py:41

commit v2 on v1

v2 whole, which is shorter than its diff:
```python
import functools

import jax
import jax.numpy as jnp
import numpy as np
from jax import lax
from jax.experimental import pallas as pl
from jax.experimental.pallas import tpu as pltpu
from jax.sharding import PartitionSpec as P

HD = 128
REQ = 8
NEGATIVE = -1e30
SCALE = float(HD**-0.5 * np.log2(np.e))
STAT_ROWS = 16


def params(mib=24):
    return pltpu.CompilerParams(vmem_limit_bytes=mib * 2**20)


def cost(flops, moved, exps=0):
    return pl.CostEstimate(flops=int(flops), bytes_accessed=int(moved), transcendentals=int(exps))


def cycle_of(group):
    if group == 2:
        return [0, 2, 4, 6, 7, 5, 3, 1]
    return list(range(REQ))


def pick(table, index):
    result = jnp.int32(table[0])
    for place, value in enumerate(table):
        result = jnp.where(index == place, jnp.int32(value), result)
    return result


def swap(value, axis, mask):
    pairs = [(source, source ^ mask) for source in range(lax.axis_size(axis))]
    return lax.ppermute(value, axis, pairs)


def turn(value, cycle, group, way):
    count = len(cycle)
    pairs = []
    for place in range(count):
        source, target = cycle[place], cycle[(place + way) % count]
        pairs += [(source * group + m, target * group + m) for m in range(group)]
    return lax.ppermute(value, "seq", pairs)


def rotated(vectors, cosine, sine):
    return vectors * cosine + pltpu.roll(vectors, HD // 2, 1) * sine


def angles(positions):
    half = HD // 2
    freqs = 10000.0 ** (-jnp.arange(half, dtype=jnp.float32) / half)
    angle = positions.astype(jnp.float32)[:, None] * freqs
    cosine, sine = jnp.cos(angle), jnp.sin(angle)
    return (
        jnp.concatenate([cosine, cosine], axis=1),
        jnp.concatenate([-sine, sine], axis=1),
    )


def lanes(start, count=HD):
    return pl.ds(pl.multiple_of(start, HD), count)


def after(value, *others):
    return lax.optimization_barrier((value, *others))[0]


VMEM = pl.BlockSpec(memory_space=pltpu.VMEM)
SMEM = pl.BlockSpec(memory_space=pltpu.SMEM)


def part_kernel(*refs):
    *pieces, apart, result_scratch = refs
    result = apart
    for i, piece in enumerate(pieces):
        count = piece.shape[0]
        scratch = result_scratch.at[i]
        scratch[...] = piece.reshape(2 * count, HD)[...].astype(jnp.float32)
        span = slice(i * HD, (i + 1) * HD)
        for j in range(2):
            result[j, :, span] = scratch[pl.ds(j, count, stride=2), :].astype(jnp.bfloat16)


def part_keyval(block, name):
    count, _, width = block.shape
    heads = width // HD
    specs = [
        pl.BlockSpec((count, 2, HD), functools.partial(lambda i, _: (0, 0, i), i))
        for i in range(heads)
    ]
    return pl.pallas_call(
        part_kernel,
        grid=(1,),
        in_specs=specs,
        out_specs=pl.BlockSpec((2, count, width), lambda _: (0, 0, 0)),
        out_shape=jax.ShapeDtypeStruct((2, count, width), jnp.bfloat16),
        scratch_shapes=[pltpu.VMEM((heads, 2 * count, HD), jnp.float32)],
        compiler_params=params(16),
        cost_estimate=cost(0, 8 * count * width),
        name=name,
    )(*[block] * heads)


def query_kernel(*refs):
    *pieces, weight, cosine, sine, query, normed = refs
    rows, columns = pieces[0].shape
    index = lax.axis_index("tp")
    features = columns * len(pieces)
    values = [piece[...].astype(jnp.float32) for piece in pieces]
    mean = sum(jnp.sum(v, axis=1, keepdims=True) for v in values) / features
    values = [v - mean for v in values]
    spread = sum(jnp.sum(v * v, axis=1, keepdims=True) for v in values) / features
    inverse = lax.rsqrt(spread + 1e-05)
    for shift, v in enumerate(values):
        normed[:, lanes((index ^ shift) * columns, columns)] = (v * inverse).astype(jnp.bfloat16)
    width = weight.shape[1]
    wide = min(width, 2 * HD)
    for base in range(0, width, wide):
        product = jnp.dot(
            normed[...], weight[:, base : base + wide], preferred_element_type=jnp.float32
        )
        for start in range(0, wide, HD):
            query[:, base + start : base + start + HD] = rotated(
                product[:, start : start + HD], cosine[...], sine[...]
            ).astype(jnp.bfloat16)


def project_query(pieces, w_query, cosine, sine):
    rows, columns = pieces[0].shape
    depth, width = w_query.shape
    return pl.pallas_call(
        query_kernel,
        in_specs=[VMEM] * (len(pieces) + 3),
        out_specs=[VMEM] * 2,
        out_shape=[
            jax.ShapeDtypeStruct((rows, width), jnp.bfloat16),
            jax.ShapeDtypeStruct((rows, depth), jnp.bfloat16),
        ],
        compiler_params=params(24),
        cost_estimate=cost(2 * rows * depth * width, 2 * depth * width),
        name="project_query",
    )(*pieces, w_query, cosine, sine)


def keyval_kernel(together, *refs):
    normed = refs[0]
    weights = refs[1 : 1 + together]
    cosine, sine, keys, values, cache, spaced = refs[1 + together : 7 + together]
    woven = refs[7 + together]
    rows, depth = normed.shape

    @pl.when(pl.program_id(0) == 0)
    def _():
        source = lax.broadcasted_iota(jnp.int32, (HD, 2 * HD), 0)
        target = lax.broadcasted_iota(jnp.int32, (HD, 2 * HD), 1)
        for j in range(2):
            spread = jnp.where(target == 2 * source + j, 1.0, 0.0).astype(jnp.bfloat16)
            for start in range(0, depth, HD):
                spaced[j * rows : (j + 1) * rows, 2 * start : 2 * (start + HD)] = jnp.dot(
                    normed[:, start : start + HD], spread, preferred_element_type=jnp.float32
                ).astype(jnp.bfloat16)

    flat = [weight.reshape(2 * depth, HD)[...] for weight in weights]
    total = jnp.dot(
        spaced[...], jnp.concatenate(flat, axis=1), preferred_element_type=jnp.float32
    )
    for i in range(together):
        span = slice(i * HD, (i + 1) * HD)
        key = rotated(total[:rows, span], cosine[...], sine[...]).astype(jnp.bfloat16)
        value = total[rows:, span].astype(jnp.bfloat16)
        keys[:, span] = key
        values[:, span] = value
        place = woven.at[i]
        place[pl.ds(0, rows, stride=2), :] = key.astype(jnp.float32)
        place[pl.ds(1, rows, stride=2), :] = value.astype(jnp.float32)
        cache[:, :, span] = place[...].astype(jnp.bfloat16).reshape(rows, 2, HD)


def project_keyval(normed, w_keyval, cosine, sine):
    rows, depth = normed.shape
    width = w_keyval.shape[2]
    together = min(2, width // HD)
    wide = together * HD
    whole = lambda shape: pl.BlockSpec(shape, lambda i: (0, 0))
    column = pl.BlockSpec((rows, wide), lambda i: (0, i))
    weights = [
        pl.BlockSpec((depth, 2, HD), functools.partial(lambda j, i: (0, 0, together * i + j), j))
        for j in range(together)
    ]
    return pl.pallas_call(
        functools.partial(keyval_kernel, together),
        grid=(width // wide,),
        in_specs=[whole((rows, depth)), *weights, whole((rows, HD)), whole((rows, HD))],
        out_specs=[column, column, pl.BlockSpec((rows, 2, wide), lambda i: (0, 0, i))],
        out_shape=[
            jax.ShapeDtypeStruct((rows, width), jnp.bfloat16),
            jax.ShapeDtypeStruct((rows, width), jnp.bfloat16),
            jax.ShapeDtypeStruct((rows, 2, width), jnp.bfloat16),
        ],
        scratch_shapes=[
            pltpu.VMEM((2 * rows, 2 * depth), jnp.bfloat16),
            pltpu.VMEM((together, 2 * rows, HD), jnp.float32),
        ],
        compiler_params=params(24),
        cost_estimate=cost(4 * rows * depth * width, 4 * depth * width),
        name="project_keyval",
    )(normed, *[w_keyval] * together, cosine, sine)


def column_of(stats, lane):
    place = lax.broadcasted_iota(jnp.int32, stats.shape, 1)
    return jnp.sum(jnp.where(place == lane, stats, 0.0), axis=1, keepdims=True)


def with_column(stats, lane, column):
    place = lax.broadcasted_iota(jnp.int32, stats.shape, 1)
    return jnp.where(place == lane, column, stats)


def attend_kernel(spec, *refs):
    group, steps, piece, own, first, last = spec
    refs = list(refs)
    take = lambda count: [refs.pop(0) for _ in range(count)]
    lengths, shared, table = take(3)
    queries = take(group)
    blocks = take(len(steps))
    if own:
        tail, fresh_keys, fresh_values = take(3)
    if not first:
        old_mix, old_stats = take(2)
    if last:
        result, result_stats = take(2)
        parts = take(group - 1)
        stats = take(1)[0]
    else:
        mix, stats = take(2)
    bias = take(1)[0]
    if own:
        causal = take(1)[0]
    rows, width = queries[0].shape
    heads = width // HD
    cycle = cycle_of(group)
    seq = lax.axis_index("seq")
    request, member = seq // group, seq % group
    place = pick(list(np.argsort(cycle)), request)
    edges = []
    count = 0
    if own:
        block_size = 128
        slots = tail.shape[1] // block_size
        for i in range(slots):
            wanted = seq * slots + i
            number = jnp.int32(0)
            for j in range(table.shape[1]):
                number = jnp.where(table[request, j] == wanted, jnp.int32(j), number)
            edges.append((count, block_size, number * block_size, lengths[request]))
            count += block_size
    for (step, begin), block in zip(steps, blocks):
        origin = pick(cycle, lax.rem(place + step + REQ, REQ))
        size = block.shape[1]
        edges.append((count, size, (origin * group + member) * piece + begin, shared[0]))
        count += size
    for begin, size, start, length in edges:
        positions = start + lax.broadcasted_iota(jnp.int32, (size, HD), 0)
        lane = lax.broadcasted_iota(jnp.int32, (size, HD), 1)
        bias[begin : begin + size, :] = jnp.where(
            (positions >= length) & (lane == 0), NEGATIVE, 0.0
        ).astype(jnp.bfloat16)
    if own:
        bias[count : count + rows, :] = jnp.zeros((rows, HD), jnp.bfloat16)
        theirs = member * rows + lax.broadcasted_iota(jnp.int32, (rows, rows), 1)
        for shift in range(group):
            mine = (member ^ shift) * rows + lax.broadcasted_iota(jnp.int32, (rows, rows), 0)
            causal[shift * rows : (shift + 1) * rows, :] = jnp.where(theirs <= mine, 0.0, NEGATIVE)
    stats[...] = jnp.zeros_like(stats)
    unit = jnp.where(
        lax.broadcasted_iota(jnp.int32, (group * rows, HD), 1) == 0, 1.0, 0.0
    ).astype(jnp.bfloat16)
    across = (((1,), (1,)), ((), ()))

    def one_head(head):
        span = lanes(head * HD)
        query = jnp.concatenate([q[:, span] for q in queries], axis=0)
        keys = [block[0, :, span] for block in blocks]
        values = [block[1, :, span] for block in blocks]
        if own:
            keys = [tail[0, :, span], *keys, fresh_keys[:, span]]
            values = [tail[1, :, span], *values, fresh_values[:, span]]
        keys = jnp.concatenate(keys, axis=0)
        values = jnp.concatenate(values, axis=0)
        scores = lax.dot_general(
            jnp.concatenate([query, unit], axis=1),
            jnp.concatenate([keys, bias[...]], axis=1),
            across,
            preferred_element_type=jnp.float32,
        )
        if own:
            scores = jnp.concatenate([scores[:, :count], scores[:, count:] + causal[...]], axis=1)
        top = jnp.max(scores, axis=1, keepdims=True)
        if not first:
            old = column_of(old_stats[...], head)
            top = jnp.maximum(top, old * (1.0 / SCALE))
        weights = jnp.exp2((scores - top) * SCALE).astype(jnp.bfloat16)
        mixed = jnp.dot(
            weights,
            jnp.concatenate([values, jnp.ones_like(values)], axis=1),
            preferred_element_type=jnp.float32,
        )
        total, summed = mixed[:, :HD], mixed[:, HD:]
        if not first:
            factor = jnp.exp2(old - top * SCALE)
            total = total + old_mix[:, span] * factor
            summed = summed + factor
        even = total / summed
        stats[...] = with_column(stats[...], head, top * SCALE + jnp.log2(summed))
        if last:
            result[:, span] = even[:rows]
            for shift in range(1, group):
                parts[shift - 1][:rows, span] = even[shift * rows : (shift + 1) * rows].astype(
                    jnp.bfloat16
                )
        else:
            mix[:, span] = even

    together = min(2, heads)

    def some_heads(i, _):
        for j in range(together):
            one_head(together * i + j)
        return 0

    lax.fori_loop(0, heads // together, some_heads, 0)
    if last:
        result_stats[...] = stats[:rows, :]
        for shift in range(1, group):
            line = jnp.transpose(stats[shift * rows : (shift + 1) * rows, :])[:heads, :]
            packed = []
            for _ in range(3):
                rounded = line.astype(jnp.bfloat16).astype(jnp.float32)
                packed.append(rounded)
                line = line - rounded
            gap = -3 * heads % STAT_ROWS
            if gap:
                packed.append(jnp.zeros((gap, rows), jnp.float32))
            packed = jnp.concatenate(packed, axis=0).astype(jnp.bfloat16)
            for j in range(packed.shape[0] // STAT_ROWS):
                parts[shift - 1][rows:, j * rows : (j + 1) * rows] = packed[
                    j * STAT_ROWS : (j + 1) * STAT_ROWS
                ]


def attend(tail_len, shared_len, tail_table, queries, steps, blocks, own, old, last, name):
    group = len(queries)
    rows, width = queries[0].shape
    operands = [tail_len, shared_len, tail_table, *queries, *blocks]
    piece = blocks[0].shape[1]
    plain = sum(block.shape[1] for block in blocks)
    if own:
        operands += own
        plain += own[0].shape[1]
    if old:
        operands += old
    count = plain + (rows if own else 0)
    flat_stats = jax.ShapeDtypeStruct((group * rows, HD), jnp.float32)
    scratch = [pltpu.VMEM((count, HD), jnp.bfloat16)]
    if own:
        scratch.append(pltpu.VMEM((group * rows, rows), jnp.float32))
    if last:
        out_shape = [
            jax.ShapeDtypeStruct((rows, width), jnp.float32),
            jax.ShapeDtypeStruct((rows, HD), jnp.float32),
        ] + [jax.ShapeDtypeStruct((rows + STAT_ROWS, width), jnp.bfloat16)] * (group - 1)
        scratch.insert(0, pltpu.VMEM((group * rows, HD), jnp.float32))
    else:
        out_shape = [jax.ShapeDtypeStruct((group * rows, width), jnp.float32), flat_stats]
    scores = group * rows * count * (width // HD)
    return pl.pallas_call(
        functools.partial(
            attend_kernel, (group, steps, piece, bool(own), not old, last)
        ),
        in_specs=[SMEM] * 3 + [VMEM] * (len(operands) - 3),
        out_specs=[VMEM] * len(out_shape),
        out_shape=out_shape,
        scratch_shapes=scratch,
        compiler_params=params(32),
        cost_estimate=cost(4 * scores * HD, 4 * count * width, scores),
        name=name,
    )(*operands)


def combine_kernel(*refs):
    result, stats, *refs = refs
    *parts, weight, attended, sent = refs[: len(refs)]
    rows, width = result.shape
    heads = width // HD
    extents = [stats[...]]
    for part in parts:
        tile = part[rows:, :].astype(jnp.float32)
        groups = -(-3 * heads // STAT_ROWS)
        lines = jnp.concatenate(
            [tile[:, j * rows : (j + 1) * rows] for j in range(groups)], axis=0
        )
        line = sum(lines[i * heads : (i + 1) * heads] for i in range(3))
        line = jnp.concatenate([line, jnp.zeros((HD - heads, rows), jnp.float32)], axis=0)
        extents.append(jnp.transpose(line))
    top = functools.reduce(jnp.maximum, extents)
    shares = [jnp.exp2(extent - top) for extent in extents]
    whole = sum(shares)
    shares = [share / whole for share in shares]
    for head in range(heads):
        span = slice(head * HD, (head + 1) * HD)
        mixes = [result[:, span]] + [part[:rows, span].astype(jnp.float32) for part in parts]
        mixed = sum(mix * share[:, head : head + 1] for mix, share in zip(mixes, shares))
        attended[:, span] = mixed.astype(jnp.bfloat16)
    index = lax.axis_index("tp")
    ways = sent.shape[0] + 1
    columns = weight.shape[1] // ways
    for shift in range(1, ways):
        sent[shift - 1] = jnp.dot(
            attended[...],
            weight[:, lanes((index ^ shift) * columns, columns)],
            preferred_element_type=jnp.float32,
        ).astype(jnp.bfloat16)


def combine(result, stats, parts, w_out, ways):
    rows, width = result.shape
    columns = w_out.shape[1] // ways
    return pl.pallas_call(
        combine_kernel,
        in_specs=[VMEM] * (3 + len(parts)),
        out_specs=[VMEM] * 2,
        out_shape=[
            jax.ShapeDtypeStruct((rows, width), jnp.bfloat16),
            jax.ShapeDtypeStruct((ways - 1, rows, columns), jnp.bfloat16),
        ],
        compiler_params=params(20),
        cost_estimate=cost(2 * rows * width * columns * (ways - 1), 2 * width * w_out.shape[1]),
        name="combine_send",
    )(result, stats, *parts, w_out)


def keep_kernel(attended, weight, hidden, kept):
    columns = hidden.shape[1]
    product = jnp.dot(
        attended[...],
        weight[:, lanes(lax.axis_index("tp") * columns, columns)],
        preferred_element_type=jnp.float32,
    )
    kept[...] = product + hidden[...].astype(jnp.float32)


def keep(attended, w_out, hidden):
    rows, width = attended.shape
    return pl.pallas_call(
        keep_kernel,
        in_specs=[VMEM] * 3,
        out_specs=VMEM,
        out_shape=jax.ShapeDtypeStruct(hidden.shape, jnp.float32),
        compiler_params=params(20),
        cost_estimate=cost(2 * rows * width * hidden.shape[1], 2 * width * w_out.shape[1]),
        name="keep_own",
    )(attended, w_out, hidden)


def local(
    hidden_in, w_query, w_keyval, w_out, prompt_cache, tail_cache, tail_table, tail_len, shared_len
):
    rows = hidden_in.shape[0]
    group = lax.axis_size("seq") // REQ
    ways = lax.axis_size("tp")
    cycle = cycle_of(group)
    seq = lax.axis_index("seq")
    request = seq // group
    member = seq % group
    half = REQ // 2
    middle = prompt_cache.shape[0] // 2

    pieces = [hidden_in] + [swap(hidden_in, "tp", shift) for shift in range(1, ways)]
    prompt = part_keyval(prompt_cache, "part_prompt")
    ahead, behind = [prompt], [prompt]

    def step(*others):
        for blocks, way in ((ahead, 1), (behind, -1)):
            blocks.append(turn(after(blocks[-1], *others), cycle, group, way))

    step()
    own_length = lax.dynamic_index_in_dim(tail_len, request, 0, keepdims=False)
    positions = shared_len[0] + own_length + member * rows + jnp.arange(rows, dtype=jnp.int32)
    cosine, sine = angles(positions)
    query, normed = project_query(pieces, w_query, cosine, sine)
    queries = [query] + [swap(query, "seq", shift) for shift in range(1, group)]
    fresh_keys, fresh_values, new_cache = project_keyval(normed, w_keyval, cosine, sine)
    step(fresh_keys)
    tail = part_keyval(tail_cache.reshape(-1, 2, tail_cache.shape[3]), "part_tail")

    numbers = (tail_len, shared_len, tail_table, queries)
    near = [(0, 0), (-1, 0), (1, 0)]
    state = attend(
        *numbers,
        near,
        [prompt, ahead[1], behind[1]],
        [tail, fresh_keys, fresh_values],
        None,
        False,
        "attend_near",
    )
    step(state[1])
    state = attend(
        *numbers, [(-2, 0), (2, 0)], [ahead[2], behind[2]], None, state, False, "attend_mid"
    )
    far_low = turn(after(ahead[3], state[1])[:, :middle], cycle, group, 1)
    far_high = turn(after(behind[3], state[1])[:, middle:], cycle, group, -1)
    far = [(-3, 0), (3, 0), (-half, 0), (half, middle)]
    far_blocks = [ahead[3], behind[3], far_low, far_high]
    result, stats, *parts = attend(*numbers, far, far_blocks, None, state, True, "attend_far")
    parts = [swap(part, "seq", shift + 1) for shift, part in enumerate(parts)]
    attended, sent = combine(result, stats, parts, w_out, ways)
    received = [swap(sent[shift - 1], "tp", shift) for shift in range(1, ways)]
    total = keep(attended, w_out, hidden_in)
    for part in received:
        total = total + part.astype(jnp.float32)
    return (total.astype(jnp.bfloat16), new_cache)


def solution(mesh):
    return jax.shard_map(
        local,
        mesh=mesh,
        in_specs=(
            P("seq", "tp"),
            P(None, "tp"),
            P(None, None, "tp"),
            P("tp", None),
            P("seq", None, "tp"),
            P("seq", None, None, "tp"),
            P(),
            P(),
            P(),
        ),
        out_specs=(P("seq", "tp"), P("seq", None, "tp")),
        check_vma=False,
    )
```

time: 105 us -> 91.6 us (0.87)
  Pallas kernels: 50.5 us -> 40.9 us
  waiting for transfers between devices: 33.6 us -> 25.7 us
  local copies, waits for them, and re-layouts: 4.35 us -> 8.93 us
    pallas_call x5 -> x9, Pallas kernels: 50.5 us -> 40.9 us  [the longest x3 19.6 us: attend(): pl.pallas_call(functools.partial(attend_kernel, (group, steps, piece, boo...]
    ppermute x8, waiting for transfers between devices: 21.6 us -> 13.3 us  [turn(): return lax.ppermute(value, 'seq', pairs)]
    unnamed x21 -> x25, local copies, waits for them, and re-layouts: 2.75 us -> 8.31 us
  transfers between devices with their start and end apart: 12 -> 12, of which waited for: 7 -> 6; matrix products, arithmetic and copies ran while one was open for 2% -> 2% of each run, Pallas kernels for 33% -> 36%
where the time goes in v2:
time: 91.6 us; the launch traced here: 91.3 us
  Pallas kernels  40.9 us (45%)
  waiting for transfers between devices  25.7 us (28%)
  starting transfers between devices  12 us (13%)
  local copies, waits for them, and re-layouts  8.93 us (10%)
  between operations  2.13 us (2%)
  other arithmetic  1.63 us (2%)
    pallas_call x3, Pallas kernels, attend(): pl.pallas_call(functools.partial(attend_kernel, (group, steps, piece, boo...  19.6 us
    pallas_call x1, Pallas kernels, project_keyval(): pl.pallas_call(functools.partial(keyval_kernel, together), grid=(width //...  14.1 us
    ppermute x8, waiting for transfers between devices, turn(): return lax.ppermute(value, 'seq', pairs)  13.3 us
    ppermute x4, waiting for transfers between devices, swap(): return lax.ppermute(value, axis, pairs)  12.4 us
    ppermute x8, starting transfers between devices, turn(): return lax.ppermute(value, 'seq', pairs)  9.27 us
    unnamed x25, local copies, waits for them, and re-layouts  8.31 us
    pallas_call x2, Pallas kernels, part_keyval(): pl.pallas_call(part_kernel, grid=(1,), in_specs=specs, out_specs=pl.Block...  2.99 us
    ppermute x4, starting transfers between devices, swap(): return lax.ppermute(value, axis, pairs)  2.7 us
  transfers between devices with their start and end apart: 12, of which 6 were waited for; matrix products, arithmetic and copies ran while one was open for 2% of the time, Pallas kernels for 36%

profile of v2, /device:TPU:0, one launch (start us, length us, event | category | flops | bytes accessed | tf_op | source)
XLA Modules:
  0.0 91.3 jit_solution(16149052201095797389)
XLA Ops:
  0.6 1.0 %copy-done.1 = bf16[128,2,1024]{2,1,0:T(2,128)(2,1)S(1)} copy-done((bf16[128,2,1024]{2,1,0:T(2,128)(2,1)S(1)}, bf16[128,2,1024]{2,1,0:T(2,128)(2,1)}, u32[]{:S(2)}) %copy-start.1) | copy-done | bytes 524312
  1.7 1.0 %part_prompt.1.refs_5_ = bf16[2,128,1024]{2,1,0:T(8,128)(2,1)S(1)} custom-call(bf16[128,2,1024]{2,1,0:T(2,128)(2,1)S(1)} %copy-done.1, bf16[128,2,1024]{2,1,0:T(2,128)(2,1)S(1)} %copy-done.1, bf16[128,2,1024]{2,1,0:T(2,128)(2,1)S(1)} %copy-done.1, bf16[128,2,1024]{2,1,0:T(2,128)(2,1)S(1)} %copy-done.1, bf16[128,2,1024]{2,1,0:T(2,128)(2,1)S(1)} %copy-done.1, ...), custom_call_target="tpu_custom_call" | custom-call | bytes 1048576 | tf_op jit(solution)/shard_map/part_prompt/pallas_call | solution.py:99
  2.7 3.1 %collective-permute-start.2 = (bf16[2,128,1024]{2,1,0:T(8,128)(2,1)S(1)}, bf16[2,128,1024]{2,1,0:T(8,128)(2,1)}, u32[]{:S(2)}, u32[]{:S(2)}) collective-permute-start(bf16[2,128,1024]{2,1,0:T(8,128)(2,1)S(1)} %part_prompt.1.refs_5_), channel_id=1, source_target_pairs={{0,8},{2,10},{8,16},{10,18},{16,24},{18,26},{24,28},{26,30},{28,20... | collective-permute-start | bytes 1572872 | tf_op jit(solution)/shard_map/ppermute | solution.py:50
  6.4 0.6 dynamic_slice.4
  7.7 0.5 fusion
  8.4 2.2 %copy-done.4 = bf16[2048,1024]{1,0:T(8,128)(2,1)S(1)} copy-done((bf16[2048,1024]{1,0:T(8,128)(2,1)S(1)}, bf16[2048,1024]{1,0:T(8,128)(2,1)}, u32[]{:S(2)}) %copy-start.4) | copy-done | bytes 4194328
  10.6 2.0 %project_query.1 = (bf16[256,1024]{1,0:T(8,128)(2,1)S(1)}, bf16[256,2048]{1,0:T(8,128)(2,1)S(1)}) custom-call(bf16[256,1024]{1,0:T(8,128)(2,1)S(1)} %copy-done.5, bf16[256,1024]{1,0:T(8,128)(2,1)S(1)} %collective-permute-done.refs_1_, bf16[2048,1024]{1,0:T(8,128)(2,1)S(1)} %copy-done.4, f32[256,128]{1,0:T(8,128)S(1)} %get-tuple-element.45.refs_3_, ...), custom_call_target="tpu_custom_call" | custom-call | flops 1073741824 | bytes 4194304 | tf_op jit(solution)/shard_map/project_query/pallas_call | solution.py:139
  12.6 2.0 %collective-permute-start.1 = (bf16[256,1024]{1,0:T(8,128)(2,1)S(1)}, bf16[256,1024]{1,0:T(8,128)(2,1)S(1)}, u32[]{:S(2)}, u32[]{:S(2)}) collective-permute-start(bf16[256,1024]{1,0:T(8,128)(2,1)S(1)} %get-tuple-element.22.refs_3_), channel_id=1, source_target_pairs={{0,2},{2,0},{4,6},{6,4},{8,10},{10,8},{12,14},{14,12},{16,18},{18,... | collective-permute-start | bytes 1572872 | tf_op jit(solution)/shard_map/ppermute | solution.py:41
  14.6 3.4 %copy-done.2 = bf16[2048,2,1024]{2,1,0:T(2,128)(2,1)S(1)} copy-done((bf16[2048,2,1024]{2,1,0:T(2,128)(2,1)S(1)}, bf16[2048,2,1024]{2,1,0:T(2,128)(2,1)}, u32[]{:S(2)}) %copy-start.2) | copy-done | bytes 8388632
  18.0 14.1 %project_keyval.1 = (bf16[256,1024]{1,0:T(8,128)(2,1)S(1)}, bf16[256,1024]{1,0:T(8,128)(2,1)S(1)}, bf16[256,2,1024]{2,1,0:T(2,128)(2,1)}) custom-call(bf16[256,2048]{1,0:T(8,128)(2,1)S(1)} %get-tuple-element.23.refs_0_, bf16[2048,2,1024]{2,1,0:T(2,128)(2,1)S(1)} %copy-done.2, bf16[2048,2,1024]{2,1,0:T(2,128)(2,1)S(1)} %copy-done.2, ...), custom_call_target="tpu_custom_call" | custom-call | flops 2147483648 | bytes 8388608 | tf_op jit(solution)/shard_map/project_keyval/pallas_call | solution.py:198
  32.1 0.8 copy-done.7
  32.9 0.8 copy-done.9
  33.7 1.5 %collective-permute-start.6 = (bf16[2,128,1024]{2,1,0:T(8,128)(2,1)}, bf16[2,128,1024]{2,1,0:T(8,128)(2,1)}, u32[]{:S(2)}, u32[]{:S(2)}) collective-permute-start(bf16[2,128,1024]{2,1,0:T(8,128)(2,1)} %collective-permute-done.4.refs_7_), channel_id=1, source_target_pairs={{0,4},{2,6},{8,0},{10,2},{16,8},{18,10},{24,16},{26,18},{28,24},{3... | collective-permute-start | bytes 1572872 | tf_op jit(solution)/shard_map/ppermute | solution.py:50
  35.2 0.5 collective-permute-start.3
  35.8 2.0 %part_tail.1.refs_8_ = bf16[2,256,1024]{2,1,0:T(8,128)(2,1)S(1)} custom-call(bf16[256,2,1024]{2,1,0:T(2,128)(2,1)S(1)} %bitcast.3, bf16[256,2,1024]{2,1,0:T(2,128)(2,1)S(1)} %bitcast.4, bf16[256,2,1024]{2,1,0:T(2,128)(2,1)S(1)} %bitcast.5, bf16[256,2,1024]{2,1,0:T(2,128)(2,1)S(1)} %bitcast.6, bf16[256,2,1024]{2,1,0:T(2,128)(2,1)S(1)} %bitcast.7, ...), custom_call_target="tpu_custom_call" | custom-call | bytes 2097152 | tf_op jit(solution)/shard_map/part_tail/pallas_call | solution.py:99
  37.9 9.2 %attend_near.1 = (f32[512,1024]{1,0:T(8,128)S(1)}, f32[512,128]{1,0:T(8,128)S(1)}) custom-call(s32[8]{0:T(128)S(1)} %copy-done.6, s32[1]{0:T(128)S(6)} %copy.14.refs_1_, s32[8,4]{1,0:T(8,128)S(1)} %copy.13.refs_2_, bf16[256,1024]{1,0:T(8,128)(2,1)S(1)} %get-tuple-element.22.refs_3_, bf16[256,1024]{1,0:T(8,128)(2,1)S(1)} %collective-permute-done.1.refs_4_, ...), custom_call_target="tpu_custom_call" | custom-call | flops 1879048192 | bytes 3670016 | tf_op jit(solution)/shard_map/attend_near/pallas_call | solution.py:385
  47.1 1.0 %collective-permute-done.6.refs_6_ = bf16[2,128,1024]{2,1,0:T(8,128)(2,1)} collective-permute-done((bf16[2,128,1024]{2,1,0:T(8,128)(2,1)}, bf16[2,128,1024]{2,1,0:T(8,128)(2,1)}, u32[]{:S(2)}, u32[]{:S(2)}) %collective-permute-start.6) | collective-permute-done | bytes 524320 | tf_op jit(solution)/shard_map/ppermute | solution.py:50
  48.1 1.5 %collective-permute-start.7 = (bf16[2,128,1024]{2,1,0:T(8,128)(2,1)}, bf16[2,128,1024]{2,1,0:T(8,128)(2,1)S(1)}, u32[]{:S(2)}, u32[]{:S(2)}) collective-permute-start(bf16[2,128,1024]{2,1,0:T(8,128)(2,1)} %collective-permute-done.6.refs_6_), channel_id=1, source_target_pairs={{0,4},{2,6},{8,0},{10,2},{16,8},{18,10},{24,16},{26,18},{28,24},{3... | collective-permute-start | bytes 1572872 | tf_op jit(solution)/shard_map/ppermute | solution.py:50
  49.6 0.5 collective-permute-start.5
  50.1 5.0 %attend_mid.1 = (f32[512,1024]{1,0:T(8,128)S(1)}, f32[512,128]{1,0:T(8,128)S(1)}) custom-call(s32[8]{0:T(128)S(1)} %copy-done.6, s32[1]{0:T(128)S(6)} %copy.14.refs_1_, s32[8,4]{1,0:T(8,128)S(1)} %copy.13.refs_2_, bf16[256,1024]{1,0:T(8,128)(2,1)S(1)} %get-tuple-element.22.refs_3_, bf16[256,1024]{1,0:T(8,128)(2,1)S(1)} %collective-permute-done.1.refs_4_, ...), custom_call_target="tpu_custom_call" | custom-call | flops 536870912 | bytes 1048576 | tf_op jit(solution)/shard_map/attend_mid/pallas_call | solution.py:385
  55.1 6.4 %collective-permute-done.7.refs_6_ = bf16[2,128,1024]{2,1,0:T(8,128)(2,1)S(1)} collective-permute-done((bf16[2,128,1024]{2,1,0:T(8,128)(2,1)}, bf16[2,128,1024]{2,1,0:T(8,128)(2,1)S(1)}, u32[]{:S(2)}, u32[]{:S(2)}) %collective-permute-start.7) | collective-permute-done | bytes 524320 | tf_op jit(solution)/shard_map/ppermute | solution.py:50
  61.5 1.6 %collective-permute-start.9 = (bf16[2,64,1024]{2,1,0:T(8,128)(2,1)S(1)}, bf16[2,64,1024]{2,1,0:T(8,128)(2,1)S(1)}, u32[]{:S(2)}, u32[]{:S(2)}) collective-permute-start(bf16[2,64,1024]{2,1,0:T(8,128)(2,1)S(1)} %slice.7), channel_id=1, source_target_pairs={{0,4},{2,6},{8,0},{10,2},{16,8},{18,10},{24,16},{26,18},{28,24},{3... | collective-permute-start | bytes 786440 | tf_op jit(solution)/shard_map/ppermute | solution.py:50
  63.1 0.6 collective-permute-start.8
  63.7 4.6 %collective-permute-done.9.refs_8_ = bf16[2,64,1024]{2,1,0:T(8,128)(2,1)S(1)} collective-permute-done((bf16[2,64,1024]{2,1,0:T(8,128)(2,1)S(1)}, bf16[2,64,1024]{2,1,0:T(8,128)(2,1)S(1)}, u32[]{:S(2)}, u32[]{:S(2)}) %collective-permute-start.9) | collective-permute-done | bytes 262176 | tf_op jit(solution)/shard_map/ppermute | solution.py:50
  68.3 1.3 %collective-permute-done.8.refs_7_ = bf16[2,64,1024]{2,1,0:T(8,128)(2,1)S(1)} collective-permute-done((bf16[2,64,1024]{2,1,0:T(8,128)(2,1)S(1)}, bf16[2,64,1024]{2,1,0:T(8,128)(2,1)S(1)}, u32[]{:S(2)}, u32[]{:S(2)}) %collective-permute-start.8) | collective-permute-done | bytes 262176 | tf_op jit(solution)/shard_map/ppermute | solution.py:50
  69.6 5.4 %attend_far.1 = (f32[256,1024]{1,0:T(8,128)S(1)}, f32[256,128]{1,0:T(8,128)S(1)}, bf16[272,1024]{1,0:T(8,128)(2,1)S(1)}) custom-call(s32[8]{0:T(128)S(1)} %copy-done.6, s32[1]{0:T(128)S(6)} %copy.14.refs_1_, s32[8,4]{1,0:T(8,128)S(1)} %copy.13.refs_2_, bf16[256,1024]{1,0:T(8,128)(2,1)S(1)} %get-tuple-element.22.refs_3_, ...), custom_call_target="tpu_custom_call" | custom-call | flops 805306368 | bytes 1572864 | tf_op jit(solution)/shard_map/attend_far/pallas_call | solution.py:385
  75.0 0.6 collective-permute-start.10
  75.7 11.3 %collective-permute-done.10.refs_2_ = bf16[272,1024]{1,0:T(8,128)(2,1)S(1)} collective-permute-done((bf16[272,1024]{1,0:T(8,128)(2,1)S(1)}, bf16[272,1024]{1,0:T(8,128)(2,1)S(1)}, u32[]{:S(2)}, u32[]{:S(2)}) %collective-permute-start.10) | collective-permute-done | bytes 557088 | tf_op jit(solution)/shard_map/ppermute | solution.py:41
  86.9 1.4 %combine_send.1 = (bf16[256,1024]{1,0:T(8,128)(2,1)S(1)}, bf16[1,256,1024]{2,1,0:T(8,128)(2,1)S(1)}) custom-call(f32[256,1024]{1,0:T(8,128)S(1)} %get-tuple-element.36.refs_0_, f32[256,128]{1,0:T(8,128)S(1)} %get-tuple-element.37.refs_1_, bf16[272,1024]{1,0:T(8,128)(2,1)S(1)} %collective-permute-done.10.refs_2_, bf16[1024,2048]{1,0:T(8,128)(2,1)S(1)} %copy-done.3), custom_call_target="tpu_custom_call" | custom-call | flops 536870912 | bytes 4194304 | tf_op jit(solution)/shard_map/combine_send/pallas_call | solution.py:437
  88.5 0.7 keep_own.1
  89.2 1.2 %collective-permute-done.11 = bf16[256,1024]{1,0:T(8,128)(2,1)S(1)} collective-permute-done((bf16[256,1024]{1,0:T(8,128)(2,1)S(1)}, bf16[256,1024]{1,0:T(8,128)(2,1)S(1)}, u32[]{:S(2)}, u32[]{:S(2)}) %collective-permute-start.11) | collective-permute-done | bytes 524320 | tf_op jit(solution)/shard_map/ppermute | solution.py:41
  90.4 0.9 %add_convert_fusion = bf16[256,1024]{1,0:T(8,128)(2,1)} fusion(f32[256,1024]{1,0:T(8,128)S(1)} %keep_own.1, bf16[256,1024]{1,0:T(8,128)(2,1)S(1)} %collective-permute-done.11), kind=kLoop, calls=%fused_computation | loop fusion | flops 786432 | bytes 2097152 | tf_op jit(solution)/shard_map/convert_element_type | solution.py:531
  (34 shorter events, 0.4 us)
Async XLA Ops:
  0.6 1.0 %copy-start.1 = (bf16[128,2,1024]{2,1,0:T(2,128)(2,1)S(1)}, bf16[128,2,1024]{2,1,0:T(2,128)(2,1)}, u32[]{:S(2)}) copy-start(bf16[128,2,1024]{2,1,0:T(2,128)(2,1)} %refs_7_.1) | copy-start | bytes 1572868
  1.7 4.1 %copy-start.5 = (bf16[256,1024]{1,0:T(8,128)(2,1)S(1)}, bf16[256,1024]{1,0:T(8,128)(2,1)}, u32[]{:S(2)}) copy-start(bf16[256,1024]{1,0:T(8,128)(2,1)} %hidden.1) | copy-start | bytes 1572868
  1.7 4.7 %copy-start.6 = (s32[8]{0:T(128)S(1)}, s32[8]{0:T(128)}, u32[]{:S(2)}) copy-start(s32[8]{0:T(128)} %refs_0_.9) | copy-start | bytes 100
  2.7 32.5 %collective-permute-start.2 = (bf16[2,128,1024]{2,1,0:T(8,128)(2,1)S(1)}, bf16[2,128,1024]{2,1,0:T(8,128)(2,1)}, u32[]{:S(2)}, u32[]{:S(2)}) collective-permute-start(bf16[2,128,1024]{2,1,0:T(8,128)(2,1)S(1)} %part_prompt.1.refs_5_), channel_id=1, source_target_pairs={{0,8},{2,10},{8,16},{10,18},{16,24},{18,26},{24,28},{26,30},{28,20... | collective-permute-start | bytes 1572872 | tf_op jit(solution)/shard_map/ppermute | solution.py:50
  5.7 28.0 %collective-permute-start.4 = (bf16[2,128,1024]{2,1,0:T(8,128)(2,1)S(1)}, bf16[2,128,1024]{2,1,0:T(8,128)(2,1)}, u32[]{:S(2)}, u32[]{:S(2)}) collective-permute-start(bf16[2,128,1024]{2,1,0:T(8,128)(2,1)S(1)} %part_prompt.1.refs_5_), channel_id=1, source_target_pairs={{0,4},{2,6},{8,0},{10,2},{16,8},{18,10},{24,16},{26,18},{28,24},{3... | collective-permute-start | bytes 1572872 | tf_op jit(solution)/shard_map/ppermute | solution.py:50
  5.7 2.6 %collective-permute-start = (bf16[256,1024]{1,0:T(8,128)(2,1)S(1)}, bf16[256,1024]{1,0:T(8,128)(2,1)S(1)}, u32[]{:S(2)}, u32[]{:S(2)}) collective-permute-start(bf16[256,1024]{1,0:T(8,128)(2,1)S(1)} %copy-done.5), channel_id=1, source_target_pairs={{0,1},{1,0},{2,3},{3,2},{4,5},{5,4},{6,7},{7,6},{8,9},{9,8},{10,11... | collective-permute-start | bytes 1572872 | tf_op jit(solution)/shard_map/ppermute | solution.py:41
  8.4 2.2 %copy-start.4 = (bf16[2048,1024]{1,0:T(8,128)(2,1)S(1)}, bf16[2048,1024]{1,0:T(8,128)(2,1)}, u32[]{:S(2)}) copy-start(bf16[2048,1024]{1,0:T(8,128)(2,1)} %refs_2_.6) | copy-start | bytes 12582916
  12.6 25.2 %collective-permute-start.1 = (bf16[256,1024]{1,0:T(8,128)(2,1)S(1)}, bf16[256,1024]{1,0:T(8,128)(2,1)S(1)}, u32[]{:S(2)}, u32[]{:S(2)}) collective-permute-start(bf16[256,1024]{1,0:T(8,128)(2,1)S(1)} %get-tuple-element.22.refs_3_), channel_id=1, source_target_pairs={{0,2},{2,0},{4,6},{6,4},{8,10},{10,8},{12,14},{14,12},{16,18},{18,... | collective-permute-start | bytes 1572872 | tf_op jit(solution)/shard_map/ppermute | solution.py:41
  14.6 3.4 %copy-start.2 = (bf16[2048,2,1024]{2,1,0:T(2,128)(2,1)S(1)}, bf16[2048,2,1024]{2,1,0:T(2,128)(2,1)}, u32[]{:S(2)}) copy-start(bf16[2048,2,1024]{2,1,0:T(2,128)(2,1)} %refs_2_.8) | copy-start | bytes 25165828
  18.0 17.7 %copy-start.11 = (s32[8,4]{0,1:T(4,128)S(1)}, s32[8,4]{0,1:T(4,128)}, u32[]{:S(2)}) copy-start(s32[8,4]{0,1:T(4,128)} %param.15) | copy-start | bytes 388
  18.0 17.8 %copy-start = (bf16[2,128,2,1024]{3,2,1,0:T(2,128)(2,1)S(1)}, bf16[2,128,2,1024]{3,2,1,0:T(2,128)(2,1)}, u32[]{:S(2)}) copy-start(bf16[2,128,2,1024]{3,2,1,0:T(2,128)(2,1)} %param.14) | copy-start | bytes 3145732
  32.1 0.8 copy-start.7
  32.9 0.8 copy-start.9
  33.7 14.4 %collective-permute-start.6 = (bf16[2,128,1024]{2,1,0:T(8,128)(2,1)}, bf16[2,128,1024]{2,1,0:T(8,128)(2,1)}, u32[]{:S(2)}, u32[]{:S(2)}) collective-permute-start(bf16[2,128,1024]{2,1,0:T(8,128)(2,1)} %collective-permute-done.4.refs_7_), channel_id=1, source_target_pairs={{0,4},{2,6},{8,0},{10,2},{16,8},{18,10},{24,16},{26,18},{28,24},{3... | collective-permute-start | bytes 1572872 | tf_op jit(solution)/shard_map/ppermute | solution.py:50
  35.2 14.4 %collective-permute-start.3 = (bf16[2,128,1024]{2,1,0:T(8,128)(2,1)}, bf16[2,128,1024]{2,1,0:T(8,128)(2,1)}, u32[]{:S(2)}, u32[]{:S(2)}) collective-permute-start(bf16[2,128,1024]{2,1,0:T(8,128)(2,1)} %collective-permute-done.2.refs_6_), channel_id=1, source_target_pairs={{0,8},{2,10},{8,16},{10,18},{16,24},{18,26},{24,28},{26,30},{28,20... | collective-permute-start | bytes 1572872 | tf_op jit(solution)/shard_map/ppermute | solution.py:50
  35.8 2.1 %copy-start.8 = (bf16[256,1024]{1,0:T(8,128)(2,1)S(1)}, bf16[256,1024]{1,0:T(8,128)(2,1)}, u32[]{:S(2)}) copy-start(bf16[256,1024]{1,0:T(8,128)(2,1)} %copy-done.7) | copy-start | bytes 1572868
  35.8 2.1 %copy-start.10 = (bf16[256,1024]{1,0:T(8,128)(2,1)S(1)}, bf16[256,1024]{1,0:T(8,128)(2,1)}, u32[]{:S(2)}) copy-start(bf16[256,1024]{1,0:T(8,128)(2,1)} %copy-done.9) | copy-start | bytes 1572868
  48.1 13.5 %collective-permute-start.7 = (bf16[2,128,1024]{2,1,0:T(8,128)(2,1)}, bf16[2,128,1024]{2,1,0:T(8,128)(2,1)S(1)}, u32[]{:S(2)}, u32[]{:S(2)}) collective-permute-start(bf16[2,128,1024]{2,1,0:T(8,128)(2,1)} %collective-permute-done.6.refs_6_), channel_id=1, source_target_pairs={{0,4},{2,6},{8,0},{10,2},{16,8},{18,10},{24,16},{26,18},{28,24},{3... | collective-permute-start | bytes 1572872 | tf_op jit(solution)/shard_map/ppermute | solution.py:50
  49.6 13.5 %collective-permute-start.5 = (bf16[2,128,1024]{2,1,0:T(8,128)(2,1)}, bf16[2,128,1024]{2,1,0:T(8,128)(2,1)S(1)}, u32[]{:S(2)}, u32[]{:S(2)}) collective-permute-start(bf16[2,128,1024]{2,1,0:T(8,128)(2,1)} %collective-permute-done.3.refs_5_), channel_id=1, source_target_pairs={{0,8},{2,10},{8,16},{10,18},{16,24},{18,26},{24,28},{26,30},{28,20... | collective-permute-start | bytes 1572872 | tf_op jit(solution)/shard_map/ppermute | solution.py:50
  50.1 36.9 %copy-start.3 = (bf16[1024,2048]{1,0:T(8,128)(2,1)S(1)}, bf16[1024,2048]{1,0:T(8,128)(2,1)}, u32[]{:S(2)}) copy-start(bf16[1024,2048]{1,0:T(8,128)(2,1)} %weight.1) | copy-start | bytes 12582916
  61.5 6.8 %collective-permute-start.9 = (bf16[2,64,1024]{2,1,0:T(8,128)(2,1)S(1)}, bf16[2,64,1024]{2,1,0:T(8,128)(2,1)S(1)}, u32[]{:S(2)}, u32[]{:S(2)}) collective-permute-start(bf16[2,64,1024]{2,1,0:T(8,128)(2,1)S(1)} %slice.7), channel_id=1, source_target_pairs={{0,4},{2,6},{8,0},{10,2},{16,8},{18,10},{24,16},{26,18},{28,24},{3... | collective-permute-start | bytes 786440 | tf_op jit(solution)/shard_map/ppermute | solution.py:50
  63.1 6.5 %collective-permute-start.8 = (bf16[2,64,1024]{2,1,0:T(8,128)(2,1)S(1)}, bf16[2,64,1024]{2,1,0:T(8,128)(2,1)S(1)}, u32[]{:S(2)}, u32[]{:S(2)}) collective-permute-start(bf16[2,64,1024]{2,1,0:T(8,128)(2,1)S(1)} %slice.6), channel_id=1, source_target_pairs={{0,8},{2,10},{8,16},{10,18},{16,24},{18,26},{24,28},{26,30},{28,20... | collective-permute-start | bytes 786440 | tf_op jit(solution)/shard_map/ppermute | solution.py:50
  75.0 11.9 %collective-permute-start.10 = (bf16[272,1024]{1,0:T(8,128)(2,1)S(1)}, bf16[272,1024]{1,0:T(8,128)(2,1)S(1)}, u32[]{:S(2)}, u32[]{:S(2)}) collective-permute-start(bf16[272,1024]{1,0:T(8,128)(2,1)S(1)} %get-tuple-element.38), channel_id=1, source_target_pairs={{0,2},{2,0},{4,6},{6,4},{8,10},{10,8},{12,14},{14,12},{16,18},{18,... | collective-permute-start | bytes 1671176 | tf_op jit(solution)/shard_map/ppermute | solution.py:41
  88.4 2.0 %collective-permute-start.11 = (bf16[256,1024]{1,0:T(8,128)(2,1)S(1)}, bf16[256,1024]{1,0:T(8,128)(2,1)S(1)}, u32[]{:S(2)}, u32[]{:S(2)}) collective-permute-start(bf16[256,1024]{1,0:T(8,128)(2,1)S(1)} %bitcast.11), channel_id=1, source_target_pairs={{0,1},{1,0},{2,3},{3,2},{4,5},{5,4},{6,7},{7,6},{8,9},{9,8},{10,11... | collective-permute-start | bytes 1572872 | tf_op jit(solution)/shard_map/ppermute | solution.py:41

commit v3 on v2

v3 whole, which is shorter than its diff:
```python
import functools

import jax
import jax.numpy as jnp
import numpy as np
from jax import lax
from jax.experimental import pallas as pl
from jax.experimental.pallas import tpu as pltpu
from jax.sharding import PartitionSpec as P

HD = 128
REQ = 8
NEGATIVE = -1e30
SCALE = float(HD**-0.5 * np.log2(np.e))
STAT_ROWS = 16


def params(mib=24):
    return pltpu.CompilerParams(vmem_limit_bytes=mib * 2**20)


def cost(flops, moved, exps=0):
    return pl.CostEstimate(flops=int(flops), bytes_accessed=int(moved), transcendentals=int(exps))


def cycle_of(group):
    if group == 2:
        return [0, 2, 4, 6, 7, 5, 3, 1]
    return list(range(REQ))


def pick(table, index):
    result = jnp.int32(table[0])
    for place, value in enumerate(table):
        result = jnp.where(index == place, jnp.int32(value), result)
    return result


def swap(value, axis, mask):
    pairs = [(source, source ^ mask) for source in range(lax.axis_size(axis))]
    return lax.ppermute(value, axis, pairs)


def turn(value, cycle, group, way):
    count = len(cycle)
    pairs = []
    for place in range(count):
        source, target = cycle[place], cycle[(place + way) % count]
        pairs += [(source * group + m, target * group + m) for m in range(group)]
    return lax.ppermute(value, "seq", pairs)


def rotated(vectors, cosine, sine):
    return vectors * cosine + pltpu.roll(vectors, HD // 2, 1) * sine


def angles(positions):
    half = HD // 2
    freqs = 10000.0 ** (-jnp.arange(half, dtype=jnp.float32) / half)
    angle = positions.astype(jnp.float32)[:, None] * freqs
    cosine, sine = jnp.cos(angle), jnp.sin(angle)
    return (
        jnp.concatenate([cosine, cosine], axis=1),
        jnp.concatenate([-sine, sine], axis=1),
    )


def lanes(start, count=HD):
    return pl.ds(pl.multiple_of(start, HD), count)


def after(value, *others):
    return lax.optimization_barrier((value, *others))[0]


VMEM = pl.BlockSpec(memory_space=pltpu.VMEM)
HBM = pl.BlockSpec(memory_space=pltpu.HBM)
SMEM = pl.BlockSpec(memory_space=pltpu.SMEM)


def viewed(block):
    count, pair, width = block.shape
    return block.reshape(count, pair, width // HD, HD).transpose(0, 2, 1, 3)


def take_apart(block, apart, begin, result, offset):
    count, heads = block.shape[:2]
    stride = 2 * heads
    flat = block.reshape(count * stride, HD)
    apart[begin * stride : (begin + count) * stride, :] = flat[...].astype(jnp.float32)
    for head in range(heads):
        for j in range(2):
            result[j, offset : offset + count, head * HD : (head + 1) * HD] = apart[
                pl.ds(begin * stride + 2 * head + j, count, stride=stride), :
            ].astype(jnp.bfloat16)


def part_kernel(*refs):
    *blocks, result, apart = refs
    offset = 0
    for block in blocks:
        take_apart(block, apart, offset, result, offset)
        offset += block.shape[0]


def part_keyval(blocks, name):
    count = sum(block.shape[0] for block in blocks)
    heads = blocks[0].shape[1]
    return pl.pallas_call(
        part_kernel,
        in_specs=[VMEM] * len(blocks),
        out_specs=VMEM,
        out_shape=jax.ShapeDtypeStruct((2, count, heads * HD), jnp.bfloat16),
        scratch_shapes=[pltpu.VMEM((2 * heads * count, HD), jnp.float32)],
        compiler_params=params(16),
        cost_estimate=cost(0, 8 * count * heads * HD),
        name=name,
    )(*blocks)


def query_kernel(*refs):
    *pieces, weight, cosine, sine, query, normed, near, arrived = refs
    count, _, wide = near.shape
    copies = [
        pltpu.make_async_copy(
            weight.at[:, pl.ds(i * wide, wide)], near.at[i], arrived.at[i]
        )
        for i in range(count)
    ]
    for copy in copies:
        copy.start()
    rows, columns = pieces[0].shape
    index = lax.axis_index("tp")
    features = columns * len(pieces)
    values = [piece[...].astype(jnp.float32) for piece in pieces]
    mean = sum(jnp.sum(v, axis=1, keepdims=True) for v in values) / features
    values = [v - mean for v in values]
    spread = sum(jnp.sum(v * v, axis=1, keepdims=True) for v in values) / features
    inverse = lax.rsqrt(spread + 1e-05)
    for shift, v in enumerate(values):
        normed[:, lanes((index ^ shift) * columns, columns)] = (v * inverse).astype(jnp.bfloat16)
    for i, copy in enumerate(copies):
        copy.wait()
        product = jnp.dot(normed[...], near[i], preferred_element_type=jnp.float32)
        for start in range(0, wide, HD):
            query[:, i * wide + start : i * wide + start + HD] = rotated(
                product[:, start : start + HD], cosine[...], sine[...]
            ).astype(jnp.bfloat16)


def project_query(pieces, w_query, cosine, sine):
    rows, columns = pieces[0].shape
    depth, width = w_query.shape
    wide = min(width, 2 * HD)
    return pl.pallas_call(
        query_kernel,
        in_specs=[VMEM] * len(pieces) + [HBM, VMEM, VMEM],
        out_specs=[VMEM] * 2,
        out_shape=[
            jax.ShapeDtypeStruct((rows, width), jnp.bfloat16),
            jax.ShapeDtypeStruct((rows, depth), jnp.bfloat16),
        ],
        scratch_shapes=[
            pltpu.VMEM((width // wide, depth, wide), jnp.bfloat16),
            pltpu.SemaphoreType.DMA((width // wide,)),
        ],
        compiler_params=params(60),
        cost_estimate=cost(2 * rows * depth * width, 2 * depth * width),
        name="project_query",
    )(*pieces, w_query, cosine, sine)


def keyval_kernel(
    normed, weight, cosine, sine, keys, values, cache, near, arrived, apart, total, woven
):
    parts, chunk, heads = near.shape[:3]
    rows = normed.shape[0]
    stride = 2 * heads
    copies = [
        pltpu.make_async_copy(weight.at[pl.ds(i * chunk, chunk)], near.at[i], arrived.at[i])
        for i in range(parts)
    ]
    for copy in copies:
        copy.start()
    for i, copy in enumerate(copies):
        copy.wait()
        flat = apart.at[i % 2]
        flat[...] = near.at[i].reshape(chunk * stride, HD)[...].astype(jnp.float32)
        for head in range(heads):
            both = [
                flat[pl.ds(2 * head + j, chunk, stride=stride), :].astype(jnp.bfloat16)
                for j in range(2)
            ]
            product = jnp.dot(
                normed[:, i * chunk : (i + 1) * chunk],
                jnp.concatenate(both, axis=1),
                preferred_element_type=jnp.float32,
            )
            span = slice(2 * head * HD, 2 * (head + 1) * HD)
            if i == 0:
                total[:, span] = product
            else:
                total[:, span] += product
    for head in range(heads):
        span = slice(head * HD, (head + 1) * HD)
        begin = 2 * head * HD
        key = rotated(total[:, begin : begin + HD], cosine[...], sine[...]).astype(jnp.bfloat16)
        value = total[:, begin + HD : begin + 2 * HD].astype(jnp.bfloat16)
        keys[:, span] = key
        values[:, span] = value
        woven[pl.ds(2 * head, rows, stride=stride), :] = key.astype(jnp.float32)
        woven[pl.ds(2 * head + 1, rows, stride=stride), :] = value.astype(jnp.float32)
    cache.reshape(rows * stride, HD)[...] = woven[...].astype(jnp.bfloat16)


def project_keyval(normed, w_keyval, cosine, sine):
    rows, depth = normed.shape
    weight = viewed(w_keyval)
    heads = weight.shape[1]
    width = heads * HD
    chunk = min(depth, 256)
    keys, values, cache = pl.pallas_call(
        keyval_kernel,
        in_specs=[VMEM, HBM, VMEM, VMEM],
        out_specs=[VMEM] * 3,
        out_shape=[
            jax.ShapeDtypeStruct((rows, width), jnp.bfloat16),
            jax.ShapeDtypeStruct((rows, width), jnp.bfloat16),
            jax.ShapeDtypeStruct((rows, heads, 2, HD), jnp.bfloat16),
        ],
        scratch_shapes=[
            pltpu.VMEM((depth // chunk, chunk, heads, 2, HD), jnp.bfloat16),
            pltpu.SemaphoreType.DMA((depth // chunk,)),
            pltpu.VMEM((2, 2 * heads * chunk, HD), jnp.float32),
            pltpu.VMEM((rows, 2 * width), jnp.float32),
            pltpu.VMEM((2 * heads * rows, HD), jnp.float32),
        ],
        compiler_params=params(57),
        cost_estimate=cost(4 * rows * depth * width, 4 * depth * width),
        name="project_keyval",
    )(normed, weight, cosine, sine)
    return keys, values, cache.transpose(0, 2, 1, 3).reshape(rows, 2, width)


def column_of(stats, lane):
    place = lax.broadcasted_iota(jnp.int32, stats.shape, 1)
    return jnp.sum(jnp.where(place == lane, stats, 0.0), axis=1, keepdims=True)


def with_column(stats, lane, column):
    place = lax.broadcasted_iota(jnp.int32, stats.shape, 1)
    return jnp.where(place == lane, column, stats)


def attend_kernel(spec, *refs):
    group, shifts, rings, slots, piece, fresh, first, last = spec
    refs = list(refs)
    take = lambda count: [refs.pop(0) for _ in range(count)]
    lengths, shared, table = take(3)
    queries = take(len(shifts))
    if fresh:
        block, fresh_keys, fresh_values = take(3)
    else:
        raw = take(len(rings))
    if not first:
        old_mixes, old_stats = take(len(shifts)), take(len(shifts))
    if last:
        results = take(len(shifts))
        mine_stats = take(1) if 0 in shifts else []
    else:
        results, new_stats = take(len(shifts)), take(len(shifts))
    bias, stats = take(2)
    if fresh:
        causal = take(1)[0]
    else:
        block, apart = take(2)
    rows, width = queries[0].shape
    heads = width // HD
    cycle = cycle_of(group)
    seq = lax.axis_index("seq")
    request, member = seq // group, seq % group
    place = pick(list(np.argsort(cycle)), request)
    edges = []
    count = 0
    block_size = 128
    for i in range(slots):
        wanted = seq * slots + i
        number = jnp.int32(0)
        for j in range(table.shape[1]):
            number = jnp.where(table[request, j] == wanted, jnp.int32(j), number)
        edges.append((count, block_size, number * block_size, lengths[request]))
        count += block_size
    for step, begin, size in rings:
        origin = pick(cycle, lax.rem(place + step + REQ, REQ))
        edges.append((count, size, (origin * group + member) * piece + begin, shared[0]))
        count += size
    for begin, size, start, length in edges:
        positions = start + lax.broadcasted_iota(jnp.int32, (size, HD), 0)
        lane = lax.broadcasted_iota(jnp.int32, (size, HD), 1)
        bias[begin : begin + size, :] = jnp.where(
            (positions >= length) & (lane == 0), NEGATIVE, 0.0
        ).astype(jnp.bfloat16)
    if fresh:
        bias[count : count + rows, :] = jnp.zeros((rows, HD), jnp.bfloat16)
        theirs = member * rows + lax.broadcasted_iota(jnp.int32, (rows, rows), 1)
        for i, shift in enumerate(shifts):
            mine = (member ^ shift) * rows + lax.broadcasted_iota(jnp.int32, (rows, rows), 0)
            causal[i * rows : (i + 1) * rows, :] = jnp.where(theirs <= mine, 0.0, NEGATIVE)
    else:
        offset = 0
        for piece_ref in raw:
            take_apart(piece_ref, apart, offset, block, offset)
            offset += piece_ref.shape[0]
    stats[...] = jnp.zeros_like(stats)
    unit = jnp.where(
        lax.broadcasted_iota(jnp.int32, (len(shifts) * rows, HD), 1) == 0, 1.0, 0.0
    ).astype(jnp.bfloat16)
    across = (((1,), (1,)), ((), ()))

    def stacked(values):
        return values[0] if len(values) == 1 else jnp.concatenate(values, axis=0)

    def one_head(head):
        span = lanes(head * HD)
        query = stacked([q[:, span] for q in queries])
        keys = [block[0, :, span]]
        values = [block[1, :, span]]
        if fresh:
            keys.append(fresh_keys[:, span])
            values.append(fresh_values[:, span])
        keys, values = stacked(keys), stacked(values)
        scores = lax.dot_general(
            jnp.concatenate([query, unit], axis=1),
            jnp.concatenate([keys, bias[...]], axis=1),
            across,
            preferred_element_type=jnp.float32,
        )
        if fresh:
            scores = jnp.concatenate([scores[:, :count], scores[:, count:] + causal[...]], axis=1)
        top = jnp.max(scores, axis=1, keepdims=True)
        if not first:
            old = stacked([column_of(s[...], head) for s in old_stats])
            top = jnp.maximum(top, old * (1.0 / SCALE))
        weights = jnp.exp2((scores - top) * SCALE).astype(jnp.bfloat16)
        mixed = jnp.dot(
            weights,
            jnp.concatenate([values, jnp.ones_like(values)], axis=1),
            preferred_element_type=jnp.float32,
        )
        total, summed = mixed[:, :HD], mixed[:, HD:]
        if not first:
            factor = jnp.exp2(old - top * SCALE)
            total = total + stacked([mix[:, span] for mix in old_mixes]) * factor
            summed = summed + factor
        even = total / summed
        stats[...] = with_column(stats[...], head, top * SCALE + jnp.log2(summed))
        for i, result in enumerate(results):
            result[:rows, span] = even[i * rows : (i + 1) * rows].astype(result.dtype)

    together = min(2, heads)

    def some_heads(i, _):
        for j in range(together):
            one_head(together * i + j)
        return 0

    lax.fori_loop(0, heads // together, some_heads, 0)
    for i, shift in enumerate(shifts):
        own_rows = stats[i * rows : (i + 1) * rows, :]
        if not last:
            new_stats[i][...] = own_rows
        elif shift == 0:
            mine_stats[0][...] = own_rows
        else:
            line = jnp.transpose(own_rows)[:heads, :]
            packed = []
            for _ in range(3):
                rounded = line.astype(jnp.bfloat16).astype(jnp.float32)
                packed.append(rounded)
                line = line - rounded
            gap = -3 * heads % STAT_ROWS
            if gap:
                packed.append(jnp.zeros((gap, rows), jnp.float32))
            packed = jnp.concatenate(packed, axis=0).astype(jnp.bfloat16)
            for j in range(packed.shape[0] // STAT_ROWS):
                results[i][rows:, j * rows : (j + 1) * rows] = packed[
                    j * STAT_ROWS : (j + 1) * STAT_ROWS
                ]


def attend(facts, queries, shifts, rings, slots, piece, blocks, old, last, name):
    group = len(queries)
    queries = [queries[shift] for shift in shifts]
    rows, width = queries[0].shape
    heads = width // HD
    fresh = blocks[0].ndim == 3
    operands = [*facts, *queries, *blocks]
    if old:
        operands += [old[shift][0] for shift in shifts] + [old[shift][1] for shift in shifts]
    plain = blocks[0].shape[1] if fresh else sum(block.shape[0] for block in blocks)
    count = plain + (rows if fresh else 0)
    many = len(shifts) * rows
    scratch = [pltpu.VMEM((count, HD), jnp.bfloat16), pltpu.VMEM((many, HD), jnp.float32)]
    if fresh:
        scratch.append(pltpu.VMEM((many, rows), jnp.float32))
    else:
        scratch.append(pltpu.VMEM((2, count, width), jnp.bfloat16))
        scratch.append(pltpu.VMEM((2 * heads * count, HD), jnp.float32))
    state = jax.ShapeDtypeStruct((rows, width), jnp.float32)
    state_stats = jax.ShapeDtypeStruct((rows, HD), jnp.float32)
    sent = jax.ShapeDtypeStruct((rows + STAT_ROWS, width), jnp.bfloat16)
    if last:
        out_shape = [sent if shift else state for shift in shifts]
        out_shape += [state_stats] * (0 in shifts)
    else:
        out_shape = [state] * len(shifts) + [state_stats] * len(shifts)
    scores = many * count * heads
    results = pl.pallas_call(
        functools.partial(
            attend_kernel, (group, shifts, rings, slots, piece, fresh, not old, last)
        ),
        in_specs=[SMEM] * 3 + [VMEM] * (len(operands) - 3),
        out_specs=[VMEM] * len(out_shape),
        out_shape=out_shape,
        scratch_shapes=scratch,
        compiler_params=params(28),
        cost_estimate=cost(4 * scores * HD, 4 * count * width, scores),
        name=name,
    )(*operands)
    if last:
        return results
    return {
        shift: (results[i], results[len(shifts) + i]) for i, shift in enumerate(shifts)
    }


def combine_kernel(*refs):
    result, stats, *refs = refs
    *parts, weight, attended, sent = refs[: len(refs)]
    rows, width = result.shape
    heads = width // HD
    extents = [stats[...]]
    for part in parts:
        tile = part[rows:, :].astype(jnp.float32)
        groups = -(-3 * heads // STAT_ROWS)
        lines = jnp.concatenate(
            [tile[:, j * rows : (j + 1) * rows] for j in range(groups)], axis=0
        )
        line = sum(lines[i * heads : (i + 1) * heads] for i in range(3))
        line = jnp.concatenate([line, jnp.zeros((HD - heads, rows), jnp.float32)], axis=0)
        extents.append(jnp.transpose(line))
    top = functools.reduce(jnp.maximum, extents)
    shares = [jnp.exp2(extent - top) for extent in extents]
    whole = sum(shares)
    shares = [share / whole for share in shares]
    for head in range(heads):
        span = slice(head * HD, (head + 1) * HD)
        mixes = [result[:, span]] + [part[:rows, span].astype(jnp.float32) for part in parts]
        mixed = sum(mix * share[:, head : head + 1] for mix, share in zip(mixes, shares))
        attended[:, span] = mixed.astype(jnp.bfloat16)
    index = lax.axis_index("tp")
    ways = sent.shape[0] + 1
    columns = weight.shape[1] // ways
    for shift in range(1, ways):
        sent[shift - 1] = jnp.dot(
            attended[...],
            weight[:, lanes((index ^ shift) * columns, columns)],
            preferred_element_type=jnp.float32,
        ).astype(jnp.bfloat16)


def combine(result, stats, parts, w_out, ways):
    rows, width = result.shape
    columns = w_out.shape[1] // ways
    return pl.pallas_call(
        combine_kernel,
        in_specs=[VMEM] * (3 + len(parts)),
        out_specs=[VMEM] * 2,
        out_shape=[
            jax.ShapeDtypeStruct((rows, width), jnp.bfloat16),
            jax.ShapeDtypeStruct((ways - 1, rows, columns), jnp.bfloat16),
        ],
        compiler_params=params(20),
        cost_estimate=cost(2 * rows * width * columns * (ways - 1), 2 * width * w_out.shape[1]),
        name="combine_send",
    )(result, stats, *parts, w_out)


def keep_kernel(attended, weight, hidden, kept):
    columns = hidden.shape[1]
    product = jnp.dot(
        attended[...],
        weight[:, lanes(lax.axis_index("tp") * columns, columns)],
        preferred_element_type=jnp.float32,
    )
    kept[...] = product + hidden[...].astype(jnp.float32)


def keep(attended, w_out, hidden):
    rows, width = attended.shape
    return pl.pallas_call(
        keep_kernel,
        in_specs=[VMEM] * 3,
        out_specs=VMEM,
        out_shape=jax.ShapeDtypeStruct(hidden.shape, jnp.float32),
        compiler_params=params(20),
        cost_estimate=cost(2 * rows * width * hidden.shape[1], 2 * width * w_out.shape[1]),
        name="keep_own",
    )(attended, w_out, hidden)


def local(
    hidden_in, w_query, w_keyval, w_out, prompt_cache, tail_cache, tail_table, tail_len, shared_len
):
    rows = hidden_in.shape[0]
    group = lax.axis_size("seq") // REQ
    ways = lax.axis_size("tp")
    cycle = cycle_of(group)
    seq = lax.axis_index("seq")
    request = seq // group
    member = seq % group
    half = REQ // 2
    piece = prompt_cache.shape[0]
    middle = piece // 2

    pieces = [hidden_in] + [swap(hidden_in, "tp", shift) for shift in range(1, ways)]
    prompt = viewed(prompt_cache)
    ahead, behind = [prompt], [prompt]

    def step(*others):
        for blocks, way in ((ahead, 1), (behind, -1)):
            blocks.append(turn(after(blocks[-1], *others), cycle, group, way))

    step()
    own_length = lax.dynamic_index_in_dim(tail_len, request, 0, keepdims=False)
    positions = shared_len[0] + own_length + member * rows + jnp.arange(rows, dtype=jnp.int32)
    cosine, sine = angles(positions)
    query, normed = project_query(pieces, w_query, cosine, sine)
    queries = [query] + [swap(query, "seq", shift) for shift in range(1, group)]
    fresh_keys, fresh_values, new_cache = project_keyval(normed, w_keyval, cosine, sine)
    step(fresh_keys)
    tail = viewed(tail_cache.reshape(-1, 2, tail_cache.shape[3]))
    slots = tail_cache.shape[0]
    near_block = part_keyval([tail, prompt, ahead[1], behind[1]], "part_near")

    facts = (tail_len, shared_len, tail_table)
    others = list(range(1, group))
    near = (
        [(0, 0, piece), (-1, 0, piece), (1, 0, piece)],
        slots,
        piece,
        [near_block, fresh_keys, fresh_values],
        None,
        False,
    )
    state = attend(facts, queries, [0], *near, "attend_near_own")
    ready = after(queries[1], state[0][1])
    state |= attend(facts, [query, ready, *queries[2:]], others, *near, "attend_near_others")
    step(state[1][1])
    rings = [(-2, 0, piece), (2, 0, piece)]
    state = attend(
        facts, queries, [0, *others], rings, 0, piece, [ahead[2], behind[2]], state, False, "attend_mid"
    )
    far_low = turn(after(ahead[3], state[1][1])[:middle], cycle, group, 1)
    far_high = turn(after(behind[3], state[1][1])[middle:], cycle, group, -1)
    rings = [(-3, 0, piece), (3, 0, piece), (-half, 0, middle), (half, middle, piece - middle)]
    far_blocks = [ahead[3], behind[3], far_low, far_high]
    far = (rings, 0, piece, far_blocks, state, True)
    parts = attend(facts, queries, others, *far, "attend_far_others")
    ready = after(query, parts[0])
    result, stats = attend(facts, [ready, *queries[1:]], [0], *far, "attend_far_own")
    parts = [swap(part, "seq", shift + 1) for shift, part in enumerate(parts)]
    attended, sent = combine(result, stats, parts, w_out, ways)
    received = [swap(sent[shift - 1], "tp", shift) for shift in range(1, ways)]
    total = keep(attended, w_out, hidden_in)
    for part in received:
        total = total + part.astype(jnp.float32)
    return (total.astype(jnp.bfloat16), new_cache)


def solution(mesh):
    return jax.shard_map(
        local,
        mesh=mesh,
        in_specs=(
            P("seq", "tp"),
            P(None, "tp"),
            P(None, None, "tp"),
            P("tp", None),
            P("seq", None, "tp"),
            P("seq", None, None, "tp"),
            P(),
            P(),
            P(),
        ),
        out_specs=(P("seq", "tp"), P("seq", None, "tp")),
        check_vma=False,
    )
```

time: 91.6 us -> 99 us (1.081)
  Pallas kernels: 40.9 us -> 64.4 us
  waiting for transfers between devices: 25.7 us -> 14.3 us
  local copies, waits for them, and re-layouts: 8.93 us -> 3.56 us
    pallas_call x7 -> x8, Pallas kernels: 38.8 us -> 62.2 us  [the longest x5 33.4 us: attend(): pl.pallas_call(functools.partial(attend_kernel, (group, shifts, rings, sl...]
    unnamed x25 -> x21, local copies, waits for them, and re-layouts: 8.31 us -> 1.95 us
    ppermute x4, waiting for transfers between devices: 12.4 us -> 6.52 us  [swap(): return lax.ppermute(value, axis, pairs)]
    ppermute x8, waiting for transfers between devices: 13.3 us -> 7.76 us  [turn(): return lax.ppermute(value, 'seq', pairs)]
  transfers between devices with their start and end apart: 12 -> 12, of which waited for: 6 -> 5; matrix products, arithmetic and copies ran while one was open for 2% -> 3% of each run, Pallas kernels for 36% -> 57%
where the time goes in v3:
time: 99 us; the launch traced here: 98.7 us
  Pallas kernels  64.4 us (65%)
  waiting for transfers between devices  14.3 us (14%)
  starting transfers between devices  12 us (12%)
  local copies, waits for them, and re-layouts  3.56 us (4%)
  other arithmetic  2.33 us (2%)
  between operations  2.14 us (2%)
    pallas_call x5, Pallas kernels, attend(): pl.pallas_call(functools.partial(attend_kernel, (group, shifts, rings, sl...  33.4 us
    pallas_call x1, Pallas kernels, project_keyval(): pl.pallas_call(keyval_kernel, in_specs=[VMEM, HBM, VMEM, VMEM], out_specs...  16.4 us
    ppermute x8, starting transfers between devices, turn(): return lax.ppermute(value, 'seq', pairs)  9.43 us
    ppermute x8, waiting for transfers between devices, turn(): return lax.ppermute(value, 'seq', pairs)  7.76 us
    ppermute x4, waiting for transfers between devices, swap(): return lax.ppermute(value, axis, pairs)  6.52 us
    pallas_call x1, Pallas kernels, project_query(): pl.pallas_call(query_kernel, in_specs=[VMEM] * len(pieces) + [HBM, VMEM,...  6.38 us
    pallas_call x1, Pallas kernels, part_keyval(): pl.pallas_call(part_kernel, in_specs=[VMEM] * len(blocks), out_specs=VMEM...  5.98 us
    ppermute x4, starting transfers between devices, swap(): return lax.ppermute(value, axis, pairs)  2.58 us
  transfers between devices with their start and end apart: 12, of which 5 were waited for; matrix products, arithmetic and copies ran while one was open for 3% of the time, Pallas kernels for 57%

profile of v3, /device:TPU:0, one launch (start us, length us, event | category | flops | bytes accessed | tf_op | source)
XLA Modules:
  0.0 98.7 jit_solution(18329390430434713283)
XLA Ops:
  0.6 3.0 %collective-permute-start.4 = (bf16[128,8,2,128]{3,2,1,0:T(2,128)(2,1)}, bf16[128,8,2,128]{3,2,1,0:T(2,128)(2,1)}, u32[]{:S(2)}, u32[]{:S(2)}) collective-permute-start(bf16[128,8,2,128]{3,2,1,0:T(2,128)(2,1)} %bitcast.15), channel_id=1, source_target_pairs={{0,4},{2,6},{8,0},{10,2},{16,8},{18,10},{24,16},{26,18},{28,24},{3... | collective-permute-start | bytes 1572872 | tf_op jit(solution)/shard_map/ppermute | solution.py:50
  4.4 1.2 %dynamic_slice.4 = s32[1]{0:T(128)} dynamic-slice(s32[8]{0:T(128)} %refs_0_.11, s32[]{:T(128)S(6)} %select_n.16), dynamic_slice_sizes={1} | dynamic-slice | bytes 12 | tf_op jit(solution)/shard_map/jit(dynamic_index_in_dim)/dynamic_slice | solution.py:535
  6.4 0.5 fusion
  6.9 0.8 pad_maximum_fusion
  7.8 0.8 copy-done.8
  8.5 6.4 %project_query.1 = (bf16[256,1024]{1,0:T(8,128)(2,1)}, bf16[256,2048]{1,0:T(8,128)(2,1)}) custom-call(bf16[256,1024]{1,0:T(8,128)(2,1)} %hidden.1, bf16[256,1024]{1,0:T(8,128)(2,1)} %copy-done.8, bf16[2048,1024]{1,0:T(8,128)(2,1)} %refs_2_.6, f32[256,128]{1,0:T(8,128)} %get-tuple-element.55.refs_3_.cosine, f32[256,128]{1,0:T(8,128)} %get-tuple-element.56.refs_4_.sine), custom_call_target="tpu_custom_call" | custom-call | flops 1073741824 | bytes 4194304 | tf_op jit(solution)/shard_map/project_query/pallas_call | solution.py:155
  14.9 1.9 %collective-permute-start.1 = (bf16[256,1024]{1,0:T(8,128)(2,1)}, bf16[256,1024]{1,0:T(8,128)(2,1)S(1)}, u32[]{:S(2)}, u32[]{:S(2)}) collective-permute-start(bf16[256,1024]{1,0:T(8,128)(2,1)} %get-tuple-element.44.refs_3_), channel_id=1, source_target_pairs={{0,2},{2,0},{4,6},{6,4},{8,10},{10,8},{12,14},{14,12},{16,18},{18,... | collective-permute-start | bytes 1572872 | tf_op jit(solution)/shard_map/ppermute | solution.py:41
  16.9 16.4 %project_keyval.1 = (bf16[256,1024]{1,0:T(8,128)(2,1)}, bf16[256,1024]{1,0:T(8,128)(2,1)}, bf16[256,8,2,128]{3,2,1,0:T(2,128)(2,1)}) custom-call(bf16[256,2048]{1,0:T(8,128)(2,1)} %get-tuple-element.28.normed, bf16[2048,8,2,128]{3,2,1,0:T(2,128)(2,1)} %bitcast.19, f32[256,128]{1,0:T(8,128)} %get-tuple-element.55.refs_3_.cosine, ...), custom_call_target="tpu_custom_call" | custom-call | flops 2147483648 | bytes 8388608 | tf_op jit(solution)/shard_map/project_keyval/pallas_call | solution.py:222
  33.3 1.6 %collective-permute-start.3 = (bf16[128,8,2,128]{3,2,1,0:T(2,128)(2,1)}, bf16[128,8,2,128]{3,2,1,0:T(2,128)(2,1)}, u32[]{:S(2)}, u32[]{:S(2)}) collective-permute-start(bf16[128,8,2,128]{3,2,1,0:T(2,128)(2,1)} %collective-permute-done.2.refs_2_), channel_id=1, source_target_pairs={{0,8},{2,10},{8,16},{10,18},{16,24},{18,26},{24,28},{26,30},{28,20... | collective-permute-start | bytes 1572872 | tf_op jit(solution)/shard_map/ppermute | solution.py:50
  35.0 0.4 collective-permute-start.6
  35.5 1.0 %copy-done.6 = bf16[128,2,1024]{2,1,0:T(2,128)(2,1)S(1)} copy-done((bf16[128,2,1024]{2,1,0:T(2,128)(2,1)S(1)}, bf16[128,2,1024]{2,1,0:T(2,128)(2,1)}, u32[]{:S(2)}) %copy-start.6) | copy-done | bytes 524312
  36.6 6.0 %part_near.1.refs_4_ = bf16[2,640,1024]{2,1,0:T(8,128)(2,1)S(1)} custom-call(bf16[256,8,2,128]{3,2,1,0:T(2,128)(2,1)S(1)} %bitcast.14, bf16[128,8,2,128]{3,2,1,0:T(2,128)(2,1)S(1)} %bitcast.17, bf16[128,8,2,128]{3,2,1,0:T(2,128)(2,1)} %collective-permute-done.2.refs_2_, bf16[128,8,2,128]{3,2,1,0:T(2,128)(2,1)} %collective-permute-done.4.refs_3_), custom_call_target="tpu_custom_call" | custom-call | bytes 5242880 | tf_op jit(solution)/shard_map/part_near/pallas_call | solution.py:109
  42.6 5.4 %attend_near_own.1 = (f32[256,1024]{1,0:T(8,128)S(1)}, f32[256,128]{1,0:T(8,128)S(1)}) custom-call(s32[8]{0:T(128)S(1)} %copy-done.7, s32[1]{0:T(128)S(6)} %copy.16.refs_1_, s32[8,4]{1,0:T(8,128)S(1)} %copy.15.refs_2_, bf16[256,1024]{1,0:T(8,128)(2,1)S(1)} %copy-done.1, bf16[2,640,1024]{2,1,0:T(8,128)(2,1)S(1)} %part_near.1.refs_4_, ...), custom_call_target="tpu_custom_call" | custom-call | flops 939524096 | bytes 3670016 | tf_op jit(solution)/shard_map/attend_near_own/pallas_call | solution.py:418
  48.0 5.4 %attend_near_others.1 = (f32[256,1024]{1,0:T(8,128)S(1)}, f32[256,128]{1,0:T(8,128)S(1)}) custom-call(s32[8]{0:T(128)S(1)} %copy-done.7, s32[1]{0:T(128)S(6)} %copy.16.refs_1_, s32[8,4]{1,0:T(8,128)S(1)} %copy.15.refs_2_, bf16[256,1024]{1,0:T(8,128)(2,1)S(1)} %collective-permute-done.1.refs_3_.refs_4_, bf16[2,640,1024]{2,1,0:T(8,128)(2,1)S(1)} %part_near.1.refs_4_, ...), custom_call_target="tpu_custom_call" | custom-call | flops 939524096 | bytes 3670016 | tf_op jit(solution)/shard_map/attend_near_others/pallas_call | solution.py:418
  53.4 1.6 %collective-permute-start.5 = (bf16[128,8,2,128]{3,2,1,0:T(2,128)(2,1)}, bf16[128,8,2,128]{3,2,1,0:T(2,128)(2,1)S(1)}, u32[]{:S(2)}, u32[]{:S(2)}) collective-permute-start(bf16[128,8,2,128]{3,2,1,0:T(2,128)(2,1)} %collective-permute-done.3.refs_5_), channel_id=1, source_target_pairs={{0,8},{2,10},{8,16},{10,18},{16,24},{18,26},{24,28},{26,30},{28,20... | collective-permute-start | bytes 1572872 | tf_op jit(solution)/shard_map/ppermute | solution.py:50
  55.0 0.4 collective-permute-start.7
  55.5 10.2 %attend_mid.1 = (f32[256,1024]{1,0:T(8,128)S(1)}, f32[256,1024]{1,0:T(8,128)S(1)}, f32[256,128]{1,0:T(8,128)S(1)}, f32[256,128]{1,0:T(8,128)S(1)}) custom-call(s32[8]{0:T(128)S(1)} %copy-done.7, s32[1]{0:T(128)S(6)} %copy.16.refs_1_, s32[8,4]{1,0:T(8,128)S(1)} %copy.15.refs_2_, bf16[256,1024]{1,0:T(8,128)(2,1)S(1)} %copy-done.1, ...), custom_call_target="tpu_custom_call" | custom-call | flops 536870912 | bytes 1048576 | tf_op jit(solution)/shard_map/attend_mid/pallas_call | solution.py:418
  65.7 1.5 %collective-permute-done.5.refs_4_ = bf16[128,8,2,128]{3,2,1,0:T(2,128)(2,1)S(1)} collective-permute-done((bf16[128,8,2,128]{3,2,1,0:T(2,128)(2,1)}, bf16[128,8,2,128]{3,2,1,0:T(2,128)(2,1)S(1)}, u32[]{:S(2)}, u32[]{:S(2)}) %collective-permute-start.5) | collective-permute-done | bytes 524320 | tf_op jit(solution)/shard_map/ppermute | solution.py:50
  67.2 0.2 slice.6
  67.3 1.6 %collective-permute-start.8 = (bf16[64,8,2,128]{3,2,1,0:T(2,128)(2,1)S(1)}, bf16[64,8,2,128]{3,2,1,0:T(2,128)(2,1)S(1)}, u32[]{:S(2)}, u32[]{:S(2)}) collective-permute-start(bf16[64,8,2,128]{3,2,1,0:T(2,128)(2,1)S(1)} %slice.6), channel_id=1, source_target_pairs={{0,8},{2,10},{8,16},{10,18},{16,24},{18,26},{24,28},{26,30},{28,20... | collective-permute-start | bytes 786440 | tf_op jit(solution)/shard_map/ppermute | solution.py:50
  69.0 0.2 slice.7
  69.2 0.5 collective-permute-start.9
  69.7 4.7 %collective-permute-done.8.refs_6_ = bf16[64,8,2,128]{3,2,1,0:T(2,128)(2,1)S(1)} collective-permute-done((bf16[64,8,2,128]{3,2,1,0:T(2,128)(2,1)S(1)}, bf16[64,8,2,128]{3,2,1,0:T(2,128)(2,1)S(1)}, u32[]{:S(2)}, u32[]{:S(2)}) %collective-permute-start.8) | collective-permute-done | bytes 262176 | tf_op jit(solution)/shard_map/ppermute | solution.py:50
  74.4 1.5 %collective-permute-done.9.refs_7_ = bf16[64,8,2,128]{3,2,1,0:T(2,128)(2,1)S(1)} collective-permute-done((bf16[64,8,2,128]{3,2,1,0:T(2,128)(2,1)S(1)}, bf16[64,8,2,128]{3,2,1,0:T(2,128)(2,1)S(1)}, u32[]{:S(2)}, u32[]{:S(2)}) %collective-permute-start.9) | collective-permute-done | bytes 262176 | tf_op jit(solution)/shard_map/ppermute | solution.py:50
  75.9 6.3 %attend_far_others.1 = bf16[272,1024]{1,0:T(8,128)(2,1)S(1)} custom-call(s32[8]{0:T(128)S(1)} %copy-done.7, s32[1]{0:T(128)S(6)} %copy.16.refs_1_, s32[8,4]{1,0:T(8,128)S(1)} %copy.15.refs_2_, bf16[256,1024]{1,0:T(8,128)(2,1)S(1)} %collective-permute-done.1.refs_3_.refs_4_, bf16[128,8,2,128]{3,2,1,0:T(2,128)(2,1)S(1)} %collective-permute-done.5.refs_4_, ...), custom_call_target="tpu_custom_call" | custom-call | flops 402653184 | bytes 1572864 | tf_op jit(solution)/shard_map/attend_far_others/pallas_call | solution.py:418
  82.2 0.6 collective-permute-start.10
  82.8 6.2 %attend_far_own.1 = (f32[256,1024]{1,0:T(8,128)S(1)}, f32[256,128]{1,0:T(8,128)S(1)}) custom-call(s32[8]{0:T(128)S(1)} %copy-done.7, s32[1]{0:T(128)S(6)} %copy.16.refs_1_, s32[8,4]{1,0:T(8,128)S(1)} %copy.15.refs_2_, bf16[256,1024]{1,0:T(8,128)(2,1)S(1)} %copy-done.1, bf16[128,8,2,128]{3,2,1,0:T(2,128)(2,1)S(1)} %collective-permute-done.5.refs_4_, ...), custom_call_target="tpu_custom_call" | custom-call | flops 402653184 | bytes 1572864 | tf_op jit(solution)/shard_map/attend_far_own/pallas_call | solution.py:418
  89.0 5.4 %collective-permute-done.10.refs_2_ = bf16[272,1024]{1,0:T(8,128)(2,1)S(1)} collective-permute-done((bf16[272,1024]{1,0:T(8,128)(2,1)S(1)}, bf16[272,1024]{1,0:T(8,128)(2,1)S(1)}, u32[]{:S(2)}, u32[]{:S(2)}) %collective-permute-start.10) | collective-permute-done | bytes 557088 | tf_op jit(solution)/shard_map/ppermute | solution.py:41
  94.3 1.4 %combine_send.1 = (bf16[256,1024]{1,0:T(8,128)(2,1)S(1)}, bf16[1,256,1024]{2,1,0:T(8,128)(2,1)S(1)}) custom-call(f32[256,1024]{1,0:T(8,128)S(1)} %get-tuple-element.47.refs_0_, f32[256,128]{1,0:T(8,128)S(1)} %get-tuple-element.48.refs_1_, bf16[272,1024]{1,0:T(8,128)(2,1)S(1)} %collective-permute-done.10.refs_2_, bf16[1024,2048]{1,0:T(8,128)(2,1)S(1)} %copy-done), custom_call_target="tpu_custom_call" | custom-call | flops 536870912 | bytes 4194304 | tf_op jit(solution)/shard_map/combine_send/pallas_call | solution.py:475
  95.9 0.7 keep_own.1
  96.6 1.2 %collective-permute-done.11 = bf16[256,1024]{1,0:T(8,128)(2,1)S(1)} collective-permute-done((bf16[256,1024]{1,0:T(8,128)(2,1)S(1)}, bf16[256,1024]{1,0:T(8,128)(2,1)S(1)}, u32[]{:S(2)}, u32[]{:S(2)}) %collective-permute-start.11) | collective-permute-done | bytes 524320 | tf_op jit(solution)/shard_map/ppermute | solution.py:41
  97.7 0.9 add_convert_fusion
  (31 shorter events, 0.4 us)
Async XLA Ops:
  0.6 34.4 %collective-permute-start.4 = (bf16[128,8,2,128]{3,2,1,0:T(2,128)(2,1)}, bf16[128,8,2,128]{3,2,1,0:T(2,128)(2,1)}, u32[]{:S(2)}, u32[]{:S(2)}) collective-permute-start(bf16[128,8,2,128]{3,2,1,0:T(2,128)(2,1)} %bitcast.15), channel_id=1, source_target_pairs={{0,4},{2,6},{8,0},{10,2},{16,8},{18,10},{24,16},{26,18},{28,24},{3... | collective-permute-start | bytes 1572872 | tf_op jit(solution)/shard_map/ppermute | solution.py:50
  3.6 29.7 %collective-permute-start.2 = (bf16[128,8,2,128]{3,2,1,0:T(2,128)(2,1)}, bf16[128,8,2,128]{3,2,1,0:T(2,128)(2,1)}, u32[]{:S(2)}, u32[]{:S(2)}) collective-permute-start(bf16[128,8,2,128]{3,2,1,0:T(2,128)(2,1)} %bitcast.16), channel_id=1, source_target_pairs={{0,8},{2,10},{8,16},{10,18},{16,24},{18,26},{24,28},{26,30},{28,20... | collective-permute-start | bytes 1572872 | tf_op jit(solution)/shard_map/ppermute | solution.py:50
  3.8 4.0 %collective-permute-start = (bf16[256,1024]{1,0:T(8,128)(2,1)}, bf16[256,1024]{1,0:T(8,128)(2,1)S(1)}, u32[]{:S(2)}, u32[]{:S(2)}) collective-permute-start(bf16[256,1024]{1,0:T(8,128)(2,1)} %hidden.1), channel_id=1, source_target_pairs={{0,1},{1,0},{2,3},{3,2},{4,5},{5,4},{6,7},{7,6},{8,9},{9,8},{10,11... | collective-permute-start | bytes 1572872 | tf_op jit(solution)/shard_map/ppermute | solution.py:41
  7.7 0.8 copy-start.8
  14.9 33.0 %collective-permute-start.1 = (bf16[256,1024]{1,0:T(8,128)(2,1)}, bf16[256,1024]{1,0:T(8,128)(2,1)S(1)}, u32[]{:S(2)}, u32[]{:S(2)}) collective-permute-start(bf16[256,1024]{1,0:T(8,128)(2,1)} %get-tuple-element.44.refs_3_), channel_id=1, source_target_pairs={{0,2},{2,0},{4,6},{6,4},{8,10},{10,8},{12,14},{14,12},{16,18},{18,... | collective-permute-start | bytes 1572872 | tf_op jit(solution)/shard_map/ppermute | solution.py:41
  16.9 18.6 %copy-start.9 = (s32[8,4]{0,1:T(4,128)S(1)}, s32[8,4]{0,1:T(4,128)}, u32[]{:S(2)}) copy-start(s32[8,4]{0,1:T(4,128)} %param.15) | copy-start | bytes 388
  16.9 18.6 %copy-start.5 = (bf16[2,128,2,1024]{3,2,1,0:T(2,128)(2,1)S(1)}, bf16[2,128,2,1024]{3,2,1,0:T(2,128)(2,1)}, u32[]{:S(2)}) copy-start(bf16[2,128,2,1024]{3,2,1,0:T(2,128)(2,1)} %param.14) | copy-start | bytes 3145732
  16.9 25.7 %copy-start.7 = (s32[8]{0:T(128)S(1)}, s32[8]{0:T(128)}, u32[]{:S(2)}) copy-start(s32[8]{0:T(128)} %refs_0_.11) | copy-start | bytes 100
  33.3 9.3 %copy-start.1 = (bf16[256,1024]{1,0:T(8,128)(2,1)S(1)}, bf16[256,1024]{1,0:T(8,128)(2,1)}, u32[]{:S(2)}) copy-start(bf16[256,1024]{1,0:T(8,128)(2,1)} %get-tuple-element.44.refs_3_) | copy-start | bytes 1572868
  33.3 9.3 %copy-start.3 = (bf16[256,1024]{1,0:T(8,128)(2,1)S(1)}, bf16[256,1024]{1,0:T(8,128)(2,1)}, u32[]{:S(2)}) copy-start(bf16[256,1024]{1,0:T(8,128)(2,1)} %get-tuple-element.29.refs_5_) | copy-start | bytes 1572868
  33.3 9.3 %copy-start.4 = (bf16[256,1024]{1,0:T(8,128)(2,1)S(1)}, bf16[256,1024]{1,0:T(8,128)(2,1)}, u32[]{:S(2)}) copy-start(bf16[256,1024]{1,0:T(8,128)(2,1)} %get-tuple-element.31.refs_6_) | copy-start | bytes 1572868
  33.3 20.0 %collective-permute-start.3 = (bf16[128,8,2,128]{3,2,1,0:T(2,128)(2,1)}, bf16[128,8,2,128]{3,2,1,0:T(2,128)(2,1)}, u32[]{:S(2)}, u32[]{:S(2)}) collective-permute-start(bf16[128,8,2,128]{3,2,1,0:T(2,128)(2,1)} %collective-permute-done.2.refs_2_), channel_id=1, source_target_pairs={{0,8},{2,10},{8,16},{10,18},{16,24},{18,26},{24,28},{26,30},{28,20... | collective-permute-start | bytes 1572872 | tf_op jit(solution)/shard_map/ppermute | solution.py:50
  35.0 20.0 %collective-permute-start.6 = (bf16[128,8,2,128]{3,2,1,0:T(2,128)(2,1)}, bf16[128,8,2,128]{3,2,1,0:T(2,128)(2,1)}, u32[]{:S(2)}, u32[]{:S(2)}) collective-permute-start(bf16[128,8,2,128]{3,2,1,0:T(2,128)(2,1)} %collective-permute-done.4.refs_3_), channel_id=1, source_target_pairs={{0,4},{2,6},{8,0},{10,2},{16,8},{18,10},{24,16},{26,18},{28,24},{3... | collective-permute-start | bytes 1572872 | tf_op jit(solution)/shard_map/ppermute | solution.py:50
  35.5 1.0 %copy-start.6 = (bf16[128,2,1024]{2,1,0:T(2,128)(2,1)S(1)}, bf16[128,2,1024]{2,1,0:T(2,128)(2,1)}, u32[]{:S(2)}) copy-start(bf16[128,2,1024]{2,1,0:T(2,128)(2,1)} %param.13) | copy-start | bytes 1572868
  53.4 13.8 %collective-permute-start.5 = (bf16[128,8,2,128]{3,2,1,0:T(2,128)(2,1)}, bf16[128,8,2,128]{3,2,1,0:T(2,128)(2,1)S(1)}, u32[]{:S(2)}, u32[]{:S(2)}) collective-permute-start(bf16[128,8,2,128]{3,2,1,0:T(2,128)(2,1)} %collective-permute-done.3.refs_5_), channel_id=1, source_target_pairs={{0,8},{2,10},{8,16},{10,18},{16,24},{18,26},{24,28},{26,30},{28,20... | collective-permute-start | bytes 1572872 | tf_op jit(solution)/shard_map/ppermute | solution.py:50
  55.0 13.9 %collective-permute-start.7 = (bf16[128,8,2,128]{3,2,1,0:T(2,128)(2,1)}, bf16[128,8,2,128]{3,2,1,0:T(2,128)(2,1)S(1)}, u32[]{:S(2)}, u32[]{:S(2)}) collective-permute-start(bf16[128,8,2,128]{3,2,1,0:T(2,128)(2,1)} %collective-permute-done.6.refs_6_), channel_id=1, source_target_pairs={{0,4},{2,6},{8,0},{10,2},{16,8},{18,10},{24,16},{26,18},{28,24},{3... | collective-permute-start | bytes 1572872 | tf_op jit(solution)/shard_map/ppermute | solution.py:50
  65.6 28.7 %copy-start = (bf16[1024,2048]{1,0:T(8,128)(2,1)S(1)}, bf16[1024,2048]{1,0:T(8,128)(2,1)}, u32[]{:S(2)}) copy-start(bf16[1024,2048]{1,0:T(8,128)(2,1)} %weight.1) | copy-start | bytes 12582916
  67.3 7.0 %collective-permute-start.8 = (bf16[64,8,2,128]{3,2,1,0:T(2,128)(2,1)S(1)}, bf16[64,8,2,128]{3,2,1,0:T(2,128)(2,1)S(1)}, u32[]{:S(2)}, u32[]{:S(2)}) collective-permute-start(bf16[64,8,2,128]{3,2,1,0:T(2,128)(2,1)S(1)} %slice.6), channel_id=1, source_target_pairs={{0,8},{2,10},{8,16},{10,18},{16,24},{18,26},{24,28},{26,30},{28,20... | collective-permute-start | bytes 786440 | tf_op jit(solution)/shard_map/ppermute | solution.py:50
  69.2 6.8 %collective-permute-start.9 = (bf16[64,8,2,128]{3,2,1,0:T(2,128)(2,1)S(1)}, bf16[64,8,2,128]{3,2,1,0:T(2,128)(2,1)S(1)}, u32[]{:S(2)}, u32[]{:S(2)}) collective-permute-start(bf16[64,8,2,128]{3,2,1,0:T(2,128)(2,1)S(1)} %slice.7), channel_id=1, source_target_pairs={{0,4},{2,6},{8,0},{10,2},{16,8},{18,10},{24,16},{26,18},{28,24},{3... | collective-permute-start | bytes 786440 | tf_op jit(solution)/shard_map/ppermute | solution.py:50
  82.2 12.2 %collective-permute-start.10 = (bf16[272,1024]{1,0:T(8,128)(2,1)S(1)}, bf16[272,1024]{1,0:T(8,128)(2,1)S(1)}, u32[]{:S(2)}, u32[]{:S(2)}) collective-permute-start(bf16[272,1024]{1,0:T(8,128)(2,1)S(1)} %attend_far_others.1), channel_id=1, source_target_pairs={{0,2},{2,0},{4,6},{6,4},{8,10},{10,8},{12,14},{14,12},{16,18},{18,... | collective-permute-start | bytes 1671176 | tf_op jit(solution)/shard_map/ppermute | solution.py:41
  82.8 13.1 %copy-start.2 = (bf16[256,1024]{1,0:T(8,128)(2,1)S(1)}, bf16[256,1024]{1,0:T(8,128)(2,1)}, u32[]{:S(2)}) copy-start(bf16[256,1024]{1,0:T(8,128)(2,1)} %hidden.1) | copy-start | bytes 1572868
  95.8 2.0 %collective-permute-start.11 = (bf16[256,1024]{1,0:T(8,128)(2,1)S(1)}, bf16[256,1024]{1,0:T(8,128)(2,1)S(1)}, u32[]{:S(2)}, u32[]{:S(2)}) collective-permute-start(bf16[256,1024]{1,0:T(8,128)(2,1)S(1)} %bitcast.18), channel_id=1, source_target_pairs={{0,1},{1,0},{2,3},{3,2},{4,5},{5,4},{6,7},{7,6},{8,9},{9,8},{10,11... | collective-permute-start | bytes 1572872 | tf_op jit(solution)/shard_map/ppermute | solution.py:41

commit v4 on v3

--- a/solution.py
+++ b/solution.py
@@ -10,6 +10,7 @@
 
 HD = 128
 REQ = 8
+BLK = 128
 NEGATIVE = -1e30
 SCALE = float(HD**-0.5 * np.log2(np.e))
 STAT_ROWS = 16
@@ -83,23 +84,44 @@
     return block.reshape(count, pair, width // HD, HD).transpose(0, 2, 1, 3)
 
 
-def take_apart(block, apart, begin, result, offset):
+def order_rows(stride, back):
+    rows = 2 * HD
+    places = rows // stride
+    row = lax.broadcasted_iota(jnp.int32, (rows, rows), 1 if back else 0)
+    column = lax.broadcasted_iota(jnp.int32, (rows, rows), 0 if back else 1)
+    source = lax.rem(row, places) * stride + lax.div(row, places)
+    return jnp.where(column == source, 1.0, 0.0).astype(jnp.bfloat16)
+
+
+def reordered(order, tiles):
+    both = tiles[0] if len(tiles) == 1 else jnp.concatenate(tiles, axis=1)
+    mixed = jnp.dot(order, both, preferred_element_type=jnp.float32).astype(jnp.bfloat16)
+    return [mixed[:, i * HD : (i + 1) * HD] for i in range(len(tiles))]
+
+
+def take_apart(block, order, result, offset):
     count, heads = block.shape[:2]
     stride = 2 * heads
+    places = 2 * HD // stride
     flat = block.reshape(count * stride, HD)
-    apart[begin * stride : (begin + count) * stride, :] = flat[...].astype(jnp.float32)
-    for head in range(heads):
-        for j in range(2):
-            result[j, offset : offset + count, head * HD : (head + 1) * HD] = apart[
-                pl.ds(begin * stride + 2 * head + j, count, stride=stride), :
-            ].astype(jnp.bfloat16)
+    for start in range(0, count, 2 * places):
+        starts = [at for at in (start, start + places) if at < count]
+        tiles = [flat[at * stride : (at + places) * stride, :] for at in starts]
+        for at, tile in zip(starts, reordered(order, tiles)):
+            for head in range(heads):
+                for j in range(2):
+                    line = (2 * head + j) * places
+                    result[
+                        j, offset + at : offset + at + places, head * HD : (head + 1) * HD
+                    ] = tile[line : line + places]
 
 
 def part_kernel(*refs):
-    *blocks, result, apart = refs
+    *blocks, result = refs
+    order = order_rows(2 * blocks[0].shape[1], False)
     offset = 0
     for block in blocks:
-        take_apart(block, apart, offset, result, offset)
+        take_apart(block, order, result, offset)
         offset += block.shape[0]
 
 
@@ -111,7 +133,6 @@
         in_specs=[VMEM] * len(blocks),
         out_specs=VMEM,
         out_shape=jax.ShapeDtypeStruct((2, count, heads * HD), jnp.bfloat16),
-        scratch_shapes=[pltpu.VMEM((2 * heads * count, HD), jnp.float32)],
         compiler_params=params(16),
         cost_estimate=cost(0, 8 * count * heads * HD),
         name=name,
@@ -119,12 +140,10 @@
 
 
 def query_kernel(*refs):
-    *pieces, weight, cosine, sine, query, normed, near, arrived = refs
-    count, _, wide = near.shape
+    *pieces, weight, cosine, sine, query, normed, near, total, arrived = refs
+    count, depth, width = near.shape
     copies = [
-        pltpu.make_async_copy(
-            weight.at[:, pl.ds(i * wide, wide)], near.at[i], arrived.at[i]
-        )
+        pltpu.make_async_copy(weight.at[pl.ds(i * depth, depth)], near.at[i], arrived.at[i])
         for i in range(count)
     ]
     for copy in copies:
@@ -139,19 +158,30 @@
     inverse = lax.rsqrt(spread + 1e-05)
     for shift, v in enumerate(values):
         normed[:, lanes((index ^ shift) * columns, columns)] = (v * inverse).astype(jnp.bfloat16)
+    wide = min(width, 2 * HD)
     for i, copy in enumerate(copies):
         copy.wait()
-        product = jnp.dot(normed[...], near[i], preferred_element_type=jnp.float32)
-        for start in range(0, wide, HD):
-            query[:, i * wide + start : i * wide + start + HD] = rotated(
-                product[:, start : start + HD], cosine[...], sine[...]
-            ).astype(jnp.bfloat16)
+        for base in range(0, width, wide):
+            span = slice(base, base + wide)
+            product = jnp.dot(
+                normed[:, i * depth : (i + 1) * depth],
+                near[i, :, span],
+                preferred_element_type=jnp.float32,
+            )
+            if i:
+                product += total[:, span]
+            if i < count - 1:
+                total[:, span] = product
+                continue
+            for start in range(0, wide, HD):
+                query[:, base + start : base + start + HD] = rotated(
+                    product[:, start : start + HD], cosine[...], sine[...]
+                ).astype(jnp.bfloat16)
 
 
 def project_query(pieces, w_query, cosine, sine):
     rows, columns = pieces[0].shape
     depth, width = w_query.shape
-    wide = min(width, 2 * HD)
     return pl.pallas_call(
         query_kernel,
         in_specs=[VMEM] * len(pieces) + [HBM, VMEM, VMEM],
@@ -161,8 +191,9 @@
             jax.ShapeDtypeStruct((rows, depth), jnp.bfloat16),
         ],
         scratch_shapes=[
-            pltpu.VMEM((width // wide, depth, wide), jnp.bfloat16),
-            pltpu.SemaphoreType.DMA((width // wide,)),
+            pltpu.VMEM((2, depth // 2, width), jnp.bfloat16),
+            pltpu.VMEM((rows, width), jnp.float32),
+            pltpu.SemaphoreType.DMA((2,)),
         ],
         compiler_params=params(60),
         cost_estimate=cost(2 * rows * depth * width, 2 * depth * width),
@@ -171,7 +202,7 @@
 
 
 def keyval_kernel(
-    normed, weight, cosine, sine, keys, values, cache, near, arrived, apart, total, woven
+    normed, weight, cosine, sine, keys, values, cache, near, arrived, apart, total
 ):
     parts, chunk, heads = near.shape[:3]
     rows = normed.shape[0]
@@ -182,18 +213,16 @@
     ]
     for copy in copies:
         copy.start()
+    order = order_rows(stride, False)
     for i, copy in enumerate(copies):
         copy.wait()
-        flat = apart.at[i % 2]
-        flat[...] = near.at[i].reshape(chunk * stride, HD)[...].astype(jnp.float32)
+        here = apart.at[i % 2]
+        take_apart(near.at[i], order, here, 0)
         for head in range(heads):
-            both = [
-                flat[pl.ds(2 * head + j, chunk, stride=stride), :].astype(jnp.bfloat16)
-                for j in range(2)
-            ]
+            span = slice(head * HD, (head + 1) * HD)
             product = jnp.dot(
                 normed[:, i * chunk : (i + 1) * chunk],
-                jnp.concatenate(both, axis=1),
+                jnp.concatenate([here[0, :, span], here[1, :, span]], axis=1),
                 preferred_element_type=jnp.float32,
             )
             span = slice(2 * head * HD, 2 * (head + 1) * HD)
@@ -208,9 +237,24 @@
         value = total[:, begin + HD : begin + 2 * HD].astype(jnp.bfloat16)
         keys[:, span] = key
         values[:, span] = value
-        woven[pl.ds(2 * head, rows, stride=stride), :] = key.astype(jnp.float32)
-        woven[pl.ds(2 * head + 1, rows, stride=stride), :] = value.astype(jnp.float32)
-    cache.reshape(rows * stride, HD)[...] = woven[...].astype(jnp.bfloat16)
+    order = order_rows(stride, True)
+    places = 2 * HD // stride
+    flat = cache.reshape(rows * stride, HD)
+    for start in range(0, rows, 2 * places):
+        starts = [at for at in (start, start + places) if at < rows]
+        tiles = [
+            jnp.concatenate(
+                [
+                    pair[at : at + places, head * HD : (head + 1) * HD]
+                    for head in range(heads)
+                    for pair in (keys, values)
+                ],
+                axis=0,
+            )
+            for at in starts
+        ]
+        for at, tile in zip(starts, reordered(order, tiles)):
+            flat[at * stride : (at + places) * stride, :] = tile
 
 
 def project_keyval(normed, w_keyval, cosine, sine):
@@ -218,7 +262,7 @@
     weight = viewed(w_keyval)
     heads = weight.shape[1]
     width = heads * HD
-    chunk = min(depth, 256)
+    chunk = min(depth, 512)
     keys, values, cache = pl.pallas_call(
         keyval_kernel,
         in_specs=[VMEM, HBM, VMEM, VMEM],
@@ -231,9 +275,8 @@
         scratch_shapes=[
             pltpu.VMEM((depth // chunk, chunk, heads, 2, HD), jnp.bfloat16),
             pltpu.SemaphoreType.DMA((depth // chunk,)),
-            pltpu.VMEM((2, 2 * heads * chunk, HD), jnp.float32),
+            pltpu.VMEM((2, 2, chunk, width), jnp.bfloat16),
             pltpu.VMEM((rows, 2 * width), jnp.float32),
-            pltpu.VMEM((2 * heads * rows, HD), jnp.float32),
         ],
         compiler_params=params(57),
         cost_estimate=cost(4 * rows * depth * width, 4 * depth * width),
@@ -259,7 +302,7 @@
     lengths, shared, table = take(3)
     queries = take(len(shifts))
     if fresh:
-        block, fresh_keys, fresh_values = take(3)
+        *parted, fresh_keys, fresh_values = take(fresh)
     else:
         raw = take(len(rings))
     if not first:
@@ -273,7 +316,7 @@
     if fresh:
         causal = take(1)[0]
     else:
-        block, apart = take(2)
+        parted = take(1)
     rows, width = queries[0].shape
     heads = width // HD
     cycle = cycle_of(group)
@@ -282,7 +325,7 @@
     place = pick(list(np.argsort(cycle)), request)
     edges = []
     count = 0
-    block_size = 128
+    block_size = BLK
     for i in range(slots):
         wanted = seq * slots + i
         number = jnp.int32(0)
@@ -308,8 +351,9 @@
             causal[i * rows : (i + 1) * rows, :] = jnp.where(theirs <= mine, 0.0, NEGATIVE)
     else:
         offset = 0
+        order = order_rows(2 * heads, False)
         for piece_ref in raw:
-            take_apart(piece_ref, apart, offset, block, offset)
+            take_apart(piece_ref, order, parted[0], offset)
             offset += piece_ref.shape[0]
     stats[...] = jnp.zeros_like(stats)
     unit = jnp.where(
@@ -323,8 +367,8 @@
     def one_head(head):
         span = lanes(head * HD)
         query = stacked([q[:, span] for q in queries])
-        keys = [block[0, :, span]]
-        values = [block[1, :, span]]
+        keys = [block[0, :, span] for block in parted]
+        values = [block[1, :, span] for block in parted]
         if fresh:
             keys.append(fresh_keys[:, span])
             values.append(fresh_values[:, span])
@@ -393,11 +437,11 @@
     queries = [queries[shift] for shift in shifts]
     rows, width = queries[0].shape
     heads = width // HD
-    fresh = blocks[0].ndim == 3
+    fresh = len(blocks) if blocks[0].ndim == 3 else 0
     operands = [*facts, *queries, *blocks]
     if old:
         operands += [old[shift][0] for shift in shifts] + [old[shift][1] for shift in shifts]
-    plain = blocks[0].shape[1] if fresh else sum(block.shape[0] for block in blocks)
+    plain = sum(size for _, _, size in rings) + BLK * slots
     count = plain + (rows if fresh else 0)
     many = len(shifts) * rows
     scratch = [pltpu.VMEM((count, HD), jnp.bfloat16), pltpu.VMEM((many, HD), jnp.float32)]
@@ -405,7 +449,6 @@
         scratch.append(pltpu.VMEM((many, rows), jnp.float32))
     else:
         scratch.append(pltpu.VMEM((2, count, width), jnp.bfloat16))
-        scratch.append(pltpu.VMEM((2 * heads * count, HD), jnp.float32))
     state = jax.ShapeDtypeStruct((rows, width), jnp.float32)
     state_stats = jax.ShapeDtypeStruct((rows, HD), jnp.float32)
     sent = jax.ShapeDtypeStruct((rows + STAT_ROWS, width), jnp.bfloat16)
@@ -537,11 +580,13 @@
     cosine, sine = angles(positions)
     query, normed = project_query(pieces, w_query, cosine, sine)
     queries = [query] + [swap(query, "seq", shift) for shift in range(1, group)]
-    fresh_keys, fresh_values, new_cache = project_keyval(normed, w_keyval, cosine, sine)
-    step(fresh_keys)
     tail = viewed(tail_cache.reshape(-1, 2, tail_cache.shape[3]))
     slots = tail_cache.shape[0]
-    near_block = part_keyval([tail, prompt, ahead[1], behind[1]], "part_near")
+    own_block = part_keyval([after(tail, query), prompt], "part_own")
+    step(own_block)
+    ready = after(normed, ahead[1], behind[1])
+    fresh_keys, fresh_values, new_cache = project_keyval(ready, w_keyval, cosine, sine)
+    near_block = part_keyval([ahead[1], behind[1]], "part_near")
 
     facts = (tail_len, shared_len, tail_table)
     others = list(range(1, group))
@@ -549,14 +594,14 @@
         [(0, 0, piece), (-1, 0, piece), (1, 0, piece)],
         slots,
         piece,
-        [near_block, fresh_keys, fresh_values],
+        [own_block, near_block, fresh_keys, fresh_values],
         None,
         False,
     )
     state = attend(facts, queries, [0], *near, "attend_near_own")
-    ready = after(queries[1], state[0][1])
+    ready = after(queries[1], state[0][1], ahead[2], behind[2])
     state |= attend(facts, [query, ready, *queries[2:]], others, *near, "attend_near_others")
-    step(state[1][1])
+    step(state[0][1])
     rings = [(-2, 0, piece), (2, 0, piece)]
     state = attend(
         facts, queries, [0, *others], rings, 0, piece, [ahead[2], behind[2]], state, False, "attend_mid"

time: 99 us -> 88.1 us (0.89)
  Pallas kernels: 64.4 us -> 52.3 us
  local copies, waits for them, and re-layouts: 3.56 us -> 4.59 us
    pallas_call x5, Pallas kernels: 33.4 us -> 28.6 us  [attend(): pl.pallas_call(functools.partial(attend_kernel, (group, shifts, rings, sl...]
    pallas_call x1, Pallas kernels: 16.4 us -> 13.1 us  [project_keyval(): pl.pallas_call(keyval_kernel, in_specs=[VMEM, HBM, VMEM, VMEM], out_specs...]
    pallas_call x1 -> x2, Pallas kernels: 5.98 us -> 3.19 us  [part_keyval(): pl.pallas_call(part_kernel, in_specs=[VMEM] * len(blocks), out_specs=VMEM...]
    pallas_call x1, Pallas kernels: 6.38 us -> 5.17 us  [project_query(): pl.pallas_call(query_kernel, in_specs=[VMEM] * len(pieces) + [HBM, VMEM,...]
    ppermute x4, waiting for transfers between devices: 6.52 us -> 7.62 us  [swap(): return lax.ppermute(value, axis, pairs)]
    unnamed x21 -> x23, local copies, waits for them, and re-layouts: 1.95 us -> 2.99 us
  transfers between devices with their start and end apart: 12 -> 12, of which waited for: 5 -> 5; matrix products, arithmetic and copies ran while one was open for 3% -> 4% of each run, Pallas kernels for 57% -> 53%
where the time goes in v4:
time: 88.1 us; the launch traced here: 87.8 us
  Pallas kernels  52.3 us (59%)
  waiting for transfers between devices  14.9 us (17%)
  starting transfers between devices  11.5 us (13%)
  local copies, waits for them, and re-layouts  4.59 us (5%)
  other arithmetic  2.33 us (3%)
  between operations  2.16 us (2%)
    pallas_call x5, Pallas kernels, attend(): pl.pallas_call(functools.partial(attend_kernel, (group, shifts, rings, sl...  28.6 us
    pallas_call x1, Pallas kernels, project_keyval(): pl.pallas_call(keyval_kernel, in_specs=[VMEM, HBM, VMEM, VMEM], out_specs...  13.1 us
    ppermute x8, starting transfers between devices, turn(): return lax.ppermute(value, 'seq', pairs)  9.38 us
    ppermute x4, waiting for transfers between devices, swap(): return lax.ppermute(value, axis, pairs)  7.62 us
    ppermute x8, waiting for transfers between devices, turn(): return lax.ppermute(value, 'seq', pairs)  7.32 us
    pallas_call x1, Pallas kernels, project_query(): pl.pallas_call(query_kernel, in_specs=[VMEM] * len(pieces) + [HBM, VMEM,...  5.17 us
    pallas_call x2, Pallas kernels, part_keyval(): pl.pallas_call(part_kernel, in_specs=[VMEM] * len(blocks), out_specs=VMEM...  3.19 us
    unnamed x23, local copies, waits for them, and re-layouts  2.99 us
  transfers between devices with their start and end apart: 12, of which 5 were waited for; matrix products, arithmetic and copies ran while one was open for 4% of the time, Pallas kernels for 53%

profile of v4, /device:TPU:0, one launch (start us, length us, event | category | flops | bytes accessed | tf_op | source)
XLA Modules:
  0.0 87.8 jit_solution(11597808735467028011)
XLA Ops:
  0.7 3.0 %collective-permute-start.4 = (bf16[128,8,2,128]{3,2,1,0:T(2,128)(2,1)}, bf16[128,8,2,128]{3,2,1,0:T(2,128)(2,1)}, u32[]{:S(2)}, u32[]{:S(2)}) collective-permute-start(bf16[128,8,2,128]{3,2,1,0:T(2,128)(2,1)} %bitcast.15), channel_id=1, source_target_pairs={{0,4},{2,6},{8,0},{10,2},{16,8},{18,10},{24,16},{26,18},{28,24},{3... | collective-permute-start | bytes 1572872 | tf_op jit(solution)/shard_map/ppermute | solution.py:51
  4.5 1.2 %dynamic_slice.4 = s32[1]{0:T(128)} dynamic-slice(s32[8]{0:T(128)} %refs_0_.11, s32[]{:T(128)S(6)} %select_n.16), dynamic_slice_sizes={1} | dynamic-slice | bytes 12 | tf_op jit(solution)/shard_map/jit(dynamic_index_in_dim)/dynamic_slice | solution.py:578
  6.4 0.5 fusion
  6.9 0.8 pad_maximum_fusion
  7.8 0.8 copy-done.9
  8.6 5.2 %project_query.1 = (bf16[256,1024]{1,0:T(8,128)(2,1)}, bf16[256,2048]{1,0:T(8,128)(2,1)}) custom-call(bf16[256,1024]{1,0:T(8,128)(2,1)} %hidden.1, bf16[256,1024]{1,0:T(8,128)(2,1)} %copy-done.9, bf16[2048,1024]{1,0:T(8,128)(2,1)} %refs_2_.6, f32[256,128]{1,0:T(8,128)} %get-tuple-element.59.refs_3_.cosine, f32[256,128]{1,0:T(8,128)} %get-tuple-element.60.refs_4_.sine), custom_call_target="tpu_custom_call" | custom-call | flops 1073741824 | bytes 4194304 | tf_op jit(solution)/shard_map/project_query/pallas_call | solution.py:185
  13.8 1.1 %part_own.1.refs_4_ = bf16[2,384,1024]{2,1,0:T(8,128)(2,1)S(1)} custom-call(bf16[256,8,2,128]{3,2,1,0:T(2,128)(2,1)S(1)} %bitcast.14, bf16[128,8,2,128]{3,2,1,0:T(2,128)(2,1)S(1)} %bitcast.17), custom_call_target="tpu_custom_call" | custom-call | bytes 3145728 | tf_op jit(solution)/shard_map/part_own/pallas_call | solution.py:131
  14.9 2.5 %collective-permute-done.2.refs_0_ = bf16[128,8,2,128]{3,2,1,0:T(2,128)(2,1)} collective-permute-done((bf16[128,8,2,128]{3,2,1,0:T(2,128)(2,1)}, bf16[128,8,2,128]{3,2,1,0:T(2,128)(2,1)}, u32[]{:S(2)}, u32[]{:S(2)}) %collective-permute-start.2) | collective-permute-done | bytes 524320 | tf_op jit(solution)/shard_map/ppermute | solution.py:51
  17.4 0.4 collective-permute-start.3
  17.8 1.6 %collective-permute-start.6 = (bf16[128,8,2,128]{3,2,1,0:T(2,128)(2,1)}, bf16[128,8,2,128]{3,2,1,0:T(2,128)(2,1)S(1)}, u32[]{:S(2)}, u32[]{:S(2)}) collective-permute-start(bf16[128,8,2,128]{3,2,1,0:T(2,128)(2,1)} %collective-permute-done.4.refs_1_), channel_id=1, source_target_pairs={{0,4},{2,6},{8,0},{10,2},{16,8},{18,10},{24,16},{26,18},{28,24},{3... | collective-permute-start | bytes 1572872 | tf_op jit(solution)/shard_map/ppermute | solution.py:51
  19.5 1.5 %collective-permute-start.1 = (bf16[256,1024]{1,0:T(8,128)(2,1)}, bf16[256,1024]{1,0:T(8,128)(2,1)S(1)}, u32[]{:S(2)}, u32[]{:S(2)}) collective-permute-start(bf16[256,1024]{1,0:T(8,128)(2,1)} %get-tuple-element.48.refs_3_), channel_id=1, source_target_pairs={{0,2},{2,0},{4,6},{6,4},{8,10},{10,8},{12,14},{14,12},{16,18},{18,... | collective-permute-start | bytes 1572872 | tf_op jit(solution)/shard_map/ppermute | solution.py:42
  21.0 13.1 %project_keyval.1 = (bf16[256,1024]{1,0:T(8,128)(2,1)}, bf16[256,1024]{1,0:T(8,128)(2,1)}, bf16[256,8,2,128]{3,2,1,0:T(2,128)(2,1)}) custom-call(bf16[256,2048]{1,0:T(8,128)(2,1)} %get-tuple-element.33.normed, bf16[2048,8,2,128]{3,2,1,0:T(2,128)(2,1)} %bitcast.19, f32[256,128]{1,0:T(8,128)} %get-tuple-element.59.refs_3_.cosine, ...), custom_call_target="tpu_custom_call" | custom-call | flops 2147483648 | bytes 8388608 | tf_op jit(solution)/shard_map/project_keyval/pallas_call | solution.py:266
  34.1 2.0 %part_near.1.refs_5_ = bf16[2,256,1024]{2,1,0:T(8,128)(2,1)S(1)} custom-call(bf16[128,8,2,128]{3,2,1,0:T(2,128)(2,1)} %collective-permute-done.2.refs_0_, bf16[128,8,2,128]{3,2,1,0:T(2,128)(2,1)} %collective-permute-done.4.refs_1_), custom_call_target="tpu_custom_call" | custom-call | bytes 2097152 | tf_op jit(solution)/shard_map/part_near/pallas_call | solution.py:131
  36.2 1.0 %copy-done.3 = bf16[256,1024]{1,0:T(8,128)(2,1)S(1)} copy-done((bf16[256,1024]{1,0:T(8,128)(2,1)S(1)}, bf16[256,1024]{1,0:T(8,128)(2,1)}, u32[]{:S(2)}) %copy-start.3) | copy-done | bytes 524312
  37.3 1.0 %copy-done.4 = bf16[256,1024]{1,0:T(8,128)(2,1)S(1)} copy-done((bf16[256,1024]{1,0:T(8,128)(2,1)S(1)}, bf16[256,1024]{1,0:T(8,128)(2,1)}, u32[]{:S(2)}) %copy-start.4) | copy-done | bytes 524312
  38.3 5.4 %attend_near_own.1 = (f32[256,1024]{1,0:T(8,128)S(1)}, f32[256,128]{1,0:T(8,128)S(1)}) custom-call(s32[8]{0:T(128)S(1)} %copy-done.8, s32[1]{0:T(128)S(6)} %copy.16.refs_1_, s32[8,4]{1,0:T(8,128)S(1)} %copy.15.refs_2_, bf16[256,1024]{1,0:T(8,128)(2,1)S(1)} %copy-done.1, bf16[2,384,1024]{2,1,0:T(8,128)(2,1)S(1)} %part_own.1.refs_4_, ...), custom_call_target="tpu_custom_call" | custom-call | flops 939524096 | bytes 3670016 | tf_op jit(solution)/shard_map/attend_near_own/pallas_call | solution.py:461
  43.7 0.6 collective-permute-start.5
  44.3 1.5 %collective-permute-start.7 = (bf16[128,8,2,128]{3,2,1,0:T(2,128)(2,1)S(1)}, bf16[128,8,2,128]{3,2,1,0:T(2,128)(2,1)S(1)}, u32[]{:S(2)}, u32[]{:S(2)}) collective-permute-start(bf16[128,8,2,128]{3,2,1,0:T(2,128)(2,1)S(1)} %collective-permute-done.6.refs_6_), channel_id=1, source_target_pairs={{0,4},{2,6},{8,0},{10,2},{16,8},{18,10},{24,16},{26,18},{28,24},{3... | collective-permute-start | bytes 1572872 | tf_op jit(solution)/shard_map/ppermute | solution.py:51
  45.8 5.4 %attend_near_others.1 = (f32[256,1024]{1,0:T(8,128)S(1)}, f32[256,128]{1,0:T(8,128)S(1)}) custom-call(s32[8]{0:T(128)S(1)} %copy-done.8, s32[1]{0:T(128)S(6)} %copy.16.refs_1_, s32[8,4]{1,0:T(8,128)S(1)} %copy.15.refs_2_, bf16[256,1024]{1,0:T(8,128)(2,1)S(1)} %collective-permute-done.1.refs_3_.refs_4_, bf16[2,384,1024]{2,1,0:T(8,128)(2,1)S(1)} %part_own.1.refs_4_, ...), custom_call_target="tpu_custom_call" | custom-call | flops 939524096 | bytes 3670016 | tf_op jit(solution)/shard_map/attend_near_others/pallas_call | solution.py:461
  51.2 8.5 %attend_mid.1 = (f32[256,1024]{1,0:T(8,128)S(1)}, f32[256,1024]{1,0:T(8,128)S(1)}, f32[256,128]{1,0:T(8,128)S(1)}, f32[256,128]{1,0:T(8,128)S(1)}) custom-call(s32[8]{0:T(128)S(1)} %copy-done.8, s32[1]{0:T(128)S(6)} %copy.16.refs_1_, s32[8,4]{1,0:T(8,128)S(1)} %copy.15.refs_2_, bf16[256,1024]{1,0:T(8,128)(2,1)S(1)} %copy-done.1, ...), custom_call_target="tpu_custom_call" | custom-call | flops 536870912 | bytes 1048576 | tf_op jit(solution)/shard_map/attend_mid/pallas_call | solution.py:461
  59.9 0.6 collective-permute-start.8
  60.7 1.6 %collective-permute-start.9 = (bf16[64,8,2,128]{3,2,1,0:T(2,128)(2,1)S(1)}, bf16[64,8,2,128]{3,2,1,0:T(2,128)(2,1)S(1)}, u32[]{:S(2)}, u32[]{:S(2)}) collective-permute-start(bf16[64,8,2,128]{3,2,1,0:T(2,128)(2,1)S(1)} %slice.7), channel_id=1, source_target_pairs={{0,4},{2,6},{8,0},{10,2},{16,8},{18,10},{24,16},{26,18},{28,24},{3... | collective-permute-start | bytes 786440 | tf_op jit(solution)/shard_map/ppermute | solution.py:51
  62.2 4.1 %collective-permute-done.8.refs_6_ = bf16[64,8,2,128]{3,2,1,0:T(2,128)(2,1)S(1)} collective-permute-done((bf16[64,8,2,128]{3,2,1,0:T(2,128)(2,1)S(1)}, bf16[64,8,2,128]{3,2,1,0:T(2,128)(2,1)S(1)}, u32[]{:S(2)}, u32[]{:S(2)}) %collective-permute-start.8) | collective-permute-done | bytes 262176 | tf_op jit(solution)/shard_map/ppermute | solution.py:51
  66.3 0.7 collective-permute-done.9.refs_7_
  67.1 4.7 %attend_far_others.1 = bf16[272,1024]{1,0:T(8,128)(2,1)S(1)} custom-call(s32[8]{0:T(128)S(1)} %copy-done.8, s32[1]{0:T(128)S(6)} %copy.16.refs_1_, s32[8,4]{1,0:T(8,128)S(1)} %copy.15.refs_2_, bf16[256,1024]{1,0:T(8,128)(2,1)S(1)} %collective-permute-done.1.refs_3_.refs_4_, bf16[128,8,2,128]{3,2,1,0:T(2,128)(2,1)S(1)} %collective-permute-done.5.refs_4_, ...), custom_call_target="tpu_custom_call" | custom-call | flops 402653184 | bytes 1572864 | tf_op jit(solution)/shard_map/attend_far_others/pallas_call | solution.py:461
  71.8 0.5 collective-permute-start.10
  72.3 4.6 %attend_far_own.1 = (f32[256,1024]{1,0:T(8,128)S(1)}, f32[256,128]{1,0:T(8,128)S(1)}) custom-call(s32[8]{0:T(128)S(1)} %copy-done.8, s32[1]{0:T(128)S(6)} %copy.16.refs_1_, s32[8,4]{1,0:T(8,128)S(1)} %copy.15.refs_2_, bf16[256,1024]{1,0:T(8,128)(2,1)S(1)} %copy-done.1, bf16[128,8,2,128]{3,2,1,0:T(2,128)(2,1)S(1)} %collective-permute-done.5.refs_4_, ...), custom_call_target="tpu_custom_call" | custom-call | flops 402653184 | bytes 1572864 | tf_op jit(solution)/shard_map/attend_far_own/pallas_call | solution.py:461
  77.0 6.5 %collective-permute-done.10.refs_2_ = bf16[272,1024]{1,0:T(8,128)(2,1)S(1)} collective-permute-done((bf16[272,1024]{1,0:T(8,128)(2,1)S(1)}, bf16[272,1024]{1,0:T(8,128)(2,1)S(1)}, u32[]{:S(2)}, u32[]{:S(2)}) %collective-permute-start.10) | collective-permute-done | bytes 557088 | tf_op jit(solution)/shard_map/ppermute | solution.py:42
  83.4 1.4 %combine_send.1 = (bf16[256,1024]{1,0:T(8,128)(2,1)S(1)}, bf16[1,256,1024]{2,1,0:T(8,128)(2,1)S(1)}) custom-call(f32[256,1024]{1,0:T(8,128)S(1)} %get-tuple-element.51.refs_0_, f32[256,128]{1,0:T(8,128)S(1)} %get-tuple-element.52.refs_1_, bf16[272,1024]{1,0:T(8,128)(2,1)S(1)} %collective-permute-done.10.refs_2_, bf16[1024,2048]{1,0:T(8,128)(2,1)S(1)} %copy-done), custom_call_target="tpu_custom_call" | custom-call | flops 536870912 | bytes 4194304 | tf_op jit(solution)/shard_map/combine_send/pallas_call | solution.py:518
  84.9 0.7 keep_own.1
  85.7 1.2 %collective-permute-done.11 = bf16[256,1024]{1,0:T(8,128)(2,1)S(1)} collective-permute-done((bf16[256,1024]{1,0:T(8,128)(2,1)S(1)}, bf16[256,1024]{1,0:T(8,128)(2,1)S(1)}, u32[]{:S(2)}, u32[]{:S(2)}) %collective-permute-start.11) | collective-permute-done | bytes 524320 | tf_op jit(solution)/shard_map/ppermute | solution.py:42
  86.8 0.9 %add_convert_fusion = bf16[256,1024]{1,0:T(8,128)(2,1)} fusion(f32[256,1024]{1,0:T(8,128)S(1)} %keep_own.1, bf16[256,1024]{1,0:T(8,128)(2,1)S(1)} %collective-permute-done.11), kind=kLoop, calls=%fused_computation | loop fusion | flops 786432 | bytes 2097152 | tf_op jit(solution)/shard_map/convert_element_type | solution.py:623
  (34 shorter events, 0.7 us)
Async XLA Ops:
  0.6 13.1 %copy-start.7 = (bf16[128,2,1024]{2,1,0:T(2,128)(2,1)S(1)}, bf16[128,2,1024]{2,1,0:T(2,128)(2,1)}, u32[]{:S(2)}) copy-start(bf16[128,2,1024]{2,1,0:T(2,128)(2,1)} %param.13) | copy-start | bytes 1572868
  0.6 13.1 %copy-start.6 = (bf16[2,128,2,1024]{3,2,1,0:T(2,128)(2,1)S(1)}, bf16[2,128,2,1024]{3,2,1,0:T(2,128)(2,1)}, u32[]{:S(2)}) copy-start(bf16[2,128,2,1024]{3,2,1,0:T(2,128)(2,1)} %param.14) | copy-start | bytes 3145732
  0.7 17.1 %collective-permute-start.4 = (bf16[128,8,2,128]{3,2,1,0:T(2,128)(2,1)}, bf16[128,8,2,128]{3,2,1,0:T(2,128)(2,1)}, u32[]{:S(2)}, u32[]{:S(2)}) collective-permute-start(bf16[128,8,2,128]{3,2,1,0:T(2,128)(2,1)} %bitcast.15), channel_id=1, source_target_pairs={{0,4},{2,6},{8,0},{10,2},{16,8},{18,10},{24,16},{26,18},{28,24},{3... | collective-permute-start | bytes 1572872 | tf_op jit(solution)/shard_map/ppermute | solution.py:51
  3.7 13.7 %collective-permute-start.2 = (bf16[128,8,2,128]{3,2,1,0:T(2,128)(2,1)}, bf16[128,8,2,128]{3,2,1,0:T(2,128)(2,1)}, u32[]{:S(2)}, u32[]{:S(2)}) collective-permute-start(bf16[128,8,2,128]{3,2,1,0:T(2,128)(2,1)} %bitcast.16), channel_id=1, source_target_pairs={{0,8},{2,10},{8,16},{10,18},{16,24},{18,26},{24,28},{26,30},{28,20... | collective-permute-start | bytes 1572872 | tf_op jit(solution)/shard_map/ppermute | solution.py:51
  3.8 4.0 %collective-permute-start = (bf16[256,1024]{1,0:T(8,128)(2,1)}, bf16[256,1024]{1,0:T(8,128)(2,1)S(1)}, u32[]{:S(2)}, u32[]{:S(2)}) collective-permute-start(bf16[256,1024]{1,0:T(8,128)(2,1)} %hidden.1), channel_id=1, source_target_pairs={{0,1},{1,0},{2,3},{3,2},{4,5},{5,4},{6,7},{7,6},{8,9},{9,8},{10,11... | collective-permute-start | bytes 1572872 | tf_op jit(solution)/shard_map/ppermute | solution.py:42
  7.8 0.8 copy-start.9
  8.6 10.8 %copy-start.10 = (s32[8,4]{0,1:T(4,128)S(1)}, s32[8,4]{0,1:T(4,128)}, u32[]{:S(2)}) copy-start(s32[8,4]{0,1:T(4,128)} %param.15) | copy-start | bytes 388
  17.4 26.3 %collective-permute-start.3 = (bf16[128,8,2,128]{3,2,1,0:T(2,128)(2,1)}, bf16[128,8,2,128]{3,2,1,0:T(2,128)(2,1)S(1)}, u32[]{:S(2)}, u32[]{:S(2)}) collective-permute-start(bf16[128,8,2,128]{3,2,1,0:T(2,128)(2,1)} %collective-permute-done.2.refs_0_), channel_id=1, source_target_pairs={{0,8},{2,10},{8,16},{10,18},{16,24},{18,26},{24,28},{26,30},{28,20... | collective-permute-start | bytes 1572872 | tf_op jit(solution)/shard_map/ppermute | solution.py:51
  17.8 26.5 %collective-permute-start.6 = (bf16[128,8,2,128]{3,2,1,0:T(2,128)(2,1)}, bf16[128,8,2,128]{3,2,1,0:T(2,128)(2,1)S(1)}, u32[]{:S(2)}, u32[]{:S(2)}) collective-permute-start(bf16[128,8,2,128]{3,2,1,0:T(2,128)(2,1)} %collective-permute-done.4.refs_1_), channel_id=1, source_target_pairs={{0,4},{2,6},{8,0},{10,2},{16,8},{18,10},{24,16},{26,18},{28,24},{3... | collective-permute-start | bytes 1572872 | tf_op jit(solution)/shard_map/ppermute | solution.py:51
  19.5 26.3 %collective-permute-start.1 = (bf16[256,1024]{1,0:T(8,128)(2,1)}, bf16[256,1024]{1,0:T(8,128)(2,1)S(1)}, u32[]{:S(2)}, u32[]{:S(2)}) collective-permute-start(bf16[256,1024]{1,0:T(8,128)(2,1)} %get-tuple-element.48.refs_3_), channel_id=1, source_target_pairs={{0,2},{2,0},{4,6},{6,4},{8,10},{10,8},{12,14},{14,12},{16,18},{18,... | collective-permute-start | bytes 1572872 | tf_op jit(solution)/shard_map/ppermute | solution.py:42
  21.0 15.2 %copy-start.1 = (bf16[256,1024]{1,0:T(8,128)(2,1)S(1)}, bf16[256,1024]{1,0:T(8,128)(2,1)}, u32[]{:S(2)}) copy-start(bf16[256,1024]{1,0:T(8,128)(2,1)} %get-tuple-element.48.refs_3_) | copy-start | bytes 1572868
  21.0 15.2 %copy-start.8 = (s32[8]{0:T(128)S(1)}, s32[8]{0:T(128)}, u32[]{:S(2)}) copy-start(s32[8]{0:T(128)} %refs_0_.11) | copy-start | bytes 100
  34.1 11.7 %copy-start.5 = (bf16[256,1024]{1,0:T(8,128)(2,1)S(1)}, bf16[256,1024]{1,0:T(8,128)(2,1)}, u32[]{:S(2)}) copy-start(bf16[256,1024]{1,0:T(8,128)(2,1)} %get-tuple-element.35.refs_7_) | copy-start | bytes 1572868
  36.2 1.0 %copy-start.3 = (bf16[256,1024]{1,0:T(8,128)(2,1)S(1)}, bf16[256,1024]{1,0:T(8,128)(2,1)}, u32[]{:S(2)}) copy-start(bf16[256,1024]{1,0:T(8,128)(2,1)} %get-tuple-element.34.refs_6_) | copy-start | bytes 1572868
  37.3 1.0 %copy-start.4 = (bf16[256,1024]{1,0:T(8,128)(2,1)S(1)}, bf16[256,1024]{1,0:T(8,128)(2,1)}, u32[]{:S(2)}) copy-start(bf16[256,1024]{1,0:T(8,128)(2,1)} %get-tuple-element.35.refs_7_) | copy-start | bytes 1572868
  43.7 16.0 %collective-permute-start.5 = (bf16[128,8,2,128]{3,2,1,0:T(2,128)(2,1)S(1)}, bf16[128,8,2,128]{3,2,1,0:T(2,128)(2,1)S(1)}, u32[]{:S(2)}, u32[]{:S(2)}) collective-permute-start(bf16[128,8,2,128]{3,2,1,0:T(2,128)(2,1)S(1)} %collective-permute-done.3.refs_5_), channel_id=1, source_target_pairs={{0,8},{2,10},{8,16},{10,18},{16,24},{18,26},{24,28},{26,30},{28,20... | collective-permute-start | bytes 1572872 | tf_op jit(solution)/shard_map/ppermute | solution.py:51
  44.3 16.2 %collective-permute-start.7 = (bf16[128,8,2,128]{3,2,1,0:T(2,128)(2,1)S(1)}, bf16[128,8,2,128]{3,2,1,0:T(2,128)(2,1)S(1)}, u32[]{:S(2)}, u32[]{:S(2)}) collective-permute-start(bf16[128,8,2,128]{3,2,1,0:T(2,128)(2,1)S(1)} %collective-permute-done.6.refs_6_), channel_id=1, source_target_pairs={{0,4},{2,6},{8,0},{10,2},{16,8},{18,10},{24,16},{26,18},{28,24},{3... | collective-permute-start | bytes 1572872 | tf_op jit(solution)/shard_map/ppermute | solution.py:51
  59.7 23.7 %copy-start = (bf16[1024,2048]{1,0:T(8,128)(2,1)S(1)}, bf16[1024,2048]{1,0:T(8,128)(2,1)}, u32[]{:S(2)}) copy-start(bf16[1024,2048]{1,0:T(8,128)(2,1)} %weight.1) | copy-start | bytes 12582916
  59.9 6.4 %collective-permute-start.8 = (bf16[64,8,2,128]{3,2,1,0:T(2,128)(2,1)S(1)}, bf16[64,8,2,128]{3,2,1,0:T(2,128)(2,1)S(1)}, u32[]{:S(2)}, u32[]{:S(2)}) collective-permute-start(bf16[64,8,2,128]{3,2,1,0:T(2,128)(2,1)S(1)} %slice.6), channel_id=1, source_target_pairs={{0,8},{2,10},{8,16},{10,18},{16,24},{18,26},{24,28},{26,30},{28,20... | collective-permute-start | bytes 786440 | tf_op jit(solution)/shard_map/ppermute | solution.py:51
  60.7 6.4 %collective-permute-start.9 = (bf16[64,8,2,128]{3,2,1,0:T(2,128)(2,1)S(1)}, bf16[64,8,2,128]{3,2,1,0:T(2,128)(2,1)S(1)}, u32[]{:S(2)}, u32[]{:S(2)}) collective-permute-start(bf16[64,8,2,128]{3,2,1,0:T(2,128)(2,1)S(1)} %slice.7), channel_id=1, source_target_pairs={{0,4},{2,6},{8,0},{10,2},{16,8},{18,10},{24,16},{26,18},{28,24},{3... | collective-permute-start | bytes 786440 | tf_op jit(solution)/shard_map/ppermute | solution.py:51
  71.8 11.6 %collective-permute-start.10 = (bf16[272,1024]{1,0:T(8,128)(2,1)S(1)}, bf16[272,1024]{1,0:T(8,128)(2,1)S(1)}, u32[]{:S(2)}, u32[]{:S(2)}) collective-permute-start(bf16[272,1024]{1,0:T(8,128)(2,1)S(1)} %attend_far_others.1), channel_id=1, source_target_pairs={{0,2},{2,0},{4,6},{6,4},{8,10},{10,8},{12,14},{14,12},{16,18},{18,... | collective-permute-start | bytes 1671176 | tf_op jit(solution)/shard_map/ppermute | solution.py:42
  72.3 12.6 %copy-start.2 = (bf16[256,1024]{1,0:T(8,128)(2,1)S(1)}, bf16[256,1024]{1,0:T(8,128)(2,1)}, u32[]{:S(2)}) copy-start(bf16[256,1024]{1,0:T(8,128)(2,1)} %hidden.1) | copy-start | bytes 1572868
  84.8 2.0 %collective-permute-start.11 = (bf16[256,1024]{1,0:T(8,128)(2,1)S(1)}, bf16[256,1024]{1,0:T(8,128)(2,1)S(1)}, u32[]{:S(2)}, u32[]{:S(2)}) collective-permute-start(bf16[256,1024]{1,0:T(8,128)(2,1)S(1)} %bitcast.18), channel_id=1, source_target_pairs={{0,1},{1,0},{2,3},{3,2},{4,5},{5,4},{6,7},{7,6},{8,9},{9,8},{10,11... | collective-permute-start | bytes 1572872 | tf_op jit(solution)/shard_map/ppermute | solution.py:42

commit v5 on v4

--- a/solution.py
+++ b/solution.py
@@ -140,15 +140,8 @@
 
 
 def query_kernel(*refs):
-    *pieces, weight, cosine, sine, query, normed, near, total, arrived = refs
-    count, depth, width = near.shape
-    copies = [
-        pltpu.make_async_copy(weight.at[pl.ds(i * depth, depth)], near.at[i], arrived.at[i])
-        for i in range(count)
-    ]
-    for copy in copies:
-        copy.start()
-    rows, columns = pieces[0].shape
+    *pieces, weight, cosine, sine, query, normed = refs
+    columns = pieces[0].shape[1]
     index = lax.axis_index("tp")
     features = columns * len(pieces)
     values = [piece[...].astype(jnp.float32) for piece in pieces]
@@ -158,25 +151,16 @@
     inverse = lax.rsqrt(spread + 1e-05)
     for shift, v in enumerate(values):
         normed[:, lanes((index ^ shift) * columns, columns)] = (v * inverse).astype(jnp.bfloat16)
+    width = weight.shape[1]
     wide = min(width, 2 * HD)
-    for i, copy in enumerate(copies):
-        copy.wait()
-        for base in range(0, width, wide):
-            span = slice(base, base + wide)
-            product = jnp.dot(
-                normed[:, i * depth : (i + 1) * depth],
-                near[i, :, span],
-                preferred_element_type=jnp.float32,
-            )
-            if i:
-                product += total[:, span]
-            if i < count - 1:
-                total[:, span] = product
-                continue
-            for start in range(0, wide, HD):
-                query[:, base + start : base + start + HD] = rotated(
-                    product[:, start : start + HD], cosine[...], sine[...]
-                ).astype(jnp.bfloat16)
+    for base in range(0, width, wide):
+        product = jnp.dot(
+            normed[...], weight[:, base : base + wide], preferred_element_type=jnp.float32
+        )
+        for start in range(0, wide, HD):
+            query[:, base + start : base + start + HD] = rotated(
+                product[:, start : start + HD], cosine[...], sine[...]
+            ).astype(jnp.bfloat16)
 
 
 def project_query(pieces, w_query, cosine, sine):
@@ -184,59 +168,70 @@
     depth, width = w_query.shape
     return pl.pallas_call(
         query_kernel,
-        in_specs=[VMEM] * len(pieces) + [HBM, VMEM, VMEM],
+        in_specs=[VMEM] * (len(pieces) + 3),
         out_specs=[VMEM] * 2,
         out_shape=[
             jax.ShapeDtypeStruct((rows, width), jnp.bfloat16),
             jax.ShapeDtypeStruct((rows, depth), jnp.bfloat16),
         ],
-        scratch_shapes=[
-            pltpu.VMEM((2, depth // 2, width), jnp.bfloat16),
-            pltpu.VMEM((rows, width), jnp.float32),
-            pltpu.SemaphoreType.DMA((2,)),
-        ],
-        compiler_params=params(60),
+        compiler_params=params(20),
         cost_estimate=cost(2 * rows * depth * width, 2 * depth * width),
         name="project_query",
     )(*pieces, w_query, cosine, sine)
 
 
-def keyval_kernel(
-    normed, weight, cosine, sine, keys, values, cache, near, arrived, apart, total
-):
-    parts, chunk, heads = near.shape[:3]
-    rows = normed.shape[0]
-    stride = 2 * heads
+def weight_kernel(weight, result, near, arrived):
+    slots, chunk, heads = near.shape[:3]
+    count = weight.shape[0] // chunk
     copies = [
-        pltpu.make_async_copy(weight.at[pl.ds(i * chunk, chunk)], near.at[i], arrived.at[i])
-        for i in range(parts)
+        pltpu.make_async_copy(
+            weight.at[pl.ds(i * chunk, chunk)], near.at[i % slots], arrived.at[i]
+        )
+        for i in range(count)
     ]
-    for copy in copies:
+    for copy in copies[:slots]:
         copy.start()
-    order = order_rows(stride, False)
+    order = order_rows(2 * heads, False)
     for i, copy in enumerate(copies):
         copy.wait()
-        here = apart.at[i % 2]
-        take_apart(near.at[i], order, here, 0)
-        for head in range(heads):
-            span = slice(head * HD, (head + 1) * HD)
-            product = jnp.dot(
-                normed[:, i * chunk : (i + 1) * chunk],
-                jnp.concatenate([here[0, :, span], here[1, :, span]], axis=1),
-                preferred_element_type=jnp.float32,
-            )
-            span = slice(2 * head * HD, 2 * (head + 1) * HD)
-            if i == 0:
-                total[:, span] = product
-            else:
-                total[:, span] += product
+        take_apart(near.at[i % slots], order, result, i * chunk)
+        if i + slots < count:
+            copies[i + slots].start()
+
+
+def part_weights(w_keyval):
+    weight = viewed(w_keyval)
+    depth, heads = weight.shape[:2]
+    chunk = min(depth, 256)
+    count = depth // chunk
+    return pl.pallas_call(
+        weight_kernel,
+        in_specs=[HBM],
+        out_specs=VMEM,
+        out_shape=jax.ShapeDtypeStruct((2, depth, heads * HD), jnp.bfloat16),
+        scratch_shapes=[
+            pltpu.VMEM((min(4, count), chunk, heads, 2, HD), jnp.bfloat16),
+            pltpu.SemaphoreType.DMA((count,)),
+        ],
+        compiler_params=params(38),
+        cost_estimate=cost(2**12 * depth * heads * HD, 8 * depth * heads * HD),
+        name="part_weights",
+    )(weight)
+
+
+def keyval_kernel(normed, weight, cosine, sine, keys, values, cache):
+    rows = normed.shape[0]
+    heads = weight.shape[2] // HD
+    stride = 2 * heads
     for head in range(heads):
         span = slice(head * HD, (head + 1) * HD)
-        begin = 2 * head * HD
-        key = rotated(total[:, begin : begin + HD], cosine[...], sine[...]).astype(jnp.bfloat16)
-        value = total[:, begin + HD : begin + 2 * HD].astype(jnp.bfloat16)
-        keys[:, span] = key
-        values[:, span] = value
+        product = jnp.dot(
+            normed[...],
+            jnp.concatenate([weight[0, :, span], weight[1, :, span]], axis=1),
+            preferred_element_type=jnp.float32,
+        )
+        keys[:, span] = rotated(product[:, :HD], cosine[...], sine[...]).astype(jnp.bfloat16)
+        values[:, span] = product[:, HD:].astype(jnp.bfloat16)
     order = order_rows(stride, True)
     places = 2 * HD // stride
     flat = cache.reshape(rows * stride, HD)
@@ -257,37 +252,24 @@
             flat[at * stride : (at + places) * stride, :] = tile
 
 
-def project_keyval(normed, w_keyval, cosine, sine):
+def project_keyval(normed, weight, cosine, sine):
     rows, depth = normed.shape
-    weight = viewed(w_keyval)
-    heads = weight.shape[1]
-    width = heads * HD
-    chunk = min(depth, 512)
+    width = weight.shape[2]
+    heads = width // HD
     keys, values, cache = pl.pallas_call(
         keyval_kernel,
-        in_specs=[VMEM, HBM, VMEM, VMEM],
+        in_specs=[VMEM] * 4,
         out_specs=[VMEM] * 3,
         out_shape=[
             jax.ShapeDtypeStruct((rows, width), jnp.bfloat16),
             jax.ShapeDtypeStruct((rows, width), jnp.bfloat16),
             jax.ShapeDtypeStruct((rows, heads, 2, HD), jnp.bfloat16),
         ],
-        scratch_shapes=[
-            pltpu.VMEM((depth // chunk, chunk, heads, 2, HD), jnp.bfloat16),
-            pltpu.SemaphoreType.DMA((depth // chunk,)),
-            pltpu.VMEM((2, 2, chunk, width), jnp.bfloat16),
-            pltpu.VMEM((rows, 2 * width), jnp.float32),
-        ],
-        compiler_params=params(57),
+        compiler_params=params(20),
         cost_estimate=cost(4 * rows * depth * width, 4 * depth * width),
         name="project_keyval",
     )(normed, weight, cosine, sine)
     return keys, values, cache.transpose(0, 2, 1, 3).reshape(rows, 2, width)
-
-
-def column_of(stats, lane):
-    place = lax.broadcasted_iota(jnp.int32, stats.shape, 1)
-    return jnp.sum(jnp.where(place == lane, stats, 0.0), axis=1, keepdims=True)
 
 
 def with_column(stats, lane, column):
@@ -307,12 +289,14 @@
         raw = take(len(rings))
     if not first:
         old_mixes, old_stats = take(len(shifts)), take(len(shifts))
+    results = take(len(shifts))
     if last:
-        results = take(len(shifts))
         mine_stats = take(1) if 0 in shifts else []
+        bias, stats = take(2)
+        stats[...] = jnp.zeros_like(stats)
     else:
-        results, new_stats = take(len(shifts)), take(len(shifts))
-    bias, stats = take(2)
+        new_stats = take(len(shifts))
+        bias = take(1)[0]
     if fresh:
         causal = take(1)[0]
     else:
@@ -355,7 +339,6 @@
         for piece_ref in raw:
             take_apart(piece_ref, order, parted[0], offset)
             offset += piece_ref.shape[0]
-    stats[...] = jnp.zeros_like(stats)
     unit = jnp.where(
         lax.broadcasted_iota(jnp.int32, (len(shifts) * rows, HD), 1) == 0, 1.0, 0.0
     ).astype(jnp.bfloat16)
@@ -383,8 +366,8 @@
             scores = jnp.concatenate([scores[:, :count], scores[:, count:] + causal[...]], axis=1)
         top = jnp.max(scores, axis=1, keepdims=True)
         if not first:
-            old = stacked([column_of(s[...], head) for s in old_stats])
-            top = jnp.maximum(top, old * (1.0 / SCALE))
+            old = stacked([s[:, span] for s in old_stats])
+            top = jnp.maximum(top, old[:, :1] * (1.0 / SCALE))
         weights = jnp.exp2((scores - top) * SCALE).astype(jnp.bfloat16)
         mixed = jnp.dot(
             weights,
@@ -397,11 +380,16 @@
             total = total + stacked([mix[:, span] for mix in old_mixes]) * factor
             summed = summed + factor
         even = total / summed
-        stats[...] = with_column(stats[...], head, top * SCALE + jnp.log2(summed))
+        extent = top * SCALE + jnp.log2(summed)
+        if last:
+            stats[...] = with_column(stats[...], head, extent)
+        else:
+            for i, new in enumerate(new_stats):
+                new[:, span] = extent[i * rows : (i + 1) * rows]
         for i, result in enumerate(results):
             result[:rows, span] = even[i * rows : (i + 1) * rows].astype(result.dtype)
 
-    together = min(2, heads)
+    together = min(4, heads)
 
     def some_heads(i, _):
         for j in range(together):
@@ -409,11 +397,11 @@
         return 0
 
     lax.fori_loop(0, heads // together, some_heads, 0)
+    if not last:
+        return
     for i, shift in enumerate(shifts):
         own_rows = stats[i * rows : (i + 1) * rows, :]
-        if not last:
-            new_stats[i][...] = own_rows
-        elif shift == 0:
+        if shift == 0:
             mine_stats[0][...] = own_rows
         else:
             line = jnp.transpose(own_rows)[:heads, :]
@@ -444,7 +432,9 @@
     plain = sum(size for _, _, size in rings) + BLK * slots
     count = plain + (rows if fresh else 0)
     many = len(shifts) * rows
-    scratch = [pltpu.VMEM((count, HD), jnp.bfloat16), pltpu.VMEM((many, HD), jnp.float32)]
+    scratch = [pltpu.VMEM((count, HD), jnp.bfloat16)]
+    if last:
+        scratch.append(pltpu.VMEM((many, HD), jnp.float32))
     if fresh:
         scratch.append(pltpu.VMEM((many, rows), jnp.float32))
     else:
@@ -456,7 +446,7 @@
         out_shape = [sent if shift else state for shift in shifts]
         out_shape += [state_stats] * (0 in shifts)
     else:
-        out_shape = [state] * len(shifts) + [state_stats] * len(shifts)
+        out_shape = [state] * (2 * len(shifts))
     scores = many * count * heads
     results = pl.pallas_call(
         functools.partial(
@@ -566,6 +556,7 @@
     piece = prompt_cache.shape[0]
     middle = piece // 2
 
+    weight = part_weights(w_keyval)
     pieces = [hidden_in] + [swap(hidden_in, "tp", shift) for shift in range(1, ways)]
     prompt = viewed(prompt_cache)
     ahead, behind = [prompt], [prompt]
@@ -578,6 +569,7 @@
     own_length = lax.dynamic_index_in_dim(tail_len, request, 0, keepdims=False)
     positions = shared_len[0] + own_length + member * rows + jnp.arange(rows, dtype=jnp.int32)
     cosine, sine = angles(positions)
+    pieces[0] = after(pieces[0], weight)
     query, normed = project_query(pieces, w_query, cosine, sine)
     queries = [query] + [swap(query, "seq", shift) for shift in range(1, group)]
     tail = viewed(tail_cache.reshape(-1, 2, tail_cache.shape[3]))
@@ -585,7 +577,7 @@
     own_block = part_keyval([after(tail, query), prompt], "part_own")
     step(own_block)
     ready = after(normed, ahead[1], behind[1])
-    fresh_keys, fresh_values, new_cache = project_keyval(ready, w_keyval, cosine, sine)
+    fresh_keys, fresh_values, new_cache = project_keyval(ready, weight, cosine, sine)
     near_block = part_keyval([ahead[1], behind[1]], "part_near")
 
     facts = (tail_len, shared_len, tail_table)
@@ -603,14 +595,15 @@
     state |= attend(facts, [query, ready, *queries[2:]], others, *near, "attend_near_others")
     step(state[0][1])
     rings = [(-2, 0, piece), (2, 0, piece)]
-    state = attend(
-        facts, queries, [0, *others], rings, 0, piece, [ahead[2], behind[2]], state, False, "attend_mid"
-    )
+    mid = (rings, 0, piece, [ahead[2], behind[2]], state, False, "attend_second")
+    state = attend(facts, queries, [0, *others], *mid)
     far_low = turn(after(ahead[3], state[1][1])[:middle], cycle, group, 1)
     far_high = turn(after(behind[3], state[1][1])[middle:], cycle, group, -1)
-    rings = [(-3, 0, piece), (3, 0, piece), (-half, 0, middle), (half, middle, piece - middle)]
-    far_blocks = [ahead[3], behind[3], far_low, far_high]
-    far = (rings, 0, piece, far_blocks, state, True)
+    rings = [(-3, 0, piece), (3, 0, piece)]
+    mid = (rings, 0, piece, [ahead[3], behind[3]], state, False, "attend_third")
+    state = attend(facts, queries, [0, *others], *mid)
+    rings = [(-half, 0, middle), (half, middle, piece - middle)]
+    far = (rings, 0, piece, [far_low, far_high], state, True)
     parts = attend(facts, queries, others, *far, "attend_far_others")
     ready = after(query, parts[0])
     result, stats = attend(facts, [ready, *queries[1:]], [0], *far, "attend_far_own")

time: 88.1 us -> 93.4 us (1.060)
  local copies, waits for them, and re-layouts: 4.59 us -> 12.7 us
  waiting for transfers between devices: 14.9 us -> 9.44 us
  Pallas kernels: 52.3 us -> 55.1 us
    unnamed x23, local copies, waits for them, and re-layouts: 2.99 us -> 11.8 us
    ppermute x8, waiting for transfers between devices: 7.32 us -> 0.02 us  [turn(): return lax.ppermute(value, 'seq', pairs)]
    pallas_call x5 -> x6, Pallas kernels: 28.6 us -> 35.7 us  [attend(): pl.pallas_call(functools.partial(attend_kernel, (group, shifts, rings, sl...]
    pallas_call x2 -> x3, Pallas kernels: 18.3 us -> 14.1 us  [the longest x1 7.8 us: part_weights(): pl.pallas_call(weight_kernel, in_specs=[HBM], out_specs=VMEM, out_shape=j...]
    ppermute x4, waiting for transfers between devices: 7.62 us -> 9.42 us  [swap(): return lax.ppermute(value, axis, pairs)]
  transfers between devices with their start and end apart: 12 -> 12, of which waited for: 5 -> 2; matrix products, arithmetic and copies ran while one was open for 4% -> 2% of each run, Pallas kernels for 53% -> 53%
where the time goes in v5:
time: 93.4 us; the launch traced here: 93 us
  Pallas kernels  55.1 us (59%)
  local copies, waits for them, and re-layouts  12.7 us (14%)
  starting transfers between devices  12 us (13%)
  waiting for transfers between devices  9.44 us (10%)
  between operations  2.22 us (2%)
  other arithmetic  1.63 us (2%)
    pallas_call x6, Pallas kernels, attend(): pl.pallas_call(functools.partial(attend_kernel, (group, shifts, rings, sl...  35.7 us
    unnamed x23, local copies, waits for them, and re-layouts  11.8 us
    ppermute x8, starting transfers between devices, turn(): return lax.ppermute(value, 'seq', pairs)  9.82 us
    ppermute x4, waiting for transfers between devices, swap(): return lax.ppermute(value, axis, pairs)  9.42 us
    pallas_call x1, Pallas kernels, part_weights(): pl.pallas_call(weight_kernel, in_specs=[HBM], out_specs=VMEM, out_shape=j...  7.8 us
    pallas_call x1, Pallas kernels, project_keyval(): pl.pallas_call(keyval_kernel, in_specs=[VMEM] * 4, out_specs=[VMEM] * 3,...  4.29 us
    pallas_call x2, Pallas kernels, part_keyval(): pl.pallas_call(part_kernel, in_specs=[VMEM] * len(blocks), out_specs=VMEM...  3.13 us
    ppermute x4, starting transfers between devices, swap(): return lax.ppermute(value, axis, pairs)  2.16 us
  transfers between devices with their start and end apart: 12, of which 2 were waited for; matrix products, arithmetic and copies ran while one was open for 2% of the time, Pallas kernels for 53%

profile of v5, /device:TPU:0, one launch (start us, length us, event | category | flops | bytes accessed | tf_op | source)
XLA Modules:
  0.0 93.0 jit_solution(7495355870271692214)
XLA Ops:
  0.6 3.1 %collective-permute-start.2 = (bf16[128,8,2,128]{3,2,1,0:T(2,128)(2,1)}, bf16[128,8,2,128]{3,2,1,0:T(2,128)(2,1)}, u32[]{:S(2)}, u32[]{:S(2)}) collective-permute-start(bf16[128,8,2,128]{3,2,1,0:T(2,128)(2,1)} %bitcast.15), channel_id=1, source_target_pairs={{0,8},{2,10},{8,16},{10,18},{16,24},{18,26},{24,28},{26,30},{28,20... | collective-permute-start | bytes 1572872 | tf_op jit(solution)/shard_map/ppermute | solution.py:51
  4.4 7.8 %part_weights.1.weight = bf16[2,2048,1024]{2,1,0:T(8,128)(2,1)S(1)} custom-call(bf16[2048,8,2,128]{3,2,1,0:T(2,128)(2,1)} %bitcast.19), custom_call_target="tpu_custom_call" | custom-call | flops 8589934592 | bytes 16777216 | tf_op jit(solution)/shard_map/part_weights/pallas_call | solution.py:207
  12.2 3.3 %copy-done.1 = bf16[2,2048,1024]{2,1,0:T(8,128)(2,1)} copy-done((bf16[2,2048,1024]{2,1,0:T(8,128)(2,1)}, bf16[2,2048,1024]{2,1,0:T(8,128)(2,1)S(1)}, u32[]{:S(2)}) %copy-start.1) | copy-done | bytes 8388632
  15.5 0.6 dynamic_slice.4
  16.7 0.5 fusion
  17.5 2.2 %copy-done.3 = bf16[2048,1024]{1,0:T(8,128)(2,1)S(1)} copy-done((bf16[2048,1024]{1,0:T(8,128)(2,1)S(1)}, bf16[2048,1024]{1,0:T(8,128)(2,1)}, u32[]{:S(2)}) %copy-start.3) | copy-done | bytes 4194328
  19.6 2.0 %project_query.1 = (bf16[256,1024]{1,0:T(8,128)(2,1)S(1)}, bf16[256,2048]{1,0:T(8,128)(2,1)S(1)}) custom-call(bf16[256,1024]{1,0:T(8,128)(2,1)S(1)} %copy-done.4, bf16[256,1024]{1,0:T(8,128)(2,1)S(1)} %collective-permute-done.refs_1_, bf16[2048,1024]{1,0:T(8,128)(2,1)S(1)} %copy-done.3, f32[256,128]{1,0:T(8,128)S(1)} %get-tuple-element.69.refs_3_.cosine, ...), custom_call_target="tpu_custom_call" | custom-call | flops 1073741824 | bytes 4194304 | tf_op jit(solution)/shard_map/project_query/pallas_call | solution.py:169
  21.7 1.6 %copy-done.5 = bf16[2,128,2,1024]{3,2,1,0:T(2,128)(2,1)S(1)} copy-done((bf16[2,128,2,1024]{3,2,1,0:T(2,128)(2,1)S(1)}, bf16[2,128,2,1024]{3,2,1,0:T(2,128)(2,1)}, u32[]{:S(2)}) %copy-start.5) | copy-done | bytes 1048600
  23.3 1.1 %part_own.1.refs_4_ = bf16[2,384,1024]{2,1,0:T(8,128)(2,1)S(1)} custom-call(bf16[256,8,2,128]{3,2,1,0:T(2,128)(2,1)S(1)} %bitcast.14, bf16[128,8,2,128]{3,2,1,0:T(2,128)(2,1)S(1)} %bitcast.17), custom_call_target="tpu_custom_call" | custom-call | bytes 3145728 | tf_op jit(solution)/shard_map/part_own/pallas_call | solution.py:131
  24.5 2.0 %collective-permute-start.6 = (bf16[128,8,2,128]{3,2,1,0:T(2,128)(2,1)}, bf16[128,8,2,128]{3,2,1,0:T(2,128)(2,1)}, u32[]{:S(2)}, u32[]{:S(2)}) collective-permute-start(bf16[128,8,2,128]{3,2,1,0:T(2,128)(2,1)} %collective-permute-done.4.refs_1_), channel_id=1, source_target_pairs={{0,4},{2,6},{8,0},{10,2},{16,8},{18,10},{24,16},{26,18},{28,24},{3... | collective-permute-start | bytes 1572872 | tf_op jit(solution)/shard_map/ppermute | solution.py:51
  26.5 0.3 collective-permute-start.3
  26.9 1.7 %collective-permute-start.1 = (bf16[256,1024]{1,0:T(8,128)(2,1)S(1)}, bf16[256,1024]{1,0:T(8,128)(2,1)S(1)}, u32[]{:S(2)}, u32[]{:S(2)}) collective-permute-start(bf16[256,1024]{1,0:T(8,128)(2,1)S(1)} %get-tuple-element.58.refs_3_), channel_id=1, source_target_pairs={{0,2},{2,0},{4,6},{6,4},{8,10},{10,8},{12,14},{14,12},{16,18},{18,... | collective-permute-start | bytes 1572872 | tf_op jit(solution)/shard_map/ppermute | solution.py:42
  28.6 3.4 %copy-done.2 = bf16[2,2048,1024]{2,1,0:T(8,128)(2,1)S(1)} copy-done((bf16[2,2048,1024]{2,1,0:T(8,128)(2,1)S(1)}, bf16[2,2048,1024]{2,1,0:T(8,128)(2,1)}, u32[]{:S(2)}) %copy-start.2) | copy-done | bytes 8388632
  31.9 1.2 %copy-done.7 = bf16[256,2048]{1,0:T(8,128)(2,1)S(1)} copy-done((bf16[256,2048]{1,0:T(8,128)(2,1)S(1)}, bf16[256,2048]{1,0:T(8,128)(2,1)}, u32[]{:S(2)}) %copy-start.7) | copy-done | bytes 1048600
  33.2 4.3 %project_keyval.1 = (bf16[256,1024]{1,0:T(8,128)(2,1)S(1)}, bf16[256,1024]{1,0:T(8,128)(2,1)S(1)}, bf16[256,8,2,128]{3,2,1,0:T(2,128)(2,1)}) custom-call(bf16[256,2048]{1,0:T(8,128)(2,1)S(1)} %copy-done.7, bf16[2,2048,1024]{2,1,0:T(8,128)(2,1)S(1)} %copy-done.2, f32[256,128]{1,0:T(8,128)S(1)} %get-tuple-element.69.refs_3_.cosine, ...), custom_call_target="tpu_custom_call" | custom-call | flops 2147483648 | bytes 8388608 | tf_op jit(solution)/shard_map/project_keyval/pallas_call | solution.py:259
  37.5 2.0 %part_near.1.refs_5_ = bf16[2,256,1024]{2,1,0:T(8,128)(2,1)S(1)} custom-call(bf16[128,8,2,128]{3,2,1,0:T(2,128)(2,1)} %collective-permute-done.2.refs_0_, bf16[128,8,2,128]{3,2,1,0:T(2,128)(2,1)} %collective-permute-done.4.refs_1_), custom_call_target="tpu_custom_call" | custom-call | bytes 2097152 | tf_op jit(solution)/shard_map/part_near/pallas_call | solution.py:131
  39.5 4.3 %attend_near_own.1 = (f32[256,1024]{1,0:T(8,128)S(1)}, f32[256,1024]{1,0:T(8,128)S(1)}) custom-call(s32[8]{0:T(128)S(1)} %copy-done.9, s32[1]{0:T(128)S(6)} %copy.17.refs_1_, s32[8,4]{1,0:T(8,128)S(1)} %copy.16.refs_2_, bf16[256,1024]{1,0:T(8,128)(2,1)S(1)} %get-tuple-element.58.refs_3_, bf16[2,384,1024]{2,1,0:T(8,128)(2,1)S(1)} %part_own.1.refs_4_, ...), custom_call_target="tpu_custom_call" | custom-call | flops 939524096 | bytes 3670016 | tf_op jit(solution)/shard_map/attend_near_own/pallas_call | solution.py:451
  43.8 1.6 %collective-permute-start.8 = (bf16[128,8,2,128]{3,2,1,0:T(2,128)(2,1)}, bf16[128,8,2,128]{3,2,1,0:T(2,128)(2,1)S(1)}, u32[]{:S(2)}, u32[]{:S(2)}) collective-permute-start(bf16[128,8,2,128]{3,2,1,0:T(2,128)(2,1)} %collective-permute-done.6.refs_6_), channel_id=1, source_target_pairs={{0,4},{2,6},{8,0},{10,2},{16,8},{18,10},{24,16},{26,18},{28,24},{3... | collective-permute-start | bytes 1572872 | tf_op jit(solution)/shard_map/ppermute | solution.py:51
  45.3 0.5 collective-permute-start.5
  45.8 4.3 %attend_near_others.1 = (f32[256,1024]{1,0:T(8,128)S(1)}, f32[256,1024]{1,0:T(8,128)S(1)}) custom-call(s32[8]{0:T(128)S(1)} %copy-done.9, s32[1]{0:T(128)S(6)} %copy.17.refs_1_, s32[8,4]{1,0:T(8,128)S(1)} %copy.16.refs_2_, bf16[256,1024]{1,0:T(8,128)(2,1)S(1)} %collective-permute-done.1.refs_3_.refs_4_, bf16[2,384,1024]{2,1,0:T(8,128)(2,1)S(1)} %part_own.1.refs_4_, ...), custom_call_target="tpu_custom_call" | custom-call | flops 939524096 | bytes 3670016 | tf_op jit(solution)/shard_map/attend_near_others/pallas_call | solution.py:451
  50.1 9.1 %attend_second.1 = (f32[256,1024]{1,0:T(8,128)S(1)}, f32[256,1024]{1,0:T(8,128)S(1)}, f32[256,1024]{1,0:T(8,128)S(1)}, f32[256,1024]{1,0:T(8,128)S(1)}) custom-call(s32[8]{0:T(128)S(1)} %copy-done.9, s32[1]{0:T(128)S(6)} %copy.17.refs_1_, s32[8,4]{1,0:T(8,128)S(1)} %copy.16.refs_2_, bf16[256,1024]{1,0:T(8,128)(2,1)S(1)} %get-tuple-element.58.refs_3_, ...), custom_call_target="tpu_custom_call" | custom-call | flops 536870912 | bytes 1048576 | tf_op jit(solution)/shard_map/attend_second/pallas_call | solution.py:451
  59.5 1.6 %collective-permute-start.9 = (bf16[64,8,2,128]{3,2,1,0:T(2,128)(2,1)S(1)}, bf16[64,8,2,128]{3,2,1,0:T(2,128)(2,1)S(1)}, u32[]{:S(2)}, u32[]{:S(2)}) collective-permute-start(bf16[64,8,2,128]{3,2,1,0:T(2,128)(2,1)S(1)} %slice.7), channel_id=1, source_target_pairs={{0,4},{2,6},{8,0},{10,2},{16,8},{18,10},{24,16},{26,18},{28,24},{3... | collective-permute-start | bytes 786440 | tf_op jit(solution)/shard_map/ppermute | solution.py:51
  61.2 0.8 collective-permute-start.7
  62.0 8.7 %attend_third.1 = (f32[256,1024]{1,0:T(8,128)S(1)}, f32[256,1024]{1,0:T(8,128)S(1)}, f32[256,1024]{1,0:T(8,128)S(1)}, f32[256,1024]{1,0:T(8,128)S(1)}) custom-call(s32[8]{0:T(128)S(1)} %copy-done.9, s32[1]{0:T(128)S(6)} %copy.17.refs_1_, s32[8,4]{1,0:T(8,128)S(1)} %copy.16.refs_2_, bf16[256,1024]{1,0:T(8,128)(2,1)S(1)} %get-tuple-element.58.refs_3_, ...), custom_call_target="tpu_custom_call" | custom-call | flops 536870912 | bytes 1048576 | tf_op jit(solution)/shard_map/attend_third/pallas_call | solution.py:451
  70.8 4.7 %attend_far_others.1 = bf16[272,1024]{1,0:T(8,128)(2,1)S(1)} custom-call(s32[8]{0:T(128)S(1)} %copy-done.9, s32[1]{0:T(128)S(6)} %copy.17.refs_1_, s32[8,4]{1,0:T(8,128)S(1)} %copy.16.refs_2_, bf16[256,1024]{1,0:T(8,128)(2,1)S(1)} %collective-permute-done.1.refs_3_.refs_4_, bf16[64,8,2,128]{3,2,1,0:T(2,128)(2,1)S(1)} %collective-permute-done.7.refs_4_, ...), custom_call_target="tpu_custom_call" | custom-call | flops 134217728 | bytes 524288 | tf_op jit(solution)/shard_map/attend_far_others/pallas_call | solution.py:451
  75.5 0.4 collective-permute-start.10
  75.8 4.6 %attend_far_own.1 = (f32[256,1024]{1,0:T(8,128)S(1)}, f32[256,128]{1,0:T(8,128)S(1)}) custom-call(s32[8]{0:T(128)S(1)} %copy-done.9, s32[1]{0:T(128)S(6)} %copy.17.refs_1_, s32[8,4]{1,0:T(8,128)S(1)} %copy.16.refs_2_, bf16[256,1024]{1,0:T(8,128)(2,1)S(1)} %get-tuple-element.58.refs_3_, bf16[64,8,2,128]{3,2,1,0:T(2,128)(2,1)S(1)} %collective-permute-done.7.refs_4_, ...), custom_call_target="tpu_custom_call" | custom-call | flops 134217728 | bytes 524288 | tf_op jit(solution)/shard_map/attend_far_own/pallas_call | solution.py:451
  80.4 8.3 %collective-permute-done.10.refs_2_ = bf16[272,1024]{1,0:T(8,128)(2,1)S(1)} collective-permute-done((bf16[272,1024]{1,0:T(8,128)(2,1)S(1)}, bf16[272,1024]{1,0:T(8,128)(2,1)S(1)}, u32[]{:S(2)}, u32[]{:S(2)}) %collective-permute-start.10) | collective-permute-done | bytes 557088 | tf_op jit(solution)/shard_map/ppermute | solution.py:42
  88.7 1.4 %combine_send.1 = (bf16[256,1024]{1,0:T(8,128)(2,1)S(1)}, bf16[1,256,1024]{2,1,0:T(8,128)(2,1)S(1)}) custom-call(f32[256,1024]{1,0:T(8,128)S(1)} %get-tuple-element.61.refs_0_, f32[256,128]{1,0:T(8,128)S(1)} %get-tuple-element.62.refs_1_, bf16[272,1024]{1,0:T(8,128)(2,1)S(1)} %collective-permute-done.10.refs_2_, bf16[1024,2048]{1,0:T(8,128)(2,1)S(1)} %copy-done), custom_call_target="tpu_custom_call" | custom-call | flops 536870912 | bytes 4194304 | tf_op jit(solution)/shard_map/combine_send/pallas_call | solution.py:508
  90.2 0.7 keep_own.1
  90.9 1.2 %collective-permute-done.11 = bf16[256,1024]{1,0:T(8,128)(2,1)S(1)} collective-permute-done((bf16[256,1024]{1,0:T(8,128)(2,1)S(1)}, bf16[256,1024]{1,0:T(8,128)(2,1)S(1)}, u32[]{:S(2)}, u32[]{:S(2)}) %collective-permute-start.11) | collective-permute-done | bytes 524320 | tf_op jit(solution)/shard_map/ppermute | solution.py:42
  92.1 0.9 %add_convert_fusion = bf16[256,1024]{1,0:T(8,128)(2,1)} fusion(f32[256,1024]{1,0:T(8,128)S(1)} %keep_own.1, bf16[256,1024]{1,0:T(8,128)(2,1)S(1)} %collective-permute-done.11), kind=kLoop, calls=%fused_computation | loop fusion | flops 786432 | bytes 2097152 | tf_op jit(solution)/shard_map/convert_element_type | solution.py:616
  (36 shorter events, 0.7 us)
Async XLA Ops:
  0.6 25.9 %collective-permute-start.2 = (bf16[128,8,2,128]{3,2,1,0:T(2,128)(2,1)}, bf16[128,8,2,128]{3,2,1,0:T(2,128)(2,1)}, u32[]{:S(2)}, u32[]{:S(2)}) collective-permute-start(bf16[128,8,2,128]{3,2,1,0:T(2,128)(2,1)} %bitcast.15), channel_id=1, source_target_pairs={{0,8},{2,10},{8,16},{10,18},{16,24},{18,26},{24,28},{26,30},{28,20... | collective-permute-start | bytes 1572872 | tf_op jit(solution)/shard_map/ppermute | solution.py:51
  3.7 20.8 %collective-permute-start.4 = (bf16[128,8,2,128]{3,2,1,0:T(2,128)(2,1)}, bf16[128,8,2,128]{3,2,1,0:T(2,128)(2,1)}, u32[]{:S(2)}, u32[]{:S(2)}) collective-permute-start(bf16[128,8,2,128]{3,2,1,0:T(2,128)(2,1)} %bitcast.16), channel_id=1, source_target_pairs={{0,4},{2,6},{8,0},{10,2},{16,8},{18,10},{24,16},{26,18},{28,24},{3... | collective-permute-start | bytes 1572872 | tf_op jit(solution)/shard_map/ppermute | solution.py:51
  3.7 13.7 %collective-permute-start = (bf16[256,1024]{1,0:T(8,128)(2,1)}, bf16[256,1024]{1,0:T(8,128)(2,1)S(1)}, u32[]{:S(2)}, u32[]{:S(2)}) collective-permute-start(bf16[256,1024]{1,0:T(8,128)(2,1)} %hidden.1), channel_id=1, source_target_pairs={{0,1},{1,0},{2,3},{3,2},{4,5},{5,4},{6,7},{7,6},{8,9},{9,8},{10,11... | collective-permute-start | bytes 1572872 | tf_op jit(solution)/shard_map/ppermute | solution.py:42
  4.4 11.1 %copy-start.9 = (s32[8]{0:T(128)S(1)}, s32[8]{0:T(128)}, u32[]{:S(2)}) copy-start(s32[8]{0:T(128)} %refs_0_.12) | copy-start | bytes 100
  4.4 13.1 %copy-start.4 = (bf16[256,1024]{1,0:T(8,128)(2,1)S(1)}, bf16[256,1024]{1,0:T(8,128)(2,1)}, u32[]{:S(2)}) copy-start(bf16[256,1024]{1,0:T(8,128)(2,1)} %hidden.1) | copy-start | bytes 1572868
  12.2 3.3 %copy-start.1 = (bf16[2,2048,1024]{2,1,0:T(8,128)(2,1)}, bf16[2,2048,1024]{2,1,0:T(8,128)(2,1)S(1)}, u32[]{:S(2)}) copy-start(bf16[2,2048,1024]{2,1,0:T(8,128)(2,1)S(1)} %part_weights.1.weight) | copy-start | bytes 25165828
  15.5 6.2 %copy-start.8 = (bf16[128,2,1024]{2,1,0:T(2,128)(2,1)S(1)}, bf16[128,2,1024]{2,1,0:T(2,128)(2,1)}, u32[]{:S(2)}) copy-start(bf16[128,2,1024]{2,1,0:T(2,128)(2,1)} %param.13) | copy-start | bytes 1572868
  17.5 2.2 %copy-start.3 = (bf16[2048,1024]{1,0:T(8,128)(2,1)S(1)}, bf16[2048,1024]{1,0:T(8,128)(2,1)}, u32[]{:S(2)}) copy-start(bf16[2048,1024]{1,0:T(8,128)(2,1)} %refs_2_.7) | copy-start | bytes 12582916
  19.6 7.1 %copy-start.10 = (s32[8,4]{0,1:T(4,128)S(1)}, s32[8,4]{0,1:T(4,128)}, u32[]{:S(2)}) copy-start(s32[8,4]{0,1:T(4,128)} %param.15) | copy-start | bytes 388
  21.7 2.8 %copy-start.6 = (bf16[256,2048]{1,0:T(8,128)(2,1)}, bf16[256,2048]{1,0:T(8,128)(2,1)S(1)}, u32[]{:S(2)}) copy-start(bf16[256,2048]{1,0:T(8,128)(2,1)S(1)} %get-tuple-element.39.normed) | copy-start | bytes 3145732
  21.7 1.6 %copy-start.5 = (bf16[2,128,2,1024]{3,2,1,0:T(2,128)(2,1)S(1)}, bf16[2,128,2,1024]{3,2,1,0:T(2,128)(2,1)}, u32[]{:S(2)}) copy-start(bf16[2,128,2,1024]{3,2,1,0:T(2,128)(2,1)} %param.14) | copy-start | bytes 3145732
  24.5 19.3 %collective-permute-start.6 = (bf16[128,8,2,128]{3,2,1,0:T(2,128)(2,1)}, bf16[128,8,2,128]{3,2,1,0:T(2,128)(2,1)}, u32[]{:S(2)}, u32[]{:S(2)}) collective-permute-start(bf16[128,8,2,128]{3,2,1,0:T(2,128)(2,1)} %collective-permute-done.4.refs_1_), channel_id=1, source_target_pairs={{0,4},{2,6},{8,0},{10,2},{16,8},{18,10},{24,16},{26,18},{28,24},{3... | collective-permute-start | bytes 1572872 | tf_op jit(solution)/shard_map/ppermute | solution.py:51
  26.5 18.8 %collective-permute-start.3 = (bf16[128,8,2,128]{3,2,1,0:T(2,128)(2,1)}, bf16[128,8,2,128]{3,2,1,0:T(2,128)(2,1)S(1)}, u32[]{:S(2)}, u32[]{:S(2)}) collective-permute-start(bf16[128,8,2,128]{3,2,1,0:T(2,128)(2,1)} %collective-permute-done.2.refs_0_), channel_id=1, source_target_pairs={{0,8},{2,10},{8,16},{10,18},{16,24},{18,26},{24,28},{26,30},{28,20... | collective-permute-start | bytes 1572872 | tf_op jit(solution)/shard_map/ppermute | solution.py:51
  26.9 19.0 %collective-permute-start.1 = (bf16[256,1024]{1,0:T(8,128)(2,1)S(1)}, bf16[256,1024]{1,0:T(8,128)(2,1)S(1)}, u32[]{:S(2)}, u32[]{:S(2)}) collective-permute-start(bf16[256,1024]{1,0:T(8,128)(2,1)S(1)} %get-tuple-element.58.refs_3_), channel_id=1, source_target_pairs={{0,2},{2,0},{4,6},{6,4},{8,10},{10,8},{12,14},{14,12},{16,18},{18,... | collective-permute-start | bytes 1572872 | tf_op jit(solution)/shard_map/ppermute | solution.py:42
  28.6 3.4 %copy-start.2 = (bf16[2,2048,1024]{2,1,0:T(8,128)(2,1)S(1)}, bf16[2,2048,1024]{2,1,0:T(8,128)(2,1)}, u32[]{:S(2)}) copy-start(bf16[2,2048,1024]{2,1,0:T(8,128)(2,1)} %copy-done.1) | copy-start | bytes 25165828
  31.9 1.2 %copy-start.7 = (bf16[256,2048]{1,0:T(8,128)(2,1)S(1)}, bf16[256,2048]{1,0:T(8,128)(2,1)}, u32[]{:S(2)}) copy-start(bf16[256,2048]{1,0:T(8,128)(2,1)} %copy-done.6) | copy-start | bytes 3145732
  43.8 15.5 %collective-permute-start.8 = (bf16[128,8,2,128]{3,2,1,0:T(2,128)(2,1)}, bf16[128,8,2,128]{3,2,1,0:T(2,128)(2,1)S(1)}, u32[]{:S(2)}, u32[]{:S(2)}) collective-permute-start(bf16[128,8,2,128]{3,2,1,0:T(2,128)(2,1)} %collective-permute-done.6.refs_6_), channel_id=1, source_target_pairs={{0,4},{2,6},{8,0},{10,2},{16,8},{18,10},{24,16},{26,18},{28,24},{3... | collective-permute-start | bytes 1572872 | tf_op jit(solution)/shard_map/ppermute | solution.py:51
  45.3 15.7 %collective-permute-start.5 = (bf16[128,8,2,128]{3,2,1,0:T(2,128)(2,1)S(1)}, bf16[128,8,2,128]{3,2,1,0:T(2,128)(2,1)S(1)}, u32[]{:S(2)}, u32[]{:S(2)}) collective-permute-start(bf16[128,8,2,128]{3,2,1,0:T(2,128)(2,1)S(1)} %collective-permute-done.3.refs_5_), channel_id=1, source_target_pairs={{0,8},{2,10},{8,16},{10,18},{16,24},{18,26},{24,28},{26,30},{28,20... | collective-permute-start | bytes 1572872 | tf_op jit(solution)/shard_map/ppermute | solution.py:51
  59.5 11.2 %collective-permute-start.9 = (bf16[64,8,2,128]{3,2,1,0:T(2,128)(2,1)S(1)}, bf16[64,8,2,128]{3,2,1,0:T(2,128)(2,1)S(1)}, u32[]{:S(2)}, u32[]{:S(2)}) collective-permute-start(bf16[64,8,2,128]{3,2,1,0:T(2,128)(2,1)S(1)} %slice.7), channel_id=1, source_target_pairs={{0,4},{2,6},{8,0},{10,2},{16,8},{18,10},{24,16},{26,18},{28,24},{3... | collective-permute-start | bytes 786440 | tf_op jit(solution)/shard_map/ppermute | solution.py:51
  61.2 9.5 %collective-permute-start.7 = (bf16[64,8,2,128]{3,2,1,0:T(2,128)(2,1)S(1)}, bf16[64,8,2,128]{3,2,1,0:T(2,128)(2,1)S(1)}, u32[]{:S(2)}, u32[]{:S(2)}) collective-permute-start(bf16[64,8,2,128]{3,2,1,0:T(2,128)(2,1)S(1)} %slice.6), channel_id=1, source_target_pairs={{0,8},{2,10},{8,16},{10,18},{16,24},{18,26},{24,28},{26,30},{28,20... | collective-permute-start | bytes 786440 | tf_op jit(solution)/shard_map/ppermute | solution.py:51
  70.7 18.0 %copy-start = (bf16[1024,2048]{1,0:T(8,128)(2,1)S(1)}, bf16[1024,2048]{1,0:T(8,128)(2,1)}, u32[]{:S(2)}) copy-start(bf16[1024,2048]{1,0:T(8,128)(2,1)} %weight.1) | copy-start | bytes 12582916
  75.5 13.2 %collective-permute-start.10 = (bf16[272,1024]{1,0:T(8,128)(2,1)S(1)}, bf16[272,1024]{1,0:T(8,128)(2,1)S(1)}, u32[]{:S(2)}, u32[]{:S(2)}) collective-permute-start(bf16[272,1024]{1,0:T(8,128)(2,1)S(1)} %attend_far_others.1), channel_id=1, source_target_pairs={{0,2},{2,0},{4,6},{6,4},{8,10},{10,8},{12,14},{14,12},{16,18},{18,... | collective-permute-start | bytes 1671176 | tf_op jit(solution)/shard_map/ppermute | solution.py:42
  90.1 2.0 %collective-permute-start.11 = (bf16[256,1024]{1,0:T(8,128)(2,1)S(1)}, bf16[256,1024]{1,0:T(8,128)(2,1)S(1)}, u32[]{:S(2)}, u32[]{:S(2)}) collective-permute-start(bf16[256,1024]{1,0:T(8,128)(2,1)S(1)} %bitcast.18), channel_id=1, source_target_pairs={{0,1},{1,0},{2,3},{3,2},{4,5},{5,4},{6,7},{7,6},{8,9},{9,8},{10,11... | collective-permute-start | bytes 1572872 | tf_op jit(solution)/shard_map/ppermute | solution.py:42

commit v6 on v5

v6 whole, which is shorter than its diff:
```python
import functools

import jax
import jax.numpy as jnp
import numpy as np
from jax import lax
from jax.experimental import pallas as pl
from jax.experimental.pallas import tpu as pltpu
from jax.sharding import PartitionSpec as P

HD = 128
REQ = 8
BLK = 128
NEGATIVE = -1e30
SCALE = float(HD**-0.5 * np.log2(np.e))


def params(mib=24):
    return pltpu.CompilerParams(vmem_limit_bytes=mib * 2**20)


def cost(flops, moved, exps=0):
    return pl.CostEstimate(flops=int(flops), bytes_accessed=int(moved), transcendentals=int(exps))


def cycle_of(group):
    if group == 2:
        return [0, 2, 4, 6, 7, 5, 3, 1]
    return list(range(REQ))


def pick(table, index):
    result = jnp.int32(table[0])
    for place, value in enumerate(table):
        result = jnp.where(index == place, jnp.int32(value), result)
    return result


def swap(value, axis, mask):
    pairs = [(source, source ^ mask) for source in range(lax.axis_size(axis))]
    return lax.ppermute(value, axis, pairs)


def turn(value, cycle, group, way):
    count = len(cycle)
    pairs = []
    for place in range(count):
        source, target = cycle[place], cycle[(place + way) % count]
        pairs += [(source * group + m, target * group + m) for m in range(group)]
    return lax.ppermute(value, "seq", pairs)


def rotated(vectors, cosine, sine):
    return vectors * cosine + pltpu.roll(vectors, HD // 2, 1) * sine


def position_kernel(lengths, shared, positions):
    rows = positions.shape[0]
    group = lax.axis_size("seq") // REQ
    seq = lax.axis_index("seq")
    start = shared[0] + lengths[seq // group] + (seq % group) * rows
    places = start + lax.broadcasted_iota(jnp.int32, positions.shape, 0)
    positions[...] = places.astype(jnp.float32)


def angles(tail_len, shared_len, rows):
    half = HD // 2
    positions = pl.pallas_call(
        position_kernel,
        in_specs=[SMEM] * 2,
        out_specs=VMEM,
        out_shape=jax.ShapeDtypeStruct((rows, HD), jnp.float32),
        compiler_params=params(8),
        cost_estimate=cost(rows * HD, 4 * rows * HD),
        name="positions",
    )(tail_len, shared_len)
    lane = jnp.arange(HD, dtype=jnp.int32)
    freqs = 10000.0 ** (-(lane % half).astype(jnp.float32) / half)
    angle = positions * freqs
    return jnp.cos(angle), jnp.sin(angle) * jnp.where(lane < half, -1.0, 1.0)


def lanes(start, count=HD):
    return pl.ds(pl.multiple_of(start, HD), count)


def after(value, *others):
    return lax.optimization_barrier((value, *others))[0]


VMEM = pl.BlockSpec(memory_space=pltpu.VMEM)
HBM = pl.BlockSpec(memory_space=pltpu.HBM)
SMEM = pl.BlockSpec(memory_space=pltpu.SMEM)


def viewed(block):
    count, pair, width = block.shape
    return block.reshape(count, pair, width // HD, HD).transpose(0, 2, 1, 3)


def order_rows(stride, back):
    rows = 2 * HD
    places = rows // stride
    row = lax.broadcasted_iota(jnp.int32, (rows, rows), 1 if back else 0)
    column = lax.broadcasted_iota(jnp.int32, (rows, rows), 0 if back else 1)
    source = lax.rem(row, places) * stride + lax.div(row, places)
    return jnp.where(column == source, 1.0, 0.0).astype(jnp.bfloat16)


def reordered(order, tiles):
    both = tiles[0] if len(tiles) == 1 else jnp.concatenate(tiles, axis=1)
    mixed = jnp.dot(order, both, preferred_element_type=jnp.float32).astype(jnp.bfloat16)
    return [mixed[:, i * HD : (i + 1) * HD] for i in range(len(tiles))]


def take_apart(block, order, keys, values, offset):
    count, heads = block.shape[:2]
    stride = 2 * heads
    places = 2 * HD // stride
    flat = block.reshape(count * stride, HD)
    for start in range(0, count, 2 * places):
        starts = [at for at in (start, start + places) if at < count]
        tiles = [flat[at * stride : (at + places) * stride, :] for at in starts]
        for at, tile in zip(starts, reordered(order, tiles)):
            for head in range(heads):
                for j, result in enumerate((keys, values)):
                    line = (2 * head + j) * places
                    result[offset + at : offset + at + places, head * HD : (head + 1) * HD] = tile[
                        line : line + places
                    ]


ACROSS = (((1,), (1,)), ((), ()))


def unit_matrix(size):
    row = lax.broadcasted_iota(jnp.int32, (size, size), 0)
    column = lax.broadcasted_iota(jnp.int32, (size, size), 1)
    return jnp.where(row == column, 1.0, 0.0).astype(jnp.bfloat16)


def turned_over(unit, value):
    return lax.dot_general(unit, value, ACROSS, preferred_element_type=jnp.float32).astype(
        jnp.bfloat16
    )


def turn_heads(values, result):
    unit = unit_matrix(HD)
    for start in range(0, values.shape[1], HD):
        result[start : start + HD, :] = turned_over(unit, values[:, start : start + HD])


def part_kernel(*refs):
    *blocks, keys, turned, token, values = refs
    order = order_rows(2 * blocks[0].shape[1], False)
    offset = 0
    for block in blocks:
        take_apart(block, order, keys, values, offset)
        offset += block.shape[0]
    turn_heads(values, turned)
    token[...] = jnp.zeros_like(token)


TOKEN = jax.ShapeDtypeStruct((8, HD), jnp.float32)


def part_keyval(blocks, name):
    count = sum(block.shape[0] for block in blocks)
    width = blocks[0].shape[1] * HD
    return pl.pallas_call(
        part_kernel,
        in_specs=[VMEM] * len(blocks),
        out_specs=[VMEM] * 3,
        out_shape=[
            jax.ShapeDtypeStruct((count, width), jnp.bfloat16),
            jax.ShapeDtypeStruct((width, count), jnp.bfloat16),
            TOKEN,
        ],
        scratch_shapes=[pltpu.VMEM((count, width), jnp.bfloat16)],
        compiler_params=params(16),
        cost_estimate=cost(2**10 * count * width, 8 * count * width),
        name=name,
    )(*blocks)


def query_kernel(*refs):
    *pieces, weight, cosine, sine, query, normed = refs
    columns = pieces[0].shape[1]
    index = lax.axis_index("tp")
    features = columns * len(pieces)
    values = [piece[...].astype(jnp.float32) for piece in pieces]
    mean = sum(jnp.sum(v, axis=1, keepdims=True) for v in values) / features
    values = [v - mean for v in values]
    spread = sum(jnp.sum(v * v, axis=1, keepdims=True) for v in values) / features
    inverse = lax.rsqrt(spread + 1e-05)
    for shift, v in enumerate(values):
        normed[:, lanes((index ^ shift) * columns, columns)] = (v * inverse).astype(jnp.bfloat16)
    width = weight.shape[1]
    wide = min(width, 2 * HD)
    for base in range(0, width, wide):
        product = jnp.dot(
            normed[...], weight[:, base : base + wide], preferred_element_type=jnp.float32
        )
        for start in range(0, wide, HD):
            query[:, base + start : base + start + HD] = rotated(
                product[:, start : start + HD], cosine[...], sine[...]
            ).astype(jnp.bfloat16)


def project_query(pieces, w_query, cosine, sine):
    rows, columns = pieces[0].shape
    depth, width = w_query.shape
    return pl.pallas_call(
        query_kernel,
        in_specs=[VMEM] * (len(pieces) + 3),
        out_specs=[VMEM] * 2,
        out_shape=[
            jax.ShapeDtypeStruct((rows, width), jnp.bfloat16),
            jax.ShapeDtypeStruct((rows, depth), jnp.bfloat16),
        ],
        compiler_params=params(20),
        cost_estimate=cost(2 * rows * depth * width, 2 * depth * width),
        name="project_query",
    )(*pieces, w_query, cosine, sine)


def weight_kernel(weight, result, token, near, arrived):
    slots, chunk, heads = near.shape[:3]
    count = weight.shape[0] // chunk
    copies = [
        pltpu.make_async_copy(
            weight.at[pl.ds(i * chunk, chunk)], near.at[i % slots], arrived.at[i]
        )
        for i in range(count)
    ]
    for copy in copies[:slots]:
        copy.start()
    order = order_rows(2 * heads, False)
    for i, copy in enumerate(copies):
        copy.wait()
        take_apart(near.at[i % slots], order, result.at[0], result.at[1], i * chunk)
        if i + slots < count:
            copies[i + slots].start()
    token[...] = jnp.zeros_like(token)


def part_weights(w_keyval):
    weight = viewed(w_keyval)
    depth, heads = weight.shape[:2]
    chunk = min(depth, 256)
    count = depth // chunk
    return pl.pallas_call(
        weight_kernel,
        in_specs=[HBM],
        out_specs=[VMEM] * 2,
        out_shape=[jax.ShapeDtypeStruct((2, depth, heads * HD), jnp.bfloat16), TOKEN],
        scratch_shapes=[
            pltpu.VMEM((count, chunk, heads, 2, HD), jnp.bfloat16),
            pltpu.SemaphoreType.DMA((count,)),
        ],
        compiler_params=params(38),
        cost_estimate=cost(2**12 * depth * heads * HD, 8 * depth * heads * HD),
        name="part_weights",
    )(weight)


def keyval_kernel(normed, weight, cosine, sine, keys, turned, cache, values):
    rows = normed.shape[0]
    heads = weight.shape[2] // HD
    stride = 2 * heads
    for head in range(heads):
        span = slice(head * HD, (head + 1) * HD)
        product = jnp.dot(
            normed[...],
            jnp.concatenate([weight[0, :, span], weight[1, :, span]], axis=1),
            preferred_element_type=jnp.float32,
        )
        keys[:, span] = rotated(product[:, :HD], cosine[...], sine[...]).astype(jnp.bfloat16)
        values[:, span] = product[:, HD:].astype(jnp.bfloat16)
    turn_heads(values, turned)
    order = order_rows(stride, True)
    places = 2 * HD // stride
    flat = cache.reshape(rows * stride, HD)
    for start in range(0, rows, 2 * places):
        starts = [at for at in (start, start + places) if at < rows]
        tiles = [
            jnp.concatenate(
                [
                    pair[at : at + places, head * HD : (head + 1) * HD]
                    for head in range(heads)
                    for pair in (keys, values)
                ],
                axis=0,
            )
            for at in starts
        ]
        for at, tile in zip(starts, reordered(order, tiles)):
            flat[at * stride : (at + places) * stride, :] = tile


def project_keyval(normed, weight, cosine, sine):
    rows, depth = normed.shape
    width = weight.shape[2]
    heads = width // HD
    keys, turned, cache = pl.pallas_call(
        keyval_kernel,
        in_specs=[VMEM] * 4,
        out_specs=[VMEM] * 3,
        out_shape=[
            jax.ShapeDtypeStruct((rows, width), jnp.bfloat16),
            jax.ShapeDtypeStruct((width, rows), jnp.bfloat16),
            jax.ShapeDtypeStruct((rows, heads, 2, HD), jnp.bfloat16),
        ],
        scratch_shapes=[pltpu.VMEM((rows, width), jnp.bfloat16)],
        compiler_params=params(20),
        cost_estimate=cost(4 * rows * depth * width, 4 * depth * width),
        name="project_keyval",
    )(normed, weight, cosine, sine)
    return keys, turned, cache.transpose(0, 2, 1, 3).reshape(rows, 2, width)


def attend_kernel(spec, *refs):
    group, shifts, rings, slots, piece, parted, first, last = spec
    refs = list(refs)
    take = lambda count: [refs.pop(0) for _ in range(count)]
    lengths, shared, table = take(3)
    queries = take(len(shifts))
    if parted:
        blocks = take(2 * parted)
        many_keys, many_turned = blocks[::2], blocks[1::2]
    else:
        raw = take(len(rings))
    if not first:
        old_mixes, old_extents = take(len(shifts)), take(len(shifts))
    results = take(len(shifts))
    extents = [None if last and shift else take(1)[0] for shift in shifts]
    token, bias = take(2)
    extents = [take(1)[0] if extent is None else extent for extent in extents]
    if parted:
        causal = take(1)[0]
    else:
        keys_here, turned_here, values_here = take(3)
        many_keys, many_turned = [keys_here], [turned_here]
    rows, width = queries[0].shape
    heads = width // HD
    cycle = cycle_of(group)
    seq = lax.axis_index("seq")
    request, member = seq // group, seq % group
    place = pick(list(np.argsort(cycle)), request)
    edges = []
    count = 0
    for i in range(slots):
        wanted = seq * slots + i
        number = jnp.int32(0)
        for j in range(table.shape[0]):
            number = jnp.where(table[j, request] == wanted, jnp.int32(j), number)
        edges.append((count, BLK, number * BLK, lengths[request]))
        count += BLK
    for step, begin, size in rings:
        origin = pick(cycle, lax.rem(place + step + REQ, REQ))
        edges.append((count, size, (origin * group + member) * piece + begin, shared[0]))
        count += size
    for begin, size, start, length in edges:
        positions = start + lax.broadcasted_iota(jnp.int32, (size, HD), 0)
        lane = lax.broadcasted_iota(jnp.int32, (size, HD), 1)
        bias[begin : begin + size, :] = jnp.where(
            (positions >= length) & (lane == 0), NEGATIVE, 0.0
        ).astype(jnp.bfloat16)
    if parted:
        bias[count : count + rows, :] = jnp.zeros((rows, HD), jnp.bfloat16)
        theirs = member * rows + lax.broadcasted_iota(jnp.int32, (rows, rows), 0)
        for i, shift in enumerate(shifts):
            mine = (member ^ shift) * rows + lax.broadcasted_iota(jnp.int32, (rows, rows), 1)
            causal[i] = jnp.where(theirs <= mine, 0.0, NEGATIVE)
    else:
        offset = 0
        order = order_rows(2 * heads, False)
        for block in raw:
            take_apart(block, order, keys_here, values_here, offset)
            offset += block.shape[0]
        turn_heads(values_here, turned_here)
    token[...] = jnp.zeros_like(token)
    unit = jnp.where(lax.broadcasted_iota(jnp.int32, (rows, HD), 1) == 0, 1.0, 0.0)
    unit = unit.astype(jnp.bfloat16)

    def one_head(head):
        span = lanes(head * HD)
        line = pl.ds(head, 1)
        keys = jnp.concatenate([keys[:, span] for keys in many_keys], axis=0)
        keys = jnp.concatenate([keys, bias[...]], axis=1)
        values = jnp.concatenate([turned[span, :] for turned in many_turned], axis=1)
        for i in range(len(shifts)):
            query = jnp.concatenate([queries[i][:, span], unit], axis=1)
            scores = lax.dot_general(keys, query, ACROSS, preferred_element_type=jnp.float32)
            if parted:
                scores = jnp.concatenate([scores[:count], scores[count:] + causal[i]], axis=0)
            top = jnp.max(scores, axis=0, keepdims=True)
            if not first:
                old = old_extents[i][line, :]
                top = jnp.maximum(top, old * (1.0 / SCALE))
            weights = jnp.exp2((scores - top) * SCALE)
            summed = jnp.sum(weights, axis=0, keepdims=True)
            mixed = jnp.dot(
                values, weights.astype(jnp.bfloat16), preferred_element_type=jnp.float32
            )
            if not first:
                factor = jnp.exp2(old - top * SCALE)
                summed = summed + factor
                mixed = mixed + old_mixes[i][span, :] * factor
            mixed = mixed * (1.0 / summed)
            extents[i][line, :] = top * SCALE + jnp.log2(summed)
            results[i][span, :] = mixed.astype(results[i].dtype)

    together = min(4, heads)

    def some_heads(i, _):
        for j in range(together):
            one_head(together * i + j)
        return 0

    lax.fori_loop(0, heads // together, some_heads, 0)
    for i, shift in enumerate(shifts):
        if last and shift:
            line = extents[i][:heads, :]
            packed = []
            for _ in range(3):
                rounded = line.astype(jnp.bfloat16).astype(jnp.float32)
                packed.append(rounded)
                line = line - rounded
            gap = stat_rows(heads) - 3 * heads
            if gap:
                packed.append(jnp.zeros((gap, rows), jnp.float32))
            results[i][width:, :] = jnp.concatenate(packed, axis=0).astype(jnp.bfloat16)


def stat_rows(heads):
    return -(-3 * heads // 16) * 16


def attend(facts, queries, shifts, rings, slots, piece, blocks, old, last, name):
    group = len(queries)
    queries = [queries[shift] for shift in shifts]
    rows, width = queries[0].shape
    heads = width // HD
    parted = len(blocks) // 2 if blocks[0].ndim == 2 else 0
    operands = [*facts, *queries, *blocks]
    if old:
        operands += [old[shift][0] for shift in shifts] + [old[shift][1] for shift in shifts]
    count = sum(size for _, _, size in rings) + BLK * slots + (rows if parted else 0)
    scratch = [pltpu.VMEM((count, HD), jnp.bfloat16)]
    lines = (max(heads, 8), rows)
    scratch += [pltpu.VMEM(lines, jnp.float32) for shift in shifts if last and shift]
    if parted:
        scratch.append(pltpu.VMEM((len(shifts), rows, rows), jnp.float32))
    else:
        scratch += [
            pltpu.VMEM((count, width), jnp.bfloat16),
            pltpu.VMEM((width, count), jnp.bfloat16),
            pltpu.VMEM((count, width), jnp.bfloat16),
        ]
    mixes = [
        jax.ShapeDtypeStruct((width + stat_rows(heads), rows), jnp.bfloat16)
        if last and shift
        else jax.ShapeDtypeStruct((width, rows), jnp.float32)
        for shift in shifts
    ]
    extents = [
        jax.ShapeDtypeStruct(lines, jnp.float32) for shift in shifts if not (last and shift)
    ]
    scores = len(shifts) * rows * count * heads
    results = pl.pallas_call(
        functools.partial(
            attend_kernel, (group, shifts, rings, slots, piece, parted, not old, last)
        ),
        in_specs=[SMEM] * 3 + [VMEM] * (len(operands) - 3),
        out_specs=[VMEM] * (len(mixes) + len(extents) + 1),
        out_shape=[*mixes, *extents, TOKEN],
        scratch_shapes=scratch,
        compiler_params=params(24),
        cost_estimate=cost(4 * scores * HD, 4 * count * width, scores),
        name=name,
    )(*operands)
    if last:
        return results
    state = {shift: (results[i], results[len(shifts) + i]) for i, shift in enumerate(shifts)}
    return state, results[-1]


def combine_kernel(*refs):
    result, extent, *parts, weight, attended, sent = refs
    width, rows = result.shape
    heads = width // HD
    extents = [extent[:heads, :]]
    for part in parts:
        lines = part[width:, :].astype(jnp.float32)
        extents.append(sum(lines[i * heads : (i + 1) * heads] for i in range(3)))
    top = functools.reduce(jnp.maximum, extents)
    shares = [jnp.exp2(extent - top) for extent in extents]
    whole = sum(shares)
    shares = [share / whole for share in shares]
    unit = unit_matrix(rows)
    for head in range(heads):
        span = slice(head * HD, (head + 1) * HD)
        mixes = [result[span, :]] + [part[span, :].astype(jnp.float32) for part in parts]
        mixed = sum(mix * share[head : head + 1] for mix, share in zip(mixes, shares))
        attended[:, span] = turned_over(unit, mixed.astype(jnp.bfloat16))
    index = lax.axis_index("tp")
    ways = sent.shape[0] + 1
    columns = weight.shape[1] // ways
    for shift in range(1, ways):
        sent[shift - 1] = jnp.dot(
            attended[...],
            weight[:, lanes((index ^ shift) * columns, columns)],
            preferred_element_type=jnp.float32,
        ).astype(jnp.bfloat16)


def combine(result, extent, parts, w_out, ways):
    width, rows = result.shape
    columns = w_out.shape[1] // ways
    return pl.pallas_call(
        combine_kernel,
        in_specs=[VMEM] * (3 + len(parts)),
        out_specs=[VMEM] * 2,
        out_shape=[
            jax.ShapeDtypeStruct((rows, width), jnp.bfloat16),
            jax.ShapeDtypeStruct((ways - 1, rows, columns), jnp.bfloat16),
        ],
        compiler_params=params(20),
        cost_estimate=cost(2 * rows * width * columns * (ways - 1), 2 * width * w_out.shape[1]),
        name="combine_send",
    )(result, extent, *parts, w_out)


def keep_kernel(attended, weight, hidden, kept):
    columns = hidden.shape[1]
    product = jnp.dot(
        attended[...],
        weight[:, lanes(lax.axis_index("tp") * columns, columns)],
        preferred_element_type=jnp.float32,
    )
    kept[...] = product + hidden[...].astype(jnp.float32)


def keep(attended, w_out, hidden):
    rows, width = attended.shape
    return pl.pallas_call(
        keep_kernel,
        in_specs=[VMEM] * 3,
        out_specs=VMEM,
        out_shape=jax.ShapeDtypeStruct(hidden.shape, jnp.float32),
        compiler_params=params(20),
        cost_estimate=cost(2 * rows * width * hidden.shape[1], 2 * width * w_out.shape[1]),
        name="keep_own",
    )(attended, w_out, hidden)


def local(
    hidden_in, w_query, w_keyval, w_out, prompt_cache, tail_cache, tail_table, tail_len, shared_len
):
    rows = hidden_in.shape[0]
    group = lax.axis_size("seq") // REQ
    ways = lax.axis_size("tp")
    cycle = cycle_of(group)
    half = REQ // 2
    piece = prompt_cache.shape[0]
    middle = piece // 2

    pieces = [hidden_in] + [swap(hidden_in, "tp", shift) for shift in range(1, ways)]
    prompt = viewed(prompt_cache)
    ahead, behind = [prompt], [prompt]

    def step(*others):
        for blocks, way in ((ahead, 1), (behind, -1)):
            blocks.append(turn(after(blocks[-1], *others), cycle, group, way))

    step()
    cosine, sine = angles(tail_len, shared_len, rows)
    weight, token = part_weights(w_keyval)
    pieces[0] = after(pieces[0], token)
    query, normed = project_query(pieces, w_query, cosine, sine)
    queries = [query] + [swap(query, "seq", shift) for shift in range(1, group)]
    tail = viewed(tail_cache.reshape(-1, 2, tail_cache.shape[3]))
    slots = tail_cache.shape[0]
    *own_block, token = part_keyval([tail, prompt], "part_own")
    step(token)
    *near_block, token = part_keyval([ahead[1], behind[1]], "part_near")
    fresh_keys, fresh_turned, new_cache = project_keyval(normed, weight, cosine, sine)

    table = tail_table.T
    facts = (tail_len, shared_len, table)
    others = list(range(1, group))
    near = (
        [(0, 0, piece), (-1, 0, piece), (1, 0, piece)],
        slots,
        piece,
        [*own_block, *near_block, fresh_keys, fresh_turned],
        None,
        False,
    )
    state, token = attend(facts, queries, [0], *near, "attend_near_own")
    step(token)
    ready = (after(tail_len, token), shared_len, table)
    state_others, token = attend(ready, queries, others, *near, "attend_near_others")
    state |= state_others
    rings = [(-2, 0, piece), (2, 0, piece)]
    second = (rings, 0, piece, [ahead[2], behind[2]], state, False, "attend_second")
    state, token = attend(facts, queries, [0, *others], *second)
    far_low = turn(after(ahead[3], token)[:middle], cycle, group, 1)
    far_high = turn(after(behind[3], token)[middle:], cycle, group, -1)
    rings = [(-3, 0, piece), (3, 0, piece)]
    third = (rings, 0, piece, [ahead[3], behind[3]], state, False, "attend_third")
    state, token = attend(facts, queries, [0, *others], *third)
    rings = [(-half, 0, middle), (half, middle, piece - middle)]
    far = (rings, 0, piece, [far_low, far_high], state, True)
    *parts, token = attend(facts, queries, others, *far, "attend_far_others")
    ready = (after(tail_len, token), shared_len, table)
    result, extent, token = attend(ready, queries, [0], *far, "attend_far_own")
    parts = [swap(part, "seq", shift + 1) for shift, part in enumerate(parts)]
    attended, sent = combine(result, extent, parts, w_out, ways)
    received = [swap(sent[shift - 1], "tp", shift) for shift in range(1, ways)]
    total = keep(attended, w_out, hidden_in)
    for part in received:
        total = total + part.astype(jnp.float32)
    return (total.astype(jnp.bfloat16), new_cache)


def solution(mesh):
    return jax.shard_map(
        local,
        mesh=mesh,
        in_specs=(
            P("seq", "tp"),
            P(None, "tp"),
            P(None, None, "tp"),
            P("tp", None),
            P("seq", None, "tp"),
            P("seq", None, None, "tp"),
            P(),
            P(),
            P(),
        ),
        out_specs=(P("seq", "tp"), P("seq", None, "tp")),
        check_vma=False,
    )
```

time: 93.4 us -> 75.8 us (0.81)
  local copies, waits for them, and re-layouts: 12.7 us -> 0.39 us
  Pallas kernels: 55.1 us -> 50.2 us
  waiting for transfers between devices: 9.44 us -> 10.5 us
    unnamed x23 -> x14, local copies, waits for them, and re-layouts: 11.8 us -> 0.03 us
    pallas_call x6, Pallas kernels: 35.7 us -> 29.5 us  [attend(): pl.pallas_call(functools.partial(attend_kernel, (group, shifts, rings, sl...]
    pallas_call x3 -> x4, Pallas kernels: 10.9 us -> 12.4 us  [the longest x1 8.37 us: part_weights(): pl.pallas_call(weight_kernel, in_specs=[HBM], out_specs=[VMEM] * 2, out_s...]
    ppermute x8, waiting for transfers between devices: 0.02 us -> 1.04 us  [turn(): return lax.ppermute(value, 'seq', pairs)]
  transfers between devices with their start and end apart: 12 -> 12, of which waited for: 2 -> 4; matrix products, arithmetic and copies ran while one was open for 2% -> 1% of each run, Pallas kernels for 53% -> 60%
where the time goes in v6:
time: 75.8 us; the launch traced here: 75.7 us
  Pallas kernels  50.2 us (66%)
  starting transfers between devices  11.7 us (15%)
  waiting for transfers between devices  10.5 us (14%)
  between operations  1.47 us (2%)
  other arithmetic  1.43 us (2%)
    pallas_call x6, Pallas kernels, attend(): pl.pallas_call(functools.partial(attend_kernel, (group, shifts, rings, sl...  29.5 us
    ppermute x4, waiting for transfers between devices, swap(): return lax.ppermute(value, axis, pairs)  9.44 us
    ppermute x8, starting transfers between devices, turn(): return lax.ppermute(value, 'seq', pairs)  9.32 us
    pallas_call x1, Pallas kernels, part_weights(): pl.pallas_call(weight_kernel, in_specs=[HBM], out_specs=[VMEM] * 2, out_s...  8.37 us
    pallas_call x1, Pallas kernels, project_keyval(): pl.pallas_call(keyval_kernel, in_specs=[VMEM] * 4, out_specs=[VMEM] * 3,...  4.46 us
    pallas_call x2, Pallas kernels, part_keyval(): pl.pallas_call(part_kernel, in_specs=[VMEM] * len(blocks), out_specs=[VME...  3.45 us
    ppermute x4, starting transfers between devices, swap(): return lax.ppermute(value, axis, pairs)  2.37 us
    pallas_call x1, Pallas kernels, project_query(): pl.pallas_call(query_kernel, in_specs=[VMEM] * (len(pieces) + 3), out_spe...  2.08 us
  transfers between devices with their start and end apart: 12, of which 4 were waited for; matrix products, arithmetic and copies ran while one was open for 1% of the time, Pallas kernels for 60%

profile of v6, /device:TPU:0, one launch (start us, length us, event | category | flops | bytes accessed | tf_op | source)
XLA Modules:
  0.0 75.7 jit_solution(12949344400649301605)
XLA Ops:
  0.6 3.1 %collective-permute-start.1 = (bf16[128,8,2,128]{3,2,1,0:T(2,128)(2,1)}, bf16[128,8,2,128]{3,2,1,0:T(2,128)(2,1)S(1)}, u32[]{:S(2)}, u32[]{:S(2)}) collective-permute-start(bf16[128,8,2,128]{3,2,1,0:T(2,128)(2,1)} %bitcast.15), channel_id=1, source_target_pairs={{0,8},{2,10},{8,16},{10,18},{16,24},{18,26},{24,28},{26,30},{28,20... | collective-permute-start | bytes 1572872 | tf_op jit(solution)/shard_map/ppermute | solution.py:50
  3.8 8.4 %part_weights.1 = (bf16[2,2048,1024]{2,1,0:T(8,128)(2,1)S(1)}, f32[8,128]{1,0:T(8,128)}) custom-call(bf16[2048,8,2,128]{3,2,1,0:T(2,128)(2,1)} %bitcast.25), custom_call_target="tpu_custom_call" | custom-call | flops 8589934592 | bytes 16777216 | tf_op jit(solution)/shard_map/part_weights/pallas_call | solution.py:253
  12.8 0.6 positions.1
  13.4 1.9 %part_own.1 = (bf16[384,1024]{1,0:T(8,128)(2,1)S(1)}, bf16[1024,384]{1,0:T(8,128)(2,1)S(1)}, f32[8,128]{1,0:T(8,128)}) custom-call(bf16[256,8,2,128]{3,2,1,0:T(2,128)(2,1)S(1)} %bitcast.14, bf16[128,8,2,128]{3,2,1,0:T(2,128)(2,1)S(1)} %bitcast.17), custom_call_target="tpu_custom_call" | custom-call | flops 402653184 | bytes 3145728 | tf_op jit(solution)/shard_map/part_own/pallas_call | solution.py:171
  15.3 0.4 collective-permute-done.1.refs_0_
  15.8 1.8 %collective-permute-start.2 = (bf16[128,8,2,128]{3,2,1,0:T(2,128)(2,1)S(1)}, bf16[128,8,2,128]{3,2,1,0:T(2,128)(2,1)S(1)}, u32[]{:S(2)}, u32[]{:S(2)}) collective-permute-start(bf16[128,8,2,128]{3,2,1,0:T(2,128)(2,1)S(1)} %collective-permute-done.1.refs_0_), channel_id=1, source_target_pairs={{0,8},{2,10},{8,16},{10,18},{16,24},{18,26},{24,28},{26,30},{28,20... | collective-permute-start | bytes 1572872 | tf_op jit(solution)/shard_map/ppermute | solution.py:50
  17.6 0.2 collective-permute-start.6
  17.8 0.5 sine_multiply_fusion
  18.3 2.1 %project_query.1 = (bf16[256,1024]{1,0:T(8,128)(2,1)S(1)}, bf16[256,2048]{1,0:T(8,128)(2,1)S(1)}) custom-call(bf16[256,1024]{1,0:T(8,128)(2,1)S(1)} %copy-done.2, bf16[256,1024]{1,0:T(8,128)(2,1)S(1)} %collective-permute-done.refs_1_, bf16[2048,1024]{1,0:T(8,128)(2,1)S(1)} %copy-done.1, f32[256,128]{1,0:T(8,128)S(1)} %get-tuple-element.77.refs_3_.cosine, ...), custom_call_target="tpu_custom_call" | custom-call | flops 1073741824 | bytes 4194304 | tf_op jit(solution)/shard_map/project_query/pallas_call | solution.py:214
  20.4 1.8 %collective-permute-start.5 = (bf16[256,1024]{1,0:T(8,128)(2,1)S(1)}, bf16[256,1024]{1,0:T(8,128)(2,1)S(1)}, u32[]{:S(2)}, u32[]{:S(2)}) collective-permute-start(bf16[256,1024]{1,0:T(8,128)(2,1)S(1)} %get-tuple-element.39.refs_3_), channel_id=1, source_target_pairs={{0,2},{2,0},{4,6},{6,4},{8,10},{10,8},{12,14},{14,12},{16,18},{18,... | collective-permute-start | bytes 1572872 | tf_op jit(solution)/shard_map/ppermute | solution.py:41
  22.2 4.5 %project_keyval.1 = (bf16[256,1024]{1,0:T(8,128)(2,1)S(1)}, bf16[1024,256]{1,0:T(8,128)(2,1)S(1)}, bf16[256,8,2,128]{3,2,1,0:T(2,128)(2,1)}) custom-call(bf16[256,2048]{1,0:T(8,128)(2,1)S(1)} %get-tuple-element.46.normed, bf16[2,2048,1024]{2,1,0:T(8,128)(2,1)S(1)} %get-tuple-element.47.weight, f32[256,128]{1,0:T(8,128)S(1)} %get-tuple-element.77.refs_3_.cosine, ...), custom_call_target="tpu_custom_call" | custom-call | flops 2147483648 | bytes 8388608 | tf_op jit(solution)/shard_map/project_keyval/pallas_call | solution.py:306
  26.6 1.5 %part_near.1 = (bf16[256,1024]{1,0:T(8,128)(2,1)S(1)}, bf16[1024,256]{1,0:T(8,128)(2,1)S(1)}, f32[8,128]{1,0:T(8,128)}) custom-call(bf16[128,8,2,128]{3,2,1,0:T(2,128)(2,1)S(1)} %collective-permute-done.1.refs_0_, bf16[128,8,2,128]{3,2,1,0:T(2,128)(2,1)S(1)} %collective-permute-done.3.refs_1_), custom_call_target="tpu_custom_call" | custom-call | flops 268435456 | bytes 2097152 | tf_op jit(solution)/shard_map/part_near/pallas_call | solution.py:171
  28.2 5.5 %attend_near_own.1 = (f32[1024,256]{1,0:T(8,128)S(1)}, f32[8,256]{1,0:T(8,128)S(1)}, f32[8,128]{1,0:T(8,128)}) custom-call(s32[8]{0:T(128)S(1)} %copy-done.6, s32[1]{0:T(128)S(6)} %copy.11.shared.refs_1_, s32[4,8]{1,0:T(4,128)S(1)} %bitcast.18, bf16[256,1024]{1,0:T(8,128)(2,1)S(1)} %get-tuple-element.39.refs_3_, ...), custom_call_target="tpu_custom_call" | custom-call | flops 939524096 | bytes 3670016 | tf_op jit(solution)/shard_map/attend_near_own/pallas_call | solution.py:472
  33.7 1.6 %collective-permute-start.8 = (bf16[128,8,2,128]{3,2,1,0:T(2,128)(2,1)S(1)}, bf16[128,8,2,128]{3,2,1,0:T(2,128)(2,1)S(1)}, u32[]{:S(2)}, u32[]{:S(2)}) collective-permute-start(bf16[128,8,2,128]{3,2,1,0:T(2,128)(2,1)S(1)} %collective-permute-done.6.refs_6_), channel_id=1, source_target_pairs={{0,4},{2,6},{8,0},{10,2},{16,8},{18,10},{24,16},{26,18},{28,24},{3... | collective-permute-start | bytes 1572872 | tf_op jit(solution)/shard_map/ppermute | solution.py:50
  35.3 0.5 collective-permute-start.4
  35.8 5.5 %attend_near_others.1 = (f32[1024,256]{1,0:T(8,128)S(1)}, f32[8,256]{1,0:T(8,128)S(1)}, f32[8,128]{1,0:T(8,128)}) custom-call(s32[8]{0:T(128)S(1)} %copy-done.6, s32[1]{0:T(128)S(6)} %copy.11.shared.refs_1_, s32[4,8]{1,0:T(4,128)S(1)} %bitcast.19, bf16[256,1024]{1,0:T(8,128)(2,1)S(1)} %collective-permute-done.5.refs_3_.refs_4_, ...), custom_call_target="tpu_custom_call" | custom-call | flops 939524096 | bytes 3670016 | tf_op jit(solution)/shard_map/attend_near_others/pallas_call | solution.py:472
  41.4 5.9 %attend_second.1 = (f32[1024,256]{1,0:T(8,128)S(1)}, f32[1024,256]{1,0:T(8,128)S(1)}, f32[8,256]{1,0:T(8,128)S(1)}, f32[8,256]{1,0:T(8,128)S(1)}, f32[8,128]{1,0:T(8,128)}) custom-call(s32[8]{0:T(128)S(1)} %copy-done.6, s32[1]{0:T(128)S(6)} %copy.11.shared.refs_1_, s32[4,8]{1,0:T(4,128)S(1)} %bitcast.20, bf16[256,1024]{1,0:T(8,128)(2,1)S(1)} %get-tuple-element.39.refs_3_, ...), custom_call_target="tpu_custom_call" | custom-call | flops 536870912 | bytes 1048576 | tf_op jit(solution)/shard_map/attend_second/pallas_call | solution.py:472
  47.2 0.2 slice.7
  47.4 1.6 %collective-permute-start.9 = (bf16[64,8,2,128]{3,2,1,0:T(2,128)(2,1)S(1)}, bf16[64,8,2,128]{3,2,1,0:T(2,128)(2,1)S(1)}, u32[]{:S(2)}, u32[]{:S(2)}) collective-permute-start(bf16[64,8,2,128]{3,2,1,0:T(2,128)(2,1)S(1)} %slice.7), channel_id=1, source_target_pairs={{0,4},{2,6},{8,0},{10,2},{16,8},{18,10},{24,16},{26,18},{28,24},{3... | collective-permute-start | bytes 786440 | tf_op jit(solution)/shard_map/ppermute | solution.py:50
  49.0 0.2 slice.6
  49.2 0.6 collective-permute-start.7
  49.7 5.9 %attend_third.1 = (f32[1024,256]{1,0:T(8,128)S(1)}, f32[1024,256]{1,0:T(8,128)S(1)}, f32[8,256]{1,0:T(8,128)S(1)}, f32[8,256]{1,0:T(8,128)S(1)}, f32[8,128]{1,0:T(8,128)}) custom-call(s32[8]{0:T(128)S(1)} %copy-done.6, s32[1]{0:T(128)S(6)} %copy.11.shared.refs_1_, s32[4,8]{1,0:T(4,128)S(1)} %bitcast.21, bf16[256,1024]{1,0:T(8,128)(2,1)S(1)} %get-tuple-element.39.refs_3_, ...), custom_call_target="tpu_custom_call" | custom-call | flops 536870912 | bytes 1048576 | tf_op jit(solution)/shard_map/attend_third/pallas_call | solution.py:472
  55.6 0.6 collective-permute-done.7.refs_4_
  56.2 3.4 %attend_far_others.1 = (bf16[1056,256]{1,0:T(8,128)(2,1)S(1)}, f32[8,128]{1,0:T(8,128)}) custom-call(s32[8]{0:T(128)S(1)} %copy-done.6, s32[1]{0:T(128)S(6)} %copy.11.shared.refs_1_, s32[4,8]{1,0:T(4,128)S(1)} %bitcast.22, bf16[256,1024]{1,0:T(8,128)(2,1)S(1)} %collective-permute-done.5.refs_3_.refs_4_, ...), custom_call_target="tpu_custom_call" | custom-call | flops 134217728 | bytes 524288 | tf_op jit(solution)/shard_map/attend_far_others/pallas_call | solution.py:472
  59.6 0.5 collective-permute-start.10
  60.1 3.3 %attend_far_own.1 = (f32[1024,256]{1,0:T(8,128)S(1)}, f32[8,256]{1,0:T(8,128)S(1)}, f32[8,128]{1,0:T(8,128)}) custom-call(s32[8]{0:T(128)S(1)} %copy-done.6, s32[1]{0:T(128)S(6)} %copy.11.shared.refs_1_, s32[4,8]{1,0:T(4,128)S(1)} %bitcast.23, bf16[256,1024]{1,0:T(8,128)(2,1)S(1)} %get-tuple-element.39.refs_3_, ...), custom_call_target="tpu_custom_call" | custom-call | flops 134217728 | bytes 524288 | tf_op jit(solution)/shard_map/attend_far_own/pallas_call | solution.py:472
  63.4 8.3 %collective-permute-done.10.refs_2_ = bf16[1056,256]{1,0:T(8,128)(2,1)S(1)} collective-permute-done((bf16[1056,256]{1,0:T(8,128)(2,1)S(1)}, bf16[1056,256]{1,0:T(8,128)(2,1)S(1)}, u32[]{:S(2)}, u32[]{:S(2)}) %collective-permute-start.10) | collective-permute-done | bytes 540704 | tf_op jit(solution)/shard_map/ppermute | solution.py:41
  71.7 1.0 %combine_send.1 = (bf16[256,1024]{1,0:T(8,128)(2,1)S(1)}, bf16[1,256,1024]{2,1,0:T(8,128)(2,1)S(1)}) custom-call(f32[1024,256]{1,0:T(8,128)S(1)} %get-tuple-element.68.refs_0_, f32[8,256]{1,0:T(8,128)S(1)} %get-tuple-element.69.refs_1_, bf16[1056,256]{1,0:T(8,128)(2,1)S(1)} %collective-permute-done.10.refs_2_, bf16[1024,2048]{1,0:T(8,128)(2,1)S(1)} %copy-done), custom_call_target="tpu_custom_call" | custom-call | flops 536870912 | bytes 4194304 | tf_op jit(solution)/shard_map/combine_send/pallas_call | solution.py:522
  72.7 0.1 collective-permute-start.11
  72.8 0.7 keep_own.1
  73.6 1.2 %collective-permute-done.11 = bf16[256,1024]{1,0:T(8,128)(2,1)S(1)} collective-permute-done((bf16[256,1024]{1,0:T(8,128)(2,1)S(1)}, bf16[256,1024]{1,0:T(8,128)(2,1)S(1)}, u32[]{:S(2)}, u32[]{:S(2)}) %collective-permute-start.11) | collective-permute-done | bytes 524320 | tf_op jit(solution)/shard_map/ppermute | solution.py:41
  74.7 1.0 %add_convert_fusion = bf16[256,1024]{1,0:T(8,128)(2,1)} fusion(f32[256,1024]{1,0:T(8,128)S(1)} %keep_own.1, bf16[256,1024]{1,0:T(8,128)(2,1)S(1)} %collective-permute-done.11), kind=kLoop, calls=%fused_computation | loop fusion | flops 786432 | bytes 2097152 | tf_op jit(solution)/shard_map/convert_element_type | solution.py:626
  (25 shorter events, 0.1 us)
Async XLA Ops:
  0.6 15.2 %collective-permute-start.1 = (bf16[128,8,2,128]{3,2,1,0:T(2,128)(2,1)}, bf16[128,8,2,128]{3,2,1,0:T(2,128)(2,1)S(1)}, u32[]{:S(2)}, u32[]{:S(2)}) collective-permute-start(bf16[128,8,2,128]{3,2,1,0:T(2,128)(2,1)} %bitcast.15), channel_id=1, source_target_pairs={{0,8},{2,10},{8,16},{10,18},{16,24},{18,26},{24,28},{26,30},{28,20... | collective-permute-start | bytes 1572872 | tf_op jit(solution)/shard_map/ppermute | solution.py:50
  3.7 13.9 %collective-permute-start.3 = (bf16[128,8,2,128]{3,2,1,0:T(2,128)(2,1)}, bf16[128,8,2,128]{3,2,1,0:T(2,128)(2,1)S(1)}, u32[]{:S(2)}, u32[]{:S(2)}) collective-permute-start(bf16[128,8,2,128]{3,2,1,0:T(2,128)(2,1)} %bitcast.16), channel_id=1, source_target_pairs={{0,4},{2,6},{8,0},{10,2},{16,8},{18,10},{24,16},{26,18},{28,24},{3... | collective-permute-start | bytes 1572872 | tf_op jit(solution)/shard_map/ppermute | solution.py:50
  3.7 14.6 %collective-permute-start = (bf16[256,1024]{1,0:T(8,128)(2,1)}, bf16[256,1024]{1,0:T(8,128)(2,1)S(1)}, u32[]{:S(2)}, u32[]{:S(2)}) collective-permute-start(bf16[256,1024]{1,0:T(8,128)(2,1)} %hidden.1), channel_id=1, source_target_pairs={{0,1},{1,0},{2,3},{3,2},{4,5},{5,4},{6,7},{7,6},{8,9},{9,8},{10,11... | collective-permute-start | bytes 1572872 | tf_op jit(solution)/shard_map/ppermute | solution.py:41
  3.7 9.1 %copy-start.6 = (s32[8]{0:T(128)S(1)}, s32[8]{0:T(128)}, u32[]{:S(2)}) copy-start(s32[8]{0:T(128)} %refs_0_.10) | copy-start | bytes 100
  3.7 9.7 %copy-start.3 = (bf16[2,128,2,1024]{3,2,1,0:T(2,128)(2,1)S(1)}, bf16[2,128,2,1024]{3,2,1,0:T(2,128)(2,1)}, u32[]{:S(2)}) copy-start(bf16[2,128,2,1024]{3,2,1,0:T(2,128)(2,1)} %param.14) | copy-start | bytes 3145732
  3.7 9.7 %copy-start.4 = (bf16[128,2,1024]{2,1,0:T(2,128)(2,1)S(1)}, bf16[128,2,1024]{2,1,0:T(2,128)(2,1)}, u32[]{:S(2)}) copy-start(bf16[128,2,1024]{2,1,0:T(2,128)(2,1)} %param.13) | copy-start | bytes 1572868
  3.7 14.6 %copy-start.1 = (bf16[2048,1024]{1,0:T(8,128)(2,1)S(1)}, bf16[2048,1024]{1,0:T(8,128)(2,1)}, u32[]{:S(2)}) copy-start(bf16[2048,1024]{1,0:T(8,128)(2,1)} %refs_2_.1) | copy-start | bytes 12582916
  3.7 14.6 %copy-start.2 = (bf16[256,1024]{1,0:T(8,128)(2,1)S(1)}, bf16[256,1024]{1,0:T(8,128)(2,1)}, u32[]{:S(2)}) copy-start(bf16[256,1024]{1,0:T(8,128)(2,1)} %hidden.1) | copy-start | bytes 1572868
  15.3 12.8 %copy-start.5 = (s32[8,4]{0,1:T(4,128)S(1)}, s32[8,4]{0,1:T(4,128)}, u32[]{:S(2)}) copy-start(s32[8,4]{0,1:T(4,128)} %param.15) | copy-start | bytes 388
  15.8 19.5 %collective-permute-start.2 = (bf16[128,8,2,128]{3,2,1,0:T(2,128)(2,1)S(1)}, bf16[128,8,2,128]{3,2,1,0:T(2,128)(2,1)S(1)}, u32[]{:S(2)}, u32[]{:S(2)}) collective-permute-start(bf16[128,8,2,128]{3,2,1,0:T(2,128)(2,1)S(1)} %collective-permute-done.1.refs_0_), channel_id=1, source_target_pairs={{0,8},{2,10},{8,16},{10,18},{16,24},{18,26},{24,28},{26,30},{28,20... | collective-permute-start | bytes 1572872 | tf_op jit(solution)/shard_map/ppermute | solution.py:50
  17.6 16.1 %collective-permute-start.6 = (bf16[128,8,2,128]{3,2,1,0:T(2,128)(2,1)S(1)}, bf16[128,8,2,128]{3,2,1,0:T(2,128)(2,1)S(1)}, u32[]{:S(2)}, u32[]{:S(2)}) collective-permute-start(bf16[128,8,2,128]{3,2,1,0:T(2,128)(2,1)S(1)} %collective-permute-done.3.refs_1_), channel_id=1, source_target_pairs={{0,4},{2,6},{8,0},{10,2},{16,8},{18,10},{24,16},{26,18},{28,24},{3... | collective-permute-start | bytes 1572872 | tf_op jit(solution)/shard_map/ppermute | solution.py:50
  20.4 15.4 %collective-permute-start.5 = (bf16[256,1024]{1,0:T(8,128)(2,1)S(1)}, bf16[256,1024]{1,0:T(8,128)(2,1)S(1)}, u32[]{:S(2)}, u32[]{:S(2)}) collective-permute-start(bf16[256,1024]{1,0:T(8,128)(2,1)S(1)} %get-tuple-element.39.refs_3_), channel_id=1, source_target_pairs={{0,2},{2,0},{4,6},{6,4},{8,10},{10,8},{12,14},{14,12},{16,18},{18,... | collective-permute-start | bytes 1572872 | tf_op jit(solution)/shard_map/ppermute | solution.py:41
  33.7 38.0 %copy-start = (bf16[1024,2048]{1,0:T(8,128)(2,1)S(1)}, bf16[1024,2048]{1,0:T(8,128)(2,1)}, u32[]{:S(2)}) copy-start(bf16[1024,2048]{1,0:T(8,128)(2,1)} %weight.1) | copy-start | bytes 12582916
  33.7 13.5 %collective-permute-start.8 = (bf16[128,8,2,128]{3,2,1,0:T(2,128)(2,1)S(1)}, bf16[128,8,2,128]{3,2,1,0:T(2,128)(2,1)S(1)}, u32[]{:S(2)}, u32[]{:S(2)}) collective-permute-start(bf16[128,8,2,128]{3,2,1,0:T(2,128)(2,1)S(1)} %collective-permute-done.6.refs_6_), channel_id=1, source_target_pairs={{0,4},{2,6},{8,0},{10,2},{16,8},{18,10},{24,16},{26,18},{28,24},{3... | collective-permute-start | bytes 1572872 | tf_op jit(solution)/shard_map/ppermute | solution.py:50
  35.3 13.7 %collective-permute-start.4 = (bf16[128,8,2,128]{3,2,1,0:T(2,128)(2,1)S(1)}, bf16[128,8,2,128]{3,2,1,0:T(2,128)(2,1)S(1)}, u32[]{:S(2)}, u32[]{:S(2)}) collective-permute-start(bf16[128,8,2,128]{3,2,1,0:T(2,128)(2,1)S(1)} %collective-permute-done.2.refs_5_), channel_id=1, source_target_pairs={{0,8},{2,10},{8,16},{10,18},{16,24},{18,26},{24,28},{26,30},{28,20... | collective-permute-start | bytes 1572872 | tf_op jit(solution)/shard_map/ppermute | solution.py:50
  47.4 8.2 %collective-permute-start.9 = (bf16[64,8,2,128]{3,2,1,0:T(2,128)(2,1)S(1)}, bf16[64,8,2,128]{3,2,1,0:T(2,128)(2,1)S(1)}, u32[]{:S(2)}, u32[]{:S(2)}) collective-permute-start(bf16[64,8,2,128]{3,2,1,0:T(2,128)(2,1)S(1)} %slice.7), channel_id=1, source_target_pairs={{0,4},{2,6},{8,0},{10,2},{16,8},{18,10},{24,16},{26,18},{28,24},{3... | collective-permute-start | bytes 786440 | tf_op jit(solution)/shard_map/ppermute | solution.py:50
  49.2 7.0 %collective-permute-start.7 = (bf16[64,8,2,128]{3,2,1,0:T(2,128)(2,1)S(1)}, bf16[64,8,2,128]{3,2,1,0:T(2,128)(2,1)S(1)}, u32[]{:S(2)}, u32[]{:S(2)}) collective-permute-start(bf16[64,8,2,128]{3,2,1,0:T(2,128)(2,1)S(1)} %slice.6), channel_id=1, source_target_pairs={{0,8},{2,10},{8,16},{10,18},{16,24},{18,26},{24,28},{26,30},{28,20... | collective-permute-start | bytes 786440 | tf_op jit(solution)/shard_map/ppermute | solution.py:50
  59.6 12.1 %collective-permute-start.10 = (bf16[1056,256]{1,0:T(8,128)(2,1)S(1)}, bf16[1056,256]{1,0:T(8,128)(2,1)S(1)}, u32[]{:S(2)}, u32[]{:S(2)}) collective-permute-start(bf16[1056,256]{1,0:T(8,128)(2,1)S(1)} %get-tuple-element.72), channel_id=1, source_target_pairs={{0,2},{2,0},{4,6},{6,4},{8,10},{10,8},{12,14},{14,12},{16,18},{18,... | collective-permute-start | bytes 1622024 | tf_op jit(solution)/shard_map/ppermute | solution.py:41
  72.7 2.0 %collective-permute-start.11 = (bf16[256,1024]{1,0:T(8,128)(2,1)S(1)}, bf16[256,1024]{1,0:T(8,128)(2,1)S(1)}, u32[]{:S(2)}, u32[]{:S(2)}) collective-permute-start(bf16[256,1024]{1,0:T(8,128)(2,1)S(1)} %bitcast.24), channel_id=1, source_target_pairs={{0,1},{1,0},{2,3},{3,2},{4,5},{5,4},{6,7},{7,6},{8,9},{9,8},{10,11... | collective-permute-start | bytes 1572872 | tf_op jit(solution)/shard_map/ppermute | solution.py:41

commit v7 on v6

--- a/solution.py
+++ b/solution.py
@@ -95,7 +95,8 @@
 
 def viewed(block):
     count, pair, width = block.shape
-    return block.reshape(count, pair, width // HD, HD).transpose(0, 2, 1, 3)
+    heads = width // HD
+    return block.reshape(count, pair, heads, HD).transpose(0, 2, 1, 3).reshape(-1, HD)
 
 
 def order_rows(stride, back):
@@ -114,13 +115,13 @@
 
 
 def take_apart(block, order, keys, values, offset):
-    count, heads = block.shape[:2]
+    heads = keys.shape[1] // HD
     stride = 2 * heads
+    count = block.shape[0] // stride
     places = 2 * HD // stride
-    flat = block.reshape(count * stride, HD)
     for start in range(0, count, 2 * places):
         starts = [at for at in (start, start + places) if at < count]
-        tiles = [flat[at * stride : (at + places) * stride, :] for at in starts]
+        tiles = [block[at * stride : (at + places) * stride, :] for at in starts]
         for at, tile in zip(starts, reordered(order, tiles)):
             for head in range(heads):
                 for j, result in enumerate((keys, values)):
@@ -153,11 +154,12 @@
 
 def part_kernel(*refs):
     *blocks, keys, turned, token, values = refs
-    order = order_rows(2 * blocks[0].shape[1], False)
+    stride = keys.shape[1] * 2 // HD
+    order = order_rows(stride, False)
     offset = 0
     for block in blocks:
         take_apart(block, order, keys, values, offset)
-        offset += block.shape[0]
+        offset += block.shape[0] // stride
     turn_heads(values, turned)
     token[...] = jnp.zeros_like(token)
 
@@ -165,9 +167,8 @@
 TOKEN = jax.ShapeDtypeStruct((8, HD), jnp.float32)
 
 
-def part_keyval(blocks, name):
-    count = sum(block.shape[0] for block in blocks)
-    width = blocks[0].shape[1] * HD
+def part_keyval(blocks, width, name):
+    count = sum(block.shape[0] for block in blocks) * HD // (2 * width)
     return pl.pallas_call(
         part_kernel,
         in_specs=[VMEM] * len(blocks),
@@ -185,7 +186,8 @@
 
 
 def query_kernel(*refs):
-    *pieces, weight, cosine, sine, query, normed = refs
+    *pieces, weight, cosine, sine, query, normed, token = refs
+    token[...] = jnp.zeros_like(token)
     columns = pieces[0].shape[1]
     index = lax.axis_index("tp")
     features = columns * len(pieces)
@@ -214,10 +216,11 @@
     return pl.pallas_call(
         query_kernel,
         in_specs=[VMEM] * (len(pieces) + 3),
-        out_specs=[VMEM] * 2,
+        out_specs=[VMEM] * 3,
         out_shape=[
             jax.ShapeDtypeStruct((rows, width), jnp.bfloat16),
             jax.ShapeDtypeStruct((rows, depth), jnp.bfloat16),
+            TOKEN,
         ],
         compiler_params=params(20),
         cost_estimate=cost(2 * rows * depth * width, 2 * depth * width),
@@ -226,8 +229,9 @@
 
 
 def weight_kernel(weight, result, token, near, arrived):
-    slots, chunk, heads = near.shape[:3]
+    slots, chunk = near.shape[:2]
     count = weight.shape[0] // chunk
+    stride = result.shape[2] * 2 // HD
     copies = [
         pltpu.make_async_copy(
             weight.at[pl.ds(i * chunk, chunk)], near.at[i % slots], arrived.at[i]
@@ -236,31 +240,31 @@
     ]
     for copy in copies[:slots]:
         copy.start()
-    order = order_rows(2 * heads, False)
+    order = order_rows(stride, False)
     for i, copy in enumerate(copies):
         copy.wait()
-        take_apart(near.at[i % slots], order, result.at[0], result.at[1], i * chunk)
+        take_apart(near.at[i % slots], order, result.at[0], result.at[1], i * chunk // stride)
         if i + slots < count:
             copies[i + slots].start()
     token[...] = jnp.zeros_like(token)
 
 
 def part_weights(w_keyval):
+    depth, _, width = w_keyval.shape
     weight = viewed(w_keyval)
-    depth, heads = weight.shape[:2]
-    chunk = min(depth, 256)
-    count = depth // chunk
+    count = max(depth // 256, 1)
+    chunk = weight.shape[0] // count
     return pl.pallas_call(
         weight_kernel,
         in_specs=[HBM],
         out_specs=[VMEM] * 2,
-        out_shape=[jax.ShapeDtypeStruct((2, depth, heads * HD), jnp.bfloat16), TOKEN],
+        out_shape=[jax.ShapeDtypeStruct((2, depth, width), jnp.bfloat16), TOKEN],
         scratch_shapes=[
-            pltpu.VMEM((count, chunk, heads, 2, HD), jnp.bfloat16),
+            pltpu.VMEM((count, chunk, HD), jnp.bfloat16),
             pltpu.SemaphoreType.DMA((count,)),
         ],
         compiler_params=params(38),
-        cost_estimate=cost(2**12 * depth * heads * HD, 8 * depth * heads * HD),
+        cost_estimate=cost(2**10 * depth * width, 8 * depth * width),
         name="part_weights",
     )(weight)
 
@@ -281,7 +285,6 @@
     turn_heads(values, turned)
     order = order_rows(stride, True)
     places = 2 * HD // stride
-    flat = cache.reshape(rows * stride, HD)
     for start in range(0, rows, 2 * places):
         starts = [at for at in (start, start + places) if at < rows]
         tiles = [
@@ -296,7 +299,7 @@
             for at in starts
         ]
         for at, tile in zip(starts, reordered(order, tiles)):
-            flat[at * stride : (at + places) * stride, :] = tile
+            cache[at * stride : (at + places) * stride, :] = tile
 
 
 def project_keyval(normed, weight, cosine, sine):
@@ -310,14 +313,15 @@
         out_shape=[
             jax.ShapeDtypeStruct((rows, width), jnp.bfloat16),
             jax.ShapeDtypeStruct((width, rows), jnp.bfloat16),
-            jax.ShapeDtypeStruct((rows, heads, 2, HD), jnp.bfloat16),
+            jax.ShapeDtypeStruct((rows * heads * 2, HD), jnp.bfloat16),
         ],
         scratch_shapes=[pltpu.VMEM((rows, width), jnp.bfloat16)],
         compiler_params=params(20),
         cost_estimate=cost(4 * rows * depth * width, 4 * depth * width),
         name="project_keyval",
     )(normed, weight, cosine, sine)
-    return keys, turned, cache.transpose(0, 2, 1, 3).reshape(rows, 2, width)
+    cache = cache.reshape(rows, heads, 2, HD).transpose(0, 2, 1, 3)
+    return keys, turned, cache.reshape(rows, 2, width)
 
 
 def attend_kernel(spec, *refs):
@@ -328,20 +332,20 @@
     queries = take(len(shifts))
     if parted:
         blocks = take(2 * parted)
-        many_keys, many_turned = blocks[::2], blocks[1::2]
+        sources = list(zip(blocks[::2], blocks[1::2]))
     else:
         raw = take(len(rings))
     if not first:
         old_mixes, old_extents = take(len(shifts)), take(len(shifts))
     results = take(len(shifts))
     extents = [None if last and shift else take(1)[0] for shift in shifts]
-    token, bias = take(2)
+    token, bias, first_scores, second_scores = take(4)
     extents = [take(1)[0] if extent is None else extent for extent in extents]
     if parted:
         causal = take(1)[0]
     else:
         keys_here, turned_here, values_here = take(3)
-        many_keys, many_turned = [keys_here], [turned_here]
+        sources = [(keys_here, turned_here)]
     rows, width = queries[0].shape
     heads = width // HD
     cycle = cycle_of(group)
@@ -372,54 +376,90 @@
         theirs = member * rows + lax.broadcasted_iota(jnp.int32, (rows, rows), 0)
         for i, shift in enumerate(shifts):
             mine = (member ^ shift) * rows + lax.broadcasted_iota(jnp.int32, (rows, rows), 1)
-            causal[i] = jnp.where(theirs <= mine, 0.0, NEGATIVE)
+            causal[:, i * rows : (i + 1) * rows] = jnp.where(theirs <= mine, 0.0, NEGATIVE)
     else:
         offset = 0
         order = order_rows(2 * heads, False)
         for block in raw:
             take_apart(block, order, keys_here, values_here, offset)
-            offset += block.shape[0]
+            offset += block.shape[0] // (2 * heads)
         turn_heads(values_here, turned_here)
     token[...] = jnp.zeros_like(token)
-    unit = jnp.where(lax.broadcasted_iota(jnp.int32, (rows, HD), 1) == 0, 1.0, 0.0)
+    many = len(shifts) * rows
+    unit = jnp.where(lax.broadcasted_iota(jnp.int32, (many, HD), 1) == 0, 1.0, 0.0)
     unit = unit.astype(jnp.bfloat16)
-
-    def one_head(head):
+    chunks = []
+    begin = 0
+    for source in sources:
+        length = source[0].shape[0]
+        for start in range(0, length, 2 * HD):
+            size = min(2 * HD, length - start)
+            chunks.append((source, start, size, begin + start, parted and begin == count))
+        begin += length
+
+    def beside(values, axis):
+        return values[0] if len(values) == 1 else jnp.concatenate(values, axis=axis)
+
+    def start_head(head):
+        span = lanes(head * HD)
+        query = jnp.concatenate([beside([q[:, span] for q in queries], 0), unit], axis=1)
+        return span, query
+
+    def score(state, chunk, scores, top):
+        span, query = state
+        (keys, _), start, size, at, masked = chunk
+        keys = jnp.concatenate([keys[start : start + size, span], bias[at : at + size, :]], axis=1)
+        part = lax.dot_general(keys, query, ACROSS, preferred_element_type=jnp.float32)
+        if masked:
+            part = part + causal[start : start + size, :]
+        scores[at : at + size, :] = part
+        here = jnp.max(part, axis=0, keepdims=True)
+        return here if top is None else jnp.maximum(top, here)
+
+    def mix(span, chunk, scores, top, summed, mixed):
+        (_, turned), start, size, at, _ = chunk
+        weights = jnp.exp2((scores[at : at + size, :] - top) * SCALE)
+        here = jnp.sum(weights, axis=0, keepdims=True)
+        product = jnp.dot(
+            turned[span, start : start + size],
+            weights.astype(jnp.bfloat16),
+            preferred_element_type=jnp.float32,
+        )
+        return (here, product) if summed is None else (summed + here, mixed + product)
+
+    def one_head(head, scores, top, following, next_scores):
         span = lanes(head * HD)
         line = pl.ds(head, 1)
-        keys = jnp.concatenate([keys[:, span] for keys in many_keys], axis=0)
-        keys = jnp.concatenate([keys, bias[...]], axis=1)
-        values = jnp.concatenate([turned[span, :] for turned in many_turned], axis=1)
-        for i in range(len(shifts)):
-            query = jnp.concatenate([queries[i][:, span], unit], axis=1)
-            scores = lax.dot_general(keys, query, ACROSS, preferred_element_type=jnp.float32)
-            if parted:
-                scores = jnp.concatenate([scores[:count], scores[count:] + causal[i]], axis=0)
-            top = jnp.max(scores, axis=0, keepdims=True)
-            if not first:
-                old = old_extents[i][line, :]
-                top = jnp.maximum(top, old * (1.0 / SCALE))
-            weights = jnp.exp2((scores - top) * SCALE)
-            summed = jnp.sum(weights, axis=0, keepdims=True)
-            mixed = jnp.dot(
-                values, weights.astype(jnp.bfloat16), preferred_element_type=jnp.float32
-            )
-            if not first:
-                factor = jnp.exp2(old - top * SCALE)
-                summed = summed + factor
-                mixed = mixed + old_mixes[i][span, :] * factor
-            mixed = mixed * (1.0 / summed)
-            extents[i][line, :] = top * SCALE + jnp.log2(summed)
-            results[i][span, :] = mixed.astype(results[i].dtype)
-
-    together = min(4, heads)
-
-    def some_heads(i, _):
-        for j in range(together):
-            one_head(together * i + j)
-        return 0
-
-    lax.fori_loop(0, heads // together, some_heads, 0)
+        if not first:
+            old = beside([extent[line, :] for extent in old_extents], 1)
+            top = jnp.maximum(top, old * (1.0 / SCALE))
+        state = start_head(following)
+        next_top = summed = mixed = None
+        for chunk in chunks:
+            next_top = score(state, chunk, next_scores, next_top)
+            summed, mixed = mix(span, chunk, scores, top, summed, mixed)
+        if not first:
+            factor = jnp.exp2(old - top * SCALE)
+            summed = summed + factor
+            mixed = mixed + beside([old_mix[span, :] for old_mix in old_mixes], 1) * factor
+        mixed = mixed * (1.0 / summed)
+        extent = top * SCALE + jnp.log2(summed)
+        for i, result in enumerate(results):
+            columns = slice(i * rows, (i + 1) * rows)
+            extents[i][line, :] = extent[:, columns]
+            result[span, :] = mixed[:, columns].astype(result.dtype)
+        return next_top
+
+    def two_heads(i, top):
+        top = one_head(2 * i, first_scores, top, 2 * i + 1, second_scores)
+        following = jnp.minimum(2 * i + 2, heads - 1)
+        return one_head(2 * i + 1, second_scores, top, following, first_scores)
+
+    state = start_head(0)
+    top = None
+    for chunk in chunks:
+        top = score(state, chunk, first_scores, top)
+    lax.fori_loop(0, heads // 2, two_heads, top)
     for i, shift in enumerate(shifts):
         if last and shift:
             line = extents[i][:heads, :]
@@ -438,21 +478,23 @@
     return -(-3 * heads // 16) * 16
 
 
-def attend(facts, queries, shifts, rings, slots, piece, blocks, old, last, name):
+def attend(facts, queries, shifts, rings, slots, piece, blocks, parted, old, last, name):
     group = len(queries)
     queries = [queries[shift] for shift in shifts]
     rows, width = queries[0].shape
     heads = width // HD
-    parted = len(blocks) // 2 if blocks[0].ndim == 2 else 0
+    parted = len(blocks) // 2 if parted else 0
     operands = [*facts, *queries, *blocks]
     if old:
         operands += [old[shift][0] for shift in shifts] + [old[shift][1] for shift in shifts]
     count = sum(size for _, _, size in rings) + BLK * slots + (rows if parted else 0)
+    many = len(shifts) * rows
     scratch = [pltpu.VMEM((count, HD), jnp.bfloat16)]
+    scratch += [pltpu.VMEM((count, many), jnp.float32)] * 2
     lines = (max(heads, 8), rows)
     scratch += [pltpu.VMEM(lines, jnp.float32) for shift in shifts if last and shift]
     if parted:
-        scratch.append(pltpu.VMEM((len(shifts), rows, rows), jnp.float32))
+        scratch.append(pltpu.VMEM((rows, many), jnp.float32))
     else:
         scratch += [
             pltpu.VMEM((count, width), jnp.bfloat16),
@@ -566,6 +608,8 @@
     half = REQ // 2
     piece = prompt_cache.shape[0]
     middle = piece // 2
+    width = w_query.shape[1]
+    stride = 2 * width // HD
 
     pieces = [hidden_in] + [swap(hidden_in, "tp", shift) for shift in range(1, ways)]
     prompt = viewed(prompt_cache)
@@ -577,15 +621,15 @@
 
     step()
     cosine, sine = angles(tail_len, shared_len, rows)
-    weight, token = part_weights(w_keyval)
-    pieces[0] = after(pieces[0], token)
-    query, normed = project_query(pieces, w_query, cosine, sine)
+    weight, weight_token = part_weights(w_keyval)
+    pieces[0] = after(pieces[0], weight_token)
+    query, normed, query_token = project_query(pieces, w_query, cosine, sine)
     queries = [query] + [swap(query, "seq", shift) for shift in range(1, group)]
     tail = viewed(tail_cache.reshape(-1, 2, tail_cache.shape[3]))
     slots = tail_cache.shape[0]
-    *own_block, token = part_keyval([tail, prompt], "part_own")
-    step(token)
-    *near_block, token = part_keyval([ahead[1], behind[1]], "part_near")
+    *own_block, token = part_keyval([tail, prompt], width, "part_own")
+    step(token, weight_token, query_token)
+    *near_block, token = part_keyval([ahead[1], behind[1]], width, "part_near")
     fresh_keys, fresh_turned, new_cache = project_keyval(normed, weight, cosine, sine)
 
     table = tail_table.T
@@ -596,6 +640,7 @@
         slots,
         piece,
         [*own_block, *near_block, fresh_keys, fresh_turned],
+        True,
         None,
         False,
     )
@@ -605,15 +650,15 @@
     state_others, token = attend(ready, queries, others, *near, "attend_near_others")
     state |= state_others
     rings = [(-2, 0, piece), (2, 0, piece)]
-    second = (rings, 0, piece, [ahead[2], behind[2]], state, False, "attend_second")
+    second = (rings, 0, piece, [ahead[2], behind[2]], False, state, False, "attend_second")
     state, token = attend(facts, queries, [0, *others], *second)
-    far_low = turn(after(ahead[3], token)[:middle], cycle, group, 1)
-    far_high = turn(after(behind[3], token)[middle:], cycle, group, -1)
+    far_low = turn(after(ahead[3], token)[: middle * stride], cycle, group, 1)
+    far_high = turn(after(behind[3], token)[middle * stride :], cycle, group, -1)
     rings = [(-3, 0, piece), (3, 0, piece)]
-    third = (rings, 0, piece, [ahead[3], behind[3]], state, False, "attend_third")
+    third = (rings, 0, piece, [ahead[3], behind[3]], False, state, False, "attend_third")
     state, token = attend(facts, queries, [0, *others], *third)
     rings = [(-half, 0, middle), (half, middle, piece - middle)]
-    far = (rings, 0, piece, [far_low, far_high], state, True)
+    far = (rings, 0, piece, [far_low, far_high], False, state, True)
     *parts, token = attend(facts, queries, others, *far, "attend_far_others")
     ready = (after(tail_len, token), shared_len, table)
     result, extent, token = attend(ready, queries, [0], *far, "attend_far_own")

time: 75.8 us -> 70.3 us (0.927)
  Pallas kernels: 50.2 us -> 42.1 us
  waiting for transfers between devices: 10.5 us -> 12.8 us
    pallas_call x6, Pallas kernels: 29.5 us -> 24.7 us  [attend(): pl.pallas_call(functools.partial(attend_kernel, (group, shifts, rings, sl...]
    ppermute x8, waiting for transfers between devices: 1.04 us -> 4.7 us  [turn(): return lax.ppermute(value, 'seq', pairs)]
    pallas_call x1, Pallas kernels: 8.37 us -> 5.84 us  [part_weights(): pl.pallas_call(weight_kernel, in_specs=[HBM], out_specs=[VMEM] * 2, out_s...]
    ppermute x4, waiting for transfers between devices: 9.44 us -> 8.15 us  [swap(): return lax.ppermute(value, axis, pairs)]
    pallas_call x2, Pallas kernels: 3.45 us -> 2.66 us  [part_keyval(): pl.pallas_call(part_kernel, in_specs=[VMEM] * len(blocks), out_specs=[VME...]
  transfers between devices with their start and end apart: 12 -> 12, of which waited for: 4 -> 5; matrix products, arithmetic and copies ran while one was open for 1% -> 1% of each run, Pallas kernels for 60% -> 54%
where the time goes in v7:
time: 70.3 us; the launch traced here: 70.2 us
  Pallas kernels  42.1 us (60%)
  waiting for transfers between devices  12.8 us (18%)
  starting transfers between devices  12.2 us (17%)
  between operations  1.45 us (2%)
  other arithmetic  1.43 us (2%)
    pallas_call x6, Pallas kernels, attend(): pl.pallas_call(functools.partial(attend_kernel, (group, shifts, rings, sl...  24.7 us
    ppermute x8, starting transfers between devices, turn(): return lax.ppermute(value, 'seq', pairs)  9.36 us
    ppermute x4, waiting for transfers between devices, swap(): return lax.ppermute(value, axis, pairs)  8.15 us
    pallas_call x1, Pallas kernels, part_weights(): pl.pallas_call(weight_kernel, in_specs=[HBM], out_specs=[VMEM] * 2, out_s...  5.84 us
    ppermute x8, waiting for transfers between devices, turn(): return lax.ppermute(value, 'seq', pairs)  4.7 us
    pallas_call x1, Pallas kernels, project_keyval(): pl.pallas_call(keyval_kernel, in_specs=[VMEM] * 4, out_specs=[VMEM] * 3,...  4.01 us
    ppermute x4, starting transfers between devices, swap(): return lax.ppermute(value, axis, pairs)  2.86 us
    pallas_call x2, Pallas kernels, part_keyval(): pl.pallas_call(part_kernel, in_specs=[VMEM] * len(blocks), out_specs=[VME...  2.66 us
  transfers between devices with their start and end apart: 12, of which 5 were waited for; matrix products, arithmetic and copies ran while one was open for 1% of the time, Pallas kernels for 54%

profile of v7, /device:TPU:0, one launch (start us, length us, event | category | flops | bytes accessed | tf_op | source)
XLA Modules:
  0.0 70.2 jit_solution(7081976106110453959)
XLA Ops:
  0.7 3.1 %collective-permute-start.1 = (bf16[2048,128]{1,0:T(8,128)(2,1)}, bf16[2048,128]{1,0:T(8,128)(2,1)S(1)}, u32[]{:S(2)}, u32[]{:S(2)}) collective-permute-start(bf16[2048,128]{1,0:T(8,128)(2,1)} %bitcast.23), channel_id=1, source_target_pairs={{0,8},{2,10},{8,16},{10,18},{16,24},{18,26},{24,28},{26,30},{28,20... | collective-permute-start | bytes 1572872 | tf_op jit(solution)/shard_map/ppermute | solution.py:50
  3.8 0.0 collective-permute-start.3
  3.8 5.8 %part_weights.1 = (bf16[2,2048,1024]{2,1,0:T(8,128)(2,1)S(1)}, f32[8,128]{1,0:T(8,128)}) custom-call(bf16[32768,128]{1,0:T(8,128)(2,1)} %bitcast.33), custom_call_target="tpu_custom_call" | custom-call | flops 2147483648 | bytes 16777216 | tf_op jit(solution)/shard_map/part_weights/pallas_call | solution.py:257
  10.3 0.6 positions.1
  10.9 1.5 %part_own.1 = (bf16[384,1024]{1,0:T(8,128)(2,1)S(1)}, bf16[1024,384]{1,0:T(8,128)(2,1)S(1)}, f32[8,128]{1,0:T(8,128)}) custom-call(bf16[4096,128]{1,0:T(8,128)(2,1)S(1)} %bitcast.22, bf16[2048,128]{1,0:T(8,128)(2,1)S(1)} %bitcast.25), custom_call_target="tpu_custom_call" | custom-call | flops 402653184 | bytes 3145728 | tf_op jit(solution)/shard_map/part_own/pallas_call | solution.py:172
  12.3 0.5 sine_multiply_fusion
  12.9 2.6 %project_query.1 = (bf16[256,1024]{1,0:T(8,128)(2,1)S(1)}, bf16[256,2048]{1,0:T(8,128)(2,1)S(1)}, f32[8,128]{1,0:T(8,128)}) custom-call(bf16[256,1024]{1,0:T(8,128)(2,1)S(1)} %copy-done.2, bf16[256,1024]{1,0:T(8,128)(2,1)S(1)} %collective-permute-done.refs_1_, bf16[2048,1024]{1,0:T(8,128)(2,1)S(1)} %copy-done.1, ...), custom_call_target="tpu_custom_call" | custom-call | flops 1073741824 | bytes 4194304 | tf_op jit(solution)/shard_map/project_query/pallas_call | solution.py:216
  15.4 1.9 %collective-permute-done.3.refs_1_ = bf16[2048,128]{1,0:T(8,128)(2,1)S(1)} collective-permute-done((bf16[2048,128]{1,0:T(8,128)(2,1)}, bf16[2048,128]{1,0:T(8,128)(2,1)S(1)}, u32[]{:S(2)}, u32[]{:S(2)}) %collective-permute-start.3) | collective-permute-done | bytes 524320 | tf_op jit(solution)/shard_map/ppermute | solution.py:50
  17.4 0.3 collective-permute-start.6
  17.7 1.7 %collective-permute-start.2 = (bf16[2048,128]{1,0:T(8,128)(2,1)S(1)}, bf16[2048,128]{1,0:T(8,128)(2,1)S(1)}, u32[]{:S(2)}, u32[]{:S(2)}) collective-permute-start(bf16[2048,128]{1,0:T(8,128)(2,1)S(1)} %collective-permute-done.1.refs_0_), channel_id=1, source_target_pairs={{0,8},{2,10},{8,16},{10,18},{16,24},{18,26},{24,28},{26,30},{28,20... | collective-permute-start | bytes 1572872 | tf_op jit(solution)/shard_map/ppermute | solution.py:50
  19.4 1.5 %collective-permute-start.5 = (bf16[256,1024]{1,0:T(8,128)(2,1)S(1)}, bf16[256,1024]{1,0:T(8,128)(2,1)S(1)}, u32[]{:S(2)}, u32[]{:S(2)}) collective-permute-start(bf16[256,1024]{1,0:T(8,128)(2,1)S(1)} %get-tuple-element.44.refs_3_), channel_id=1, source_target_pairs={{0,2},{2,0},{4,6},{6,4},{8,10},{10,8},{12,14},{14,12},{16,18},{18,... | collective-permute-start | bytes 1572872 | tf_op jit(solution)/shard_map/ppermute | solution.py:41
  20.9 4.0 %project_keyval.1 = (bf16[256,1024]{1,0:T(8,128)(2,1)S(1)}, bf16[1024,256]{1,0:T(8,128)(2,1)S(1)}, bf16[4096,128]{1,0:T(8,128)(2,1)}) custom-call(bf16[256,2048]{1,0:T(8,128)(2,1)S(1)} %get-tuple-element.52.normed, bf16[2,2048,1024]{2,1,0:T(8,128)(2,1)S(1)} %get-tuple-element.53.weight, f32[256,128]{1,0:T(8,128)S(1)} %get-tuple-element.83.refs_3_.cosine, ...), custom_call_target="tpu_custom_call" | custom-call | flops 2147483648 | bytes 8388608 | tf_op jit(solution)/shard_map/project_keyval/pallas_call | solution.py:309
  24.9 1.2 %part_near.1 = (bf16[256,1024]{1,0:T(8,128)(2,1)S(1)}, bf16[1024,256]{1,0:T(8,128)(2,1)S(1)}, f32[8,128]{1,0:T(8,128)}) custom-call(bf16[2048,128]{1,0:T(8,128)(2,1)S(1)} %collective-permute-done.1.refs_0_, bf16[2048,128]{1,0:T(8,128)(2,1)S(1)} %collective-permute-done.3.refs_1_), custom_call_target="tpu_custom_call" | custom-call | flops 268435456 | bytes 2097152 | tf_op jit(solution)/shard_map/part_near/pallas_call | solution.py:172
  26.1 4.8 %attend_near_own.1 = (f32[1024,256]{1,0:T(8,128)S(1)}, f32[8,256]{1,0:T(8,128)S(1)}, f32[8,128]{1,0:T(8,128)}) custom-call(s32[8]{0:T(128)S(1)} %copy-done.6, s32[1]{0:T(128)S(6)} %copy.15.shared.refs_1_, s32[4,8]{1,0:T(4,128)S(1)} %bitcast.26, bf16[256,1024]{1,0:T(8,128)(2,1)S(1)} %get-tuple-element.44.refs_3_, ...), custom_call_target="tpu_custom_call" | custom-call | flops 939524096 | bytes 3670016 | tf_op jit(solution)/shard_map/attend_near_own/pallas_call | solution.py:514
  30.9 0.9 %collective-permute-start.8 = (bf16[2048,128]{1,0:T(8,128)(2,1)S(1)}, bf16[2048,128]{1,0:T(8,128)(2,1)S(1)}, u32[]{:S(2)}, u32[]{:S(2)}) collective-permute-start(bf16[2048,128]{1,0:T(8,128)(2,1)S(1)} %collective-permute-done.6.refs_6_), channel_id=1, source_target_pairs={{0,4},{2,6},{8,0},{10,2},{16,8},{18,10},{24,16},{26,18},{28,24},{3... | collective-permute-start | bytes 1572872 | tf_op jit(solution)/shard_map/ppermute | solution.py:50
  31.7 1.1 %collective-permute-start.4 = (bf16[2048,128]{1,0:T(8,128)(2,1)S(1)}, bf16[2048,128]{1,0:T(8,128)(2,1)S(1)}, u32[]{:S(2)}, u32[]{:S(2)}) collective-permute-start(bf16[2048,128]{1,0:T(8,128)(2,1)S(1)} %collective-permute-done.2.refs_5_), channel_id=1, source_target_pairs={{0,8},{2,10},{8,16},{10,18},{16,24},{18,26},{24,28},{26,30},{28,20... | collective-permute-start | bytes 1572872 | tf_op jit(solution)/shard_map/ppermute | solution.py:50
  32.9 4.8 %attend_near_others.1 = (f32[1024,256]{1,0:T(8,128)S(1)}, f32[8,256]{1,0:T(8,128)S(1)}, f32[8,128]{1,0:T(8,128)}) custom-call(s32[8]{0:T(128)S(1)} %copy-done.6, s32[1]{0:T(128)S(6)} %copy.15.shared.refs_1_, s32[4,8]{1,0:T(4,128)S(1)} %bitcast.27, bf16[256,1024]{1,0:T(8,128)(2,1)S(1)} %collective-permute-done.5.refs_3_.refs_4_, ...), custom_call_target="tpu_custom_call" | custom-call | flops 939524096 | bytes 3670016 | tf_op jit(solution)/shard_map/attend_near_others/pallas_call | solution.py:514
  37.7 4.4 %attend_second.1 = (f32[1024,256]{1,0:T(8,128)S(1)}, f32[1024,256]{1,0:T(8,128)S(1)}, f32[8,256]{1,0:T(8,128)S(1)}, f32[8,256]{1,0:T(8,128)S(1)}, f32[8,128]{1,0:T(8,128)}) custom-call(s32[8]{0:T(128)S(1)} %copy-done.6, s32[1]{0:T(128)S(6)} %copy.15.shared.refs_1_, s32[4,8]{1,0:T(4,128)S(1)} %bitcast.28, bf16[256,1024]{1,0:T(8,128)(2,1)S(1)} %get-tuple-element.44.refs_3_, ...), custom_call_target="tpu_custom_call" | custom-call | flops 536870912 | bytes 1048576 | tf_op jit(solution)/shard_map/attend_second/pallas_call | solution.py:514
  42.1 0.8 %collective-permute-done.8.refs_6_ = bf16[2048,128]{1,0:T(8,128)(2,1)S(1)} collective-permute-done((bf16[2048,128]{1,0:T(8,128)(2,1)S(1)}, bf16[2048,128]{1,0:T(8,128)(2,1)S(1)}, u32[]{:S(2)}, u32[]{:S(2)}) %collective-permute-start.8) | collective-permute-done | bytes 524320 | tf_op jit(solution)/shard_map/ppermute | solution.py:50
  42.9 2.2 %collective-permute-start.9 = (bf16[1024,128]{1,0:T(8,128)(2,1)S(1)}, bf16[1024,128]{1,0:T(8,128)(2,1)S(1)}, u32[]{:S(2)}, u32[]{:S(2)}) collective-permute-start(bf16[1024,128]{1,0:T(8,128)(2,1)S(1)} %slice.7), channel_id=1, source_target_pairs={{0,4},{2,6},{8,0},{10,2},{16,8},{18,10},{24,16},{26,18},{28,24},{3... | collective-permute-start | bytes 786440 | tf_op jit(solution)/shard_map/ppermute | solution.py:50
  45.1 0.1 collective-permute-start.7
  45.1 4.4 %attend_third.1 = (f32[1024,256]{1,0:T(8,128)S(1)}, f32[1024,256]{1,0:T(8,128)S(1)}, f32[8,256]{1,0:T(8,128)S(1)}, f32[8,256]{1,0:T(8,128)S(1)}, f32[8,128]{1,0:T(8,128)}) custom-call(s32[8]{0:T(128)S(1)} %copy-done.6, s32[1]{0:T(128)S(6)} %copy.15.shared.refs_1_, s32[4,8]{1,0:T(4,128)S(1)} %bitcast.29, bf16[256,1024]{1,0:T(8,128)(2,1)S(1)} %get-tuple-element.44.refs_3_, ...), custom_call_target="tpu_custom_call" | custom-call | flops 536870912 | bytes 1048576 | tf_op jit(solution)/shard_map/attend_third/pallas_call | solution.py:514
  49.6 2.0 %collective-permute-done.7.refs_4_ = bf16[1024,128]{1,0:T(8,128)(2,1)S(1)} collective-permute-done((bf16[1024,128]{1,0:T(8,128)(2,1)S(1)}, bf16[1024,128]{1,0:T(8,128)(2,1)S(1)}, u32[]{:S(2)}, u32[]{:S(2)}) %collective-permute-start.7) | collective-permute-done | bytes 262176 | tf_op jit(solution)/shard_map/ppermute | solution.py:50
  51.6 3.1 %attend_far_others.1 = (bf16[1056,256]{1,0:T(8,128)(2,1)S(1)}, f32[8,128]{1,0:T(8,128)}) custom-call(s32[8]{0:T(128)S(1)} %copy-done.6, s32[1]{0:T(128)S(6)} %copy.15.shared.refs_1_, s32[4,8]{1,0:T(4,128)S(1)} %bitcast.30, bf16[256,1024]{1,0:T(8,128)(2,1)S(1)} %collective-permute-done.5.refs_3_.refs_4_, ...), custom_call_target="tpu_custom_call" | custom-call | flops 134217728 | bytes 524288 | tf_op jit(solution)/shard_map/attend_far_others/pallas_call | solution.py:514
  54.7 1.3 %collective-permute-start.10 = (bf16[1056,256]{1,0:T(8,128)(2,1)S(1)}, bf16[1056,256]{1,0:T(8,128)(2,1)S(1)}, u32[]{:S(2)}, u32[]{:S(2)}) collective-permute-start(bf16[1056,256]{1,0:T(8,128)(2,1)S(1)} %get-tuple-element.78), channel_id=1, source_target_pairs={{0,2},{2,0},{4,6},{6,4},{8,10},{10,8},{12,14},{14,12},{16,18},{18,... | collective-permute-start | bytes 1622024 | tf_op jit(solution)/shard_map/ppermute | solution.py:41
  56.0 3.2 %attend_far_own.1 = (f32[1024,256]{1,0:T(8,128)S(1)}, f32[8,256]{1,0:T(8,128)S(1)}, f32[8,128]{1,0:T(8,128)}) custom-call(s32[8]{0:T(128)S(1)} %copy-done.6, s32[1]{0:T(128)S(6)} %copy.15.shared.refs_1_, s32[4,8]{1,0:T(4,128)S(1)} %bitcast.31, bf16[256,1024]{1,0:T(8,128)(2,1)S(1)} %get-tuple-element.44.refs_3_, ...), custom_call_target="tpu_custom_call" | custom-call | flops 134217728 | bytes 524288 | tf_op jit(solution)/shard_map/attend_far_own/pallas_call | solution.py:514
  59.2 7.0 %collective-permute-done.10.refs_2_ = bf16[1056,256]{1,0:T(8,128)(2,1)S(1)} collective-permute-done((bf16[1056,256]{1,0:T(8,128)(2,1)S(1)}, bf16[1056,256]{1,0:T(8,128)(2,1)S(1)}, u32[]{:S(2)}, u32[]{:S(2)}) %collective-permute-start.10) | collective-permute-done | bytes 540704 | tf_op jit(solution)/shard_map/ppermute | solution.py:41
  66.2 1.0 %combine_send.1 = (bf16[256,1024]{1,0:T(8,128)(2,1)S(1)}, bf16[1,256,1024]{2,1,0:T(8,128)(2,1)S(1)}) custom-call(f32[1024,256]{1,0:T(8,128)S(1)} %get-tuple-element.74.refs_0_, f32[8,256]{1,0:T(8,128)S(1)} %get-tuple-element.75.refs_1_, bf16[1056,256]{1,0:T(8,128)(2,1)S(1)} %collective-permute-done.10.refs_2_, bf16[1024,2048]{1,0:T(8,128)(2,1)S(1)} %copy-done), custom_call_target="tpu_custom_call" | custom-call | flops 536870912 | bytes 4194304 | tf_op jit(solution)/shard_map/combine_send/pallas_call | solution.py:564
  67.2 0.1 collective-permute-start.11
  67.3 0.7 %keep_own.1 = f32[256,1024]{1,0:T(8,128)S(1)} custom-call(bf16[256,1024]{1,0:T(8,128)(2,1)S(1)} %get-tuple-element.79.attended, bf16[1024,2048]{1,0:T(8,128)(2,1)S(1)} %copy-done, bf16[256,1024]{1,0:T(8,128)(2,1)S(1)} %copy-done.2), custom_call_target="tpu_custom_call" | custom-call | flops 536870912 | bytes 4194304 | tf_op jit(solution)/shard_map/keep_own/pallas_call | solution.py:590
  68.0 1.2 %collective-permute-done.11 = bf16[256,1024]{1,0:T(8,128)(2,1)S(1)} collective-permute-done((bf16[256,1024]{1,0:T(8,128)(2,1)S(1)}, bf16[256,1024]{1,0:T(8,128)(2,1)S(1)}, u32[]{:S(2)}, u32[]{:S(2)}) %collective-permute-start.11) | collective-permute-done | bytes 524320 | tf_op jit(solution)/shard_map/ppermute | solution.py:41
  69.2 1.0 %add_convert_fusion = bf16[256,1024]{1,0:T(8,128)(2,1)} fusion(f32[256,1024]{1,0:T(8,128)S(1)} %keep_own.1, bf16[256,1024]{1,0:T(8,128)(2,1)S(1)} %collective-permute-done.11), kind=kLoop, calls=%fused_computation | loop fusion | flops 786432 | bytes 2097152 | tf_op jit(solution)/shard_map/convert_element_type | solution.py:671
  (25 shorter events, 0.1 us)
Async XLA Ops:
  0.6 10.2 %copy-start.4 = (bf16[128,2,1024]{2,1,0:T(2,128)(2,1)S(1)}, bf16[128,2,1024]{2,1,0:T(2,128)(2,1)}, u32[]{:S(2)}) copy-start(bf16[128,2,1024]{2,1,0:T(2,128)(2,1)} %param.13) | copy-start | bytes 1572868
  0.6 12.2 %copy-start.2 = (bf16[256,1024]{1,0:T(8,128)(2,1)S(1)}, bf16[256,1024]{1,0:T(8,128)(2,1)}, u32[]{:S(2)}) copy-start(bf16[256,1024]{1,0:T(8,128)(2,1)} %hidden.1) | copy-start | bytes 1572868
  0.7 9.6 %copy-start.6 = (s32[8]{0:T(128)S(1)}, s32[8]{0:T(128)}, u32[]{:S(2)}) copy-start(s32[8]{0:T(128)} %refs_0_.10) | copy-start | bytes 100
  0.7 10.2 %copy-start.3 = (bf16[2,128,2,1024]{3,2,1,0:T(2,128)(2,1)S(1)}, bf16[2,128,2,1024]{3,2,1,0:T(2,128)(2,1)}, u32[]{:S(2)}) copy-start(bf16[2,128,2,1024]{3,2,1,0:T(2,128)(2,1)} %param.14) | copy-start | bytes 3145732
  0.7 12.2 %copy-start.1 = (bf16[2048,1024]{1,0:T(8,128)(2,1)S(1)}, bf16[2048,1024]{1,0:T(8,128)(2,1)}, u32[]{:S(2)}) copy-start(bf16[2048,1024]{1,0:T(8,128)(2,1)} %refs_2_.1) | copy-start | bytes 12582916
  0.7 17.0 %collective-permute-start.1 = (bf16[2048,128]{1,0:T(8,128)(2,1)}, bf16[2048,128]{1,0:T(8,128)(2,1)S(1)}, u32[]{:S(2)}, u32[]{:S(2)}) collective-permute-start(bf16[2048,128]{1,0:T(8,128)(2,1)} %bitcast.23), channel_id=1, source_target_pairs={{0,8},{2,10},{8,16},{10,18},{16,24},{18,26},{24,28},{26,30},{28,20... | collective-permute-start | bytes 1572872 | tf_op jit(solution)/shard_map/ppermute | solution.py:50
  3.8 13.6 %collective-permute-start.3 = (bf16[2048,128]{1,0:T(8,128)(2,1)}, bf16[2048,128]{1,0:T(8,128)(2,1)S(1)}, u32[]{:S(2)}, u32[]{:S(2)}) collective-permute-start(bf16[2048,128]{1,0:T(8,128)(2,1)} %bitcast.24), channel_id=1, source_target_pairs={{0,4},{2,6},{8,0},{10,2},{16,8},{18,10},{24,16},{26,18},{28,24},{3... | collective-permute-start | bytes 1572872 | tf_op jit(solution)/shard_map/ppermute | solution.py:50
  3.8 9.1 %collective-permute-start = (bf16[256,1024]{1,0:T(8,128)(2,1)}, bf16[256,1024]{1,0:T(8,128)(2,1)S(1)}, u32[]{:S(2)}, u32[]{:S(2)}) collective-permute-start(bf16[256,1024]{1,0:T(8,128)(2,1)} %hidden.1), channel_id=1, source_target_pairs={{0,1},{1,0},{2,3},{3,2},{4,5},{5,4},{6,7},{7,6},{8,9},{9,8},{10,11... | collective-permute-start | bytes 1572872 | tf_op jit(solution)/shard_map/ppermute | solution.py:41
  12.3 13.8 %copy-start.5 = (s32[8,4]{0,1:T(4,128)S(1)}, s32[8,4]{0,1:T(4,128)}, u32[]{:S(2)}) copy-start(s32[8,4]{0,1:T(4,128)} %param.15) | copy-start | bytes 388
  17.4 13.5 %collective-permute-start.6 = (bf16[2048,128]{1,0:T(8,128)(2,1)S(1)}, bf16[2048,128]{1,0:T(8,128)(2,1)S(1)}, u32[]{:S(2)}, u32[]{:S(2)}) collective-permute-start(bf16[2048,128]{1,0:T(8,128)(2,1)S(1)} %collective-permute-done.3.refs_1_), channel_id=1, source_target_pairs={{0,4},{2,6},{8,0},{10,2},{16,8},{18,10},{24,16},{26,18},{28,24},{3... | collective-permute-start | bytes 1572872 | tf_op jit(solution)/shard_map/ppermute | solution.py:50
  17.7 14.1 %collective-permute-start.2 = (bf16[2048,128]{1,0:T(8,128)(2,1)S(1)}, bf16[2048,128]{1,0:T(8,128)(2,1)S(1)}, u32[]{:S(2)}, u32[]{:S(2)}) collective-permute-start(bf16[2048,128]{1,0:T(8,128)(2,1)S(1)} %collective-permute-done.1.refs_0_), channel_id=1, source_target_pairs={{0,8},{2,10},{8,16},{10,18},{16,24},{18,26},{24,28},{26,30},{28,20... | collective-permute-start | bytes 1572872 | tf_op jit(solution)/shard_map/ppermute | solution.py:50
  19.4 13.5 %collective-permute-start.5 = (bf16[256,1024]{1,0:T(8,128)(2,1)S(1)}, bf16[256,1024]{1,0:T(8,128)(2,1)S(1)}, u32[]{:S(2)}, u32[]{:S(2)}) collective-permute-start(bf16[256,1024]{1,0:T(8,128)(2,1)S(1)} %get-tuple-element.44.refs_3_), channel_id=1, source_target_pairs={{0,2},{2,0},{4,6},{6,4},{8,10},{10,8},{12,14},{14,12},{16,18},{18,... | collective-permute-start | bytes 1572872 | tf_op jit(solution)/shard_map/ppermute | solution.py:41
  30.9 35.3 %copy-start = (bf16[1024,2048]{1,0:T(8,128)(2,1)S(1)}, bf16[1024,2048]{1,0:T(8,128)(2,1)}, u32[]{:S(2)}) copy-start(bf16[1024,2048]{1,0:T(8,128)(2,1)} %weight.1) | copy-start | bytes 12582916
  30.9 12.0 %collective-permute-start.8 = (bf16[2048,128]{1,0:T(8,128)(2,1)S(1)}, bf16[2048,128]{1,0:T(8,128)(2,1)S(1)}, u32[]{:S(2)}, u32[]{:S(2)}) collective-permute-start(bf16[2048,128]{1,0:T(8,128)(2,1)S(1)} %collective-permute-done.6.refs_6_), channel_id=1, source_target_pairs={{0,4},{2,6},{8,0},{10,2},{16,8},{18,10},{24,16},{26,18},{28,24},{3... | collective-permute-start | bytes 1572872 | tf_op jit(solution)/shard_map/ppermute | solution.py:50
  31.7 13.3 %collective-permute-start.4 = (bf16[2048,128]{1,0:T(8,128)(2,1)S(1)}, bf16[2048,128]{1,0:T(8,128)(2,1)S(1)}, u32[]{:S(2)}, u32[]{:S(2)}) collective-permute-start(bf16[2048,128]{1,0:T(8,128)(2,1)S(1)} %collective-permute-done.2.refs_5_), channel_id=1, source_target_pairs={{0,8},{2,10},{8,16},{10,18},{16,24},{18,26},{24,28},{26,30},{28,20... | collective-permute-start | bytes 1572872 | tf_op jit(solution)/shard_map/ppermute | solution.py:50
  42.9 6.7 %collective-permute-start.9 = (bf16[1024,128]{1,0:T(8,128)(2,1)S(1)}, bf16[1024,128]{1,0:T(8,128)(2,1)S(1)}, u32[]{:S(2)}, u32[]{:S(2)}) collective-permute-start(bf16[1024,128]{1,0:T(8,128)(2,1)S(1)} %slice.7), channel_id=1, source_target_pairs={{0,4},{2,6},{8,0},{10,2},{16,8},{18,10},{24,16},{26,18},{28,24},{3... | collective-permute-start | bytes 786440 | tf_op jit(solution)/shard_map/ppermute | solution.py:50
  45.1 6.5 %collective-permute-start.7 = (bf16[1024,128]{1,0:T(8,128)(2,1)S(1)}, bf16[1024,128]{1,0:T(8,128)(2,1)S(1)}, u32[]{:S(2)}, u32[]{:S(2)}) collective-permute-start(bf16[1024,128]{1,0:T(8,128)(2,1)S(1)} %slice.6), channel_id=1, source_target_pairs={{0,8},{2,10},{8,16},{10,18},{16,24},{18,26},{24,28},{26,30},{28,20... | collective-permute-start | bytes 786440 | tf_op jit(solution)/shard_map/ppermute | solution.py:50
  54.7 11.5 %collective-permute-start.10 = (bf16[1056,256]{1,0:T(8,128)(2,1)S(1)}, bf16[1056,256]{1,0:T(8,128)(2,1)S(1)}, u32[]{:S(2)}, u32[]{:S(2)}) collective-permute-start(bf16[1056,256]{1,0:T(8,128)(2,1)S(1)} %get-tuple-element.78), channel_id=1, source_target_pairs={{0,2},{2,0},{4,6},{6,4},{8,10},{10,8},{12,14},{14,12},{16,18},{18,... | collective-permute-start | bytes 1622024 | tf_op jit(solution)/shard_map/ppermute | solution.py:41
  67.2 2.0 %collective-permute-start.11 = (bf16[256,1024]{1,0:T(8,128)(2,1)S(1)}, bf16[256,1024]{1,0:T(8,128)(2,1)S(1)}, u32[]{:S(2)}, u32[]{:S(2)}) collective-permute-start(bf16[256,1024]{1,0:T(8,128)(2,1)S(1)} %bitcast.32), channel_id=1, source_target_pairs={{0,1},{1,0},{2,3},{3,2},{4,5},{5,4},{6,7},{7,6},{8,9},{9,8},{10,11... | collective-permute-start | bytes 1572872 | tf_op jit(solution)/shard_map/ppermute | solution.py:41

commit v8 on v7

--- a/solution.py
+++ b/solution.py
@@ -81,6 +81,8 @@
 
 
 def lanes(start, count=HD):
+    if isinstance(start, int):
+        return pl.ds(start, count)
     return pl.ds(pl.multiple_of(start, HD), count)
 
 
@@ -153,7 +155,7 @@
 
 
 def part_kernel(*refs):
-    *blocks, keys, turned, token, values = refs
+    *blocks, keys, turned, values = refs
     stride = keys.shape[1] * 2 // HD
     order = order_rows(stride, False)
     offset = 0
@@ -161,10 +163,6 @@
         take_apart(block, order, keys, values, offset)
         offset += block.shape[0] // stride
     turn_heads(values, turned)
-    token[...] = jnp.zeros_like(token)
-
-
-TOKEN = jax.ShapeDtypeStruct((8, HD), jnp.float32)
 
 
 def part_keyval(blocks, width, name):
@@ -172,11 +170,10 @@
     return pl.pallas_call(
         part_kernel,
         in_specs=[VMEM] * len(blocks),
-        out_specs=[VMEM] * 3,
+        out_specs=[VMEM] * 2,
         out_shape=[
             jax.ShapeDtypeStruct((count, width), jnp.bfloat16),
             jax.ShapeDtypeStruct((width, count), jnp.bfloat16),
-            TOKEN,
         ],
         scratch_shapes=[pltpu.VMEM((count, width), jnp.bfloat16)],
         compiler_params=params(16),
@@ -186,8 +183,7 @@
 
 
 def query_kernel(*refs):
-    *pieces, weight, cosine, sine, query, normed, token = refs
-    token[...] = jnp.zeros_like(token)
+    *pieces, weight, cosine, sine, query, normed = refs
     columns = pieces[0].shape[1]
     index = lax.axis_index("tp")
     features = columns * len(pieces)
@@ -216,11 +212,10 @@
     return pl.pallas_call(
         query_kernel,
         in_specs=[VMEM] * (len(pieces) + 3),
-        out_specs=[VMEM] * 3,
+        out_specs=[VMEM] * 2,
         out_shape=[
             jax.ShapeDtypeStruct((rows, width), jnp.bfloat16),
             jax.ShapeDtypeStruct((rows, depth), jnp.bfloat16),
-            TOKEN,
         ],
         compiler_params=params(20),
         cost_estimate=cost(2 * rows * depth * width, 2 * depth * width),
@@ -228,7 +223,7 @@
     )(*pieces, w_query, cosine, sine)
 
 
-def weight_kernel(weight, result, token, near, arrived):
+def weight_kernel(weight, result, near, arrived):
     slots, chunk = near.shape[:2]
     count = weight.shape[0] // chunk
     stride = result.shape[2] * 2 // HD
@@ -246,7 +241,6 @@
         take_apart(near.at[i % slots], order, result.at[0], result.at[1], i * chunk // stride)
         if i + slots < count:
             copies[i + slots].start()
-    token[...] = jnp.zeros_like(token)
 
 
 def part_weights(w_keyval):
@@ -257,8 +251,8 @@
     return pl.pallas_call(
         weight_kernel,
         in_specs=[HBM],
-        out_specs=[VMEM] * 2,
-        out_shape=[jax.ShapeDtypeStruct((2, depth, width), jnp.bfloat16), TOKEN],
+        out_specs=VMEM,
+        out_shape=jax.ShapeDtypeStruct((2, depth, width), jnp.bfloat16),
         scratch_shapes=[
             pltpu.VMEM((count, chunk, HD), jnp.bfloat16),
             pltpu.SemaphoreType.DMA((count,)),
@@ -326,6 +320,7 @@
 
 def attend_kernel(spec, *refs):
     group, shifts, rings, slots, piece, parted, first, last = spec
+    fresh = slots > 0
     refs = list(refs)
     take = lambda count: [refs.pop(0) for _ in range(count)]
     lengths, shared, table = take(3)
@@ -339,13 +334,15 @@
         old_mixes, old_extents = take(len(shifts)), take(len(shifts))
     results = take(len(shifts))
     extents = [None if last and shift else take(1)[0] for shift in shifts]
-    token, bias, first_scores, second_scores = take(4)
+    if not parted:
+        sources = [tuple(take(2))]
+    bias, first_scores, second_scores = take(3)
     extents = [take(1)[0] if extent is None else extent for extent in extents]
-    if parted:
+    if fresh:
         causal = take(1)[0]
-    else:
-        keys_here, turned_here, values_here = take(3)
-        sources = [(keys_here, turned_here)]
+    if not parted:
+        values_here = take(1)[0]
+        keys_here, turned_here = sources[0]
     rows, width = queries[0].shape
     heads = width // HD
     cycle = cycle_of(group)
@@ -371,20 +368,19 @@
         bias[begin : begin + size, :] = jnp.where(
             (positions >= length) & (lane == 0), NEGATIVE, 0.0
         ).astype(jnp.bfloat16)
-    if parted:
+    if fresh:
         bias[count : count + rows, :] = jnp.zeros((rows, HD), jnp.bfloat16)
         theirs = member * rows + lax.broadcasted_iota(jnp.int32, (rows, rows), 0)
         for i, shift in enumerate(shifts):
             mine = (member ^ shift) * rows + lax.broadcasted_iota(jnp.int32, (rows, rows), 1)
             causal[:, i * rows : (i + 1) * rows] = jnp.where(theirs <= mine, 0.0, NEGATIVE)
-    else:
+    if not parted:
         offset = 0
         order = order_rows(2 * heads, False)
         for block in raw:
             take_apart(block, order, keys_here, values_here, offset)
             offset += block.shape[0] // (2 * heads)
         turn_heads(values_here, turned_here)
-    token[...] = jnp.zeros_like(token)
     many = len(shifts) * rows
     unit = jnp.where(lax.broadcasted_iota(jnp.int32, (many, HD), 1) == 0, 1.0, 0.0)
     unit = unit.astype(jnp.bfloat16)
@@ -394,21 +390,19 @@
         length = source[0].shape[0]
         for start in range(0, length, 2 * HD):
             size = min(2 * HD, length - start)
-            chunks.append((source, start, size, begin + start, parted and begin == count))
+            chunks.append((source, start, size, begin + start, fresh and begin == count))
         begin += length
 
     def beside(values, axis):
         return values[0] if len(values) == 1 else jnp.concatenate(values, axis=axis)
 
-    def start_head(head):
-        span = lanes(head * HD)
-        query = jnp.concatenate([beside([q[:, span] for q in queries], 0), unit], axis=1)
-        return span, query
-
-    def score(state, chunk, scores, top):
-        span, query = state
+    def query_of(head):
+        return jnp.concatenate([beside([q[:, lanes(head * HD)] for q in queries], 0), unit], axis=1)
+
+    def score(head, query, chunk, scores, top):
         (keys, _), start, size, at, masked = chunk
-        keys = jnp.concatenate([keys[start : start + size, span], bias[at : at + size, :]], axis=1)
+        keys = keys[start : start + size, lanes(head * HD)]
+        keys = jnp.concatenate([keys, bias[at : at + size, :]], axis=1)
         part = lax.dot_general(keys, query, ACROSS, preferred_element_type=jnp.float32)
         if masked:
             part = part + causal[start : start + size, :]
@@ -416,50 +410,69 @@
         here = jnp.max(part, axis=0, keepdims=True)
         return here if top is None else jnp.maximum(top, here)
 
-    def mix(span, chunk, scores, top, summed, mixed):
+    def mix(head, chunk, scores, top, sums):
         (_, turned), start, size, at, _ = chunk
         weights = jnp.exp2((scores[at : at + size, :] - top) * SCALE)
         here = jnp.sum(weights, axis=0, keepdims=True)
         product = jnp.dot(
-            turned[span, start : start + size],
+            turned[lanes(head * HD), start : start + size],
             weights.astype(jnp.bfloat16),
             preferred_element_type=jnp.float32,
         )
-        return (here, product) if summed is None else (summed + here, mixed + product)
-
-    def one_head(head, scores, top, following, next_scores):
-        span = lanes(head * HD)
-        line = pl.ds(head, 1)
+        return (here, product) if sums is None else (sums[0] + here, sums[1] + product)
+
+    together = min(heads // 2, 4 if count <= 256 else 1)
+
+    def some_heads(base, scores, tops, following, next_scores):
+        span = lambda k: lanes((base + k) * HD)
+        line = lambda k: pl.ds(base + k, 1)
+        each = range(together)
         if not first:
-            old = beside([extent[line, :] for extent in old_extents], 1)
-            top = jnp.maximum(top, old * (1.0 / SCALE))
-        state = start_head(following)
-        next_top = summed = mixed = None
+            olds = [beside([extent[line(k), :] for extent in old_extents], 1) for k in each]
+            tops = [jnp.maximum(top, old * (1.0 / SCALE)) for top, old in zip(tops, olds)]
+        next_tops = [None] * together
+        sums = [None] * together
+        if following is not None:
+            next_queries = [query_of(following + k) for k in each]
         for chunk in chunks:
-            next_top = score(state, chunk, next_scores, next_top)
-            summed, mixed = mix(span, chunk, scores, top, summed, mixed)
-        if not first:
-            factor = jnp.exp2(old - top * SCALE)
-            summed = summed + factor
-            mixed = mixed + beside([old_mix[span, :] for old_mix in old_mixes], 1) * factor
-        mixed = mixed * (1.0 / summed)
-        extent = top * SCALE + jnp.log2(summed)
-        for i, result in enumerate(results):
-            columns = slice(i * rows, (i + 1) * rows)
-            extents[i][line, :] = extent[:, columns]
-            result[span, :] = mixed[:, columns].astype(result.dtype)
-        return next_top
-
-    def two_heads(i, top):
-        top = one_head(2 * i, first_scores, top, 2 * i + 1, second_scores)
-        following = jnp.minimum(2 * i + 2, heads - 1)
-        return one_head(2 * i + 1, second_scores, top, following, first_scores)
-
-    state = start_head(0)
-    top = None
-    for chunk in chunks:
-        top = score(state, chunk, first_scores, top)
-    lax.fori_loop(0, heads // 2, two_heads, top)
+            for k in each:
+                if following is not None:
+                    next_tops[k] = score(
+                        following + k, next_queries[k], chunk, next_scores.at[k], next_tops[k]
+                    )
+                sums[k] = mix(base + k, chunk, scores.at[k], tops[k], sums[k])
+        for k in each:
+            summed, mixed = sums[k]
+            if not first:
+                factor = jnp.exp2(olds[k] - tops[k] * SCALE)
+                summed = summed + factor
+                old_mix = beside([old_mix[span(k), :] for old_mix in old_mixes], 1)
+                mixed = mixed + old_mix * factor
+            mixed = mixed * (1.0 / summed)
+            extent = tops[k] * SCALE + jnp.log2(summed)
+            for i, result in enumerate(results):
+                columns = slice(i * rows, (i + 1) * rows)
+                extents[i][line(k), :] = extent[:, columns]
+                result[span(k), :] = mixed[:, columns].astype(result.dtype)
+        return next_tops
+
+    def two_parts(i, tops):
+        base = 2 * together * i
+        tops = some_heads(base, first_scores, tops, base + together, second_scores)
+        following = jnp.minimum(base + 2 * together, heads - together)
+        return some_heads(base + together, second_scores, tops, following, first_scores)
+
+    tops = []
+    for k in range(together):
+        query, top = query_of(k), None
+        for chunk in chunks:
+            top = score(k, query, chunk, first_scores.at[k], top)
+        tops.append(top)
+    if heads == 2 * together:
+        tops = some_heads(0, first_scores, tops, together, second_scores)
+        some_heads(together, second_scores, tops, None, None)
+    else:
+        lax.fori_loop(0, heads // (2 * together), two_parts, tops)
     for i, shift in enumerate(shifts):
         if last and shift:
             line = extents[i][:heads, :]
@@ -487,20 +500,17 @@
     operands = [*facts, *queries, *blocks]
     if old:
         operands += [old[shift][0] for shift in shifts] + [old[shift][1] for shift in shifts]
-    count = sum(size for _, _, size in rings) + BLK * slots + (rows if parted else 0)
+    count = sum(size for _, _, size in rings) + BLK * slots + (rows if slots else 0)
     many = len(shifts) * rows
     scratch = [pltpu.VMEM((count, HD), jnp.bfloat16)]
-    scratch += [pltpu.VMEM((count, many), jnp.float32)] * 2
+    together = min(heads // 2, 4 if count <= 256 else 1)
+    scratch += [pltpu.VMEM((together, count, many), jnp.float32)] * 2
     lines = (max(heads, 8), rows)
     scratch += [pltpu.VMEM(lines, jnp.float32) for shift in shifts if last and shift]
-    if parted:
+    if slots:
         scratch.append(pltpu.VMEM((rows, many), jnp.float32))
-    else:
-        scratch += [
-            pltpu.VMEM((count, width), jnp.bfloat16),
-            pltpu.VMEM((width, count), jnp.bfloat16),
-            pltpu.VMEM((count, width), jnp.bfloat16),
-        ]
+    if not parted:
+        scratch.append(pltpu.VMEM((count, width), jnp.bfloat16))
     mixes = [
         jax.ShapeDtypeStruct((width + stat_rows(heads), rows), jnp.bfloat16)
         if last and shift
@@ -510,23 +520,31 @@
     extents = [
         jax.ShapeDtypeStruct(lines, jnp.float32) for shift in shifts if not (last and shift)
     ]
-    scores = len(shifts) * rows * count * heads
+    scores = many * count * heads
+    shapes = [*mixes, *extents]
+    if not parted:
+        shapes += [
+            jax.ShapeDtypeStruct((count, width), jnp.bfloat16),
+            jax.ShapeDtypeStruct((width, count), jnp.bfloat16),
+        ]
     results = pl.pallas_call(
         functools.partial(
             attend_kernel, (group, shifts, rings, slots, piece, parted, not old, last)
         ),
         in_specs=[SMEM] * 3 + [VMEM] * (len(operands) - 3),
-        out_specs=[VMEM] * (len(mixes) + len(extents) + 1),
-        out_shape=[*mixes, *extents, TOKEN],
+        out_specs=[VMEM] * len(shapes),
+        out_shape=shapes,
         scratch_shapes=scratch,
         compiler_params=params(24),
         cost_estimate=cost(4 * scores * HD, 4 * count * width, scores),
         name=name,
     )(*operands)
+    mixes = results[: len(shifts)]
+    extents = [*results[len(shifts) : len(shapes) - (0 if parted else 2)]]
     if last:
-        return results
-    state = {shift: (results[i], results[len(shifts) + i]) for i, shift in enumerate(shifts)}
-    return state, results[-1]
+        extents = [extents.pop(0) if shift == 0 else None for shift in shifts]
+    state = {shift: pair for shift, *pair in zip(shifts, mixes, extents)}
+    return state, results[len(results) - 2 :]
 
 
 def combine_kernel(*refs):
@@ -613,30 +631,44 @@
 
     pieces = [hidden_in] + [swap(hidden_in, "tp", shift) for shift in range(1, ways)]
     prompt = viewed(prompt_cache)
-    ahead, behind = [prompt], [prompt]
-
-    def step(*others):
-        for blocks, way in ((ahead, 1), (behind, -1)):
-            blocks.append(turn(after(blocks[-1], *others), cycle, group, way))
-
-    step()
+    halves = [prompt[: middle * stride], prompt[middle * stride :]]
+    ahead = {0: [halves[0]], 1: [halves[1]]}
+    behind = {0: [halves[0]], 1: [halves[1]]}
+
+    def step(which, *others):
+        for blocks, part, way in ((ahead, which, 1), (behind, 1 - which, -1)):
+            block = blocks[part][-1]
+            if others:
+                block = after(block, *others)
+            blocks[part].append(turn(block, cycle, group, way))
+
+    def arrived(hop):
+        blocks = [way[part][hop] for way in (ahead, behind) for part in (0, 1)]
+        rings = [(sign * hop, part * middle, middle) for sign in (-1, 1) for part in (0, 1)]
+        return blocks, rings
+
+    step(0)
+    step(1)
     cosine, sine = angles(tail_len, shared_len, rows)
-    weight, weight_token = part_weights(w_keyval)
-    pieces[0] = after(pieces[0], weight_token)
-    query, normed, query_token = project_query(pieces, w_query, cosine, sine)
+    weight = part_weights(w_keyval)
+    step(0, weight)
+    pieces[0] = after(pieces[0], weight)
+    query, normed = project_query(pieces, w_query, cosine, sine)
     queries = [query] + [swap(query, "seq", shift) for shift in range(1, group)]
     tail = viewed(tail_cache.reshape(-1, 2, tail_cache.shape[3]))
     slots = tail_cache.shape[0]
-    *own_block, token = part_keyval([tail, prompt], width, "part_own")
-    step(token, weight_token, query_token)
-    *near_block, token = part_keyval([ahead[1], behind[1]], width, "part_near")
+    own_block = part_keyval([tail, prompt], width, "part_own")
+    step(1, own_block[0], query)
     fresh_keys, fresh_turned, new_cache = project_keyval(normed, weight, cosine, sine)
+    step(0, fresh_keys)
+    blocks, rings = arrived(1)
+    near_block = part_keyval(blocks, width, "part_near")
 
     table = tail_table.T
     facts = (tail_len, shared_len, table)
     others = list(range(1, group))
     near = (
-        [(0, 0, piece), (-1, 0, piece), (1, 0, piece)],
+        [(0, 0, piece), *rings],
         slots,
         piece,
         [*own_block, *near_block, fresh_keys, fresh_turned],
@@ -644,26 +676,34 @@
         None,
         False,
     )
-    state, token = attend(facts, queries, [0], *near, "attend_near_own")
-    step(token)
-    ready = (after(tail_len, token), shared_len, table)
-    state_others, token = attend(ready, queries, others, *near, "attend_near_others")
-    state |= state_others
-    rings = [(-2, 0, piece), (2, 0, piece)]
-    second = (rings, 0, piece, [ahead[2], behind[2]], False, state, False, "attend_second")
-    state, token = attend(facts, queries, [0, *others], *second)
-    far_low = turn(after(ahead[3], token)[: middle * stride], cycle, group, 1)
-    far_high = turn(after(behind[3], token)[middle * stride :], cycle, group, -1)
-    rings = [(-3, 0, piece), (3, 0, piece)]
-    third = (rings, 0, piece, [ahead[3], behind[3]], False, state, False, "attend_third")
-    state, token = attend(facts, queries, [0, *others], *third)
+    own, _ = attend(facts, queries, [0], *near, "attend_near_own")
+    step(1, own[0][1])
+    ready = (after(tail_len, own[0][1]), shared_len, table)
+    theirs, _ = attend(ready, queries, others, *near, "attend_near_others")
+    step(0, theirs[1][1])
+    rest = []
+    rest_rings = []
+    for hop in range(2, half):
+        blocks, rings = arrived(hop)
+        name = f"attend_hop{hop}_others"
+        theirs, parted = attend(
+            facts, queries, others, rings, 0, piece, blocks, False, theirs, False, name
+        )
+        rest += parted
+        rest_rings += rings
     rings = [(-half, 0, middle), (half, middle, piece - middle)]
-    far = (rings, 0, piece, [far_low, far_high], False, state, True)
-    *parts, token = attend(facts, queries, others, *far, "attend_far_others")
-    ready = (after(tail_len, token), shared_len, table)
-    result, extent, token = attend(ready, queries, [0], *far, "attend_far_own")
-    parts = [swap(part, "seq", shift + 1) for shift, part in enumerate(parts)]
-    attended, sent = combine(result, extent, parts, w_out, ways)
+    blocks = [ahead[0][half], behind[1][half]]
+    theirs, parted = attend(
+        facts, queries, others, rings, 0, piece, blocks, False, theirs, True, "attend_far_others"
+    )
+    rest += parted
+    rest_rings += rings
+    ready = (after(tail_len, theirs[1][0]), shared_len, table)
+    own, _ = attend(
+        ready, queries, [0], rest_rings, 0, piece, rest, True, own, True, "attend_rest_own"
+    )
+    parts = [swap(theirs[shift][0], "seq", shift) for shift in others]
+    attended, sent = combine(*own[0], parts, w_out, ways)
     received = [swap(sent[shift - 1], "tp", shift) for shift in range(1, ways)]
     total = keep(attended, w_out, hidden_in)
     for part in received:

time: 70.3 us -> 70.6 us (level)
  Pallas kernels: 42.1 us -> 34.3 us
  starting transfers between devices: 12.2 us -> 18.1 us
  local copies, waits for them, and re-layouts: 0.06 us -> 2.09 us
    ppermute x8 -> x14, starting transfers between devices: 9.36 us -> 15.5 us  [turn(): return lax.ppermute(value, 'seq', pairs)]
    pallas_call x6, Pallas kernels: 24.7 us -> 18.7 us  [attend(): pl.pallas_call(functools.partial(attend_kernel, (group, shifts, rings, sl...]
    ppermute x4, waiting for transfers between devices: 8.15 us -> 10.2 us  [swap(): return lax.ppermute(value, axis, pairs)]
    ppermute x8 -> x14, waiting for transfers between devices: 4.7 us -> 2.94 us  [turn(): return lax.ppermute(value, 'seq', pairs)]
    slice x2 -> x1, local copies, waits for them, and re-layouts: 0.04 us -> 1.39 us  [local(): halves = [prompt[:middle * stride], prompt[middle * stride:]]]
    pallas_call x2, Pallas kernels: 2.66 us -> 1.64 us  [part_keyval(): pl.pallas_call(part_kernel, in_specs=[VMEM] * len(blocks), out_specs=[VME...]
  transfers between devices with their start and end apart: 12 -> 18, of which waited for: 5 -> 4; matrix products, arithmetic and copies ran while one was open for 1% -> 1% of each run, Pallas kernels for 54% -> 45%
where the time goes in v8:
time: 70.6 us; the launch traced here: 70.5 us
  Pallas kernels  34.3 us (49%)
  starting transfers between devices  18.1 us (26%)
  waiting for transfers between devices  13.1 us (19%)
  local copies, waits for them, and re-layouts  2.09 us (3%)
  between operations  1.55 us (2%)
  other arithmetic  1.42 us (2%)
    pallas_call x6, Pallas kernels, attend(): pl.pallas_call(functools.partial(attend_kernel, (group, shifts, rings, sl...  18.7 us
    ppermute x14, starting transfers between devices, turn(): return lax.ppermute(value, 'seq', pairs)  15.5 us
    ppermute x4, waiting for transfers between devices, swap(): return lax.ppermute(value, axis, pairs)  10.2 us
    pallas_call x1, Pallas kernels, part_weights(): pl.pallas_call(weight_kernel, in_specs=[HBM], out_specs=VMEM, out_shape=j...  5.5 us
    pallas_call x1, Pallas kernels, project_keyval(): pl.pallas_call(keyval_kernel, in_specs=[VMEM] * 4, out_specs=[VMEM] * 3,...  4.03 us
    ppermute x14, waiting for transfers between devices, turn(): return lax.ppermute(value, 'seq', pairs)  2.94 us
    ppermute x4, starting transfers between devices, swap(): return lax.ppermute(value, axis, pairs)  2.61 us
    pallas_call x1, Pallas kernels, project_query(): pl.pallas_call(query_kernel, in_specs=[VMEM] * (len(pieces) + 3), out_spe...  2.06 us
  transfers between devices with their start and end apart: 18, of which 4 were waited for; matrix products, arithmetic and copies ran while one was open for 1% of the time, Pallas kernels for 45%

profile of v8, /device:TPU:0, one launch (start us, length us, event | category | flops | bytes accessed | tf_op | source)
XLA Modules:
  0.0 70.5 jit_solution(16134492180428207847)
XLA Ops:
  0.6 1.4 %fusion.4 = (bf16[64,8,2,128]{3,2,1,0:T(2,128)(2,1)S(1)}, bf16[64,8,2,128]{3,2,1,0:T(2,128)(2,1)S(1)}) fusion(bf16[128,8,2,128]{3,2,1,0:T(2,128)(2,1)} %bitcast.24), kind=kLoop, calls=%fused_computation.9 | loop fusion | bytes 1048576 | tf_op jit(solution)/shard_map/slice | solution.py:634
  2.0 3.0 %collective-permute-start.6 = (bf16[1024,128]{1,0:T(8,128)(2,1)S(1)}, bf16[1024,128]{1,0:T(8,128)(2,1)S(1)}, u32[]{:S(2)}, u32[]{:S(2)}) collective-permute-start(bf16[1024,128]{1,0:T(8,128)(2,1)S(1)} %bitcast.37), channel_id=1, source_target_pairs={{0,4},{2,6},{8,0},{10,2},{16,8},{18,10},{24,16},{26,18},{28,24},{3... | collective-permute-start | bytes 786440 | tf_op jit(solution)/shard_map/ppermute | solution.py:50
  5.2 1.9 %collective-permute-start.7 = (bf16[1024,128]{1,0:T(8,128)(2,1)S(1)}, bf16[1024,128]{1,0:T(8,128)(2,1)S(1)}, u32[]{:S(2)}, u32[]{:S(2)}) collective-permute-start(bf16[1024,128]{1,0:T(8,128)(2,1)S(1)} %bitcast.35), channel_id=1, source_target_pairs={{0,4},{2,6},{8,0},{10,2},{16,8},{18,10},{24,16},{26,18},{28,24},{3... | collective-permute-start | bytes 786440 | tf_op jit(solution)/shard_map/ppermute | solution.py:50
  7.9 0.6 copy-done.6
  8.5 0.6 positions.1
  9.1 0.5 sine_multiply_fusion
  9.6 5.5 %part_weights.1.weight = bf16[2,2048,1024]{2,1,0:T(8,128)(2,1)S(1)} custom-call(bf16[32768,128]{1,0:T(8,128)(2,1)} %bitcast.34), custom_call_target="tpu_custom_call" | custom-call | flops 2147483648 | bytes 16777216 | tf_op jit(solution)/shard_map/part_weights/pallas_call | solution.py:251
  15.2 2.1 %project_query.1 = (bf16[256,1024]{1,0:T(8,128)(2,1)S(1)}, bf16[256,2048]{1,0:T(8,128)(2,1)S(1)}) custom-call(bf16[256,1024]{1,0:T(8,128)(2,1)S(1)} %copy-done.3, bf16[256,1024]{1,0:T(8,128)(2,1)S(1)} %collective-permute-done.refs_1_, bf16[2048,1024]{1,0:T(8,128)(2,1)S(1)} %copy-done.1, f32[256,128]{1,0:T(8,128)S(1)} %get-tuple-element.87.refs_3_.cosine, ...), custom_call_target="tpu_custom_call" | custom-call | flops 1073741824 | bytes 4194304 | tf_op jit(solution)/shard_map/project_query/pallas_call | solution.py:212
  17.3 1.9 %collective-permute-start.1 = (bf16[256,1024]{1,0:T(8,128)(2,1)S(1)}, bf16[256,1024]{1,0:T(8,128)(2,1)S(1)}, u32[]{:S(2)}, u32[]{:S(2)}) collective-permute-start(bf16[256,1024]{1,0:T(8,128)(2,1)S(1)} %get-tuple-element.44.refs_3_), channel_id=1, source_target_pairs={{0,2},{2,0},{4,6},{6,4},{8,10},{10,8},{12,14},{14,12},{16,18},{18,... | collective-permute-start | bytes 1572872 | tf_op jit(solution)/shard_map/ppermute | solution.py:41
  19.2 1.5 %collective-permute-start.9 = (bf16[1024,128]{1,0:T(8,128)(2,1)S(1)}, bf16[1024,128]{1,0:T(8,128)(2,1)S(1)}, u32[]{:S(2)}, u32[]{:S(2)}) collective-permute-start(bf16[1024,128]{1,0:T(8,128)(2,1)S(1)} %collective-permute-done.7.refs_3_), channel_id=1, source_target_pairs={{0,4},{2,6},{8,0},{10,2},{16,8},{18,10},{24,16},{26,18},{28,24},{3... | collective-permute-start | bytes 786440 | tf_op jit(solution)/shard_map/ppermute | solution.py:50
  20.7 0.5 collective-permute-start.3
  21.2 0.9 %part_own.1 = (bf16[384,1024]{1,0:T(8,128)(2,1)S(1)}, bf16[1024,384]{1,0:T(8,128)(2,1)S(1)}) custom-call(bf16[4096,128]{1,0:T(8,128)(2,1)S(1)} %bitcast.26, bf16[2048,128]{1,0:T(8,128)(2,1)S(1)} %bitcast.25), custom_call_target="tpu_custom_call" | custom-call | flops 402653184 | bytes 3145728 | tf_op jit(solution)/shard_map/part_own/pallas_call | solution.py:170
  22.2 1.6 %collective-permute-start.12 = (bf16[1024,128]{1,0:T(8,128)(2,1)S(1)}, bf16[1024,128]{1,0:T(8,128)(2,1)S(1)}, u32[]{:S(2)}, u32[]{:S(2)}) collective-permute-start(bf16[1024,128]{1,0:T(8,128)(2,1)S(1)} %collective-permute-done.5.refs_1_), channel_id=1, source_target_pairs={{0,8},{2,10},{8,16},{10,18},{16,24},{18,26},{24,28},{26,30},{28,20... | collective-permute-start | bytes 786440 | tf_op jit(solution)/shard_map/ppermute | solution.py:50
  24.3 4.0 %project_keyval.1 = (bf16[256,1024]{1,0:T(8,128)(2,1)S(1)}, bf16[1024,256]{1,0:T(8,128)(2,1)S(1)}, bf16[4096,128]{1,0:T(8,128)(2,1)}) custom-call(bf16[256,2048]{1,0:T(8,128)(2,1)S(1)} %get-tuple-element.46.normed, bf16[2,2048,1024]{2,1,0:T(8,128)(2,1)S(1)} %part_weights.1.weight, f32[256,128]{1,0:T(8,128)S(1)} %get-tuple-element.87.refs_3_.cosine, ...), custom_call_target="tpu_custom_call" | custom-call | flops 2147483648 | bytes 8388608 | tf_op jit(solution)/shard_map/project_keyval/pallas_call | solution.py:303
  28.3 1.5 %collective-permute-start.10 = (bf16[1024,128]{1,0:T(8,128)(2,1)S(1)}, bf16[1024,128]{1,0:T(8,128)(2,1)S(1)}, u32[]{:S(2)}, u32[]{:S(2)}) collective-permute-start(bf16[1024,128]{1,0:T(8,128)(2,1)S(1)} %collective-permute-done.9.refs_7_), channel_id=1, source_target_pairs={{0,4},{2,6},{8,0},{10,2},{16,8},{18,10},{24,16},{26,18},{28,24},{3... | collective-permute-start | bytes 786440 | tf_op jit(solution)/shard_map/ppermute | solution.py:50
  29.9 0.5 collective-permute-start.4
  30.4 0.7 part_near.1
  31.1 4.4 %attend_near_own.1 = (f32[1024,256]{1,0:T(8,128)S(1)}, f32[8,256]{1,0:T(8,128)S(1)}) custom-call(s32[8]{0:T(128)S(1)} %copy-done.7, s32[1]{0:T(128)S(6)} %copy.15.shared.refs_1_, s32[4,8]{1,0:T(4,128)S(1)} %bitcast.27, bf16[256,1024]{1,0:T(8,128)(2,1)S(1)} %get-tuple-element.44.refs_3_, bf16[384,1024]{1,0:T(8,128)(2,1)S(1)} %get-tuple-element.49.refs_4_, ...), custom_call_target="tpu_custom_call" | custom-call | flops 939524096 | bytes 3670016 | tf_op jit(solution)/shard_map/attend_near_own/pallas_call | solution.py:530
  35.5 1.6 %collective-permute-start.13 = (bf16[1024,128]{1,0:T(8,128)(2,1)S(1)}, bf16[1024,128]{1,0:T(8,128)(2,1)S(1)}, u32[]{:S(2)}, u32[]{:S(2)}) collective-permute-start(bf16[1024,128]{1,0:T(8,128)(2,1)S(1)} %collective-permute-done.12.refs_5_), channel_id=1, source_target_pairs={{0,8},{2,10},{8,16},{10,18},{16,24},{18,26},{24,28},{26,30},{28,20... | collective-permute-start | bytes 786440 | tf_op jit(solution)/shard_map/ppermute | solution.py:50
  37.6 4.3 %attend_near_others.1 = (f32[1024,256]{1,0:T(8,128)S(1)}, f32[8,256]{1,0:T(8,128)S(1)}) custom-call(s32[8]{0:T(128)S(1)} %copy-done.7, s32[1]{0:T(128)S(6)} %copy.15.shared.refs_1_, s32[4,8]{1,0:T(4,128)S(1)} %bitcast.28, bf16[256,1024]{1,0:T(8,128)(2,1)S(1)} %collective-permute-done.1.refs_3_, bf16[384,1024]{1,0:T(8,128)(2,1)S(1)} %get-tuple-element.49.refs_4_, ...), custom_call_target="tpu_custom_call" | custom-call | flops 939524096 | bytes 3670016 | tf_op jit(solution)/shard_map/attend_near_others/pallas_call | solution.py:530
  42.0 1.6 %collective-permute-start.8 = (bf16[1024,128]{1,0:T(8,128)(2,1)S(1)}, bf16[1024,128]{1,0:T(8,128)(2,1)S(1)}, u32[]{:S(2)}, u32[]{:S(2)}) collective-permute-start(bf16[1024,128]{1,0:T(8,128)(2,1)S(1)} %collective-permute-done.4.refs_4_), channel_id=1, source_target_pairs={{0,8},{2,10},{8,16},{10,18},{16,24},{18,26},{24,28},{26,30},{28,20... | collective-permute-start | bytes 786440 | tf_op jit(solution)/shard_map/ppermute | solution.py:50
  44.1 2.2 %attend_hop2_others.1 = (f32[1024,256]{1,0:T(8,128)S(1)}, f32[8,256]{1,0:T(8,128)S(1)}, bf16[256,1024]{1,0:T(8,128)(2,1)S(1)}, bf16[1024,256]{1,0:T(8,128)(2,1)S(1)}) custom-call(s32[8]{0:T(128)S(1)} %copy-done.7, s32[1]{0:T(128)S(6)} %copy.15.shared.refs_1_, s32[4,8]{1,0:T(4,128)S(1)} %bitcast.29, bf16[256,1024]{1,0:T(8,128)(2,1)S(1)} %collective-permute-done.1.refs_3_, ...), custom_call_target="tpu_custom_call" | custom-call | flops 268435456 | bytes 1048576 | tf_op jit(solution)/shard_map/attend_hop2_others/pallas_call | solution.py:530
  46.8 2.2 %attend_hop3_others.1 = (f32[1024,256]{1,0:T(8,128)S(1)}, f32[8,256]{1,0:T(8,128)S(1)}, bf16[256,1024]{1,0:T(8,128)(2,1)S(1)}, bf16[1024,256]{1,0:T(8,128)(2,1)S(1)}) custom-call(s32[8]{0:T(128)S(1)} %copy-done.7, s32[1]{0:T(128)S(6)} %copy.15.shared.refs_1_, s32[4,8]{1,0:T(4,128)S(1)} %bitcast.30, bf16[256,1024]{1,0:T(8,128)(2,1)S(1)} %collective-permute-done.1.refs_3_, ...), custom_call_target="tpu_custom_call" | custom-call | flops 268435456 | bytes 1048576 | tf_op jit(solution)/shard_map/attend_hop3_others/pallas_call | solution.py:530
  49.0 2.4 %collective-permute-done.8.refs_4_ = bf16[1024,128]{1,0:T(8,128)(2,1)S(1)} collective-permute-done((bf16[1024,128]{1,0:T(8,128)(2,1)S(1)}, bf16[1024,128]{1,0:T(8,128)(2,1)S(1)}, u32[]{:S(2)}, u32[]{:S(2)}) %collective-permute-start.8) | collective-permute-done | bytes 262176 | tf_op jit(solution)/shard_map/ppermute | solution.py:50
  51.4 1.8 %attend_far_others.1 = (bf16[1056,256]{1,0:T(8,128)(2,1)S(1)}, bf16[128,1024]{1,0:T(8,128)(2,1)S(1)}, bf16[1024,128]{1,0:T(8,128)(2,1)S(1)}) custom-call(s32[8]{0:T(128)S(1)} %copy-done.7, s32[1]{0:T(128)S(6)} %copy.15.shared.refs_1_, s32[4,8]{1,0:T(4,128)S(1)} %bitcast.31, bf16[256,1024]{1,0:T(8,128)(2,1)S(1)} %collective-permute-done.1.refs_3_, ...), custom_call_target="tpu_custom_call" | custom-call | flops 134217728 | bytes 524288 | tf_op jit(solution)/shard_map/attend_far_others/pallas_call | solution.py:530
  53.2 0.6 collective-permute-start.16
  53.8 3.7 %attend_rest_own.1 = (f32[1024,256]{1,0:T(8,128)S(1)}, f32[8,256]{1,0:T(8,128)S(1)}) custom-call(s32[8]{0:T(128)S(1)} %copy-done.7, s32[1]{0:T(128)S(6)} %copy.15.shared.refs_1_, s32[4,8]{1,0:T(4,128)S(1)} %bitcast.32, bf16[256,1024]{1,0:T(8,128)(2,1)S(1)} %get-tuple-element.44.refs_3_, bf16[256,1024]{1,0:T(8,128)(2,1)S(1)} %get-tuple-element.72.refs_4_, ...), custom_call_target="tpu_custom_call" | custom-call | flops 671088640 | bytes 2621440 | tf_op jit(solution)/shard_map/attend_rest_own/pallas_call | solution.py:530
  57.5 9.0 %collective-permute-done.16.refs_2_ = bf16[1056,256]{1,0:T(8,128)(2,1)S(1)} collective-permute-done((bf16[1056,256]{1,0:T(8,128)(2,1)S(1)}, bf16[1056,256]{1,0:T(8,128)(2,1)S(1)}, u32[]{:S(2)}, u32[]{:S(2)}) %collective-permute-start.16) | collective-permute-done | bytes 540704 | tf_op jit(solution)/shard_map/ppermute | solution.py:41
  66.5 1.0 %combine_send.1 = (bf16[256,1024]{1,0:T(8,128)(2,1)S(1)}, bf16[1,256,1024]{2,1,0:T(8,128)(2,1)S(1)}) custom-call(f32[1024,256]{1,0:T(8,128)S(1)} %get-tuple-element.79.refs_0_, f32[8,256]{1,0:T(8,128)S(1)} %get-tuple-element.80.refs_1_, bf16[1056,256]{1,0:T(8,128)(2,1)S(1)} %collective-permute-done.16.refs_2_, bf16[1024,2048]{1,0:T(8,128)(2,1)S(1)} %copy-done), custom_call_target="tpu_custom_call" | custom-call | flops 536870912 | bytes 4194304 | tf_op jit(solution)/shard_map/combine_send/pallas_call | solution.py:582
  67.6 0.7 %keep_own.1 = f32[256,1024]{1,0:T(8,128)S(1)} custom-call(bf16[256,1024]{1,0:T(8,128)(2,1)S(1)} %get-tuple-element.81.attended, bf16[1024,2048]{1,0:T(8,128)(2,1)S(1)} %copy-done, bf16[256,1024]{1,0:T(8,128)(2,1)S(1)} %copy-done.3), custom_call_target="tpu_custom_call" | custom-call | flops 536870912 | bytes 4194304 | tf_op jit(solution)/shard_map/keep_own/pallas_call | solution.py:608
  68.4 1.2 %collective-permute-done.17 = bf16[256,1024]{1,0:T(8,128)(2,1)S(1)} collective-permute-done((bf16[256,1024]{1,0:T(8,128)(2,1)S(1)}, bf16[256,1024]{1,0:T(8,128)(2,1)S(1)}, u32[]{:S(2)}, u32[]{:S(2)}) %collective-permute-start.17) | collective-permute-done | bytes 524320 | tf_op jit(solution)/shard_map/ppermute | solution.py:41
  69.5 0.9 %add_convert_fusion = bf16[256,1024]{1,0:T(8,128)(2,1)} fusion(f32[256,1024]{1,0:T(8,128)S(1)} %keep_own.1, bf16[256,1024]{1,0:T(8,128)(2,1)S(1)} %collective-permute-done.17), kind=kLoop, calls=%fused_computation | loop fusion | flops 786432 | bytes 2097152 | tf_op jit(solution)/shard_map/convert_element_type | solution.py:711
  (38 shorter events, 2.3 us)
Async XLA Ops:
  2.0 20.2 %collective-permute-start.6 = (bf16[1024,128]{1,0:T(8,128)(2,1)S(1)}, bf16[1024,128]{1,0:T(8,128)(2,1)S(1)}, u32[]{:S(2)}, u32[]{:S(2)}) collective-permute-start(bf16[1024,128]{1,0:T(8,128)(2,1)S(1)} %bitcast.37), channel_id=1, source_target_pairs={{0,4},{2,6},{8,0},{10,2},{16,8},{18,10},{24,16},{26,18},{28,24},{3... | collective-permute-start | bytes 786440 | tf_op jit(solution)/shard_map/ppermute | solution.py:50
  5.0 15.7 %collective-permute-start.2 = (bf16[1024,128]{1,0:T(8,128)(2,1)S(1)}, bf16[1024,128]{1,0:T(8,128)(2,1)S(1)}, u32[]{:S(2)}, u32[]{:S(2)}) collective-permute-start(bf16[1024,128]{1,0:T(8,128)(2,1)S(1)} %bitcast.38), channel_id=1, source_target_pairs={{0,8},{2,10},{8,16},{10,18},{16,24},{18,26},{24,28},{26,30},{28,20... | collective-permute-start | bytes 786440 | tf_op jit(solution)/shard_map/ppermute | solution.py:50
  5.2 14.0 %collective-permute-start.7 = (bf16[1024,128]{1,0:T(8,128)(2,1)S(1)}, bf16[1024,128]{1,0:T(8,128)(2,1)S(1)}, u32[]{:S(2)}, u32[]{:S(2)}) collective-permute-start(bf16[1024,128]{1,0:T(8,128)(2,1)S(1)} %bitcast.35), channel_id=1, source_target_pairs={{0,4},{2,6},{8,0},{10,2},{16,8},{18,10},{24,16},{26,18},{28,24},{3... | collective-permute-start | bytes 786440 | tf_op jit(solution)/shard_map/ppermute | solution.py:50
  7.1 15.1 %collective-permute-start.5 = (bf16[1024,128]{1,0:T(8,128)(2,1)S(1)}, bf16[1024,128]{1,0:T(8,128)(2,1)S(1)}, u32[]{:S(2)}, u32[]{:S(2)}) collective-permute-start(bf16[1024,128]{1,0:T(8,128)(2,1)S(1)} %bitcast.36), channel_id=1, source_target_pairs={{0,8},{2,10},{8,16},{10,18},{16,24},{18,26},{24,28},{26,30},{28,20... | collective-permute-start | bytes 786440 | tf_op jit(solution)/shard_map/ppermute | solution.py:50
  7.2 7.9 %collective-permute-start = (bf16[256,1024]{1,0:T(8,128)(2,1)}, bf16[256,1024]{1,0:T(8,128)(2,1)S(1)}, u32[]{:S(2)}, u32[]{:S(2)}) collective-permute-start(bf16[256,1024]{1,0:T(8,128)(2,1)} %hidden.1), channel_id=1, source_target_pairs={{0,1},{1,0},{2,3},{3,2},{4,5},{5,4},{6,7},{7,6},{8,9},{9,8},{10,11... | collective-permute-start | bytes 1572872 | tf_op jit(solution)/shard_map/ppermute | solution.py:41
  7.8 0.7 copy-start.6
  9.6 5.6 %copy-start.1 = (bf16[2048,1024]{1,0:T(8,128)(2,1)S(1)}, bf16[2048,1024]{1,0:T(8,128)(2,1)}, u32[]{:S(2)}) copy-start(bf16[2048,1024]{1,0:T(8,128)(2,1)} %refs_2_.1) | copy-start | bytes 12582916
  9.6 5.6 %copy-start.3 = (bf16[256,1024]{1,0:T(8,128)(2,1)S(1)}, bf16[256,1024]{1,0:T(8,128)(2,1)}, u32[]{:S(2)}) copy-start(bf16[256,1024]{1,0:T(8,128)(2,1)} %hidden.1) | copy-start | bytes 1572868
  9.6 11.6 %copy-start.2 = (bf16[128,2,1024]{2,1,0:T(2,128)(2,1)S(1)}, bf16[128,2,1024]{2,1,0:T(2,128)(2,1)}, u32[]{:S(2)}) copy-start(bf16[128,2,1024]{2,1,0:T(2,128)(2,1)} %param.13) | copy-start | bytes 1572868
  9.6 11.6 %copy-start.4 = (bf16[2,128,2,1024]{3,2,1,0:T(2,128)(2,1)S(1)}, bf16[2,128,2,1024]{3,2,1,0:T(2,128)(2,1)}, u32[]{:S(2)}) copy-start(bf16[2,128,2,1024]{3,2,1,0:T(2,128)(2,1)} %param.14) | copy-start | bytes 3145732
  15.2 15.9 %copy-start.5 = (s32[8,4]{0,1:T(4,128)S(1)}, s32[8,4]{0,1:T(4,128)}, u32[]{:S(2)}) copy-start(s32[8,4]{0,1:T(4,128)} %param.15) | copy-start | bytes 388
  15.2 15.9 %copy-start.7 = (s32[8]{0:T(128)S(1)}, s32[8]{0:T(128)}, u32[]{:S(2)}) copy-start(s32[8]{0:T(128)} %refs_0_.10) | copy-start | bytes 100
  17.3 20.3 %collective-permute-start.1 = (bf16[256,1024]{1,0:T(8,128)(2,1)S(1)}, bf16[256,1024]{1,0:T(8,128)(2,1)S(1)}, u32[]{:S(2)}, u32[]{:S(2)}) collective-permute-start(bf16[256,1024]{1,0:T(8,128)(2,1)S(1)} %get-tuple-element.44.refs_3_), channel_id=1, source_target_pairs={{0,2},{2,0},{4,6},{6,4},{8,10},{10,8},{12,14},{14,12},{16,18},{18,... | collective-permute-start | bytes 1572872 | tf_op jit(solution)/shard_map/ppermute | solution.py:41
  19.2 9.1 %collective-permute-start.9 = (bf16[1024,128]{1,0:T(8,128)(2,1)S(1)}, bf16[1024,128]{1,0:T(8,128)(2,1)S(1)}, u32[]{:S(2)}, u32[]{:S(2)}) collective-permute-start(bf16[1024,128]{1,0:T(8,128)(2,1)S(1)} %collective-permute-done.7.refs_3_), channel_id=1, source_target_pairs={{0,4},{2,6},{8,0},{10,2},{16,8},{18,10},{24,16},{26,18},{28,24},{3... | collective-permute-start | bytes 786440 | tf_op jit(solution)/shard_map/ppermute | solution.py:50
  20.7 9.2 %collective-permute-start.3 = (bf16[1024,128]{1,0:T(8,128)(2,1)S(1)}, bf16[1024,128]{1,0:T(8,128)(2,1)S(1)}, u32[]{:S(2)}, u32[]{:S(2)}) collective-permute-start(bf16[1024,128]{1,0:T(8,128)(2,1)S(1)} %collective-permute-done.2.refs_0_), channel_id=1, source_target_pairs={{0,8},{2,10},{8,16},{10,18},{16,24},{18,26},{24,28},{26,30},{28,20... | collective-permute-start | bytes 786440 | tf_op jit(solution)/shard_map/ppermute | solution.py:50
  22.2 13.3 %collective-permute-start.12 = (bf16[1024,128]{1,0:T(8,128)(2,1)S(1)}, bf16[1024,128]{1,0:T(8,128)(2,1)S(1)}, u32[]{:S(2)}, u32[]{:S(2)}) collective-permute-start(bf16[1024,128]{1,0:T(8,128)(2,1)S(1)} %collective-permute-done.5.refs_1_), channel_id=1, source_target_pairs={{0,8},{2,10},{8,16},{10,18},{16,24},{18,26},{24,28},{26,30},{28,20... | collective-permute-start | bytes 786440 | tf_op jit(solution)/shard_map/ppermute | solution.py:50
  23.8 11.7 %collective-permute-start.14 = (bf16[1024,128]{1,0:T(8,128)(2,1)S(1)}, bf16[1024,128]{1,0:T(8,128)(2,1)S(1)}, u32[]{:S(2)}, u32[]{:S(2)}) collective-permute-start(bf16[1024,128]{1,0:T(8,128)(2,1)S(1)} %collective-permute-done.6.refs_2_), channel_id=1, source_target_pairs={{0,4},{2,6},{8,0},{10,2},{16,8},{18,10},{24,16},{26,18},{28,24},{3... | collective-permute-start | bytes 786440 | tf_op jit(solution)/shard_map/ppermute | solution.py:50
  28.3 13.6 %collective-permute-start.10 = (bf16[1024,128]{1,0:T(8,128)(2,1)S(1)}, bf16[1024,128]{1,0:T(8,128)(2,1)S(1)}, u32[]{:S(2)}, u32[]{:S(2)}) collective-permute-start(bf16[1024,128]{1,0:T(8,128)(2,1)S(1)} %collective-permute-done.9.refs_7_), channel_id=1, source_target_pairs={{0,4},{2,6},{8,0},{10,2},{16,8},{18,10},{24,16},{26,18},{28,24},{3... | collective-permute-start | bytes 786440 | tf_op jit(solution)/shard_map/ppermute | solution.py:50
  29.9 12.1 %collective-permute-start.4 = (bf16[1024,128]{1,0:T(8,128)(2,1)S(1)}, bf16[1024,128]{1,0:T(8,128)(2,1)S(1)}, u32[]{:S(2)}, u32[]{:S(2)}) collective-permute-start(bf16[1024,128]{1,0:T(8,128)(2,1)S(1)} %collective-permute-done.3.refs_4_), channel_id=1, source_target_pairs={{0,8},{2,10},{8,16},{10,18},{16,24},{18,26},{24,28},{26,30},{28,20... | collective-permute-start | bytes 786440 | tf_op jit(solution)/shard_map/ppermute | solution.py:50
  35.5 31.0 %copy-start = (bf16[1024,2048]{1,0:T(8,128)(2,1)S(1)}, bf16[1024,2048]{1,0:T(8,128)(2,1)}, u32[]{:S(2)}) copy-start(bf16[1024,2048]{1,0:T(8,128)(2,1)} %weight.1) | copy-start | bytes 12582916
  35.5 11.2 %collective-permute-start.13 = (bf16[1024,128]{1,0:T(8,128)(2,1)S(1)}, bf16[1024,128]{1,0:T(8,128)(2,1)S(1)}, u32[]{:S(2)}, u32[]{:S(2)}) collective-permute-start(bf16[1024,128]{1,0:T(8,128)(2,1)S(1)} %collective-permute-done.12.refs_5_), channel_id=1, source_target_pairs={{0,8},{2,10},{8,16},{10,18},{16,24},{18,26},{24,28},{26,30},{28,20... | collective-permute-start | bytes 786440 | tf_op jit(solution)/shard_map/ppermute | solution.py:50
  37.2 9.6 %collective-permute-start.15 = (bf16[1024,128]{1,0:T(8,128)(2,1)S(1)}, bf16[1024,128]{1,0:T(8,128)(2,1)S(1)}, u32[]{:S(2)}, u32[]{:S(2)}) collective-permute-start(bf16[1024,128]{1,0:T(8,128)(2,1)S(1)} %collective-permute-done.14.refs_6_), channel_id=1, source_target_pairs={{0,4},{2,6},{8,0},{10,2},{16,8},{18,10},{24,16},{26,18},{28,24},{3... | collective-permute-start | bytes 786440 | tf_op jit(solution)/shard_map/ppermute | solution.py:50
  42.0 9.4 %collective-permute-start.8 = (bf16[1024,128]{1,0:T(8,128)(2,1)S(1)}, bf16[1024,128]{1,0:T(8,128)(2,1)S(1)}, u32[]{:S(2)}, u32[]{:S(2)}) collective-permute-start(bf16[1024,128]{1,0:T(8,128)(2,1)S(1)} %collective-permute-done.4.refs_4_), channel_id=1, source_target_pairs={{0,8},{2,10},{8,16},{10,18},{16,24},{18,26},{24,28},{26,30},{28,20... | collective-permute-start | bytes 786440 | tf_op jit(solution)/shard_map/ppermute | solution.py:50
  43.6 7.7 %collective-permute-start.11 = (bf16[1024,128]{1,0:T(8,128)(2,1)S(1)}, bf16[1024,128]{1,0:T(8,128)(2,1)S(1)}, u32[]{:S(2)}, u32[]{:S(2)}) collective-permute-start(bf16[1024,128]{1,0:T(8,128)(2,1)S(1)} %collective-permute-done.10.refs_7_), channel_id=1, source_target_pairs={{0,4},{2,6},{8,0},{10,2},{16,8},{18,10},{24,16},{26,18},{28,24},{3... | collective-permute-start | bytes 786440 | tf_op jit(solution)/shard_map/ppermute | solution.py:50
  53.2 13.3 %collective-permute-start.16 = (bf16[1056,256]{1,0:T(8,128)(2,1)S(1)}, bf16[1056,256]{1,0:T(8,128)(2,1)S(1)}, u32[]{:S(2)}, u32[]{:S(2)}) collective-permute-start(bf16[1056,256]{1,0:T(8,128)(2,1)S(1)} %get-tuple-element.70), channel_id=1, source_target_pairs={{0,2},{2,0},{4,6},{6,4},{8,10},{10,8},{12,14},{14,12},{16,18},{18,... | collective-permute-start | bytes 1622024 | tf_op jit(solution)/shard_map/ppermute | solution.py:41
  67.6 2.0 %collective-permute-start.17 = (bf16[256,1024]{1,0:T(8,128)(2,1)S(1)}, bf16[256,1024]{1,0:T(8,128)(2,1)S(1)}, u32[]{:S(2)}, u32[]{:S(2)}) collective-permute-start(bf16[256,1024]{1,0:T(8,128)(2,1)S(1)} %bitcast.33), channel_id=1, source_target_pairs={{0,1},{1,0},{2,3},{3,2},{4,5},{5,4},{6,7},{7,6},{8,9},{9,8},{10,11... | collective-permute-start | bytes 1572872 | tf_op jit(solution)/shard_map/ppermute | solution.py:41

commit v9 on v8

--- a/solution.py
+++ b/solution.py
@@ -263,10 +263,8 @@
     )(weight)
 
 
-def keyval_kernel(normed, weight, cosine, sine, keys, turned, cache, values):
-    rows = normed.shape[0]
+def keyval_kernel(normed, weight, cosine, sine, keys, values, turned):
     heads = weight.shape[2] // HD
-    stride = 2 * heads
     for head in range(heads):
         span = slice(head * HD, (head + 1) * HD)
         product = jnp.dot(
@@ -277,6 +275,29 @@
         keys[:, span] = rotated(product[:, :HD], cosine[...], sine[...]).astype(jnp.bfloat16)
         values[:, span] = product[:, HD:].astype(jnp.bfloat16)
     turn_heads(values, turned)
+
+
+def project_keyval(normed, weight, cosine, sine):
+    rows, depth = normed.shape
+    width = weight.shape[2]
+    flat = jax.ShapeDtypeStruct((rows, width), jnp.bfloat16)
+    return pl.pallas_call(
+        keyval_kernel,
+        in_specs=[VMEM] * 4,
+        out_specs=[VMEM] * 3,
+        out_shape=[flat, flat, jax.ShapeDtypeStruct((width, rows), jnp.bfloat16)],
+        compiler_params=params(20),
+        cost_estimate=cost(4 * rows * depth * width, 4 * depth * width),
+        name="project_keyval",
+    )(normed, weight, cosine, sine)
+
+
+def weave_kernel(keys, values, *refs):
+    cache, token = refs[-2:]
+    token[...] = jnp.zeros_like(token)
+    rows, width = keys.shape
+    heads = width // HD
+    stride = 2 * heads
     order = order_rows(stride, True)
     places = 2 * HD // stride
     for start in range(0, rows, 2 * places):
@@ -296,26 +317,23 @@
             cache[at * stride : (at + places) * stride, :] = tile
 
 
-def project_keyval(normed, weight, cosine, sine):
-    rows, depth = normed.shape
-    width = weight.shape[2]
+def weave(keys, values, *earlier):
+    rows, width = keys.shape
     heads = width // HD
-    keys, turned, cache = pl.pallas_call(
-        keyval_kernel,
-        in_specs=[VMEM] * 4,
-        out_specs=[VMEM] * 3,
+    cache, token = pl.pallas_call(
+        weave_kernel,
+        in_specs=[VMEM] * (2 + len(earlier)),
+        out_specs=[VMEM] * 2,
         out_shape=[
-            jax.ShapeDtypeStruct((rows, width), jnp.bfloat16),
-            jax.ShapeDtypeStruct((width, rows), jnp.bfloat16),
             jax.ShapeDtypeStruct((rows * heads * 2, HD), jnp.bfloat16),
+            jax.ShapeDtypeStruct((8, HD), jnp.float32),
         ],
-        scratch_shapes=[pltpu.VMEM((rows, width), jnp.bfloat16)],
-        compiler_params=params(20),
-        cost_estimate=cost(4 * rows * depth * width, 4 * depth * width),
-        name="project_keyval",
-    )(normed, weight, cosine, sine)
+        compiler_params=params(16),
+        cost_estimate=cost(2**10 * rows * width, 8 * rows * width),
+        name="weave_cache",
+    )(keys, values, *earlier)
     cache = cache.reshape(rows, heads, 2, HD).transpose(0, 2, 1, 3)
-    return keys, turned, cache.reshape(rows, 2, width)
+    return cache.reshape(rows, 2, width), token
 
 
 def attend_kernel(spec, *refs):
@@ -548,7 +566,7 @@
 
 
 def combine_kernel(*refs):
-    result, extent, *parts, weight, attended, sent = refs
+    result, extent, *parts, weight, _, attended, sent = refs
     width, rows = result.shape
     heads = width // HD
     extents = [extent[:heads, :]]
@@ -576,12 +594,12 @@
         ).astype(jnp.bfloat16)
 
 
-def combine(result, extent, parts, w_out, ways):
+def combine(result, extent, parts, w_out, token, ways):
     width, rows = result.shape
     columns = w_out.shape[1] // ways
     return pl.pallas_call(
         combine_kernel,
-        in_specs=[VMEM] * (3 + len(parts)),
+        in_specs=[VMEM] * (4 + len(parts)),
         out_specs=[VMEM] * 2,
         out_shape=[
             jax.ShapeDtypeStruct((rows, width), jnp.bfloat16),
@@ -590,7 +608,7 @@
         compiler_params=params(20),
         cost_estimate=cost(2 * rows * width * columns * (ways - 1), 2 * width * w_out.shape[1]),
         name="combine_send",
-    )(result, extent, *parts, w_out)
+    )(result, extent, *parts, w_out, token)
 
 
 def keep_kernel(attended, weight, hidden, kept):
@@ -649,38 +667,44 @@
 
     step(0)
     step(1)
-    cosine, sine = angles(tail_len, shared_len, rows)
     weight = part_weights(w_keyval)
     step(0, weight)
-    pieces[0] = after(pieces[0], weight)
+    cosine, sine = angles(after(tail_len, weight), shared_len, rows)
+    pieces[0] = after(pieces[0], weight, ahead[0][1], behind[1][1])
     query, normed = project_query(pieces, w_query, cosine, sine)
     queries = [query] + [swap(query, "seq", shift) for shift in range(1, group)]
     tail = viewed(tail_cache.reshape(-1, 2, tail_cache.shape[3]))
     slots = tail_cache.shape[0]
     own_block = part_keyval([tail, prompt], width, "part_own")
-    step(1, own_block[0], query)
-    fresh_keys, fresh_turned, new_cache = project_keyval(normed, weight, cosine, sine)
+    step(1, query)
+    ready = after(cosine, ahead[1][1], behind[0][1])
+    fresh_keys, fresh_values, fresh_turned = project_keyval(normed, weight, ready, sine)
     step(0, fresh_keys)
-    blocks, rings = arrived(1)
+    blocks, near_rings = arrived(1)
     near_block = part_keyval(blocks, width, "part_near")
+    step(1, near_block[0])
 
     table = tail_table.T
-    facts = (tail_len, shared_len, table)
     others = list(range(1, group))
-    near = (
-        [(0, 0, piece), *rings],
+    near_rings = [(0, 0, piece), *near_rings]
+    near = [*own_block, *near_block]
+    fresh = [fresh_keys, fresh_turned]
+    facts = (after(tail_len, ahead[1][2], behind[0][2]), shared_len, table)
+    theirs, _ = attend(
+        facts,
+        queries,
+        others,
+        near_rings,
         slots,
         piece,
-        [*own_block, *near_block, fresh_keys, fresh_turned],
+        near + fresh,
         True,
         None,
         False,
+        "attend_near_others",
     )
-    own, _ = attend(facts, queries, [0], *near, "attend_near_own")
-    step(1, own[0][1])
-    ready = (after(tail_len, own[0][1]), shared_len, table)
-    theirs, _ = attend(ready, queries, others, *near, "attend_near_others")
     step(0, theirs[1][1])
+    facts = (tail_len, shared_len, table)
     rest = []
     rest_rings = []
     for hop in range(2, half):
@@ -698,12 +722,23 @@
     )
     rest += parted
     rest_rings += rings
-    ready = (after(tail_len, theirs[1][0]), shared_len, table)
+    facts = (after(tail_len, theirs[1][0]), shared_len, table)
     own, _ = attend(
-        ready, queries, [0], rest_rings, 0, piece, rest, True, own, True, "attend_rest_own"
+        facts,
+        queries,
+        [0],
+        near_rings + rest_rings,
+        slots,
+        piece,
+        near + rest + fresh,
+        True,
+        None,
+        True,
+        "attend_own",
     )
+    new_cache, token = weave(fresh_keys, fresh_values, theirs[1][0])
     parts = [swap(theirs[shift][0], "seq", shift) for shift in others]
-    attended, sent = combine(*own[0], parts, w_out, ways)
+    attended, sent = combine(*own[0], parts, w_out, token, ways)
     received = [swap(sent[shift - 1], "tp", shift) for shift in range(1, ways)]
     total = keep(attended, w_out, hidden_in)
     for part in received:

time: 70.6 us -> 69 us (0.977)
  Pallas kernels: 34.3 us -> 32.5 us
  waiting for transfers between devices: 13.1 us -> 14.2 us
    ppermute x14, waiting for transfers between devices: 2.94 us -> 9.72 us  [turn(): return lax.ppermute(value, 'seq', pairs)]
    ppermute x4, waiting for transfers between devices: 10.2 us -> 4.51 us  [swap(): return lax.ppermute(value, axis, pairs)]
    pallas_call x6 -> x5, Pallas kernels: 18.7 us -> 16.9 us  [attend(): pl.pallas_call(functools.partial(attend_kernel, (group, shifts, rings, sl...]
    pallas_call x1, Pallas kernels: 4.03 us -> 2.54 us  [project_keyval(): pl.pallas_call(keyval_kernel, in_specs=[VMEM] * 4, out_specs=[VMEM] * 3,...]
    pallas_call x1 -> x2, Pallas kernels: 1.04 us -> 2.45 us  [the longest x1 1.42 us: weave(): pl.pallas_call(weave_kernel, in_specs=[VMEM] * (2 + len(earlier)), out_sp...]
  transfers between devices with their start and end apart: 18 -> 18, of which waited for: 4 -> 7; matrix products, arithmetic and copies ran while one was open for 1% -> 1% of each run, Pallas kernels for 45% -> 43%
where the time goes in v9:
time: 69 us; the launch traced here: 68.9 us
  Pallas kernels  32.5 us (47%)
  starting transfers between devices  17.7 us (26%)
  waiting for transfers between devices  14.2 us (21%)
  between operations  1.59 us (2%)
  local copies, waits for them, and re-layouts  1.43 us (2%)
  other arithmetic  1.42 us (2%)
    pallas_call x5, Pallas kernels, attend(): pl.pallas_call(functools.partial(attend_kernel, (group, shifts, rings, sl...  16.9 us
    ppermute x14, starting transfers between devices, turn(): return lax.ppermute(value, 'seq', pairs)  15.4 us
    ppermute x14, waiting for transfers between devices, turn(): return lax.ppermute(value, 'seq', pairs)  9.72 us
    pallas_call x1, Pallas kernels, part_weights(): pl.pallas_call(weight_kernel, in_specs=[HBM], out_specs=VMEM, out_shape=j...  5.5 us
    ppermute x4, waiting for transfers between devices, swap(): return lax.ppermute(value, axis, pairs)  4.51 us
    pallas_call x1, Pallas kernels, project_keyval(): pl.pallas_call(keyval_kernel, in_specs=[VMEM] * 4, out_specs=[VMEM] * 3,...  2.54 us
    ppermute x4, starting transfers between devices, swap(): return lax.ppermute(value, axis, pairs)  2.39 us
    pallas_call x1, Pallas kernels, project_query(): pl.pallas_call(query_kernel, in_specs=[VMEM] * (len(pieces) + 3), out_spe...  2.02 us
  transfers between devices with their start and end apart: 18, of which 7 were waited for; matrix products, arithmetic and copies ran while one was open for 1% of the time, Pallas kernels for 43%

profile of v9, /device:TPU:0, one launch (start us, length us, event | category | flops | bytes accessed | tf_op | source)
XLA Modules:
  0.0 68.9 jit_solution(13341328023391688426)
XLA Ops:
  0.6 1.4 %fusion.4 = (bf16[64,8,2,128]{3,2,1,0:T(2,128)(2,1)S(1)}, bf16[64,8,2,128]{3,2,1,0:T(2,128)(2,1)S(1)}) fusion(bf16[128,8,2,128]{3,2,1,0:T(2,128)(2,1)} %bitcast.24), kind=kLoop, calls=%fused_computation.9 | loop fusion | bytes 1048576 | tf_op jit(solution)/shard_map/slice | solution.py:652
  2.0 3.0 %collective-permute-start.6 = (bf16[1024,128]{1,0:T(8,128)(2,1)S(1)}, bf16[1024,128]{1,0:T(8,128)(2,1)S(1)}, u32[]{:S(2)}, u32[]{:S(2)}) collective-permute-start(bf16[1024,128]{1,0:T(8,128)(2,1)S(1)} %bitcast.36), channel_id=1, source_target_pairs={{0,4},{2,6},{8,0},{10,2},{16,8},{18,10},{24,16},{26,18},{28,24},{3... | collective-permute-start | bytes 786440 | tf_op jit(solution)/shard_map/ppermute | solution.py:50
  5.2 2.0 %collective-permute-start.5 = (bf16[1024,128]{1,0:T(8,128)(2,1)S(1)}, bf16[1024,128]{1,0:T(8,128)(2,1)S(1)}, u32[]{:S(2)}, u32[]{:S(2)}) collective-permute-start(bf16[1024,128]{1,0:T(8,128)(2,1)S(1)} %bitcast.34), channel_id=1, source_target_pairs={{0,8},{2,10},{8,16},{10,18},{16,24},{18,26},{24,28},{26,30},{28,20... | collective-permute-start | bytes 786440 | tf_op jit(solution)/shard_map/ppermute | solution.py:50
  7.2 5.5 %part_weights.1.weight = bf16[2,2048,1024]{2,1,0:T(8,128)(2,1)S(1)} custom-call(bf16[32768,128]{1,0:T(8,128)(2,1)} %bitcast.33), custom_call_target="tpu_custom_call" | custom-call | flops 2147483648 | bytes 16777216 | tf_op jit(solution)/shard_map/part_weights/pallas_call | solution.py:251
  13.5 0.6 positions.1
  14.6 2.4 %collective-permute-done.1.refs_3_ = bf16[1024,128]{1,0:T(8,128)(2,1)S(1)} collective-permute-done((bf16[1024,128]{1,0:T(8,128)(2,1)S(1)}, bf16[1024,128]{1,0:T(8,128)(2,1)S(1)}, u32[]{:S(2)}, u32[]{:S(2)}) %collective-permute-start.1) | collective-permute-done | bytes 262176 | tf_op jit(solution)/shard_map/ppermute | solution.py:50
  17.0 2.0 %project_query.1 = (bf16[256,1024]{1,0:T(8,128)(2,1)S(1)}, bf16[256,2048]{1,0:T(8,128)(2,1)S(1)}) custom-call(bf16[256,1024]{1,0:T(8,128)(2,1)S(1)} %copy-done.3, bf16[256,1024]{1,0:T(8,128)(2,1)S(1)} %collective-permute-done.2.refs_1_, bf16[2048,1024]{1,0:T(8,128)(2,1)S(1)} %copy-done.1, f32[256,128]{1,0:T(8,128)S(1)} %get-tuple-element.50.refs_3_.cosine, ...), custom_call_target="tpu_custom_call" | custom-call | flops 1073741824 | bytes 4194304 | tf_op jit(solution)/shard_map/project_query/pallas_call | solution.py:212
  19.1 1.7 %collective-permute-start.3 = (bf16[256,1024]{1,0:T(8,128)(2,1)S(1)}, bf16[256,1024]{1,0:T(8,128)(2,1)S(1)}, u32[]{:S(2)}, u32[]{:S(2)}) collective-permute-start(bf16[256,1024]{1,0:T(8,128)(2,1)S(1)} %get-tuple-element.47.refs_3_), channel_id=1, source_target_pairs={{0,2},{2,0},{4,6},{6,4},{8,10},{10,8},{12,14},{14,12},{16,18},{18,... | collective-permute-start | bytes 1572872 | tf_op jit(solution)/shard_map/ppermute | solution.py:41
  20.8 1.5 %collective-permute-start.11 = (bf16[1024,128]{1,0:T(8,128)(2,1)S(1)}, bf16[1024,128]{1,0:T(8,128)(2,1)S(1)}, u32[]{:S(2)}, u32[]{:S(2)}) collective-permute-start(bf16[1024,128]{1,0:T(8,128)(2,1)S(1)} %collective-permute-done.1.refs_3_), channel_id=1, source_target_pairs={{0,4},{2,6},{8,0},{10,2},{16,8},{18,10},{24,16},{26,18},{28,24},{3... | collective-permute-start | bytes 786440 | tf_op jit(solution)/shard_map/ppermute | solution.py:50
  22.8 1.6 %collective-permute-start.8 = (bf16[1024,128]{1,0:T(8,128)(2,1)S(1)}, bf16[1024,128]{1,0:T(8,128)(2,1)S(1)}, u32[]{:S(2)}, u32[]{:S(2)}) collective-permute-start(bf16[1024,128]{1,0:T(8,128)(2,1)S(1)} %collective-permute-done.5.refs_1_), channel_id=1, source_target_pairs={{0,8},{2,10},{8,16},{10,18},{16,24},{18,26},{24,28},{26,30},{28,20... | collective-permute-start | bytes 786440 | tf_op jit(solution)/shard_map/ppermute | solution.py:50
  24.9 2.5 %project_keyval.1 = (bf16[256,1024]{1,0:T(8,128)(2,1)S(1)}, bf16[256,1024]{1,0:T(8,128)(2,1)S(1)}, bf16[1024,256]{1,0:T(8,128)(2,1)S(1)}) custom-call(bf16[256,2048]{1,0:T(8,128)(2,1)S(1)} %get-tuple-element.49.normed, bf16[2,2048,1024]{2,1,0:T(8,128)(2,1)S(1)} %part_weights.1.weight, f32[256,128]{1,0:T(8,128)S(1)} %get-tuple-element.50.refs_3_.cosine, ...), custom_call_target="tpu_custom_call" | custom-call | flops 2147483648 | bytes 8388608 | tf_op jit(solution)/shard_map/project_keyval/pallas_call | solution.py:284
  27.4 2.6 %collective-permute-done.11.refs_7_ = bf16[1024,128]{1,0:T(8,128)(2,1)S(1)} collective-permute-done((bf16[1024,128]{1,0:T(8,128)(2,1)S(1)}, bf16[1024,128]{1,0:T(8,128)(2,1)S(1)}, u32[]{:S(2)}, u32[]{:S(2)}) %collective-permute-start.11) | collective-permute-done | bytes 262176 | tf_op jit(solution)/shard_map/ppermute | solution.py:50
  30.0 1.5 %collective-permute-start.12 = (bf16[1024,128]{1,0:T(8,128)(2,1)S(1)}, bf16[1024,128]{1,0:T(8,128)(2,1)S(1)}, u32[]{:S(2)}, u32[]{:S(2)}) collective-permute-start(bf16[1024,128]{1,0:T(8,128)(2,1)S(1)} %collective-permute-done.11.refs_7_), channel_id=1, source_target_pairs={{0,4},{2,6},{8,0},{10,2},{16,8},{18,10},{24,16},{26,18},{28,24},{3... | collective-permute-start | bytes 786440 | tf_op jit(solution)/shard_map/ppermute | solution.py:50
  32.1 1.0 %part_own.1 = (bf16[384,1024]{1,0:T(8,128)(2,1)S(1)}, bf16[1024,384]{1,0:T(8,128)(2,1)S(1)}) custom-call(bf16[4096,128]{1,0:T(8,128)(2,1)S(1)} %bitcast.26, bf16[2048,128]{1,0:T(8,128)(2,1)S(1)} %bitcast.25), custom_call_target="tpu_custom_call" | custom-call | flops 402653184 | bytes 3145728 | tf_op jit(solution)/shard_map/part_own/pallas_call | solution.py:170
  33.1 0.7 %part_near.1 = (bf16[256,1024]{1,0:T(8,128)(2,1)S(1)}, bf16[1024,256]{1,0:T(8,128)(2,1)S(1)}) custom-call(bf16[1024,128]{1,0:T(8,128)(2,1)S(1)} %collective-permute-done.refs_0_, bf16[1024,128]{1,0:T(8,128)(2,1)S(1)} %collective-permute-done.5.refs_1_, bf16[1024,128]{1,0:T(8,128)(2,1)S(1)} %collective-permute-done.6.refs_2_, ...), custom_call_target="tpu_custom_call" | custom-call | flops 268435456 | bytes 2097152 | tf_op jit(solution)/shard_map/part_near/pallas_call | solution.py:170
  33.8 3.4 %collective-permute-done.8.refs_5_ = bf16[1024,128]{1,0:T(8,128)(2,1)S(1)} collective-permute-done((bf16[1024,128]{1,0:T(8,128)(2,1)S(1)}, bf16[1024,128]{1,0:T(8,128)(2,1)S(1)}, u32[]{:S(2)}, u32[]{:S(2)}) %collective-permute-start.8) | collective-permute-done | bytes 262176 | tf_op jit(solution)/shard_map/ppermute | solution.py:50
  37.7 1.5 %collective-permute-start.15 = (bf16[1024,128]{1,0:T(8,128)(2,1)S(1)}, bf16[1024,128]{1,0:T(8,128)(2,1)S(1)}, u32[]{:S(2)}, u32[]{:S(2)}) collective-permute-start(bf16[1024,128]{1,0:T(8,128)(2,1)S(1)} %collective-permute-done.9.refs_6_), channel_id=1, source_target_pairs={{0,4},{2,6},{8,0},{10,2},{16,8},{18,10},{24,16},{26,18},{28,24},{3... | collective-permute-start | bytes 786440 | tf_op jit(solution)/shard_map/ppermute | solution.py:50
  39.2 4.3 %attend_near_others.1 = (f32[1024,256]{1,0:T(8,128)S(1)}, f32[8,256]{1,0:T(8,128)S(1)}) custom-call(s32[8]{0:T(128)S(1)} %copy-done.6, s32[1]{0:T(128)S(6)} %copy.15.shared.refs_1_, s32[4,8]{1,0:T(4,128)S(1)} %bitcast.27, bf16[256,1024]{1,0:T(8,128)(2,1)S(1)} %collective-permute-done.3.refs_3_, bf16[384,1024]{1,0:T(8,128)(2,1)S(1)} %get-tuple-element.56.refs_4_, ...), custom_call_target="tpu_custom_call" | custom-call | flops 939524096 | bytes 3670016 | tf_op jit(solution)/shard_map/attend_near_others/pallas_call | solution.py:548
  43.6 0.5 collective-permute-start.10
  44.1 1.5 %collective-permute-start.13 = (bf16[1024,128]{1,0:T(8,128)(2,1)S(1)}, bf16[1024,128]{1,0:T(8,128)(2,1)S(1)}, u32[]{:S(2)}, u32[]{:S(2)}) collective-permute-start(bf16[1024,128]{1,0:T(8,128)(2,1)S(1)} %collective-permute-done.12.refs_7_), channel_id=1, source_target_pairs={{0,4},{2,6},{8,0},{10,2},{16,8},{18,10},{24,16},{26,18},{28,24},{3... | collective-permute-start | bytes 786440 | tf_op jit(solution)/shard_map/ppermute | solution.py:50
  45.7 2.2 %attend_hop2_others.1 = (f32[1024,256]{1,0:T(8,128)S(1)}, f32[8,256]{1,0:T(8,128)S(1)}, bf16[256,1024]{1,0:T(8,128)(2,1)S(1)}, bf16[1024,256]{1,0:T(8,128)(2,1)S(1)}) custom-call(s32[8]{0:T(128)S(1)} %copy-done.6, s32[1]{0:T(128)S(6)} %copy.15.shared.refs_1_, s32[4,8]{1,0:T(4,128)S(1)} %bitcast.28, bf16[256,1024]{1,0:T(8,128)(2,1)S(1)} %collective-permute-done.3.refs_3_, ...), custom_call_target="tpu_custom_call" | custom-call | flops 268435456 | bytes 1048576 | tf_op jit(solution)/shard_map/attend_hop2_others/pallas_call | solution.py:548
  48.4 2.2 %attend_hop3_others.1 = (f32[1024,256]{1,0:T(8,128)S(1)}, f32[8,256]{1,0:T(8,128)S(1)}, bf16[256,1024]{1,0:T(8,128)(2,1)S(1)}, bf16[1024,256]{1,0:T(8,128)(2,1)S(1)}) custom-call(s32[8]{0:T(128)S(1)} %copy-done.6, s32[1]{0:T(128)S(6)} %copy.15.shared.refs_1_, s32[4,8]{1,0:T(4,128)S(1)} %bitcast.29, bf16[256,1024]{1,0:T(8,128)(2,1)S(1)} %collective-permute-done.3.refs_3_, ...), custom_call_target="tpu_custom_call" | custom-call | flops 268435456 | bytes 1048576 | tf_op jit(solution)/shard_map/attend_hop3_others/pallas_call | solution.py:548
  50.7 0.7 %collective-permute-done.10.refs_4_ = bf16[1024,128]{1,0:T(8,128)(2,1)S(1)} collective-permute-done((bf16[1024,128]{1,0:T(8,128)(2,1)S(1)}, bf16[1024,128]{1,0:T(8,128)(2,1)S(1)}, u32[]{:S(2)}, u32[]{:S(2)}) %collective-permute-start.10) | collective-permute-done | bytes 262176 | tf_op jit(solution)/shard_map/ppermute | solution.py:50
  51.4 1.8 %attend_far_others.1 = (bf16[1056,256]{1,0:T(8,128)(2,1)S(1)}, bf16[128,1024]{1,0:T(8,128)(2,1)S(1)}, bf16[1024,128]{1,0:T(8,128)(2,1)S(1)}) custom-call(s32[8]{0:T(128)S(1)} %copy-done.6, s32[1]{0:T(128)S(6)} %copy.15.shared.refs_1_, s32[4,8]{1,0:T(4,128)S(1)} %bitcast.30, bf16[256,1024]{1,0:T(8,128)(2,1)S(1)} %collective-permute-done.3.refs_3_, ...), custom_call_target="tpu_custom_call" | custom-call | flops 134217728 | bytes 524288 | tf_op jit(solution)/shard_map/attend_far_others/pallas_call | solution.py:548
  53.2 0.6 collective-permute-start.16
  53.8 1.4 %weave_cache.1 = (bf16[4096,128]{1,0:T(8,128)(2,1)}, f32[8,128]{1,0:T(8,128)S(1)}) custom-call(bf16[256,1024]{1,0:T(8,128)(2,1)S(1)} %get-tuple-element.51.refs_8_.refs_14_.keys, bf16[256,1024]{1,0:T(8,128)(2,1)S(1)} %get-tuple-element.83.values, bf16[1056,256]{1,0:T(8,128)(2,1)S(1)} %get-tuple-element.73.refs_0_), custom_call_target="tpu_custom_call" | custom-call | flops 268435456 | bytes 2097152 | tf_op jit(solution)/shard_map/weave_cache/pallas_call | solution.py:323
  55.2 6.3 %attend_own.1 = (f32[1024,256]{1,0:T(8,128)S(1)}, f32[8,256]{1,0:T(8,128)S(1)}) custom-call(s32[8]{0:T(128)S(1)} %copy-done.6, s32[1]{0:T(128)S(6)} %copy.15.shared.refs_1_, s32[4,8]{1,0:T(4,128)S(1)} %bitcast.31, bf16[256,1024]{1,0:T(8,128)(2,1)S(1)} %get-tuple-element.47.refs_3_, bf16[384,1024]{1,0:T(8,128)(2,1)S(1)} %get-tuple-element.56.refs_4_, ...), custom_call_target="tpu_custom_call" | custom-call | flops 1610612736 | bytes 6291456 | tf_op jit(solution)/shard_map/attend_own/pallas_call | solution.py:548
  61.6 3.3 %collective-permute-done.16.refs_2_ = bf16[1056,256]{1,0:T(8,128)(2,1)S(1)} collective-permute-done((bf16[1056,256]{1,0:T(8,128)(2,1)S(1)}, bf16[1056,256]{1,0:T(8,128)(2,1)S(1)}, u32[]{:S(2)}, u32[]{:S(2)}) %collective-permute-start.16) | collective-permute-done | bytes 540704 | tf_op jit(solution)/shard_map/ppermute | solution.py:41
  64.9 1.0 %combine_send.1 = (bf16[256,1024]{1,0:T(8,128)(2,1)S(1)}, bf16[1,256,1024]{2,1,0:T(8,128)(2,1)S(1)}) custom-call(f32[1024,256]{1,0:T(8,128)S(1)} %get-tuple-element.81.refs_0_, f32[8,256]{1,0:T(8,128)S(1)} %get-tuple-element.82.refs_1_, bf16[1056,256]{1,0:T(8,128)(2,1)S(1)} %collective-permute-done.16.refs_2_, bf16[1024,2048]{1,0:T(8,128)(2,1)S(1)} %copy-done, ...), custom_call_target="tpu_custom_call" | custom-call | flops 536870912 | bytes 4194304 | tf_op jit(solution)/shard_map/combine_send/pallas_call | solution.py:600
  66.0 0.7 %keep_own.1 = f32[256,1024]{1,0:T(8,128)S(1)} custom-call(bf16[256,1024]{1,0:T(8,128)(2,1)S(1)} %get-tuple-element.85.attended, bf16[1024,2048]{1,0:T(8,128)(2,1)S(1)} %copy-done, bf16[256,1024]{1,0:T(8,128)(2,1)S(1)} %copy-done.3), custom_call_target="tpu_custom_call" | custom-call | flops 536870912 | bytes 4194304 | tf_op jit(solution)/shard_map/keep_own/pallas_call | solution.py:626
  66.8 1.2 %collective-permute-done.17 = bf16[256,1024]{1,0:T(8,128)(2,1)S(1)} collective-permute-done((bf16[256,1024]{1,0:T(8,128)(2,1)S(1)}, bf16[256,1024]{1,0:T(8,128)(2,1)S(1)}, u32[]{:S(2)}, u32[]{:S(2)}) %collective-permute-start.17) | collective-permute-done | bytes 524320 | tf_op jit(solution)/shard_map/ppermute | solution.py:41
  67.9 0.9 %add_convert_fusion = bf16[256,1024]{1,0:T(8,128)(2,1)} fusion(f32[256,1024]{1,0:T(8,128)S(1)} %keep_own.1, bf16[256,1024]{1,0:T(8,128)(2,1)S(1)} %collective-permute-done.17), kind=kLoop, calls=%fused_computation | loop fusion | flops 786432 | bytes 2097152 | tf_op jit(solution)/shard_map/convert_element_type | solution.py:746
  (36 shorter events, 3.2 us)
Async XLA Ops:
  2.0 20.8 %collective-permute-start.6 = (bf16[1024,128]{1,0:T(8,128)(2,1)S(1)}, bf16[1024,128]{1,0:T(8,128)(2,1)S(1)}, u32[]{:S(2)}, u32[]{:S(2)}) collective-permute-start(bf16[1024,128]{1,0:T(8,128)(2,1)S(1)} %bitcast.36), channel_id=1, source_target_pairs={{0,4},{2,6},{8,0},{10,2},{16,8},{18,10},{24,16},{26,18},{28,24},{3... | collective-permute-start | bytes 786440 | tf_op jit(solution)/shard_map/ppermute | solution.py:50
  5.0 9.5 %collective-permute-start = (bf16[1024,128]{1,0:T(8,128)(2,1)S(1)}, bf16[1024,128]{1,0:T(8,128)(2,1)S(1)}, u32[]{:S(2)}, u32[]{:S(2)}) collective-permute-start(bf16[1024,128]{1,0:T(8,128)(2,1)S(1)} %bitcast.37), channel_id=1, source_target_pairs={{0,8},{2,10},{8,16},{10,18},{16,24},{18,26},{24,28},{26,30},{28,20... | collective-permute-start | bytes 786440 | tf_op jit(solution)/shard_map/ppermute | solution.py:50
  5.2 17.7 %collective-permute-start.5 = (bf16[1024,128]{1,0:T(8,128)(2,1)S(1)}, bf16[1024,128]{1,0:T(8,128)(2,1)S(1)}, u32[]{:S(2)}, u32[]{:S(2)}) collective-permute-start(bf16[1024,128]{1,0:T(8,128)(2,1)S(1)} %bitcast.34), channel_id=1, source_target_pairs={{0,8},{2,10},{8,16},{10,18},{16,24},{18,26},{24,28},{26,30},{28,20... | collective-permute-start | bytes 786440 | tf_op jit(solution)/shard_map/ppermute | solution.py:50
  7.1 9.9 %collective-permute-start.1 = (bf16[1024,128]{1,0:T(8,128)(2,1)S(1)}, bf16[1024,128]{1,0:T(8,128)(2,1)S(1)}, u32[]{:S(2)}, u32[]{:S(2)}) collective-permute-start(bf16[1024,128]{1,0:T(8,128)(2,1)S(1)} %bitcast.35), channel_id=1, source_target_pairs={{0,4},{2,6},{8,0},{10,2},{16,8},{18,10},{24,16},{26,18},{28,24},{3... | collective-permute-start | bytes 786440 | tf_op jit(solution)/shard_map/ppermute | solution.py:50
  7.2 9.8 %collective-permute-start.2 = (bf16[256,1024]{1,0:T(8,128)(2,1)}, bf16[256,1024]{1,0:T(8,128)(2,1)S(1)}, u32[]{:S(2)}, u32[]{:S(2)}) collective-permute-start(bf16[256,1024]{1,0:T(8,128)(2,1)} %hidden.1), channel_id=1, source_target_pairs={{0,1},{1,0},{2,3},{3,2},{4,5},{5,4},{6,7},{7,6},{8,9},{9,8},{10,11... | collective-permute-start | bytes 1572872 | tf_op jit(solution)/shard_map/ppermute | solution.py:41
  7.2 6.3 %copy-start.6 = (s32[8]{0:T(128)S(1)}, s32[8]{0:T(128)}, u32[]{:S(2)}) copy-start(s32[8]{0:T(128)} %refs_0_.8) | copy-start | bytes 100
  7.2 9.8 %copy-start.1 = (bf16[2048,1024]{1,0:T(8,128)(2,1)S(1)}, bf16[2048,1024]{1,0:T(8,128)(2,1)}, u32[]{:S(2)}) copy-start(bf16[2048,1024]{1,0:T(8,128)(2,1)} %refs_2_.1) | copy-start | bytes 12582916
  7.2 9.8 %copy-start.3 = (bf16[256,1024]{1,0:T(8,128)(2,1)S(1)}, bf16[256,1024]{1,0:T(8,128)(2,1)}, u32[]{:S(2)}) copy-start(bf16[256,1024]{1,0:T(8,128)(2,1)} %hidden.1) | copy-start | bytes 1572868
  12.7 19.4 %copy-start.2 = (bf16[128,2,1024]{2,1,0:T(2,128)(2,1)S(1)}, bf16[128,2,1024]{2,1,0:T(2,128)(2,1)}, u32[]{:S(2)}) copy-start(bf16[128,2,1024]{2,1,0:T(2,128)(2,1)} %param.13) | copy-start | bytes 1572868
  12.7 19.3 %copy-start.4 = (bf16[2,128,2,1024]{3,2,1,0:T(2,128)(2,1)S(1)}, bf16[2,128,2,1024]{3,2,1,0:T(2,128)(2,1)}, u32[]{:S(2)}) copy-start(bf16[2,128,2,1024]{3,2,1,0:T(2,128)(2,1)} %param.14) | copy-start | bytes 3145732
  17.0 22.2 %copy-start.5 = (s32[8,4]{0,1:T(4,128)S(1)}, s32[8,4]{0,1:T(4,128)}, u32[]{:S(2)}) copy-start(s32[8,4]{0,1:T(4,128)} %param.15) | copy-start | bytes 388
  19.1 20.2 %collective-permute-start.3 = (bf16[256,1024]{1,0:T(8,128)(2,1)S(1)}, bf16[256,1024]{1,0:T(8,128)(2,1)S(1)}, u32[]{:S(2)}, u32[]{:S(2)}) collective-permute-start(bf16[256,1024]{1,0:T(8,128)(2,1)S(1)} %get-tuple-element.47.refs_3_), channel_id=1, source_target_pairs={{0,2},{2,0},{4,6},{6,4},{8,10},{10,8},{12,14},{14,12},{16,18},{18,... | collective-permute-start | bytes 1572872 | tf_op jit(solution)/shard_map/ppermute | solution.py:41
  20.8 9.2 %collective-permute-start.11 = (bf16[1024,128]{1,0:T(8,128)(2,1)S(1)}, bf16[1024,128]{1,0:T(8,128)(2,1)S(1)}, u32[]{:S(2)}, u32[]{:S(2)}) collective-permute-start(bf16[1024,128]{1,0:T(8,128)(2,1)S(1)} %collective-permute-done.1.refs_3_), channel_id=1, source_target_pairs={{0,4},{2,6},{8,0},{10,2},{16,8},{18,10},{24,16},{26,18},{28,24},{3... | collective-permute-start | bytes 786440 | tf_op jit(solution)/shard_map/ppermute | solution.py:50
  22.3 9.2 %collective-permute-start.4 = (bf16[1024,128]{1,0:T(8,128)(2,1)S(1)}, bf16[1024,128]{1,0:T(8,128)(2,1)S(1)}, u32[]{:S(2)}, u32[]{:S(2)}) collective-permute-start(bf16[1024,128]{1,0:T(8,128)(2,1)S(1)} %collective-permute-done.refs_0_), channel_id=1, source_target_pairs={{0,8},{2,10},{8,16},{10,18},{16,24},{18,26},{24,28},{26,30},{28,20... | collective-permute-start | bytes 786440 | tf_op jit(solution)/shard_map/ppermute | solution.py:50
  22.8 14.4 %collective-permute-start.8 = (bf16[1024,128]{1,0:T(8,128)(2,1)S(1)}, bf16[1024,128]{1,0:T(8,128)(2,1)S(1)}, u32[]{:S(2)}, u32[]{:S(2)}) collective-permute-start(bf16[1024,128]{1,0:T(8,128)(2,1)S(1)} %collective-permute-done.5.refs_1_), channel_id=1, source_target_pairs={{0,8},{2,10},{8,16},{10,18},{16,24},{18,26},{24,28},{26,30},{28,20... | collective-permute-start | bytes 786440 | tf_op jit(solution)/shard_map/ppermute | solution.py:50
  24.4 13.3 %collective-permute-start.9 = (bf16[1024,128]{1,0:T(8,128)(2,1)S(1)}, bf16[1024,128]{1,0:T(8,128)(2,1)S(1)}, u32[]{:S(2)}, u32[]{:S(2)}) collective-permute-start(bf16[1024,128]{1,0:T(8,128)(2,1)S(1)} %collective-permute-done.6.refs_2_), channel_id=1, source_target_pairs={{0,4},{2,6},{8,0},{10,2},{16,8},{18,10},{24,16},{26,18},{28,24},{3... | collective-permute-start | bytes 786440 | tf_op jit(solution)/shard_map/ppermute | solution.py:50
  30.0 13.5 %collective-permute-start.12 = (bf16[1024,128]{1,0:T(8,128)(2,1)S(1)}, bf16[1024,128]{1,0:T(8,128)(2,1)S(1)}, u32[]{:S(2)}, u32[]{:S(2)}) collective-permute-start(bf16[1024,128]{1,0:T(8,128)(2,1)S(1)} %collective-permute-done.11.refs_7_), channel_id=1, source_target_pairs={{0,4},{2,6},{8,0},{10,2},{16,8},{18,10},{24,16},{26,18},{28,24},{3... | collective-permute-start | bytes 786440 | tf_op jit(solution)/shard_map/ppermute | solution.py:50
  31.6 12.0 %collective-permute-start.7 = (bf16[1024,128]{1,0:T(8,128)(2,1)S(1)}, bf16[1024,128]{1,0:T(8,128)(2,1)S(1)}, u32[]{:S(2)}, u32[]{:S(2)}) collective-permute-start(bf16[1024,128]{1,0:T(8,128)(2,1)S(1)} %collective-permute-done.4.refs_4_), channel_id=1, source_target_pairs={{0,8},{2,10},{8,16},{10,18},{16,24},{18,26},{24,28},{26,30},{28,20... | collective-permute-start | bytes 786440 | tf_op jit(solution)/shard_map/ppermute | solution.py:50
  37.2 11.2 %collective-permute-start.14 = (bf16[1024,128]{1,0:T(8,128)(2,1)S(1)}, bf16[1024,128]{1,0:T(8,128)(2,1)S(1)}, u32[]{:S(2)}, u32[]{:S(2)}) collective-permute-start(bf16[1024,128]{1,0:T(8,128)(2,1)S(1)} %collective-permute-done.8.refs_5_), channel_id=1, source_target_pairs={{0,8},{2,10},{8,16},{10,18},{16,24},{18,26},{24,28},{26,30},{28,20... | collective-permute-start | bytes 786440 | tf_op jit(solution)/shard_map/ppermute | solution.py:50
  37.7 10.8 %collective-permute-start.15 = (bf16[1024,128]{1,0:T(8,128)(2,1)S(1)}, bf16[1024,128]{1,0:T(8,128)(2,1)S(1)}, u32[]{:S(2)}, u32[]{:S(2)}) collective-permute-start(bf16[1024,128]{1,0:T(8,128)(2,1)S(1)} %collective-permute-done.9.refs_6_), channel_id=1, source_target_pairs={{0,4},{2,6},{8,0},{10,2},{16,8},{18,10},{24,16},{26,18},{28,24},{3... | collective-permute-start | bytes 786440 | tf_op jit(solution)/shard_map/ppermute | solution.py:50
  43.6 21.3 %copy-start = (bf16[1024,2048]{1,0:T(8,128)(2,1)S(1)}, bf16[1024,2048]{1,0:T(8,128)(2,1)}, u32[]{:S(2)}) copy-start(bf16[1024,2048]{1,0:T(8,128)(2,1)} %weight.1) | copy-start | bytes 12582916
  43.6 7.8 %collective-permute-start.10 = (bf16[1024,128]{1,0:T(8,128)(2,1)S(1)}, bf16[1024,128]{1,0:T(8,128)(2,1)S(1)}, u32[]{:S(2)}, u32[]{:S(2)}) collective-permute-start(bf16[1024,128]{1,0:T(8,128)(2,1)S(1)} %collective-permute-done.7.refs_4_), channel_id=1, source_target_pairs={{0,8},{2,10},{8,16},{10,18},{16,24},{18,26},{24,28},{26,30},{28,20... | collective-permute-start | bytes 786440 | tf_op jit(solution)/shard_map/ppermute | solution.py:50
  44.1 7.3 %collective-permute-start.13 = (bf16[1024,128]{1,0:T(8,128)(2,1)S(1)}, bf16[1024,128]{1,0:T(8,128)(2,1)S(1)}, u32[]{:S(2)}, u32[]{:S(2)}) collective-permute-start(bf16[1024,128]{1,0:T(8,128)(2,1)S(1)} %collective-permute-done.12.refs_7_), channel_id=1, source_target_pairs={{0,4},{2,6},{8,0},{10,2},{16,8},{18,10},{24,16},{26,18},{28,24},{3... | collective-permute-start | bytes 786440 | tf_op jit(solution)/shard_map/ppermute | solution.py:50
  53.2 11.7 %collective-permute-start.16 = (bf16[1056,256]{1,0:T(8,128)(2,1)S(1)}, bf16[1056,256]{1,0:T(8,128)(2,1)S(1)}, u32[]{:S(2)}, u32[]{:S(2)}) collective-permute-start(bf16[1056,256]{1,0:T(8,128)(2,1)S(1)} %get-tuple-element.73.refs_0_), channel_id=1, source_target_pairs={{0,2},{2,0},{4,6},{6,4},{8,10},{10,8},{12,14},{14,12},{16,18},{18,... | collective-permute-start | bytes 1622024 | tf_op jit(solution)/shard_map/ppermute | solution.py:41
  66.0 2.0 %collective-permute-start.17 = (bf16[256,1024]{1,0:T(8,128)(2,1)S(1)}, bf16[256,1024]{1,0:T(8,128)(2,1)S(1)}, u32[]{:S(2)}, u32[]{:S(2)}) collective-permute-start(bf16[256,1024]{1,0:T(8,128)(2,1)S(1)} %bitcast.32), channel_id=1, source_target_pairs={{0,1},{1,0},{2,3},{3,2},{4,5},{5,4},{6,7},{7,6},{8,9},{9,8},{10,11... | collective-permute-start | bytes 1572872 | tf_op jit(solution)/shard_map/ppermute | solution.py:41

commit v10 on v9

--- a/solution.py
+++ b/solution.py
@@ -649,9 +649,13 @@
 
     pieces = [hidden_in] + [swap(hidden_in, "tp", shift) for shift in range(1, ways)]
     prompt = viewed(prompt_cache)
-    halves = [prompt[: middle * stride], prompt[middle * stride :]]
-    ahead = {0: [halves[0]], 1: [halves[1]]}
-    behind = {0: [halves[0]], 1: [halves[1]]}
+    ahead, behind = {0: [None], 1: [None]}, {0: [None], 1: [None]}
+    nearest = []
+    for blocks, way in ((ahead, 1), (behind, -1)):
+        block = turn(prompt, cycle, group, way)
+        nearest.append(block)
+        blocks[0].append(block[: middle * stride])
+        blocks[1].append(block[middle * stride :])
 
     def step(which, *others):
         for blocks, part, way in ((ahead, which, 1), (behind, 1 - which, -1)):
@@ -665,31 +669,28 @@
         rings = [(sign * hop, part * middle, middle) for sign in (-1, 1) for part in (0, 1)]
         return blocks, rings
 
-    step(0)
-    step(1)
     weight = part_weights(w_keyval)
-    step(0, weight)
     cosine, sine = angles(after(tail_len, weight), shared_len, rows)
-    pieces[0] = after(pieces[0], weight, ahead[0][1], behind[1][1])
+    pieces[0] = after(pieces[0], weight)
     query, normed = project_query(pieces, w_query, cosine, sine)
     queries = [query] + [swap(query, "seq", shift) for shift in range(1, group)]
     tail = viewed(tail_cache.reshape(-1, 2, tail_cache.shape[3]))
     slots = tail_cache.shape[0]
     own_block = part_keyval([tail, prompt], width, "part_own")
+    step(0, weight, query)
     step(1, query)
     ready = after(cosine, ahead[1][1], behind[0][1])
     fresh_keys, fresh_values, fresh_turned = project_keyval(normed, weight, ready, sine)
     step(0, fresh_keys)
-    blocks, near_rings = arrived(1)
-    near_block = part_keyval(blocks, width, "part_near")
+    near_block = part_keyval(nearest, width, "part_near")
     step(1, near_block[0])
 
     table = tail_table.T
     others = list(range(1, group))
-    near_rings = [(0, 0, piece), *near_rings]
+    near_rings = [(0, 0, piece), (-1, 0, piece), (1, 0, piece)]
     near = [*own_block, *near_block]
     fresh = [fresh_keys, fresh_turned]
-    facts = (after(tail_len, ahead[1][2], behind[0][2]), shared_len, table)
+    facts = (tail_len, shared_len, table)
     theirs, _ = attend(
         facts,
         queries,

time: 69 us -> 65.6 us (0.951)
  local copies, waits for them, and re-layouts: 1.43 us -> 0.11 us
  starting transfers between devices: 17.7 us -> 16.7 us
  waiting for transfers between devices: 14.2 us -> 13.3 us
    ppermute x14 -> x12, starting transfers between devices: 15.4 us -> 13.4 us  [turn(): return lax.ppermute(value, 'seq', pairs)]
    slice x1 -> x2, local copies, waits for them, and re-layouts: 1.39 us -> 0.07 us  [local(): blocks[1].append(block[middle * stride:])]
    ppermute x14 -> x12, waiting for transfers between devices: 9.72 us -> 8.83 us  [turn(): return lax.ppermute(value, 'seq', pairs)]
    ppermute x4, starting transfers between devices: 2.39 us -> 3.24 us  [swap(): return lax.ppermute(value, axis, pairs)]
  transfers between devices with their start and end apart: 18 -> 16, of which waited for: 7 -> 8; matrix products, arithmetic and copies ran while one was open for 1% -> 1% of each run, Pallas kernels for 43% -> 45%
where the time goes in v10:
time: 65.6 us; the launch traced here: 65.5 us
  Pallas kernels  32.5 us (50%)
  starting transfers between devices  16.7 us (25%)
  waiting for transfers between devices  13.3 us (20%)
  between operations  1.49 us (2%)
  other arithmetic  1.42 us (2%)
    pallas_call x5, Pallas kernels, attend(): pl.pallas_call(functools.partial(attend_kernel, (group, shifts, rings, sl...  17 us
    ppermute x12, starting transfers between devices, turn(): return lax.ppermute(value, 'seq', pairs)  13.4 us
    ppermute x12, waiting for transfers between devices, turn(): return lax.ppermute(value, 'seq', pairs)  8.83 us
    pallas_call x1, Pallas kernels, part_weights(): pl.pallas_call(weight_kernel, in_specs=[HBM], out_specs=VMEM, out_shape=j...  5.5 us
    ppermute x4, waiting for transfers between devices, swap(): return lax.ppermute(value, axis, pairs)  4.48 us
    ppermute x4, starting transfers between devices, swap(): return lax.ppermute(value, axis, pairs)  3.24 us
    pallas_call x1, Pallas kernels, project_keyval(): pl.pallas_call(keyval_kernel, in_specs=[VMEM] * 4, out_specs=[VMEM] * 3,...  2.54 us
    pallas_call x1, Pallas kernels, project_query(): pl.pallas_call(query_kernel, in_specs=[VMEM] * (len(pieces) + 3), out_spe...  2.02 us
  transfers between devices with their start and end apart: 16, of which 8 were waited for; matrix products, arithmetic and copies ran while one was open for 1% of the time, Pallas kernels for 45%

profile of v10, /device:TPU:0, one launch (start us, length us, event | category | flops | bytes accessed | tf_op | source)
XLA Modules:
  0.0 65.5 jit_solution(1548196173514887100)
XLA Ops:
  0.6 3.0 %collective-permute-start.4 = (bf16[2048,128]{1,0:T(8,128)(2,1)}, bf16[2048,128]{1,0:T(8,128)(2,1)S(1)}, u32[]{:S(2)}, u32[]{:S(2)}) collective-permute-start(bf16[2048,128]{1,0:T(8,128)(2,1)} %bitcast.23), channel_id=1, source_target_pairs={{0,4},{2,6},{8,0},{10,2},{16,8},{18,10},{24,16},{26,18},{28,24},{3... | collective-permute-start | bytes 1572872 | tf_op jit(solution)/shard_map/ppermute | solution.py:50
  3.8 5.5 %part_weights.1.weight = bf16[2,2048,1024]{2,1,0:T(8,128)(2,1)S(1)} custom-call(bf16[32768,128]{1,0:T(8,128)(2,1)} %bitcast.32), custom_call_target="tpu_custom_call" | custom-call | flops 2147483648 | bytes 16777216 | tf_op jit(solution)/shard_map/part_weights/pallas_call | solution.py:251
  10.0 0.6 positions.1
  10.5 0.5 sine_multiply_fusion
  11.1 2.0 %project_query.1 = (bf16[256,1024]{1,0:T(8,128)(2,1)S(1)}, bf16[256,2048]{1,0:T(8,128)(2,1)S(1)}) custom-call(bf16[256,1024]{1,0:T(8,128)(2,1)S(1)} %copy-done.2, bf16[256,1024]{1,0:T(8,128)(2,1)S(1)} %collective-permute-done.refs_1_, bf16[2048,1024]{1,0:T(8,128)(2,1)S(1)} %copy-done.1, f32[256,128]{1,0:T(8,128)S(1)} %get-tuple-element.49.refs_3_.cosine, ...), custom_call_target="tpu_custom_call" | custom-call | flops 1073741824 | bytes 4194304 | tf_op jit(solution)/shard_map/project_query/pallas_call | solution.py:212
  13.1 1.9 %collective-permute-start.1 = (bf16[256,1024]{1,0:T(8,128)(2,1)S(1)}, bf16[256,1024]{1,0:T(8,128)(2,1)S(1)}, u32[]{:S(2)}, u32[]{:S(2)}) collective-permute-start(bf16[256,1024]{1,0:T(8,128)(2,1)S(1)} %get-tuple-element.46.refs_3_), channel_id=1, source_target_pairs={{0,2},{2,0},{4,6},{6,4},{8,10},{10,8},{12,14},{14,12},{16,18},{18,... | collective-permute-start | bytes 1572872 | tf_op jit(solution)/shard_map/ppermute | solution.py:41
  15.1 0.8 %collective-permute-done.4.refs_1_ = bf16[2048,128]{1,0:T(8,128)(2,1)S(1)} collective-permute-done((bf16[2048,128]{1,0:T(8,128)(2,1)}, bf16[2048,128]{1,0:T(8,128)(2,1)S(1)}, u32[]{:S(2)}, u32[]{:S(2)}) %collective-permute-start.4) | collective-permute-done | bytes 524320 | tf_op jit(solution)/shard_map/ppermute | solution.py:50
  15.9 1.7 %collective-permute-start.7 = (bf16[1024,128]{1,0:T(8,128)(2,1)S(1)}, bf16[1024,128]{1,0:T(8,128)(2,1)S(1)}, u32[]{:S(2)}, u32[]{:S(2)}) collective-permute-start(bf16[1024,128]{1,0:T(8,128)(2,1)S(1)} %get-tuple-element.59), channel_id=1, source_target_pairs={{0,4},{2,6},{8,0},{10,2},{16,8},{18,10},{24,16},{26,18},{28,24},{3... | collective-permute-start | bytes 786440 | tf_op jit(solution)/shard_map/ppermute | solution.py:50
  17.7 0.4 collective-permute-start.3
  18.1 1.7 %collective-permute-start.10 = (bf16[1024,128]{1,0:T(8,128)(2,1)S(1)}, bf16[1024,128]{1,0:T(8,128)(2,1)S(1)}, u32[]{:S(2)}, u32[]{:S(2)}) collective-permute-start(bf16[1024,128]{1,0:T(8,128)(2,1)S(1)} %get-tuple-element.62), channel_id=1, source_target_pairs={{0,8},{2,10},{8,16},{10,18},{16,24},{18,26},{24,28},{26,30},{28,20... | collective-permute-start | bytes 786440 | tf_op jit(solution)/shard_map/ppermute | solution.py:50
  20.1 2.5 %project_keyval.1 = (bf16[256,1024]{1,0:T(8,128)(2,1)S(1)}, bf16[256,1024]{1,0:T(8,128)(2,1)S(1)}, bf16[1024,256]{1,0:T(8,128)(2,1)S(1)}) custom-call(bf16[256,2048]{1,0:T(8,128)(2,1)S(1)} %get-tuple-element.48.normed, bf16[2,2048,1024]{2,1,0:T(8,128)(2,1)S(1)} %part_weights.1.weight, f32[256,128]{1,0:T(8,128)S(1)} %get-tuple-element.49.refs_3_.cosine, ...), custom_call_target="tpu_custom_call" | custom-call | flops 2147483648 | bytes 8388608 | tf_op jit(solution)/shard_map/project_keyval/pallas_call | solution.py:284
  22.6 2.6 %collective-permute-done.7.refs_7_ = bf16[1024,128]{1,0:T(8,128)(2,1)S(1)} collective-permute-done((bf16[1024,128]{1,0:T(8,128)(2,1)S(1)}, bf16[1024,128]{1,0:T(8,128)(2,1)S(1)}, u32[]{:S(2)}, u32[]{:S(2)}) %collective-permute-start.7) | collective-permute-done | bytes 262176 | tf_op jit(solution)/shard_map/ppermute | solution.py:50
  25.2 1.7 %collective-permute-start.8 = (bf16[1024,128]{1,0:T(8,128)(2,1)S(1)}, bf16[1024,128]{1,0:T(8,128)(2,1)S(1)}, u32[]{:S(2)}, u32[]{:S(2)}) collective-permute-start(bf16[1024,128]{1,0:T(8,128)(2,1)S(1)} %collective-permute-done.7.refs_7_), channel_id=1, source_target_pairs={{0,4},{2,6},{8,0},{10,2},{16,8},{18,10},{24,16},{26,18},{28,24},{3... | collective-permute-start | bytes 786440 | tf_op jit(solution)/shard_map/ppermute | solution.py:50
  27.3 1.0 %part_own.1 = (bf16[384,1024]{1,0:T(8,128)(2,1)S(1)}, bf16[1024,384]{1,0:T(8,128)(2,1)S(1)}) custom-call(bf16[4096,128]{1,0:T(8,128)(2,1)S(1)} %bitcast.22, bf16[2048,128]{1,0:T(8,128)(2,1)S(1)} %bitcast.25), custom_call_target="tpu_custom_call" | custom-call | flops 402653184 | bytes 3145728 | tf_op jit(solution)/shard_map/part_own/pallas_call | solution.py:170
  28.3 0.7 %part_near.1 = (bf16[256,1024]{1,0:T(8,128)(2,1)S(1)}, bf16[1024,256]{1,0:T(8,128)(2,1)S(1)}) custom-call(bf16[2048,128]{1,0:T(8,128)(2,1)S(1)} %collective-permute-done.2.refs_0_, bf16[2048,128]{1,0:T(8,128)(2,1)S(1)} %collective-permute-done.4.refs_1_), custom_call_target="tpu_custom_call" | custom-call | flops 268435456 | bytes 2097152 | tf_op jit(solution)/shard_map/part_near/pallas_call | solution.py:170
  29.0 3.5 %collective-permute-done.10.refs_5_ = bf16[1024,128]{1,0:T(8,128)(2,1)S(1)} collective-permute-done((bf16[1024,128]{1,0:T(8,128)(2,1)S(1)}, bf16[1024,128]{1,0:T(8,128)(2,1)S(1)}, u32[]{:S(2)}, u32[]{:S(2)}) %collective-permute-start.10) | collective-permute-done | bytes 262176 | tf_op jit(solution)/shard_map/ppermute | solution.py:50
  32.9 1.7 %collective-permute-start.13 = (bf16[1024,128]{1,0:T(8,128)(2,1)S(1)}, bf16[1024,128]{1,0:T(8,128)(2,1)S(1)}, u32[]{:S(2)}, u32[]{:S(2)}) collective-permute-start(bf16[1024,128]{1,0:T(8,128)(2,1)S(1)} %collective-permute-done.12.refs_6_), channel_id=1, source_target_pairs={{0,4},{2,6},{8,0},{10,2},{16,8},{18,10},{24,16},{26,18},{28,24},{3... | collective-permute-start | bytes 786440 | tf_op jit(solution)/shard_map/ppermute | solution.py:50
  34.6 4.3 %attend_near_others.1 = (f32[1024,256]{1,0:T(8,128)S(1)}, f32[8,256]{1,0:T(8,128)S(1)}) custom-call(s32[8]{0:T(128)S(1)} %copy-done.6, s32[1]{0:T(128)S(6)} %copy.15.shared.refs_1_, s32[4,8]{1,0:T(4,128)S(1)} %bitcast.26, bf16[256,1024]{1,0:T(8,128)(2,1)S(1)} %collective-permute-done.1.refs_3_, bf16[384,1024]{1,0:T(8,128)(2,1)S(1)} %get-tuple-element.52.refs_4_, ...), custom_call_target="tpu_custom_call" | custom-call | flops 939524096 | bytes 3670016 | tf_op jit(solution)/shard_map/attend_near_others/pallas_call | solution.py:548
  39.4 1.7 %collective-permute-start.9 = (bf16[1024,128]{1,0:T(8,128)(2,1)S(1)}, bf16[1024,128]{1,0:T(8,128)(2,1)S(1)}, u32[]{:S(2)}, u32[]{:S(2)}) collective-permute-start(bf16[1024,128]{1,0:T(8,128)(2,1)S(1)} %collective-permute-done.8.refs_7_), channel_id=1, source_target_pairs={{0,4},{2,6},{8,0},{10,2},{16,8},{18,10},{24,16},{26,18},{28,24},{3... | collective-permute-start | bytes 786440 | tf_op jit(solution)/shard_map/ppermute | solution.py:50
  41.1 2.2 %attend_hop2_others.1 = (f32[1024,256]{1,0:T(8,128)S(1)}, f32[8,256]{1,0:T(8,128)S(1)}, bf16[256,1024]{1,0:T(8,128)(2,1)S(1)}, bf16[1024,256]{1,0:T(8,128)(2,1)S(1)}) custom-call(s32[8]{0:T(128)S(1)} %copy-done.6, s32[1]{0:T(128)S(6)} %copy.15.shared.refs_1_, s32[4,8]{1,0:T(4,128)S(1)} %bitcast.27, bf16[256,1024]{1,0:T(8,128)(2,1)S(1)} %collective-permute-done.1.refs_3_, ...), custom_call_target="tpu_custom_call" | custom-call | flops 268435456 | bytes 1048576 | tf_op jit(solution)/shard_map/attend_hop2_others/pallas_call | solution.py:548
  43.3 0.5 collective-permute-done.11.refs_5_
  43.8 2.2 %attend_hop3_others.1 = (f32[1024,256]{1,0:T(8,128)S(1)}, f32[8,256]{1,0:T(8,128)S(1)}, bf16[256,1024]{1,0:T(8,128)(2,1)S(1)}, bf16[1024,256]{1,0:T(8,128)(2,1)S(1)}) custom-call(s32[8]{0:T(128)S(1)} %copy-done.6, s32[1]{0:T(128)S(6)} %copy.15.shared.refs_1_, s32[4,8]{1,0:T(4,128)S(1)} %bitcast.28, bf16[256,1024]{1,0:T(8,128)(2,1)S(1)} %collective-permute-done.1.refs_3_, ...), custom_call_target="tpu_custom_call" | custom-call | flops 268435456 | bytes 1048576 | tf_op jit(solution)/shard_map/attend_hop3_others/pallas_call | solution.py:548
  46.1 1.3 %collective-permute-done.6.refs_4_ = bf16[1024,128]{1,0:T(8,128)(2,1)S(1)} collective-permute-done((bf16[1024,128]{1,0:T(8,128)(2,1)S(1)}, bf16[1024,128]{1,0:T(8,128)(2,1)S(1)}, u32[]{:S(2)}, u32[]{:S(2)}) %collective-permute-start.6) | collective-permute-done | bytes 262176 | tf_op jit(solution)/shard_map/ppermute | solution.py:50
  47.4 1.8 %attend_far_others.1 = (bf16[1056,256]{1,0:T(8,128)(2,1)S(1)}, bf16[128,1024]{1,0:T(8,128)(2,1)S(1)}, bf16[1024,128]{1,0:T(8,128)(2,1)S(1)}) custom-call(s32[8]{0:T(128)S(1)} %copy-done.6, s32[1]{0:T(128)S(6)} %copy.15.shared.refs_1_, s32[4,8]{1,0:T(4,128)S(1)} %bitcast.29, bf16[256,1024]{1,0:T(8,128)(2,1)S(1)} %collective-permute-done.1.refs_3_, ...), custom_call_target="tpu_custom_call" | custom-call | flops 134217728 | bytes 524288 | tf_op jit(solution)/shard_map/attend_far_others/pallas_call | solution.py:548
  49.2 1.2 %collective-permute-start.14 = (bf16[1056,256]{1,0:T(8,128)(2,1)S(1)}, bf16[1056,256]{1,0:T(8,128)(2,1)S(1)}, u32[]{:S(2)}, u32[]{:S(2)}) collective-permute-start(bf16[1056,256]{1,0:T(8,128)(2,1)S(1)} %get-tuple-element.71.refs_0_), channel_id=1, source_target_pairs={{0,2},{2,0},{4,6},{6,4},{8,10},{10,8},{12,14},{14,12},{16,18},{18,... | collective-permute-start | bytes 1622024 | tf_op jit(solution)/shard_map/ppermute | solution.py:41
  50.4 1.4 %weave_cache.1 = (bf16[4096,128]{1,0:T(8,128)(2,1)}, f32[8,128]{1,0:T(8,128)S(1)}) custom-call(bf16[256,1024]{1,0:T(8,128)(2,1)S(1)} %get-tuple-element.50.refs_8_.refs_14_.keys, bf16[256,1024]{1,0:T(8,128)(2,1)S(1)} %get-tuple-element.81.values, bf16[1056,256]{1,0:T(8,128)(2,1)S(1)} %get-tuple-element.71.refs_0_), custom_call_target="tpu_custom_call" | custom-call | flops 268435456 | bytes 2097152 | tf_op jit(solution)/shard_map/weave_cache/pallas_call | solution.py:323
  51.9 6.3 %attend_own.1 = (f32[1024,256]{1,0:T(8,128)S(1)}, f32[8,256]{1,0:T(8,128)S(1)}) custom-call(s32[8]{0:T(128)S(1)} %copy-done.6, s32[1]{0:T(128)S(6)} %copy.15.shared.refs_1_, s32[4,8]{1,0:T(4,128)S(1)} %bitcast.30, bf16[256,1024]{1,0:T(8,128)(2,1)S(1)} %get-tuple-element.46.refs_3_, bf16[384,1024]{1,0:T(8,128)(2,1)S(1)} %get-tuple-element.52.refs_4_, ...), custom_call_target="tpu_custom_call" | custom-call | flops 1610612736 | bytes 6291456 | tf_op jit(solution)/shard_map/attend_own/pallas_call | solution.py:548
  58.2 3.3 %collective-permute-done.14.refs_2_ = bf16[1056,256]{1,0:T(8,128)(2,1)S(1)} collective-permute-done((bf16[1056,256]{1,0:T(8,128)(2,1)S(1)}, bf16[1056,256]{1,0:T(8,128)(2,1)S(1)}, u32[]{:S(2)}, u32[]{:S(2)}) %collective-permute-start.14) | collective-permute-done | bytes 540704 | tf_op jit(solution)/shard_map/ppermute | solution.py:41
  61.5 1.0 %combine_send.1 = (bf16[256,1024]{1,0:T(8,128)(2,1)S(1)}, bf16[1,256,1024]{2,1,0:T(8,128)(2,1)S(1)}) custom-call(f32[1024,256]{1,0:T(8,128)S(1)} %get-tuple-element.79.refs_0_, f32[8,256]{1,0:T(8,128)S(1)} %get-tuple-element.80.refs_1_, bf16[1056,256]{1,0:T(8,128)(2,1)S(1)} %collective-permute-done.14.refs_2_, bf16[1024,2048]{1,0:T(8,128)(2,1)S(1)} %copy-done, ...), custom_call_target="tpu_custom_call" | custom-call | flops 536870912 | bytes 4194304 | tf_op jit(solution)/shard_map/combine_send/pallas_call | solution.py:600
  62.6 0.7 %keep_own.1 = f32[256,1024]{1,0:T(8,128)S(1)} custom-call(bf16[256,1024]{1,0:T(8,128)(2,1)S(1)} %get-tuple-element.83.attended, bf16[1024,2048]{1,0:T(8,128)(2,1)S(1)} %copy-done, bf16[256,1024]{1,0:T(8,128)(2,1)S(1)} %copy-done.2), custom_call_target="tpu_custom_call" | custom-call | flops 536870912 | bytes 4194304 | tf_op jit(solution)/shard_map/keep_own/pallas_call | solution.py:626
  63.4 1.2 %collective-permute-done.15 = bf16[256,1024]{1,0:T(8,128)(2,1)S(1)} collective-permute-done((bf16[256,1024]{1,0:T(8,128)(2,1)S(1)}, bf16[256,1024]{1,0:T(8,128)(2,1)S(1)}, u32[]{:S(2)}, u32[]{:S(2)}) %collective-permute-start.15) | collective-permute-done | bytes 524320 | tf_op jit(solution)/shard_map/ppermute | solution.py:41
  64.5 0.9 %add_convert_fusion = bf16[256,1024]{1,0:T(8,128)(2,1)} fusion(f32[256,1024]{1,0:T(8,128)S(1)} %keep_own.1, bf16[256,1024]{1,0:T(8,128)(2,1)S(1)} %collective-permute-done.15), kind=kLoop, calls=%fused_computation | loop fusion | flops 786432 | bytes 2097152 | tf_op jit(solution)/shard_map/convert_element_type | solution.py:747
  (33 shorter events, 1.8 us)
Async XLA Ops:
  0.6 15.2 %collective-permute-start.4 = (bf16[2048,128]{1,0:T(8,128)(2,1)}, bf16[2048,128]{1,0:T(8,128)(2,1)S(1)}, u32[]{:S(2)}, u32[]{:S(2)}) collective-permute-start(bf16[2048,128]{1,0:T(8,128)(2,1)} %bitcast.23), channel_id=1, source_target_pairs={{0,4},{2,6},{8,0},{10,2},{16,8},{18,10},{24,16},{26,18},{28,24},{3... | collective-permute-start | bytes 1572872 | tf_op jit(solution)/shard_map/ppermute | solution.py:50
  3.6 14.0 %collective-permute-start.2 = (bf16[2048,128]{1,0:T(8,128)(2,1)}, bf16[2048,128]{1,0:T(8,128)(2,1)S(1)}, u32[]{:S(2)}, u32[]{:S(2)}) collective-permute-start(bf16[2048,128]{1,0:T(8,128)(2,1)} %bitcast.24), channel_id=1, source_target_pairs={{0,8},{2,10},{8,16},{10,18},{16,24},{18,26},{24,28},{26,30},{28,20... | collective-permute-start | bytes 1572872 | tf_op jit(solution)/shard_map/ppermute | solution.py:50
  3.8 7.3 %collective-permute-start = (bf16[256,1024]{1,0:T(8,128)(2,1)}, bf16[256,1024]{1,0:T(8,128)(2,1)S(1)}, u32[]{:S(2)}, u32[]{:S(2)}) collective-permute-start(bf16[256,1024]{1,0:T(8,128)(2,1)} %hidden.1), channel_id=1, source_target_pairs={{0,1},{1,0},{2,3},{3,2},{4,5},{5,4},{6,7},{7,6},{8,9},{9,8},{10,11... | collective-permute-start | bytes 1572872 | tf_op jit(solution)/shard_map/ppermute | solution.py:41
  3.8 6.2 %copy-start.6 = (s32[8]{0:T(128)S(1)}, s32[8]{0:T(128)}, u32[]{:S(2)}) copy-start(s32[8]{0:T(128)} %refs_0_.9) | copy-start | bytes 100
  3.8 7.3 %copy-start.1 = (bf16[2048,1024]{1,0:T(8,128)(2,1)S(1)}, bf16[2048,1024]{1,0:T(8,128)(2,1)}, u32[]{:S(2)}) copy-start(bf16[2048,1024]{1,0:T(8,128)(2,1)} %refs_2_.1) | copy-start | bytes 12582916
  3.8 7.3 %copy-start.2 = (bf16[256,1024]{1,0:T(8,128)(2,1)S(1)}, bf16[256,1024]{1,0:T(8,128)(2,1)}, u32[]{:S(2)}) copy-start(bf16[256,1024]{1,0:T(8,128)(2,1)} %hidden.1) | copy-start | bytes 1572868
  11.1 16.2 %copy-start.3 = (bf16[2,128,2,1024]{3,2,1,0:T(2,128)(2,1)S(1)}, bf16[2,128,2,1024]{3,2,1,0:T(2,128)(2,1)}, u32[]{:S(2)}) copy-start(bf16[2,128,2,1024]{3,2,1,0:T(2,128)(2,1)} %param.14) | copy-start | bytes 3145732
  11.1 16.2 %copy-start.4 = (bf16[128,2,1024]{2,1,0:T(2,128)(2,1)S(1)}, bf16[128,2,1024]{2,1,0:T(2,128)(2,1)}, u32[]{:S(2)}) copy-start(bf16[128,2,1024]{2,1,0:T(2,128)(2,1)} %param.13) | copy-start | bytes 1572868
  13.1 21.5 %copy-start.5 = (s32[8,4]{0,1:T(4,128)S(1)}, s32[8,4]{0,1:T(4,128)}, u32[]{:S(2)}) copy-start(s32[8,4]{0,1:T(4,128)} %param.15) | copy-start | bytes 388
  13.1 21.5 %collective-permute-start.1 = (bf16[256,1024]{1,0:T(8,128)(2,1)S(1)}, bf16[256,1024]{1,0:T(8,128)(2,1)S(1)}, u32[]{:S(2)}, u32[]{:S(2)}) collective-permute-start(bf16[256,1024]{1,0:T(8,128)(2,1)S(1)} %get-tuple-element.46.refs_3_), channel_id=1, source_target_pairs={{0,2},{2,0},{4,6},{6,4},{8,10},{10,8},{12,14},{14,12},{16,18},{18,... | collective-permute-start | bytes 1572872 | tf_op jit(solution)/shard_map/ppermute | solution.py:41
  15.9 9.3 %collective-permute-start.7 = (bf16[1024,128]{1,0:T(8,128)(2,1)S(1)}, bf16[1024,128]{1,0:T(8,128)(2,1)S(1)}, u32[]{:S(2)}, u32[]{:S(2)}) collective-permute-start(bf16[1024,128]{1,0:T(8,128)(2,1)S(1)} %get-tuple-element.59), channel_id=1, source_target_pairs={{0,4},{2,6},{8,0},{10,2},{16,8},{18,10},{24,16},{26,18},{28,24},{3... | collective-permute-start | bytes 786440 | tf_op jit(solution)/shard_map/ppermute | solution.py:50
  17.7 9.3 %collective-permute-start.3 = (bf16[1024,128]{1,0:T(8,128)(2,1)S(1)}, bf16[1024,128]{1,0:T(8,128)(2,1)S(1)}, u32[]{:S(2)}, u32[]{:S(2)}) collective-permute-start(bf16[1024,128]{1,0:T(8,128)(2,1)S(1)} %get-tuple-element.47), channel_id=1, source_target_pairs={{0,8},{2,10},{8,16},{10,18},{16,24},{18,26},{24,28},{26,30},{28,20... | collective-permute-start | bytes 786440 | tf_op jit(solution)/shard_map/ppermute | solution.py:50
  18.1 14.5 %collective-permute-start.10 = (bf16[1024,128]{1,0:T(8,128)(2,1)S(1)}, bf16[1024,128]{1,0:T(8,128)(2,1)S(1)}, u32[]{:S(2)}, u32[]{:S(2)}) collective-permute-start(bf16[1024,128]{1,0:T(8,128)(2,1)S(1)} %get-tuple-element.62), channel_id=1, source_target_pairs={{0,8},{2,10},{8,16},{10,18},{16,24},{18,26},{24,28},{26,30},{28,20... | collective-permute-start | bytes 786440 | tf_op jit(solution)/shard_map/ppermute | solution.py:50
  19.8 13.1 %collective-permute-start.12 = (bf16[1024,128]{1,0:T(8,128)(2,1)S(1)}, bf16[1024,128]{1,0:T(8,128)(2,1)S(1)}, u32[]{:S(2)}, u32[]{:S(2)}) collective-permute-start(bf16[1024,128]{1,0:T(8,128)(2,1)S(1)} %get-tuple-element.64), channel_id=1, source_target_pairs={{0,4},{2,6},{8,0},{10,2},{16,8},{18,10},{24,16},{26,18},{28,24},{3... | collective-permute-start | bytes 786440 | tf_op jit(solution)/shard_map/ppermute | solution.py:50
  25.2 13.8 %collective-permute-start.8 = (bf16[1024,128]{1,0:T(8,128)(2,1)S(1)}, bf16[1024,128]{1,0:T(8,128)(2,1)S(1)}, u32[]{:S(2)}, u32[]{:S(2)}) collective-permute-start(bf16[1024,128]{1,0:T(8,128)(2,1)S(1)} %collective-permute-done.7.refs_7_), channel_id=1, source_target_pairs={{0,4},{2,6},{8,0},{10,2},{16,8},{18,10},{24,16},{26,18},{28,24},{3... | collective-permute-start | bytes 786440 | tf_op jit(solution)/shard_map/ppermute | solution.py:50
  27.0 12.0 %collective-permute-start.5 = (bf16[1024,128]{1,0:T(8,128)(2,1)S(1)}, bf16[1024,128]{1,0:T(8,128)(2,1)S(1)}, u32[]{:S(2)}, u32[]{:S(2)}) collective-permute-start(bf16[1024,128]{1,0:T(8,128)(2,1)S(1)} %collective-permute-done.3.refs_4_), channel_id=1, source_target_pairs={{0,8},{2,10},{8,16},{10,18},{16,24},{18,26},{24,28},{26,30},{28,20... | collective-permute-start | bytes 786440 | tf_op jit(solution)/shard_map/ppermute | solution.py:50
  32.6 11.2 %collective-permute-start.11 = (bf16[1024,128]{1,0:T(8,128)(2,1)S(1)}, bf16[1024,128]{1,0:T(8,128)(2,1)S(1)}, u32[]{:S(2)}, u32[]{:S(2)}) collective-permute-start(bf16[1024,128]{1,0:T(8,128)(2,1)S(1)} %collective-permute-done.10.refs_5_), channel_id=1, source_target_pairs={{0,8},{2,10},{8,16},{10,18},{16,24},{18,26},{24,28},{26,30},{28,20... | collective-permute-start | bytes 786440 | tf_op jit(solution)/shard_map/ppermute | solution.py:50
  32.9 10.9 %collective-permute-start.13 = (bf16[1024,128]{1,0:T(8,128)(2,1)S(1)}, bf16[1024,128]{1,0:T(8,128)(2,1)S(1)}, u32[]{:S(2)}, u32[]{:S(2)}) collective-permute-start(bf16[1024,128]{1,0:T(8,128)(2,1)S(1)} %collective-permute-done.12.refs_6_), channel_id=1, source_target_pairs={{0,4},{2,6},{8,0},{10,2},{16,8},{18,10},{24,16},{26,18},{28,24},{3... | collective-permute-start | bytes 786440 | tf_op jit(solution)/shard_map/ppermute | solution.py:50
  38.9 22.6 %copy-start = (bf16[1024,2048]{1,0:T(8,128)(2,1)S(1)}, bf16[1024,2048]{1,0:T(8,128)(2,1)}, u32[]{:S(2)}) copy-start(bf16[1024,2048]{1,0:T(8,128)(2,1)} %weight.1) | copy-start | bytes 12582916
  39.0 8.4 %collective-permute-start.6 = (bf16[1024,128]{1,0:T(8,128)(2,1)S(1)}, bf16[1024,128]{1,0:T(8,128)(2,1)S(1)}, u32[]{:S(2)}, u32[]{:S(2)}) collective-permute-start(bf16[1024,128]{1,0:T(8,128)(2,1)S(1)} %collective-permute-done.5.refs_4_), channel_id=1, source_target_pairs={{0,8},{2,10},{8,16},{10,18},{16,24},{18,26},{24,28},{26,30},{28,20... | collective-permute-start | bytes 786440 | tf_op jit(solution)/shard_map/ppermute | solution.py:50
  39.4 8.0 %collective-permute-start.9 = (bf16[1024,128]{1,0:T(8,128)(2,1)S(1)}, bf16[1024,128]{1,0:T(8,128)(2,1)S(1)}, u32[]{:S(2)}, u32[]{:S(2)}) collective-permute-start(bf16[1024,128]{1,0:T(8,128)(2,1)S(1)} %collective-permute-done.8.refs_7_), channel_id=1, source_target_pairs={{0,4},{2,6},{8,0},{10,2},{16,8},{18,10},{24,16},{26,18},{28,24},{3... | collective-permute-start | bytes 786440 | tf_op jit(solution)/shard_map/ppermute | solution.py:50
  49.2 12.3 %collective-permute-start.14 = (bf16[1056,256]{1,0:T(8,128)(2,1)S(1)}, bf16[1056,256]{1,0:T(8,128)(2,1)S(1)}, u32[]{:S(2)}, u32[]{:S(2)}) collective-permute-start(bf16[1056,256]{1,0:T(8,128)(2,1)S(1)} %get-tuple-element.71.refs_0_), channel_id=1, source_target_pairs={{0,2},{2,0},{4,6},{6,4},{8,10},{10,8},{12,14},{14,12},{16,18},{18,... | collective-permute-start | bytes 1622024 | tf_op jit(solution)/shard_map/ppermute | solution.py:41
  62.6 2.0 %collective-permute-start.15 = (bf16[256,1024]{1,0:T(8,128)(2,1)S(1)}, bf16[256,1024]{1,0:T(8,128)(2,1)S(1)}, u32[]{:S(2)}, u32[]{:S(2)}) collective-permute-start(bf16[256,1024]{1,0:T(8,128)(2,1)S(1)} %bitcast.31), channel_id=1, source_target_pairs={{0,1},{1,0},{2,3},{3,2},{4,5},{5,4},{6,7},{7,6},{8,9},{9,8},{10,11... | collective-permute-start | bytes 1572872 | tf_op jit(solution)/shard_map/ppermute | solution.py:41

commit v11 on v10

--- a/solution.py
+++ b/solution.py
@@ -683,7 +683,6 @@
     fresh_keys, fresh_values, fresh_turned = project_keyval(normed, weight, ready, sine)
     step(0, fresh_keys)
     near_block = part_keyval(nearest, width, "part_near")
-    step(1, near_block[0])
 
     table = tail_table.T
     others = list(range(1, group))
@@ -704,6 +703,7 @@
         False,
         "attend_near_others",
     )
+    step(1, theirs[1][1])
     step(0, theirs[1][1])
     facts = (tail_len, shared_len, table)
     rest = []

time: 65.6 us -> 66 us (level)
  transfers between devices with their start and end apart: 16 -> 16, of which waited for: 8 -> 9; matrix products, arithmetic and copies ran while one was open for 1% -> 1% of each run, Pallas kernels for 45% -> 45%
where the time goes in v11:
time: 66 us; the launch traced here: 65.9 us
  Pallas kernels  32.5 us (49%)
  starting transfers between devices  16.8 us (25%)
  waiting for transfers between devices  13.6 us (21%)
  between operations  1.51 us (2%)
  other arithmetic  1.42 us (2%)
    pallas_call x5, Pallas kernels, attend(): pl.pallas_call(functools.partial(attend_kernel, (group, shifts, rings, sl...  17 us
    ppermute x12, starting transfers between devices, turn(): return lax.ppermute(value, 'seq', pairs)  13.4 us
    ppermute x12, waiting for transfers between devices, turn(): return lax.ppermute(value, 'seq', pairs)  8.81 us
    pallas_call x1, Pallas kernels, part_weights(): pl.pallas_call(weight_kernel, in_specs=[HBM], out_specs=VMEM, out_shape=j...  5.5 us
    ppermute x4, waiting for transfers between devices, swap(): return lax.ppermute(value, axis, pairs)  4.78 us
    ppermute x4, starting transfers between devices, swap(): return lax.ppermute(value, axis, pairs)  3.33 us
    pallas_call x1, Pallas kernels, project_keyval(): pl.pallas_call(keyval_kernel, in_specs=[VMEM] * 4, out_specs=[VMEM] * 3,...  2.54 us
    pallas_call x1, Pallas kernels, project_query(): pl.pallas_call(query_kernel, in_specs=[VMEM] * (len(pieces) + 3), out_spe...  2.02 us
  transfers between devices with their start and end apart: 16, of which 9 were waited for; matrix products, arithmetic and copies ran while one was open for 1% of the time, Pallas kernels for 45%

profile of v11, /device:TPU:0, one launch (start us, length us, event | category | flops | bytes accessed | tf_op | source)
XLA Modules:
  0.0 65.9 jit_solution(14927942520627922755)
XLA Ops:
  0.6 3.0 %collective-permute-start.4 = (bf16[2048,128]{1,0:T(8,128)(2,1)}, bf16[2048,128]{1,0:T(8,128)(2,1)S(1)}, u32[]{:S(2)}, u32[]{:S(2)}) collective-permute-start(bf16[2048,128]{1,0:T(8,128)(2,1)} %bitcast.23), channel_id=1, source_target_pairs={{0,4},{2,6},{8,0},{10,2},{16,8},{18,10},{24,16},{26,18},{28,24},{3... | collective-permute-start | bytes 1572872 | tf_op jit(solution)/shard_map/ppermute | solution.py:50
  3.8 5.5 %part_weights.1.weight = bf16[2,2048,1024]{2,1,0:T(8,128)(2,1)S(1)} custom-call(bf16[32768,128]{1,0:T(8,128)(2,1)} %bitcast.32), custom_call_target="tpu_custom_call" | custom-call | flops 2147483648 | bytes 16777216 | tf_op jit(solution)/shard_map/part_weights/pallas_call | solution.py:251
  10.0 0.6 positions.1
  10.5 0.5 sine_multiply_fusion
  11.1 2.0 %project_query.1 = (bf16[256,1024]{1,0:T(8,128)(2,1)S(1)}, bf16[256,2048]{1,0:T(8,128)(2,1)S(1)}) custom-call(bf16[256,1024]{1,0:T(8,128)(2,1)S(1)} %copy-done.2, bf16[256,1024]{1,0:T(8,128)(2,1)S(1)} %collective-permute-done.refs_1_, bf16[2048,1024]{1,0:T(8,128)(2,1)S(1)} %copy-done.1, f32[256,128]{1,0:T(8,128)S(1)} %get-tuple-element.49.refs_3_.cosine, ...), custom_call_target="tpu_custom_call" | custom-call | flops 1073741824 | bytes 4194304 | tf_op jit(solution)/shard_map/project_query/pallas_call | solution.py:212
  13.1 1.9 %collective-permute-start.1 = (bf16[256,1024]{1,0:T(8,128)(2,1)S(1)}, bf16[256,1024]{1,0:T(8,128)(2,1)S(1)}, u32[]{:S(2)}, u32[]{:S(2)}) collective-permute-start(bf16[256,1024]{1,0:T(8,128)(2,1)S(1)} %get-tuple-element.46.refs_3_), channel_id=1, source_target_pairs={{0,2},{2,0},{4,6},{6,4},{8,10},{10,8},{12,14},{14,12},{16,18},{18,... | collective-permute-start | bytes 1572872 | tf_op jit(solution)/shard_map/ppermute | solution.py:41
  15.1 0.8 %collective-permute-done.4.refs_1_ = bf16[2048,128]{1,0:T(8,128)(2,1)S(1)} collective-permute-done((bf16[2048,128]{1,0:T(8,128)(2,1)}, bf16[2048,128]{1,0:T(8,128)(2,1)S(1)}, u32[]{:S(2)}, u32[]{:S(2)}) %collective-permute-start.4) | collective-permute-done | bytes 524320 | tf_op jit(solution)/shard_map/ppermute | solution.py:50
  15.9 1.7 %collective-permute-start.7 = (bf16[1024,128]{1,0:T(8,128)(2,1)S(1)}, bf16[1024,128]{1,0:T(8,128)(2,1)S(1)}, u32[]{:S(2)}, u32[]{:S(2)}) collective-permute-start(bf16[1024,128]{1,0:T(8,128)(2,1)S(1)} %get-tuple-element.59), channel_id=1, source_target_pairs={{0,4},{2,6},{8,0},{10,2},{16,8},{18,10},{24,16},{26,18},{28,24},{3... | collective-permute-start | bytes 786440 | tf_op jit(solution)/shard_map/ppermute | solution.py:50
  18.1 1.7 %collective-permute-start.10 = (bf16[1024,128]{1,0:T(8,128)(2,1)S(1)}, bf16[1024,128]{1,0:T(8,128)(2,1)S(1)}, u32[]{:S(2)}, u32[]{:S(2)}) collective-permute-start(bf16[1024,128]{1,0:T(8,128)(2,1)S(1)} %get-tuple-element.62), channel_id=1, source_target_pairs={{0,8},{2,10},{8,16},{10,18},{16,24},{18,26},{24,28},{26,30},{28,20... | collective-permute-start | bytes 786440 | tf_op jit(solution)/shard_map/ppermute | solution.py:50
  20.1 2.5 %project_keyval.1 = (bf16[256,1024]{1,0:T(8,128)(2,1)S(1)}, bf16[256,1024]{1,0:T(8,128)(2,1)S(1)}, bf16[1024,256]{1,0:T(8,128)(2,1)S(1)}) custom-call(bf16[256,2048]{1,0:T(8,128)(2,1)S(1)} %get-tuple-element.48.normed, bf16[2,2048,1024]{2,1,0:T(8,128)(2,1)S(1)} %part_weights.1.weight, f32[256,128]{1,0:T(8,128)S(1)} %get-tuple-element.49.refs_3_.cosine, ...), custom_call_target="tpu_custom_call" | custom-call | flops 2147483648 | bytes 8388608 | tf_op jit(solution)/shard_map/project_keyval/pallas_call | solution.py:284
  22.6 2.6 %collective-permute-done.7.refs_7_ = bf16[1024,128]{1,0:T(8,128)(2,1)S(1)} collective-permute-done((bf16[1024,128]{1,0:T(8,128)(2,1)S(1)}, bf16[1024,128]{1,0:T(8,128)(2,1)S(1)}, u32[]{:S(2)}, u32[]{:S(2)}) %collective-permute-start.7) | collective-permute-done | bytes 262176 | tf_op jit(solution)/shard_map/ppermute | solution.py:50
  25.2 1.7 %collective-permute-start.8 = (bf16[1024,128]{1,0:T(8,128)(2,1)S(1)}, bf16[1024,128]{1,0:T(8,128)(2,1)S(1)}, u32[]{:S(2)}, u32[]{:S(2)}) collective-permute-start(bf16[1024,128]{1,0:T(8,128)(2,1)S(1)} %collective-permute-done.7.refs_7_), channel_id=1, source_target_pairs={{0,4},{2,6},{8,0},{10,2},{16,8},{18,10},{24,16},{26,18},{28,24},{3... | collective-permute-start | bytes 786440 | tf_op jit(solution)/shard_map/ppermute | solution.py:50
  27.3 1.0 %part_own.1 = (bf16[384,1024]{1,0:T(8,128)(2,1)S(1)}, bf16[1024,384]{1,0:T(8,128)(2,1)S(1)}) custom-call(bf16[4096,128]{1,0:T(8,128)(2,1)S(1)} %bitcast.22, bf16[2048,128]{1,0:T(8,128)(2,1)S(1)} %bitcast.25), custom_call_target="tpu_custom_call" | custom-call | flops 402653184 | bytes 3145728 | tf_op jit(solution)/shard_map/part_own/pallas_call | solution.py:170
  28.3 0.7 %part_near.1 = (bf16[256,1024]{1,0:T(8,128)(2,1)S(1)}, bf16[1024,256]{1,0:T(8,128)(2,1)S(1)}) custom-call(bf16[2048,128]{1,0:T(8,128)(2,1)S(1)} %collective-permute-done.2.refs_0_, bf16[2048,128]{1,0:T(8,128)(2,1)S(1)} %collective-permute-done.4.refs_1_), custom_call_target="tpu_custom_call" | custom-call | flops 268435456 | bytes 2097152 | tf_op jit(solution)/shard_map/part_near/pallas_call | solution.py:170
  29.1 4.3 %attend_near_others.1 = (f32[1024,256]{1,0:T(8,128)S(1)}, f32[8,256]{1,0:T(8,128)S(1)}) custom-call(s32[8]{0:T(128)S(1)} %copy-done.6, s32[1]{0:T(128)S(6)} %copy.15.shared.refs_1_, s32[4,8]{1,0:T(4,128)S(1)} %bitcast.26, bf16[256,1024]{1,0:T(8,128)(2,1)S(1)} %collective-permute-done.1.refs_3_, bf16[384,1024]{1,0:T(8,128)(2,1)S(1)} %get-tuple-element.52.refs_4_, ...), custom_call_target="tpu_custom_call" | custom-call | flops 939524096 | bytes 3670016 | tf_op jit(solution)/shard_map/attend_near_others/pallas_call | solution.py:548
  33.4 1.8 %collective-permute-start.11 = (bf16[1024,128]{1,0:T(8,128)(2,1)S(1)}, bf16[1024,128]{1,0:T(8,128)(2,1)S(1)}, u32[]{:S(2)}, u32[]{:S(2)}) collective-permute-start(bf16[1024,128]{1,0:T(8,128)(2,1)S(1)} %collective-permute-done.10.refs_5_), channel_id=1, source_target_pairs={{0,8},{2,10},{8,16},{10,18},{16,24},{18,26},{24,28},{26,30},{28,20... | collective-permute-start | bytes 786440 | tf_op jit(solution)/shard_map/ppermute | solution.py:50
  35.5 2.3 %collective-permute-done.5.refs_4_ = bf16[1024,128]{1,0:T(8,128)(2,1)S(1)} collective-permute-done((bf16[1024,128]{1,0:T(8,128)(2,1)S(1)}, bf16[1024,128]{1,0:T(8,128)(2,1)S(1)}, u32[]{:S(2)}, u32[]{:S(2)}) %collective-permute-start.5) | collective-permute-done | bytes 262176 | tf_op jit(solution)/shard_map/ppermute | solution.py:50
  37.8 2.0 %collective-permute-start.9 = (bf16[1024,128]{1,0:T(8,128)(2,1)S(1)}, bf16[1024,128]{1,0:T(8,128)(2,1)S(1)}, u32[]{:S(2)}, u32[]{:S(2)}) collective-permute-start(bf16[1024,128]{1,0:T(8,128)(2,1)S(1)} %collective-permute-done.8.refs_7_), channel_id=1, source_target_pairs={{0,4},{2,6},{8,0},{10,2},{16,8},{18,10},{24,16},{26,18},{28,24},{3... | collective-permute-start | bytes 786440 | tf_op jit(solution)/shard_map/ppermute | solution.py:50
  39.8 2.2 %attend_hop2_others.1 = (f32[1024,256]{1,0:T(8,128)S(1)}, f32[8,256]{1,0:T(8,128)S(1)}, bf16[256,1024]{1,0:T(8,128)(2,1)S(1)}, bf16[1024,256]{1,0:T(8,128)(2,1)S(1)}) custom-call(s32[8]{0:T(128)S(1)} %copy-done.6, s32[1]{0:T(128)S(6)} %copy.15.shared.refs_1_, s32[4,8]{1,0:T(4,128)S(1)} %bitcast.27, bf16[256,1024]{1,0:T(8,128)(2,1)S(1)} %collective-permute-done.1.refs_3_, ...), custom_call_target="tpu_custom_call" | custom-call | flops 268435456 | bytes 1048576 | tf_op jit(solution)/shard_map/attend_hop2_others/pallas_call | solution.py:548
  42.1 1.3 %collective-permute-done.11.refs_5_ = bf16[1024,128]{1,0:T(8,128)(2,1)S(1)} collective-permute-done((bf16[1024,128]{1,0:T(8,128)(2,1)S(1)}, bf16[1024,128]{1,0:T(8,128)(2,1)S(1)}, u32[]{:S(2)}, u32[]{:S(2)}) %collective-permute-start.11) | collective-permute-done | bytes 262176 | tf_op jit(solution)/shard_map/ppermute | solution.py:50
  43.4 0.9 %collective-permute-done.13.refs_6_ = bf16[1024,128]{1,0:T(8,128)(2,1)S(1)} collective-permute-done((bf16[1024,128]{1,0:T(8,128)(2,1)S(1)}, bf16[1024,128]{1,0:T(8,128)(2,1)S(1)}, u32[]{:S(2)}, u32[]{:S(2)}) %collective-permute-start.13) | collective-permute-done | bytes 262176 | tf_op jit(solution)/shard_map/ppermute | solution.py:50
  44.4 2.2 %attend_hop3_others.1 = (f32[1024,256]{1,0:T(8,128)S(1)}, f32[8,256]{1,0:T(8,128)S(1)}, bf16[256,1024]{1,0:T(8,128)(2,1)S(1)}, bf16[1024,256]{1,0:T(8,128)(2,1)S(1)}) custom-call(s32[8]{0:T(128)S(1)} %copy-done.6, s32[1]{0:T(128)S(6)} %copy.15.shared.refs_1_, s32[4,8]{1,0:T(4,128)S(1)} %bitcast.28, bf16[256,1024]{1,0:T(8,128)(2,1)S(1)} %collective-permute-done.1.refs_3_, ...), custom_call_target="tpu_custom_call" | custom-call | flops 268435456 | bytes 1048576 | tf_op jit(solution)/shard_map/attend_hop3_others/pallas_call | solution.py:548
  46.6 0.8 %collective-permute-done.6.refs_4_ = bf16[1024,128]{1,0:T(8,128)(2,1)S(1)} collective-permute-done((bf16[1024,128]{1,0:T(8,128)(2,1)S(1)}, bf16[1024,128]{1,0:T(8,128)(2,1)S(1)}, u32[]{:S(2)}, u32[]{:S(2)}) %collective-permute-start.6) | collective-permute-done | bytes 262176 | tf_op jit(solution)/shard_map/ppermute | solution.py:50
  47.4 1.8 %attend_far_others.1 = (bf16[1056,256]{1,0:T(8,128)(2,1)S(1)}, bf16[128,1024]{1,0:T(8,128)(2,1)S(1)}, bf16[1024,128]{1,0:T(8,128)(2,1)S(1)}) custom-call(s32[8]{0:T(128)S(1)} %copy-done.6, s32[1]{0:T(128)S(6)} %copy.15.shared.refs_1_, s32[4,8]{1,0:T(4,128)S(1)} %bitcast.29, bf16[256,1024]{1,0:T(8,128)(2,1)S(1)} %collective-permute-done.1.refs_3_, ...), custom_call_target="tpu_custom_call" | custom-call | flops 134217728 | bytes 524288 | tf_op jit(solution)/shard_map/attend_far_others/pallas_call | solution.py:548
  49.2 1.3 %collective-permute-start.14 = (bf16[1056,256]{1,0:T(8,128)(2,1)S(1)}, bf16[1056,256]{1,0:T(8,128)(2,1)S(1)}, u32[]{:S(2)}, u32[]{:S(2)}) collective-permute-start(bf16[1056,256]{1,0:T(8,128)(2,1)S(1)} %get-tuple-element.71.refs_0_), channel_id=1, source_target_pairs={{0,2},{2,0},{4,6},{6,4},{8,10},{10,8},{12,14},{14,12},{16,18},{18,... | collective-permute-start | bytes 1622024 | tf_op jit(solution)/shard_map/ppermute | solution.py:41
  50.5 1.4 %weave_cache.1 = (bf16[4096,128]{1,0:T(8,128)(2,1)}, f32[8,128]{1,0:T(8,128)S(1)}) custom-call(bf16[256,1024]{1,0:T(8,128)(2,1)S(1)} %get-tuple-element.50.refs_8_.refs_14_.keys, bf16[256,1024]{1,0:T(8,128)(2,1)S(1)} %get-tuple-element.81.values, bf16[1056,256]{1,0:T(8,128)(2,1)S(1)} %get-tuple-element.71.refs_0_), custom_call_target="tpu_custom_call" | custom-call | flops 268435456 | bytes 2097152 | tf_op jit(solution)/shard_map/weave_cache/pallas_call | solution.py:323
  52.0 6.3 %attend_own.1 = (f32[1024,256]{1,0:T(8,128)S(1)}, f32[8,256]{1,0:T(8,128)S(1)}) custom-call(s32[8]{0:T(128)S(1)} %copy-done.6, s32[1]{0:T(128)S(6)} %copy.15.shared.refs_1_, s32[4,8]{1,0:T(4,128)S(1)} %bitcast.30, bf16[256,1024]{1,0:T(8,128)(2,1)S(1)} %get-tuple-element.46.refs_3_, bf16[384,1024]{1,0:T(8,128)(2,1)S(1)} %get-tuple-element.52.refs_4_, ...), custom_call_target="tpu_custom_call" | custom-call | flops 1610612736 | bytes 6291456 | tf_op jit(solution)/shard_map/attend_own/pallas_call | solution.py:548
  58.3 3.6 %collective-permute-done.14.refs_2_ = bf16[1056,256]{1,0:T(8,128)(2,1)S(1)} collective-permute-done((bf16[1056,256]{1,0:T(8,128)(2,1)S(1)}, bf16[1056,256]{1,0:T(8,128)(2,1)S(1)}, u32[]{:S(2)}, u32[]{:S(2)}) %collective-permute-start.14) | collective-permute-done | bytes 540704 | tf_op jit(solution)/shard_map/ppermute | solution.py:41
  61.9 1.0 %combine_send.1 = (bf16[256,1024]{1,0:T(8,128)(2,1)S(1)}, bf16[1,256,1024]{2,1,0:T(8,128)(2,1)S(1)}) custom-call(f32[1024,256]{1,0:T(8,128)S(1)} %get-tuple-element.79.refs_0_, f32[8,256]{1,0:T(8,128)S(1)} %get-tuple-element.80.refs_1_, bf16[1056,256]{1,0:T(8,128)(2,1)S(1)} %collective-permute-done.14.refs_2_, bf16[1024,2048]{1,0:T(8,128)(2,1)S(1)} %copy-done, ...), custom_call_target="tpu_custom_call" | custom-call | flops 536870912 | bytes 4194304 | tf_op jit(solution)/shard_map/combine_send/pallas_call | solution.py:600
  63.0 0.7 %keep_own.1 = f32[256,1024]{1,0:T(8,128)S(1)} custom-call(bf16[256,1024]{1,0:T(8,128)(2,1)S(1)} %get-tuple-element.83.attended, bf16[1024,2048]{1,0:T(8,128)(2,1)S(1)} %copy-done, bf16[256,1024]{1,0:T(8,128)(2,1)S(1)} %copy-done.2), custom_call_target="tpu_custom_call" | custom-call | flops 536870912 | bytes 4194304 | tf_op jit(solution)/shard_map/keep_own/pallas_call | solution.py:626
  63.8 1.2 %collective-permute-done.15 = bf16[256,1024]{1,0:T(8,128)(2,1)S(1)} collective-permute-done((bf16[256,1024]{1,0:T(8,128)(2,1)S(1)}, bf16[256,1024]{1,0:T(8,128)(2,1)S(1)}, u32[]{:S(2)}, u32[]{:S(2)}) %collective-permute-start.15) | collective-permute-done | bytes 524320 | tf_op jit(solution)/shard_map/ppermute | solution.py:41
  64.9 0.9 %add_convert_fusion = bf16[256,1024]{1,0:T(8,128)(2,1)} fusion(f32[256,1024]{1,0:T(8,128)S(1)} %keep_own.1, bf16[256,1024]{1,0:T(8,128)(2,1)S(1)} %collective-permute-done.15), kind=kLoop, calls=%fused_computation | loop fusion | flops 786432 | bytes 2097152 | tf_op jit(solution)/shard_map/convert_element_type | solution.py:747
  (33 shorter events, 1.7 us)
Async XLA Ops:
  0.6 15.2 %collective-permute-start.4 = (bf16[2048,128]{1,0:T(8,128)(2,1)}, bf16[2048,128]{1,0:T(8,128)(2,1)S(1)}, u32[]{:S(2)}, u32[]{:S(2)}) collective-permute-start(bf16[2048,128]{1,0:T(8,128)(2,1)} %bitcast.23), channel_id=1, source_target_pairs={{0,4},{2,6},{8,0},{10,2},{16,8},{18,10},{24,16},{26,18},{28,24},{3... | collective-permute-start | bytes 1572872 | tf_op jit(solution)/shard_map/ppermute | solution.py:50
  3.6 14.0 %collective-permute-start.2 = (bf16[2048,128]{1,0:T(8,128)(2,1)}, bf16[2048,128]{1,0:T(8,128)(2,1)S(1)}, u32[]{:S(2)}, u32[]{:S(2)}) collective-permute-start(bf16[2048,128]{1,0:T(8,128)(2,1)} %bitcast.24), channel_id=1, source_target_pairs={{0,8},{2,10},{8,16},{10,18},{16,24},{18,26},{24,28},{26,30},{28,20... | collective-permute-start | bytes 1572872 | tf_op jit(solution)/shard_map/ppermute | solution.py:50
  3.8 7.3 %collective-permute-start = (bf16[256,1024]{1,0:T(8,128)(2,1)}, bf16[256,1024]{1,0:T(8,128)(2,1)S(1)}, u32[]{:S(2)}, u32[]{:S(2)}) collective-permute-start(bf16[256,1024]{1,0:T(8,128)(2,1)} %hidden.1), channel_id=1, source_target_pairs={{0,1},{1,0},{2,3},{3,2},{4,5},{5,4},{6,7},{7,6},{8,9},{9,8},{10,11... | collective-permute-start | bytes 1572872 | tf_op jit(solution)/shard_map/ppermute | solution.py:41
  3.8 6.2 %copy-start.6 = (s32[8]{0:T(128)S(1)}, s32[8]{0:T(128)}, u32[]{:S(2)}) copy-start(s32[8]{0:T(128)} %refs_0_.9) | copy-start | bytes 100
  3.8 7.3 %copy-start.1 = (bf16[2048,1024]{1,0:T(8,128)(2,1)S(1)}, bf16[2048,1024]{1,0:T(8,128)(2,1)}, u32[]{:S(2)}) copy-start(bf16[2048,1024]{1,0:T(8,128)(2,1)} %refs_2_.1) | copy-start | bytes 12582916
  3.8 7.3 %copy-start.2 = (bf16[256,1024]{1,0:T(8,128)(2,1)S(1)}, bf16[256,1024]{1,0:T(8,128)(2,1)}, u32[]{:S(2)}) copy-start(bf16[256,1024]{1,0:T(8,128)(2,1)} %hidden.1) | copy-start | bytes 1572868
  11.1 16.2 %copy-start.3 = (bf16[2,128,2,1024]{3,2,1,0:T(2,128)(2,1)S(1)}, bf16[2,128,2,1024]{3,2,1,0:T(2,128)(2,1)}, u32[]{:S(2)}) copy-start(bf16[2,128,2,1024]{3,2,1,0:T(2,128)(2,1)} %param.14) | copy-start | bytes 3145732
  11.1 16.2 %copy-start.4 = (bf16[128,2,1024]{2,1,0:T(2,128)(2,1)S(1)}, bf16[128,2,1024]{2,1,0:T(2,128)(2,1)}, u32[]{:S(2)}) copy-start(bf16[128,2,1024]{2,1,0:T(2,128)(2,1)} %param.13) | copy-start | bytes 1572868
  13.1 15.9 %copy-start.5 = (s32[8,4]{0,1:T(4,128)S(1)}, s32[8,4]{0,1:T(4,128)}, u32[]{:S(2)}) copy-start(s32[8,4]{0,1:T(4,128)} %param.15) | copy-start | bytes 388
  13.1 15.9 %collective-permute-start.1 = (bf16[256,1024]{1,0:T(8,128)(2,1)S(1)}, bf16[256,1024]{1,0:T(8,128)(2,1)S(1)}, u32[]{:S(2)}, u32[]{:S(2)}) collective-permute-start(bf16[256,1024]{1,0:T(8,128)(2,1)S(1)} %get-tuple-element.46.refs_3_), channel_id=1, source_target_pairs={{0,2},{2,0},{4,6},{6,4},{8,10},{10,8},{12,14},{14,12},{16,18},{18,... | collective-permute-start | bytes 1572872 | tf_op jit(solution)/shard_map/ppermute | solution.py:41
  15.9 9.3 %collective-permute-start.7 = (bf16[1024,128]{1,0:T(8,128)(2,1)S(1)}, bf16[1024,128]{1,0:T(8,128)(2,1)S(1)}, u32[]{:S(2)}, u32[]{:S(2)}) collective-permute-start(bf16[1024,128]{1,0:T(8,128)(2,1)S(1)} %get-tuple-element.59), channel_id=1, source_target_pairs={{0,4},{2,6},{8,0},{10,2},{16,8},{18,10},{24,16},{26,18},{28,24},{3... | collective-permute-start | bytes 786440 | tf_op jit(solution)/shard_map/ppermute | solution.py:50
  17.7 9.3 %collective-permute-start.3 = (bf16[1024,128]{1,0:T(8,128)(2,1)S(1)}, bf16[1024,128]{1,0:T(8,128)(2,1)S(1)}, u32[]{:S(2)}, u32[]{:S(2)}) collective-permute-start(bf16[1024,128]{1,0:T(8,128)(2,1)S(1)} %get-tuple-element.47), channel_id=1, source_target_pairs={{0,8},{2,10},{8,16},{10,18},{16,24},{18,26},{24,28},{26,30},{28,20... | collective-permute-start | bytes 786440 | tf_op jit(solution)/shard_map/ppermute | solution.py:50
  18.1 15.4 %collective-permute-start.10 = (bf16[1024,128]{1,0:T(8,128)(2,1)S(1)}, bf16[1024,128]{1,0:T(8,128)(2,1)S(1)}, u32[]{:S(2)}, u32[]{:S(2)}) collective-permute-start(bf16[1024,128]{1,0:T(8,128)(2,1)S(1)} %get-tuple-element.62), channel_id=1, source_target_pairs={{0,8},{2,10},{8,16},{10,18},{16,24},{18,26},{24,28},{26,30},{28,20... | collective-permute-start | bytes 786440 | tf_op jit(solution)/shard_map/ppermute | solution.py:50
  19.8 13.6 %collective-permute-start.12 = (bf16[1024,128]{1,0:T(8,128)(2,1)S(1)}, bf16[1024,128]{1,0:T(8,128)(2,1)S(1)}, u32[]{:S(2)}, u32[]{:S(2)}) collective-permute-start(bf16[1024,128]{1,0:T(8,128)(2,1)S(1)} %get-tuple-element.64), channel_id=1, source_target_pairs={{0,4},{2,6},{8,0},{10,2},{16,8},{18,10},{24,16},{26,18},{28,24},{3... | collective-permute-start | bytes 786440 | tf_op jit(solution)/shard_map/ppermute | solution.py:50
  25.2 10.3 %collective-permute-start.8 = (bf16[1024,128]{1,0:T(8,128)(2,1)S(1)}, bf16[1024,128]{1,0:T(8,128)(2,1)S(1)}, u32[]{:S(2)}, u32[]{:S(2)}) collective-permute-start(bf16[1024,128]{1,0:T(8,128)(2,1)S(1)} %collective-permute-done.7.refs_7_), channel_id=1, source_target_pairs={{0,4},{2,6},{8,0},{10,2},{16,8},{18,10},{24,16},{26,18},{28,24},{3... | collective-permute-start | bytes 786440 | tf_op jit(solution)/shard_map/ppermute | solution.py:50
  27.0 10.8 %collective-permute-start.5 = (bf16[1024,128]{1,0:T(8,128)(2,1)S(1)}, bf16[1024,128]{1,0:T(8,128)(2,1)S(1)}, u32[]{:S(2)}, u32[]{:S(2)}) collective-permute-start(bf16[1024,128]{1,0:T(8,128)(2,1)S(1)} %collective-permute-done.3.refs_4_), channel_id=1, source_target_pairs={{0,8},{2,10},{8,16},{10,18},{16,24},{18,26},{24,28},{26,30},{28,20... | collective-permute-start | bytes 786440 | tf_op jit(solution)/shard_map/ppermute | solution.py:50
  33.4 28.5 %copy-start = (bf16[1024,2048]{1,0:T(8,128)(2,1)S(1)}, bf16[1024,2048]{1,0:T(8,128)(2,1)}, u32[]{:S(2)}) copy-start(bf16[1024,2048]{1,0:T(8,128)(2,1)} %weight.1) | copy-start | bytes 12582916
  33.4 10.0 %collective-permute-start.11 = (bf16[1024,128]{1,0:T(8,128)(2,1)S(1)}, bf16[1024,128]{1,0:T(8,128)(2,1)S(1)}, u32[]{:S(2)}, u32[]{:S(2)}) collective-permute-start(bf16[1024,128]{1,0:T(8,128)(2,1)S(1)} %collective-permute-done.10.refs_5_), channel_id=1, source_target_pairs={{0,8},{2,10},{8,16},{10,18},{16,24},{18,26},{24,28},{26,30},{28,20... | collective-permute-start | bytes 786440 | tf_op jit(solution)/shard_map/ppermute | solution.py:50
  35.2 9.1 %collective-permute-start.13 = (bf16[1024,128]{1,0:T(8,128)(2,1)S(1)}, bf16[1024,128]{1,0:T(8,128)(2,1)S(1)}, u32[]{:S(2)}, u32[]{:S(2)}) collective-permute-start(bf16[1024,128]{1,0:T(8,128)(2,1)S(1)} %collective-permute-done.12.refs_6_), channel_id=1, source_target_pairs={{0,4},{2,6},{8,0},{10,2},{16,8},{18,10},{24,16},{26,18},{28,24},{3... | collective-permute-start | bytes 786440 | tf_op jit(solution)/shard_map/ppermute | solution.py:50
  37.8 9.6 %collective-permute-start.6 = (bf16[1024,128]{1,0:T(8,128)(2,1)S(1)}, bf16[1024,128]{1,0:T(8,128)(2,1)S(1)}, u32[]{:S(2)}, u32[]{:S(2)}) collective-permute-start(bf16[1024,128]{1,0:T(8,128)(2,1)S(1)} %collective-permute-done.5.refs_4_), channel_id=1, source_target_pairs={{0,8},{2,10},{8,16},{10,18},{16,24},{18,26},{24,28},{26,30},{28,20... | collective-permute-start | bytes 786440 | tf_op jit(solution)/shard_map/ppermute | solution.py:50
  37.8 9.6 %collective-permute-start.9 = (bf16[1024,128]{1,0:T(8,128)(2,1)S(1)}, bf16[1024,128]{1,0:T(8,128)(2,1)S(1)}, u32[]{:S(2)}, u32[]{:S(2)}) collective-permute-start(bf16[1024,128]{1,0:T(8,128)(2,1)S(1)} %collective-permute-done.8.refs_7_), channel_id=1, source_target_pairs={{0,4},{2,6},{8,0},{10,2},{16,8},{18,10},{24,16},{26,18},{28,24},{3... | collective-permute-start | bytes 786440 | tf_op jit(solution)/shard_map/ppermute | solution.py:50
  49.2 12.7 %collective-permute-start.14 = (bf16[1056,256]{1,0:T(8,128)(2,1)S(1)}, bf16[1056,256]{1,0:T(8,128)(2,1)S(1)}, u32[]{:S(2)}, u32[]{:S(2)}) collective-permute-start(bf16[1056,256]{1,0:T(8,128)(2,1)S(1)} %get-tuple-element.71.refs_0_), channel_id=1, source_target_pairs={{0,2},{2,0},{4,6},{6,4},{8,10},{10,8},{12,14},{14,12},{16,18},{18,... | collective-permute-start | bytes 1622024 | tf_op jit(solution)/shard_map/ppermute | solution.py:41
  63.0 2.0 %collective-permute-start.15 = (bf16[256,1024]{1,0:T(8,128)(2,1)S(1)}, bf16[256,1024]{1,0:T(8,128)(2,1)S(1)}, u32[]{:S(2)}, u32[]{:S(2)}) collective-permute-start(bf16[256,1024]{1,0:T(8,128)(2,1)S(1)} %bitcast.31), channel_id=1, source_target_pairs={{0,1},{1,0},{2,3},{3,2},{4,5},{5,4},{6,7},{7,6},{8,9},{9,8},{10,11... | collective-permute-start | bytes 1572872 | tf_op jit(solution)/shard_map/ppermute | solution.py:41

commit v12 on v11

--- a/solution.py
+++ b/solution.py
@@ -337,7 +337,7 @@
 
 
 def attend_kernel(spec, *refs):
-    group, shifts, rings, slots, piece, parted, first, last = spec
+    group, shifts, rings, slots, piece, parted, first, last, lowest, heads = spec
     fresh = slots > 0
     refs = list(refs)
     take = lambda count: [refs.pop(0) for _ in range(count)]
@@ -350,6 +350,7 @@
         raw = take(len(rings))
     if not first:
         old_mixes, old_extents = take(len(shifts)), take(len(shifts))
+        skipped = lowest if old_mixes[0].shape[0] == queries[0].shape[1] else 0
     results = take(len(shifts))
     extents = [None if last and shift else take(1)[0] for shift in shifts]
     if not parted:
@@ -362,7 +363,7 @@
         values_here = take(1)[0]
         keys_here, turned_here = sources[0]
     rows, width = queries[0].shape
-    heads = width // HD
+    stride = 2 * heads
     cycle = cycle_of(group)
     seq = lax.axis_index("seq")
     request, member = seq // group, seq % group
@@ -394,10 +395,10 @@
             causal[:, i * rows : (i + 1) * rows] = jnp.where(theirs <= mine, 0.0, NEGATIVE)
     if not parted:
         offset = 0
-        order = order_rows(2 * heads, False)
+        order = order_rows(stride, False)
         for block in raw:
             take_apart(block, order, keys_here, values_here, offset)
-            offset += block.shape[0] // (2 * heads)
+            offset += block.shape[0] // stride
         turn_heads(values_here, turned_here)
     many = len(shifts) * rows
     unit = jnp.where(lax.broadcasted_iota(jnp.int32, (many, HD), 1) == 0, 1.0, 0.0)
@@ -415,10 +416,11 @@
         return values[0] if len(values) == 1 else jnp.concatenate(values, axis=axis)
 
     def query_of(head):
-        return jnp.concatenate([beside([q[:, lanes(head * HD)] for q in queries], 0), unit], axis=1)
+        return jnp.concatenate([beside([q[:, lanes((lowest + head) * HD)] for q in queries], 0), unit], axis=1)
 
     def score(head, query, chunk, scores, top):
         (keys, _), start, size, at, masked = chunk
+        head = head + (lowest if keys.shape[1] == width else 0)
         keys = keys[start : start + size, lanes(head * HD)]
         keys = jnp.concatenate([keys, bias[at : at + size, :]], axis=1)
         part = lax.dot_general(keys, query, ACROSS, preferred_element_type=jnp.float32)
@@ -430,6 +432,7 @@
 
     def mix(head, chunk, scores, top, sums):
         (_, turned), start, size, at, _ = chunk
+        head = head + (lowest if turned.shape[0] == width else 0)
         weights = jnp.exp2((scores[at : at + size, :] - top) * SCALE)
         here = jnp.sum(weights, axis=0, keepdims=True)
         product = jnp.dot(
@@ -446,7 +449,9 @@
         line = lambda k: pl.ds(base + k, 1)
         each = range(together)
         if not first:
-            olds = [beside([extent[line(k), :] for extent in old_extents], 1) for k in each]
+            olds = [
+                beside([extent[line(skipped + k), :] for extent in old_extents], 1) for k in each
+            ]
             tops = [jnp.maximum(top, old * (1.0 / SCALE)) for top, old in zip(tops, olds)]
         next_tops = [None] * together
         sums = [None] * together
@@ -464,7 +469,7 @@
             if not first:
                 factor = jnp.exp2(olds[k] - tops[k] * SCALE)
                 summed = summed + factor
-                old_mix = beside([old_mix[span(k), :] for old_mix in old_mixes], 1)
+                old_mix = beside([old_mix[span(skipped + k), :] for old_mix in old_mixes], 1)
                 mixed = mixed + old_mix * factor
             mixed = mixed * (1.0 / summed)
             extent = tops[k] * SCALE + jnp.log2(summed)
@@ -502,18 +507,18 @@
             gap = stat_rows(heads) - 3 * heads
             if gap:
                 packed.append(jnp.zeros((gap, rows), jnp.float32))
-            results[i][width:, :] = jnp.concatenate(packed, axis=0).astype(jnp.bfloat16)
+            results[i][heads * HD :, :] = jnp.concatenate(packed, axis=0).astype(jnp.bfloat16)
 
 
 def stat_rows(heads):
     return -(-3 * heads // 16) * 16
 
 
-def attend(facts, queries, shifts, rings, slots, piece, blocks, parted, old, last, name):
+def attend(facts, queries, shifts, rings, slots, piece, blocks, parted, old, last, name, within=None):
     group = len(queries)
     queries = [queries[shift] for shift in shifts]
     rows, width = queries[0].shape
-    heads = width // HD
+    lowest, heads = within or (0, width // HD)
     parted = len(blocks) // 2 if parted else 0
     operands = [*facts, *queries, *blocks]
     if old:
@@ -528,11 +533,11 @@
     if slots:
         scratch.append(pltpu.VMEM((rows, many), jnp.float32))
     if not parted:
-        scratch.append(pltpu.VMEM((count, width), jnp.bfloat16))
+        scratch.append(pltpu.VMEM((count, heads * HD), jnp.bfloat16))
     mixes = [
-        jax.ShapeDtypeStruct((width + stat_rows(heads), rows), jnp.bfloat16)
+        jax.ShapeDtypeStruct((heads * HD + stat_rows(heads), rows), jnp.bfloat16)
         if last and shift
-        else jax.ShapeDtypeStruct((width, rows), jnp.float32)
+        else jax.ShapeDtypeStruct((heads * HD, rows), jnp.float32)
         for shift in shifts
     ]
     extents = [
@@ -542,12 +547,13 @@
     shapes = [*mixes, *extents]
     if not parted:
         shapes += [
-            jax.ShapeDtypeStruct((count, width), jnp.bfloat16),
-            jax.ShapeDtypeStruct((width, count), jnp.bfloat16),
+            jax.ShapeDtypeStruct((count, heads * HD), jnp.bfloat16),
+            jax.ShapeDtypeStruct((heads * HD, count), jnp.bfloat16),
         ]
     results = pl.pallas_call(
         functools.partial(
-            attend_kernel, (group, shifts, rings, slots, piece, parted, not old, last)
+            attend_kernel,
+            (group, shifts, rings, slots, piece, parted, not old, last, lowest, heads),
         ),
         in_specs=[SMEM] * 3 + [VMEM] * (len(operands) - 3),
         out_specs=[VMEM] * len(shapes),
@@ -565,14 +571,21 @@
     return state, results[len(results) - 2 :]
 
 
-def combine_kernel(*refs):
-    result, extent, *parts, weight, _, attended, sent = refs
-    width, rows = result.shape
-    heads = width // HD
-    extents = [extent[:heads, :]]
+def combine_kernel(pieces, *refs):
+    *pairs, weight, _, attended, sent = refs
+    results, own_extents, pairs = pairs[:pieces], pairs[pieces : 2 * pieces], pairs[2 * pieces :]
+    rows = results[0].shape[1]
+    heads = pieces * results[0].shape[0] // HD
+    few = heads // pieces
+    own = [extent[:few, :] for extent in own_extents]
+    extents = [own[0] if pieces == 1 else jnp.concatenate(own, axis=0)]
+    parts = [pairs[start : start + pieces] for start in range(0, len(pairs), pieces)]
     for part in parts:
-        lines = part[width:, :].astype(jnp.float32)
-        extents.append(sum(lines[i * heads : (i + 1) * heads] for i in range(3)))
+        here = []
+        for half in part:
+            lines = half[few * HD :, :].astype(jnp.float32)
+            here.append(sum(lines[i * few : (i + 1) * few] for i in range(3)))
+        extents.append(here[0] if pieces == 1 else jnp.concatenate(here, axis=0))
     top = functools.reduce(jnp.maximum, extents)
     shares = [jnp.exp2(extent - top) for extent in extents]
     whole = sum(shares)
@@ -580,7 +593,10 @@
     unit = unit_matrix(rows)
     for head in range(heads):
         span = slice(head * HD, (head + 1) * HD)
-        mixes = [result[span, :]] + [part[span, :].astype(jnp.float32) for part in parts]
+        line = head % few * HD
+        mixes = [results[head // few][line : line + HD, :]] + [
+            part[head // few][line : line + HD, :].astype(jnp.float32) for part in parts
+        ]
         mixed = sum(mix * share[head : head + 1] for mix, share in zip(mixes, shares))
         attended[:, span] = turned_over(unit, mixed.astype(jnp.bfloat16))
     index = lax.axis_index("tp")
@@ -594,12 +610,15 @@
         ).astype(jnp.bfloat16)
 
 
-def combine(result, extent, parts, w_out, token, ways):
-    width, rows = result.shape
+def combine(own, parts, w_out, token, ways):
+    pieces = len(own)
+    results, extents = [mix for mix, _ in own], [extent for _, extent in own]
+    rows = results[0].shape[1]
+    width = w_out.shape[0]
     columns = w_out.shape[1] // ways
     return pl.pallas_call(
-        combine_kernel,
-        in_specs=[VMEM] * (4 + len(parts)),
+        functools.partial(combine_kernel, pieces),
+        in_specs=[VMEM] * (2 * pieces + len(parts) + 2),
         out_specs=[VMEM] * 2,
         out_shape=[
             jax.ShapeDtypeStruct((rows, width), jnp.bfloat16),
@@ -608,7 +627,7 @@
         compiler_params=params(20),
         cost_estimate=cost(2 * rows * width * columns * (ways - 1), 2 * width * w_out.shape[1]),
         name="combine_send",
-    )(result, extent, *parts, w_out, token)
+    )(*results, *extents, *parts, w_out, token)
 
 
 def keep_kernel(attended, weight, hidden, kept):
@@ -649,26 +668,29 @@
 
     pieces = [hidden_in] + [swap(hidden_in, "tp", shift) for shift in range(1, ways)]
     prompt = viewed(prompt_cache)
-    ahead, behind = {0: [None], 1: [None]}, {0: [None], 1: [None]}
+    heads = width // HD
+    pieces_out = 2 if heads >= 4 else 1
+    few = heads // pieces_out
+    every = list(range(pieces_out))
+    ahead, behind = {part: [None] for part in every}, {part: [None] for part in every}
     nearest = []
     for blocks, way in ((ahead, 1), (behind, -1)):
         block = turn(prompt, cycle, group, way)
         nearest.append(block)
-        blocks[0].append(block[: middle * stride])
-        blocks[1].append(block[middle * stride :])
-
-    def step(which, *others):
-        for blocks, part, way in ((ahead, which, 1), (behind, 1 - which, -1)):
-            block = blocks[part][-1]
-            if others:
-                block = after(block, *others)
+        split = block.reshape(piece, pieces_out, 2 * few, HD)
+        for part in every:
+            blocks[part].append(split[:, part].reshape(-1, HD))
+
+    def step(part, *others):
+        for blocks, way in ((ahead, 1), (behind, -1)):
+            block = after(blocks[part][-1], *others)
+            if len(blocks[part]) == half:
+                cut = middle * 2 * few
+                block = block[:cut] if way == 1 else block[cut:]
             blocks[part].append(turn(block, cycle, group, way))
 
-    def arrived(hop):
-        blocks = [way[part][hop] for way in (ahead, behind) for part in (0, 1)]
-        rings = [(sign * hop, part * middle, middle) for sign in (-1, 1) for part in (0, 1)]
-        return blocks, rings
-
+    last_part = every[-1]
+    two = pieces_out > 1
     weight = part_weights(w_keyval)
     cosine, sine = angles(after(tail_len, weight), shared_len, rows)
     pieces[0] = after(pieces[0], weight)
@@ -676,13 +698,14 @@
     queries = [query] + [swap(query, "seq", shift) for shift in range(1, group)]
     tail = viewed(tail_cache.reshape(-1, 2, tail_cache.shape[3]))
     slots = tail_cache.shape[0]
-    own_block = part_keyval([tail, prompt], width, "part_own")
     step(0, weight, query)
-    step(1, query)
-    ready = after(cosine, ahead[1][1], behind[0][1])
+    ready = after(cosine, *nearest)
     fresh_keys, fresh_values, fresh_turned = project_keyval(normed, weight, ready, sine)
-    step(0, fresh_keys)
+    if two:
+        step(1, fresh_keys)
+    own_block = part_keyval([after(tail, fresh_keys), prompt], width, "part_own")
     near_block = part_keyval(nearest, width, "part_near")
+    step(0, own_block[0], near_block[0])
 
     table = tail_table.T
     others = list(range(1, group))
@@ -703,43 +726,71 @@
         False,
         "attend_near_others",
     )
-    step(1, theirs[1][1])
-    step(0, theirs[1][1])
-    facts = (tail_len, shared_len, table)
-    rest = []
-    rest_rings = []
-    for hop in range(2, half):
-        blocks, rings = arrived(hop)
-        name = f"attend_hop{hop}_others"
-        theirs, parted = attend(
-            facts, queries, others, rings, 0, piece, blocks, False, theirs, False, name
+    new_cache, token = weave(fresh_keys, fresh_values, theirs[1][0])
+    state = {part: theirs for part in every}
+    rest = {part: [] for part in every}
+    rest_rings = [(sign * hop, 0, piece) for hop in range(2, half) for sign in (-1, 1)]
+    far_rings = [(-half, 0, middle), (half, middle, piece - middle)]
+
+    def hop_others(facts, part, hop):
+        last = hop == half
+        rings = far_rings if last else [(-hop, 0, piece), (hop, 0, piece)]
+        state[part], made = attend(
+            facts,
+            queries,
+            others,
+            rings,
+            0,
+            piece,
+            [ahead[part][hop], behind[part][hop]],
+            False,
+            state[part],
+            last,
+            f"attend_hop{hop}_part{part}",
+            (part * few, few),
         )
-        rest += parted
-        rest_rings += rings
-    rings = [(-half, 0, middle), (half, middle, piece - middle)]
-    blocks = [ahead[0][half], behind[1][half]]
-    theirs, parted = attend(
-        facts, queries, others, rings, 0, piece, blocks, False, theirs, True, "attend_far_others"
-    )
-    rest += parted
-    rest_rings += rings
-    facts = (after(tail_len, theirs[1][0]), shared_len, table)
-    own, _ = attend(
-        facts,
-        queries,
-        [0],
-        near_rings + rest_rings,
-        slots,
-        piece,
-        near + rest + fresh,
-        True,
-        None,
-        True,
-        "attend_own",
-    )
-    new_cache, token = weave(fresh_keys, fresh_values, theirs[1][0])
-    parts = [swap(theirs[shift][0], "seq", shift) for shift in others]
-    attended, sent = combine(*own[0], parts, w_out, token, ways)
+        rest[part] += made
+
+    def attend_own(facts, part):
+        made, _ = attend(
+            facts,
+            queries,
+            [0],
+            near_rings + rest_rings + far_rings,
+            slots,
+            piece,
+            near + rest[part] + fresh,
+            True,
+            None,
+            True,
+            f"attend_own_part{part}",
+            (part * few, few),
+        )
+        return made[0]
+
+    own = {}
+    received = {}
+    hop_others(facts, 0, 2)
+    if two:
+        step(1, state[0][1][1], token)
+    step(0, state[0][1][1], token)
+    if two:
+        hop_others(facts, 1, 2)
+        facts = (after(tail_len, state[1][1][1]), shared_len, table)
+    hop_others(facts, 0, 3)
+    hop_others(facts, 0, 4)
+    received[0] = [swap(state[0][shift][0], "seq", shift) for shift in others]
+    if two:
+        step(1, state[0][1][0])
+        hop_others(facts, 1, 3)
+        facts = (after(tail_len, received[0][0]), shared_len, table)
+        hop_others(facts, 1, 4)
+        received[1] = [swap(state[1][shift][0], "seq", shift) for shift in others]
+    facts = (after(tail_len, state[last_part][1][0]), shared_len, table)
+    for part in every:
+        own[part] = attend_own(facts, part)
+    parts = [received[part][i] for i in range(len(others)) for part in every]
+    attended, sent = combine([own[part] for part in every], parts, w_out, token, ways)
     received = [swap(sent[shift - 1], "tp", shift) for shift in range(1, ways)]
     total = keep(attended, w_out, hidden_in)
     for part in received:

time: 66 us -> 70.1 us (1.062)
  Pallas kernels: 32.5 us -> 36.3 us
  waiting for transfers between devices: 13.6 us -> 10.2 us
  starting transfers between devices: 16.8 us -> 20.2 us
    pallas_call x5 -> x9, Pallas kernels: 17 us -> 20.8 us  [attend(): pl.pallas_call(functools.partial(attend_kernel, (group, shifts, rings, sl...]
    ppermute x4 -> x5, waiting for transfers between devices: 4.78 us -> 2.02 us  [swap(): return lax.ppermute(value, axis, pairs)]
    ppermute x12 -> x14, starting transfers between devices: 13.4 us -> 15.5 us  [turn(): return lax.ppermute(value, 'seq', pairs)]
    ppermute x4 -> x5, starting transfers between devices: 3.33 us -> 4.77 us  [swap(): return lax.ppermute(value, axis, pairs)]
    ppermute x12 -> x14, waiting for transfers between devices: 8.81 us -> 8.21 us  [turn(): return lax.ppermute(value, 'seq', pairs)]
  transfers between devices with their start and end apart: 16 -> 19, of which waited for: 9 -> 8; matrix products, arithmetic and copies ran while one was open for 1% -> 1% of each run, Pallas kernels for 45% -> 46%
where the time goes in v12:
time: 70.1 us; the launch traced here: 70 us
  Pallas kernels  36.3 us (52%)
  starting transfers between devices  20.2 us (29%)
  waiting for transfers between devices  10.2 us (15%)
  between operations  1.58 us (2%)
  other arithmetic  1.42 us (2%)
    pallas_call x9, Pallas kernels, attend(): pl.pallas_call(functools.partial(attend_kernel, (group, shifts, rings, sl...  20.8 us
    ppermute x14, starting transfers between devices, turn(): return lax.ppermute(value, 'seq', pairs)  15.5 us
    ppermute x14, waiting for transfers between devices, turn(): return lax.ppermute(value, 'seq', pairs)  8.21 us
    pallas_call x1, Pallas kernels, part_weights(): pl.pallas_call(weight_kernel, in_specs=[HBM], out_specs=VMEM, out_shape=j...  5.5 us
    ppermute x5, starting transfers between devices, swap(): return lax.ppermute(value, axis, pairs)  4.77 us
    pallas_call x1, Pallas kernels, project_keyval(): pl.pallas_call(keyval_kernel, in_specs=[VMEM] * 4, out_specs=[VMEM] * 3,...  2.55 us
    ppermute x5, waiting for transfers between devices, swap(): return lax.ppermute(value, axis, pairs)  2.02 us
    pallas_call x1, Pallas kernels, project_query(): pl.pallas_call(query_kernel, in_specs=[VMEM] * (len(pieces) + 3), out_spe...  2.02 us
  transfers between devices with their start and end apart: 19, of which 8 were waited for; matrix products, arithmetic and copies ran while one was open for 1% of the time, Pallas kernels for 46%

profile of v12, /device:TPU:0, one launch (start us, length us, event | category | flops | bytes accessed | tf_op | source)
XLA Modules:
  0.0 70.0 jit_solution(2771514105236607302)
XLA Ops:
  0.6 3.0 %collective-permute-start.3 = (bf16[2048,128]{1,0:T(8,128)(2,1)}, bf16[2048,128]{1,0:T(8,128)(2,1)S(1)}, u32[]{:S(2)}, u32[]{:S(2)}) collective-permute-start(bf16[2048,128]{1,0:T(8,128)(2,1)} %bitcast.43), channel_id=1, source_target_pairs={{0,4},{2,6},{8,0},{10,2},{16,8},{18,10},{24,16},{26,18},{28,24},{3... | collective-permute-start | bytes 1572872 | tf_op jit(solution)/shard_map/ppermute | solution.py:50
  3.8 5.5 %part_weights.1.weight = bf16[2,2048,1024]{2,1,0:T(8,128)(2,1)S(1)} custom-call(bf16[32768,128]{1,0:T(8,128)(2,1)} %bitcast.56), custom_call_target="tpu_custom_call" | custom-call | flops 2147483648 | bytes 16777216 | tf_op jit(solution)/shard_map/part_weights/pallas_call | solution.py:251
  11.0 4.8 %collective-permute-done.3.refs_1_ = bf16[2048,128]{1,0:T(8,128)(2,1)S(1)} collective-permute-done((bf16[2048,128]{1,0:T(8,128)(2,1)}, bf16[2048,128]{1,0:T(8,128)(2,1)S(1)}, u32[]{:S(2)}, u32[]{:S(2)}) %collective-permute-start.3) | collective-permute-done | bytes 524320 | tf_op jit(solution)/shard_map/ppermute | solution.py:50
  15.8 1.4 %collective-permute-done.2.refs_0_ = bf16[2048,128]{1,0:T(8,128)(2,1)S(1)} collective-permute-done((bf16[2048,128]{1,0:T(8,128)(2,1)}, bf16[2048,128]{1,0:T(8,128)(2,1)S(1)}, u32[]{:S(2)}, u32[]{:S(2)}) %collective-permute-start.2) | collective-permute-done | bytes 524320 | tf_op jit(solution)/shard_map/ppermute | solution.py:50
  17.4 2.0 %project_query.1 = (bf16[256,1024]{1,0:T(8,128)(2,1)S(1)}, bf16[256,2048]{1,0:T(8,128)(2,1)S(1)}) custom-call(bf16[256,1024]{1,0:T(8,128)(2,1)S(1)} %copy-done.2, bf16[256,1024]{1,0:T(8,128)(2,1)S(1)} %collective-permute-done.refs_1_, bf16[2048,1024]{1,0:T(8,128)(2,1)S(1)} %copy-done.1, f32[256,128]{1,0:T(8,128)S(1)} %get-tuple-element.66.refs_3_.cosine, ...), custom_call_target="tpu_custom_call" | custom-call | flops 1073741824 | bytes 4194304 | tf_op jit(solution)/shard_map/project_query/pallas_call | solution.py:212
  19.4 1.6 %collective-permute-start.1 = (bf16[256,1024]{1,0:T(8,128)(2,1)S(1)}, bf16[256,1024]{1,0:T(8,128)(2,1)S(1)}, u32[]{:S(2)}, u32[]{:S(2)}) collective-permute-start(bf16[256,1024]{1,0:T(8,128)(2,1)S(1)} %get-tuple-element.64.refs_3_), channel_id=1, source_target_pairs={{0,2},{2,0},{4,6},{6,4},{8,10},{10,8},{12,14},{14,12},{16,18},{18,... | collective-permute-start | bytes 1572872 | tf_op jit(solution)/shard_map/ppermute | solution.py:41
  21.5 1.5 %collective-permute-start.8 = (bf16[1024,128]{1,0:T(8,128)(2,1)S(1)}, bf16[1024,128]{1,0:T(8,128)(2,1)S(1)}, u32[]{:S(2)}, u32[]{:S(2)}) collective-permute-start(bf16[1024,128]{1,0:T(8,128)(2,1)S(1)} %get-tuple-element.82), channel_id=1, source_target_pairs={{0,4},{2,6},{8,0},{10,2},{16,8},{18,10},{24,16},{26,18},{28,24},{3... | collective-permute-start | bytes 786440 | tf_op jit(solution)/shard_map/ppermute | solution.py:50
  23.1 2.6 %project_keyval.1 = (bf16[256,1024]{1,0:T(8,128)(2,1)S(1)}, bf16[256,1024]{1,0:T(8,128)(2,1)S(1)}, bf16[1024,256]{1,0:T(8,128)(2,1)S(1)}) custom-call(bf16[256,2048]{1,0:T(8,128)(2,1)S(1)} %get-tuple-element.65.normed, bf16[2,2048,1024]{2,1,0:T(8,128)(2,1)S(1)} %part_weights.1.weight, f32[256,128]{1,0:T(8,128)S(1)} %get-tuple-element.66.refs_3_.cosine, ...), custom_call_target="tpu_custom_call" | custom-call | flops 2147483648 | bytes 8388608 | tf_op jit(solution)/shard_map/project_keyval/pallas_call | solution.py:284
  25.6 0.7 %part_near.1 = (bf16[256,1024]{1,0:T(8,128)(2,1)S(1)}, bf16[1024,256]{1,0:T(8,128)(2,1)S(1)}) custom-call(bf16[2048,128]{1,0:T(8,128)(2,1)S(1)} %collective-permute-done.2.refs_0_, bf16[2048,128]{1,0:T(8,128)(2,1)S(1)} %collective-permute-done.3.refs_1_), custom_call_target="tpu_custom_call" | custom-call | flops 268435456 | bytes 2097152 | tf_op jit(solution)/shard_map/part_near/pallas_call | solution.py:170
  26.4 1.0 %part_own.1 = (bf16[384,1024]{1,0:T(8,128)(2,1)S(1)}, bf16[1024,384]{1,0:T(8,128)(2,1)S(1)}) custom-call(bf16[4096,128]{1,0:T(8,128)(2,1)S(1)} %bitcast.42, bf16[2048,128]{1,0:T(8,128)(2,1)S(1)} %bitcast.45), custom_call_target="tpu_custom_call" | custom-call | flops 402653184 | bytes 3145728 | tf_op jit(solution)/shard_map/part_own/pallas_call | solution.py:170
  28.0 1.4 %collective-permute-start.10 = (bf16[1024,128]{1,0:T(8,128)(2,1)S(1)}, bf16[1024,128]{1,0:T(8,128)(2,1)S(1)}, u32[]{:S(2)}, u32[]{:S(2)}) collective-permute-start(bf16[1024,128]{1,0:T(8,128)(2,1)S(1)} %collective-permute-done.8.refs_5_), channel_id=1, source_target_pairs={{0,4},{2,6},{8,0},{10,2},{16,8},{18,10},{24,16},{26,18},{28,24},{3... | collective-permute-start | bytes 786440 | tf_op jit(solution)/shard_map/ppermute | solution.py:50
  30.0 1.4 %collective-permute-start.5 = (bf16[1024,128]{1,0:T(8,128)(2,1)S(1)}, bf16[1024,128]{1,0:T(8,128)(2,1)S(1)}, u32[]{:S(2)}, u32[]{:S(2)}) collective-permute-start(bf16[1024,128]{1,0:T(8,128)(2,1)S(1)} %get-tuple-element.69), channel_id=1, source_target_pairs={{0,4},{2,6},{8,0},{10,2},{16,8},{18,10},{24,16},{26,18},{28,24},{3... | collective-permute-start | bytes 786440 | tf_op jit(solution)/shard_map/ppermute | solution.py:50
  32.1 4.3 %attend_near_others.1 = (f32[1024,256]{1,0:T(8,128)S(1)}, f32[8,256]{1,0:T(8,128)S(1)}) custom-call(s32[8]{0:T(128)S(1)} %copy-done.6, s32[1]{0:T(128)S(6)} %copy.23.shared.refs_1_, s32[4,8]{1,0:T(4,128)S(1)} %bitcast.46, bf16[256,1024]{1,0:T(8,128)(2,1)S(1)} %collective-permute-done.1.refs_3_, bf16[384,1024]{1,0:T(8,128)(2,1)S(1)} %get-tuple-element.71.refs_4_, ...), custom_call_target="tpu_custom_call" | custom-call | flops 939524096 | bytes 3670016 | tf_op jit(solution)/shard_map/attend_near_others/pallas_call | solution.py:553
  36.4 1.6 %attend_hop2_part0.1 = (f32[512,256]{1,0:T(8,128)S(1)}, f32[8,256]{1,0:T(8,128)S(1)}, bf16[256,512]{1,0:T(8,128)(2,1)S(1)}, bf16[512,256]{1,0:T(8,128)(2,1)S(1)}) custom-call(s32[8]{0:T(128)S(1)} %copy-done.6, s32[1]{0:T(128)S(6)} %copy.23.shared.refs_1_, s32[4,8]{1,0:T(4,128)S(1)} %bitcast.47, bf16[256,1024]{1,0:T(8,128)(2,1)S(1)} %collective-permute-done.1.refs_3_, ...), custom_call_target="tpu_custom_call" | custom-call | flops 134217728 | bytes 1048576 | tf_op jit(solution)/shard_map/attend_hop2_part0/pallas_call | solution.py:553
  38.0 1.4 %weave_cache.1 = (bf16[4096,128]{1,0:T(8,128)(2,1)}, f32[8,128]{1,0:T(8,128)S(1)}) custom-call(bf16[256,1024]{1,0:T(8,128)(2,1)S(1)} %get-tuple-element.67.refs_8_.keys.refs_14_, bf16[256,1024]{1,0:T(8,128)(2,1)S(1)} %get-tuple-element.84.values, f32[1024,256]{1,0:T(8,128)S(1)} %get-tuple-element.76.refs_6_.refs_0_), custom_call_target="tpu_custom_call" | custom-call | flops 268435456 | bytes 2097152 | tf_op jit(solution)/shard_map/weave_cache/pallas_call | solution.py:323
  39.5 1.5 %collective-permute-start.11 = (bf16[512,128]{1,0:T(8,128)(2,1)S(1)}, bf16[512,128]{1,0:T(8,128)(2,1)S(1)}, u32[]{:S(2)}, u32[]{:S(2)}) collective-permute-start(bf16[512,128]{1,0:T(8,128)(2,1)S(1)} %slice.29), channel_id=1, source_target_pairs={{0,4},{2,6},{8,0},{10,2},{16,8},{18,10},{24,16},{26,18},{28,24},{3... | collective-permute-start | bytes 393224 | tf_op jit(solution)/shard_map/ppermute | solution.py:50
  41.5 1.4 %collective-permute-start.15 = (bf16[1024,128]{1,0:T(8,128)(2,1)S(1)}, bf16[1024,128]{1,0:T(8,128)(2,1)S(1)}, u32[]{:S(2)}, u32[]{:S(2)}) collective-permute-start(bf16[1024,128]{1,0:T(8,128)(2,1)S(1)} %collective-permute-done.5.refs_5_), channel_id=1, source_target_pairs={{0,4},{2,6},{8,0},{10,2},{16,8},{18,10},{24,16},{26,18},{28,24},{3... | collective-permute-start | bytes 786440 | tf_op jit(solution)/shard_map/ppermute | solution.py:50
  43.6 1.6 %attend_hop2_part1.1 = (f32[512,256]{1,0:T(8,128)S(1)}, f32[8,256]{1,0:T(8,128)S(1)}, bf16[256,512]{1,0:T(8,128)(2,1)S(1)}, bf16[512,256]{1,0:T(8,128)(2,1)S(1)}) custom-call(s32[8]{0:T(128)S(1)} %copy-done.6, s32[1]{0:T(128)S(6)} %copy.23.shared.refs_1_, s32[4,8]{1,0:T(4,128)S(1)} %bitcast.48, bf16[256,1024]{1,0:T(8,128)(2,1)S(1)} %collective-permute-done.1.refs_3_, ...), custom_call_target="tpu_custom_call" | custom-call | flops 134217728 | bytes 1048576 | tf_op jit(solution)/shard_map/attend_hop2_part1/pallas_call | solution.py:553
  45.2 1.6 %attend_hop3_part0.1 = (f32[512,256]{1,0:T(8,128)S(1)}, f32[8,256]{1,0:T(8,128)S(1)}, bf16[256,512]{1,0:T(8,128)(2,1)S(1)}, bf16[512,256]{1,0:T(8,128)(2,1)S(1)}) custom-call(s32[8]{0:T(128)S(1)} %copy-done.6, s32[1]{0:T(128)S(6)} %copy.23.shared.refs_1_, s32[4,8]{1,0:T(4,128)S(1)} %bitcast.49, bf16[256,1024]{1,0:T(8,128)(2,1)S(1)} %collective-permute-done.1.refs_3_, ...), custom_call_target="tpu_custom_call" | custom-call | flops 134217728 | bytes 1048576 | tf_op jit(solution)/shard_map/attend_hop3_part0/pallas_call | solution.py:553
  46.8 1.4 %attend_hop4_part0.1 = (bf16[528,256]{1,0:T(8,128)(2,1)S(1)}, bf16[128,512]{1,0:T(8,128)(2,1)S(1)}, bf16[512,128]{1,0:T(8,128)(2,1)S(1)}) custom-call(s32[8]{0:T(128)S(1)} %copy-done.6, s32[1]{0:T(128)S(6)} %copy.23.shared.refs_1_, s32[4,8]{1,0:T(4,128)S(1)} %bitcast.50, bf16[256,1024]{1,0:T(8,128)(2,1)S(1)} %collective-permute-done.1.refs_3_, ...), custom_call_target="tpu_custom_call" | custom-call | flops 67108864 | bytes 524288 | tf_op jit(solution)/shard_map/attend_hop4_part0/pallas_call | solution.py:553
  48.2 1.4 %collective-permute-start.12 = (bf16[528,256]{1,0:T(8,128)(2,1)S(1)}, bf16[528,256]{1,0:T(8,128)(2,1)S(1)}, u32[]{:S(2)}, u32[]{:S(2)}) collective-permute-start(bf16[528,256]{1,0:T(8,128)(2,1)S(1)} %get-tuple-element.92), channel_id=1, source_target_pairs={{0,2},{2,0},{4,6},{6,4},{8,10},{10,8},{12,14},{14,12},{16,18},{18,... | collective-permute-start | bytes 811016 | tf_op jit(solution)/shard_map/ppermute | solution.py:41
  50.5 1.7 %collective-permute-start.16 = (bf16[512,128]{1,0:T(8,128)(2,1)S(1)}, bf16[512,128]{1,0:T(8,128)(2,1)S(1)}, u32[]{:S(2)}, u32[]{:S(2)}) collective-permute-start(bf16[512,128]{1,0:T(8,128)(2,1)S(1)} %slice.31), channel_id=1, source_target_pairs={{0,4},{2,6},{8,0},{10,2},{16,8},{18,10},{24,16},{26,18},{28,24},{3... | collective-permute-start | bytes 393224 | tf_op jit(solution)/shard_map/ppermute | solution.py:50
  52.2 1.6 %attend_hop3_part1.1 = (f32[512,256]{1,0:T(8,128)S(1)}, f32[8,256]{1,0:T(8,128)S(1)}, bf16[256,512]{1,0:T(8,128)(2,1)S(1)}, bf16[512,256]{1,0:T(8,128)(2,1)S(1)}) custom-call(s32[8]{0:T(128)S(1)} %copy-done.6, s32[1]{0:T(128)S(6)} %copy.23.shared.refs_1_, s32[4,8]{1,0:T(4,128)S(1)} %bitcast.51, bf16[256,1024]{1,0:T(8,128)(2,1)S(1)} %collective-permute-done.1.refs_3_, ...), custom_call_target="tpu_custom_call" | custom-call | flops 134217728 | bytes 1048576 | tf_op jit(solution)/shard_map/attend_hop3_part1/pallas_call | solution.py:553
  53.8 0.8 %collective-permute-done.12.refs_4_ = bf16[528,256]{1,0:T(8,128)(2,1)S(1)} collective-permute-done((bf16[528,256]{1,0:T(8,128)(2,1)S(1)}, bf16[528,256]{1,0:T(8,128)(2,1)S(1)}, u32[]{:S(2)}, u32[]{:S(2)}) %collective-permute-start.12) | collective-permute-done | bytes 270368 | tf_op jit(solution)/shard_map/ppermute | solution.py:41
  55.5 1.4 %attend_hop4_part1.1 = (bf16[528,256]{1,0:T(8,128)(2,1)S(1)}, bf16[128,512]{1,0:T(8,128)(2,1)S(1)}, bf16[512,128]{1,0:T(8,128)(2,1)S(1)}) custom-call(s32[8]{0:T(128)S(1)} %copy-done.6, s32[1]{0:T(128)S(6)} %copy.23.shared.refs_1_, s32[4,8]{1,0:T(4,128)S(1)} %bitcast.52, bf16[256,1024]{1,0:T(8,128)(2,1)S(1)} %collective-permute-done.1.refs_3_, ...), custom_call_target="tpu_custom_call" | custom-call | flops 67108864 | bytes 524288 | tf_op jit(solution)/shard_map/attend_hop4_part1/pallas_call | solution.py:553
  56.8 1.7 %collective-permute-start.17 = (bf16[528,256]{1,0:T(8,128)(2,1)S(1)}, bf16[528,256]{1,0:T(8,128)(2,1)S(1)}, u32[]{:S(2)}, u32[]{:S(2)}) collective-permute-start(bf16[528,256]{1,0:T(8,128)(2,1)S(1)} %get-tuple-element.101), channel_id=1, source_target_pairs={{0,2},{2,0},{4,6},{6,4},{8,10},{10,8},{12,14},{14,12},{16,18},{18,... | collective-permute-start | bytes 811016 | tf_op jit(solution)/shard_map/ppermute | solution.py:41
  58.6 3.7 %attend_own_part1.1 = (f32[512,256]{1,0:T(8,128)S(1)}, f32[8,256]{1,0:T(8,128)S(1)}) custom-call(s32[8]{0:T(128)S(1)} %copy-done.6, s32[1]{0:T(128)S(6)} %copy.23.shared.refs_1_, s32[4,8]{1,0:T(4,128)S(1)} %bitcast.53, bf16[256,1024]{1,0:T(8,128)(2,1)S(1)} %get-tuple-element.64.refs_3_, bf16[384,1024]{1,0:T(8,128)(2,1)S(1)} %get-tuple-element.71.refs_4_, ...), custom_call_target="tpu_custom_call" | custom-call | flops 805306368 | bytes 6291456 | tf_op jit(solution)/shard_map/attend_own_part1/pallas_call | solution.py:553
  62.3 3.7 %attend_own_part0.1 = (f32[512,256]{1,0:T(8,128)S(1)}, f32[8,256]{1,0:T(8,128)S(1)}) custom-call(s32[8]{0:T(128)S(1)} %copy-done.6, s32[1]{0:T(128)S(6)} %copy.23.shared.refs_1_, s32[4,8]{1,0:T(4,128)S(1)} %bitcast.54, bf16[256,1024]{1,0:T(8,128)(2,1)S(1)} %get-tuple-element.64.refs_3_, bf16[384,1024]{1,0:T(8,128)(2,1)S(1)} %get-tuple-element.71.refs_4_, ...), custom_call_target="tpu_custom_call" | custom-call | flops 805306368 | bytes 6291456 | tf_op jit(solution)/shard_map/attend_own_part0/pallas_call | solution.py:553
  66.0 1.0 %combine_send.1 = (bf16[256,1024]{1,0:T(8,128)(2,1)S(1)}, bf16[1,256,1024]{2,1,0:T(8,128)(2,1)S(1)}) custom-call(f32[512,256]{1,0:T(8,128)S(1)} %get-tuple-element.109.refs_0_, f32[512,256]{1,0:T(8,128)S(1)} %get-tuple-element.116.refs_1_, f32[8,256]{1,0:T(8,128)S(1)} %get-tuple-element.117.refs_2_, f32[8,256]{1,0:T(8,128)S(1)} %get-tuple-element.118.refs_3_, ...), custom_call_target="tpu_custom_call" | custom-call | flops 536870912 | bytes 4194304 | tf_op jit(solution)/shard_map/combine_send/pallas_call | solution.py:619
  67.1 0.7 %keep_own.1 = f32[256,1024]{1,0:T(8,128)S(1)} custom-call(bf16[256,1024]{1,0:T(8,128)(2,1)S(1)} %get-tuple-element.119.attended, bf16[1024,2048]{1,0:T(8,128)(2,1)S(1)} %copy-done, bf16[256,1024]{1,0:T(8,128)(2,1)S(1)} %copy-done.2), custom_call_target="tpu_custom_call" | custom-call | flops 536870912 | bytes 4194304 | tf_op jit(solution)/shard_map/keep_own/pallas_call | solution.py:645
  67.8 1.2 %collective-permute-done.18 = bf16[256,1024]{1,0:T(8,128)(2,1)S(1)} collective-permute-done((bf16[256,1024]{1,0:T(8,128)(2,1)S(1)}, bf16[256,1024]{1,0:T(8,128)(2,1)S(1)}, u32[]{:S(2)}, u32[]{:S(2)}) %collective-permute-start.18) | collective-permute-done | bytes 524320 | tf_op jit(solution)/shard_map/ppermute | solution.py:41
  69.0 0.9 %add_convert_fusion = bf16[256,1024]{1,0:T(8,128)(2,1)} fusion(f32[256,1024]{1,0:T(8,128)S(1)} %keep_own.1, bf16[256,1024]{1,0:T(8,128)(2,1)S(1)} %collective-permute-done.18), kind=kLoop, calls=%fused_computation | loop fusion | flops 786432 | bytes 2097152 | tf_op jit(solution)/shard_map/convert_element_type | solution.py:798
  (47 shorter events, 6.7 us)
Async XLA Ops:
  0.6 15.2 %collective-permute-start.3 = (bf16[2048,128]{1,0:T(8,128)(2,1)}, bf16[2048,128]{1,0:T(8,128)(2,1)S(1)}, u32[]{:S(2)}, u32[]{:S(2)}) collective-permute-start(bf16[2048,128]{1,0:T(8,128)(2,1)} %bitcast.43), channel_id=1, source_target_pairs={{0,4},{2,6},{8,0},{10,2},{16,8},{18,10},{24,16},{26,18},{28,24},{3... | collective-permute-start | bytes 1572872 | tf_op jit(solution)/shard_map/ppermute | solution.py:50
  3.6 13.6 %collective-permute-start.2 = (bf16[2048,128]{1,0:T(8,128)(2,1)}, bf16[2048,128]{1,0:T(8,128)(2,1)S(1)}, u32[]{:S(2)}, u32[]{:S(2)}) collective-permute-start(bf16[2048,128]{1,0:T(8,128)(2,1)} %bitcast.44), channel_id=1, source_target_pairs={{0,8},{2,10},{8,16},{10,18},{16,24},{18,26},{24,28},{26,30},{28,20... | collective-permute-start | bytes 1572872 | tf_op jit(solution)/shard_map/ppermute | solution.py:50
  3.8 13.5 %collective-permute-start = (bf16[256,1024]{1,0:T(8,128)(2,1)}, bf16[256,1024]{1,0:T(8,128)(2,1)S(1)}, u32[]{:S(2)}, u32[]{:S(2)}) collective-permute-start(bf16[256,1024]{1,0:T(8,128)(2,1)} %hidden.1), channel_id=1, source_target_pairs={{0,1},{1,0},{2,3},{3,2},{4,5},{5,4},{6,7},{7,6},{8,9},{9,8},{10,11... | collective-permute-start | bytes 1572872 | tf_op jit(solution)/shard_map/ppermute | solution.py:41
  3.8 6.2 %copy-start.6 = (s32[8]{0:T(128)S(1)}, s32[8]{0:T(128)}, u32[]{:S(2)}) copy-start(s32[8]{0:T(128)} %refs_0_.12) | copy-start | bytes 100
  3.8 13.5 %copy-start.1 = (bf16[2048,1024]{1,0:T(8,128)(2,1)S(1)}, bf16[2048,1024]{1,0:T(8,128)(2,1)}, u32[]{:S(2)}) copy-start(bf16[2048,1024]{1,0:T(8,128)(2,1)} %refs_2_.1) | copy-start | bytes 12582916
  3.8 13.5 %copy-start.2 = (bf16[256,1024]{1,0:T(8,128)(2,1)S(1)}, bf16[256,1024]{1,0:T(8,128)(2,1)}, u32[]{:S(2)}) copy-start(bf16[256,1024]{1,0:T(8,128)(2,1)} %hidden.1) | copy-start | bytes 1572868
  17.3 9.0 %copy-start.3 = (bf16[2,128,2,1024]{3,2,1,0:T(2,128)(2,1)S(1)}, bf16[2,128,2,1024]{3,2,1,0:T(2,128)(2,1)}, u32[]{:S(2)}) copy-start(bf16[2,128,2,1024]{3,2,1,0:T(2,128)(2,1)} %param.14) | copy-start | bytes 3145732
  17.3 9.0 %copy-start.4 = (bf16[128,2,1024]{2,1,0:T(2,128)(2,1)S(1)}, bf16[128,2,1024]{2,1,0:T(2,128)(2,1)}, u32[]{:S(2)}) copy-start(bf16[128,2,1024]{2,1,0:T(2,128)(2,1)} %param.13) | copy-start | bytes 1572868
  17.3 14.7 %copy-start.5 = (s32[8,4]{0,1:T(4,128)S(1)}, s32[8,4]{0,1:T(4,128)}, u32[]{:S(2)}) copy-start(s32[8,4]{0,1:T(4,128)} %param.15) | copy-start | bytes 388
  19.4 12.7 %collective-permute-start.1 = (bf16[256,1024]{1,0:T(8,128)(2,1)S(1)}, bf16[256,1024]{1,0:T(8,128)(2,1)S(1)}, u32[]{:S(2)}, u32[]{:S(2)}) collective-permute-start(bf16[256,1024]{1,0:T(8,128)(2,1)S(1)} %get-tuple-element.64.refs_3_), channel_id=1, source_target_pairs={{0,2},{2,0},{4,6},{6,4},{8,10},{10,8},{12,14},{14,12},{16,18},{18,... | collective-permute-start | bytes 1572872 | tf_op jit(solution)/shard_map/ppermute | solution.py:41
  21.0 8.5 %collective-permute-start.6 = (bf16[1024,128]{1,0:T(8,128)(2,1)S(1)}, bf16[1024,128]{1,0:T(8,128)(2,1)S(1)}, u32[]{:S(2)}, u32[]{:S(2)}) collective-permute-start(bf16[1024,128]{1,0:T(8,128)(2,1)S(1)} %get-tuple-element.80), channel_id=1, source_target_pairs={{0,8},{2,10},{8,16},{10,18},{16,24},{18,26},{24,28},{26,30},{28,20... | collective-permute-start | bytes 786440 | tf_op jit(solution)/shard_map/ppermute | solution.py:50
  21.5 6.5 %collective-permute-start.8 = (bf16[1024,128]{1,0:T(8,128)(2,1)S(1)}, bf16[1024,128]{1,0:T(8,128)(2,1)S(1)}, u32[]{:S(2)}, u32[]{:S(2)}) collective-permute-start(bf16[1024,128]{1,0:T(8,128)(2,1)S(1)} %get-tuple-element.82), channel_id=1, source_target_pairs={{0,4},{2,6},{8,0},{10,2},{16,8},{18,10},{24,16},{26,18},{28,24},{3... | collective-permute-start | bytes 786440 | tf_op jit(solution)/shard_map/ppermute | solution.py:50
  28.0 11.4 %collective-permute-start.10 = (bf16[1024,128]{1,0:T(8,128)(2,1)S(1)}, bf16[1024,128]{1,0:T(8,128)(2,1)S(1)}, u32[]{:S(2)}, u32[]{:S(2)}) collective-permute-start(bf16[1024,128]{1,0:T(8,128)(2,1)S(1)} %collective-permute-done.8.refs_5_), channel_id=1, source_target_pairs={{0,4},{2,6},{8,0},{10,2},{16,8},{18,10},{24,16},{26,18},{28,24},{3... | collective-permute-start | bytes 786440 | tf_op jit(solution)/shard_map/ppermute | solution.py:50
  29.4 10.0 %collective-permute-start.7 = (bf16[1024,128]{1,0:T(8,128)(2,1)S(1)}, bf16[1024,128]{1,0:T(8,128)(2,1)S(1)}, u32[]{:S(2)}, u32[]{:S(2)}) collective-permute-start(bf16[1024,128]{1,0:T(8,128)(2,1)S(1)} %collective-permute-done.6.refs_4_), channel_id=1, source_target_pairs={{0,8},{2,10},{8,16},{10,18},{16,24},{18,26},{24,28},{26,30},{28,20... | collective-permute-start | bytes 786440 | tf_op jit(solution)/shard_map/ppermute | solution.py:50
  30.0 11.5 %collective-permute-start.5 = (bf16[1024,128]{1,0:T(8,128)(2,1)S(1)}, bf16[1024,128]{1,0:T(8,128)(2,1)S(1)}, u32[]{:S(2)}, u32[]{:S(2)}) collective-permute-start(bf16[1024,128]{1,0:T(8,128)(2,1)S(1)} %get-tuple-element.69), channel_id=1, source_target_pairs={{0,4},{2,6},{8,0},{10,2},{16,8},{18,10},{24,16},{26,18},{28,24},{3... | collective-permute-start | bytes 786440 | tf_op jit(solution)/shard_map/ppermute | solution.py:50
  31.5 11.5 %collective-permute-start.4 = (bf16[1024,128]{1,0:T(8,128)(2,1)S(1)}, bf16[1024,128]{1,0:T(8,128)(2,1)S(1)}, u32[]{:S(2)}, u32[]{:S(2)}) collective-permute-start(bf16[1024,128]{1,0:T(8,128)(2,1)S(1)} %get-tuple-element.68), channel_id=1, source_target_pairs={{0,8},{2,10},{8,16},{10,18},{16,24},{18,26},{24,28},{26,30},{28,20... | collective-permute-start | bytes 786440 | tf_op jit(solution)/shard_map/ppermute | solution.py:50
  39.5 7.3 %collective-permute-start.11 = (bf16[512,128]{1,0:T(8,128)(2,1)S(1)}, bf16[512,128]{1,0:T(8,128)(2,1)S(1)}, u32[]{:S(2)}, u32[]{:S(2)}) collective-permute-start(bf16[512,128]{1,0:T(8,128)(2,1)S(1)} %slice.29), channel_id=1, source_target_pairs={{0,4},{2,6},{8,0},{10,2},{16,8},{18,10},{24,16},{26,18},{28,24},{3... | collective-permute-start | bytes 393224 | tf_op jit(solution)/shard_map/ppermute | solution.py:50
  40.9 5.9 %collective-permute-start.9 = (bf16[512,128]{1,0:T(8,128)(2,1)S(1)}, bf16[512,128]{1,0:T(8,128)(2,1)S(1)}, u32[]{:S(2)}, u32[]{:S(2)}) collective-permute-start(bf16[512,128]{1,0:T(8,128)(2,1)S(1)} %slice.28), channel_id=1, source_target_pairs={{0,8},{2,10},{8,16},{10,18},{16,24},{18,26},{24,28},{26,30},{28,20... | collective-permute-start | bytes 393224 | tf_op jit(solution)/shard_map/ppermute | solution.py:50
  41.5 8.0 %collective-permute-start.15 = (bf16[1024,128]{1,0:T(8,128)(2,1)S(1)}, bf16[1024,128]{1,0:T(8,128)(2,1)S(1)}, u32[]{:S(2)}, u32[]{:S(2)}) collective-permute-start(bf16[1024,128]{1,0:T(8,128)(2,1)S(1)} %collective-permute-done.5.refs_5_), channel_id=1, source_target_pairs={{0,4},{2,6},{8,0},{10,2},{16,8},{18,10},{24,16},{26,18},{28,24},{3... | collective-permute-start | bytes 786440 | tf_op jit(solution)/shard_map/ppermute | solution.py:50
  43.0 7.2 %collective-permute-start.13 = (bf16[1024,128]{1,0:T(8,128)(2,1)S(1)}, bf16[1024,128]{1,0:T(8,128)(2,1)S(1)}, u32[]{:S(2)}, u32[]{:S(2)}) collective-permute-start(bf16[1024,128]{1,0:T(8,128)(2,1)S(1)} %collective-permute-done.4.refs_4_), channel_id=1, source_target_pairs={{0,8},{2,10},{8,16},{10,18},{16,24},{18,26},{24,28},{26,30},{28,20... | collective-permute-start | bytes 786440 | tf_op jit(solution)/shard_map/ppermute | solution.py:50
  45.2 20.8 %copy-start = (bf16[1024,2048]{1,0:T(8,128)(2,1)S(1)}, bf16[1024,2048]{1,0:T(8,128)(2,1)}, u32[]{:S(2)}) copy-start(bf16[1024,2048]{1,0:T(8,128)(2,1)} %weight.1) | copy-start | bytes 12582916
  48.2 6.5 %collective-permute-start.12 = (bf16[528,256]{1,0:T(8,128)(2,1)S(1)}, bf16[528,256]{1,0:T(8,128)(2,1)S(1)}, u32[]{:S(2)}, u32[]{:S(2)}) collective-permute-start(bf16[528,256]{1,0:T(8,128)(2,1)S(1)} %get-tuple-element.92), channel_id=1, source_target_pairs={{0,2},{2,0},{4,6},{6,4},{8,10},{10,8},{12,14},{14,12},{16,18},{18,... | collective-permute-start | bytes 811016 | tf_op jit(solution)/shard_map/ppermute | solution.py:41
  50.2 5.0 %collective-permute-start.14 = (bf16[512,128]{1,0:T(8,128)(2,1)S(1)}, bf16[512,128]{1,0:T(8,128)(2,1)S(1)}, u32[]{:S(2)}, u32[]{:S(2)}) collective-permute-start(bf16[512,128]{1,0:T(8,128)(2,1)S(1)} %slice.30), channel_id=1, source_target_pairs={{0,8},{2,10},{8,16},{10,18},{16,24},{18,26},{24,28},{26,30},{28,20... | collective-permute-start | bytes 393224 | tf_op jit(solution)/shard_map/ppermute | solution.py:50
  50.5 5.0 %collective-permute-start.16 = (bf16[512,128]{1,0:T(8,128)(2,1)S(1)}, bf16[512,128]{1,0:T(8,128)(2,1)S(1)}, u32[]{:S(2)}, u32[]{:S(2)}) collective-permute-start(bf16[512,128]{1,0:T(8,128)(2,1)S(1)} %slice.31), channel_id=1, source_target_pairs={{0,4},{2,6},{8,0},{10,2},{16,8},{18,10},{24,16},{26,18},{28,24},{3... | collective-permute-start | bytes 393224 | tf_op jit(solution)/shard_map/ppermute | solution.py:50
  56.8 9.1 %collective-permute-start.17 = (bf16[528,256]{1,0:T(8,128)(2,1)S(1)}, bf16[528,256]{1,0:T(8,128)(2,1)S(1)}, u32[]{:S(2)}, u32[]{:S(2)}) collective-permute-start(bf16[528,256]{1,0:T(8,128)(2,1)S(1)} %get-tuple-element.101), channel_id=1, source_target_pairs={{0,2},{2,0},{4,6},{6,4},{8,10},{10,8},{12,14},{14,12},{16,18},{18,... | collective-permute-start | bytes 811016 | tf_op jit(solution)/shard_map/ppermute | solution.py:41
  67.0 2.0 %collective-permute-start.18 = (bf16[256,1024]{1,0:T(8,128)(2,1)S(1)}, bf16[256,1024]{1,0:T(8,128)(2,1)S(1)}, u32[]{:S(2)}, u32[]{:S(2)}) collective-permute-start(bf16[256,1024]{1,0:T(8,128)(2,1)S(1)} %bitcast.55), channel_id=1, source_target_pairs={{0,1},{1,0},{2,3},{3,2},{4,5},{5,4},{6,7},{7,6},{8,9},{9,8},{10,11... | collective-permute-start | bytes 1572872 | tf_op jit(solution)/shard_map/ppermute | solution.py:41

commit v13 on v12

--- a/solution.py
+++ b/solution.py
@@ -675,15 +675,11 @@
     ahead, behind = {part: [None] for part in every}, {part: [None] for part in every}
     nearest = []
     for blocks, way in ((ahead, 1), (behind, -1)):
-        block = turn(prompt, cycle, group, way)
-        nearest.append(block)
-        split = block.reshape(piece, pieces_out, 2 * few, HD)
-        for part in every:
-            blocks[part].append(split[:, part].reshape(-1, HD))
+        nearest.append(turn(prompt, cycle, group, way))
 
     def step(part, *others):
         for blocks, way in ((ahead, 1), (behind, -1)):
-            block = after(blocks[part][-1], *others)
+            block = after(blocks[part][-1], *others) if others else blocks[part][-1]
             if len(blocks[part]) == half:
                 cut = middle * 2 * few
                 block = block[:cut] if way == 1 else block[cut:]
@@ -698,7 +694,11 @@
     queries = [query] + [swap(query, "seq", shift) for shift in range(1, group)]
     tail = viewed(tail_cache.reshape(-1, 2, tail_cache.shape[3]))
     slots = tail_cache.shape[0]
-    step(0, weight, query)
+    for blocks, block in zip((ahead, behind), nearest):
+        split = after(block, weight, query).reshape(piece, pieces_out, 2 * few, HD)
+        for part in every:
+            blocks[part].append(split[:, part].reshape(-1, HD))
+    step(0)
     ready = after(cosine, *nearest)
     fresh_keys, fresh_values, fresh_turned = project_keyval(normed, weight, ready, sine)
     if two:
@@ -726,7 +726,6 @@
         False,
         "attend_near_others",
     )
-    new_cache, token = weave(fresh_keys, fresh_values, theirs[1][0])
     state = {part: theirs for part in every}
     rest = {part: [] for part in every}
     rest_rings = [(sign * hop, 0, piece) for hop in range(2, half) for sign in (-1, 1)]
@@ -771,17 +770,17 @@
     own = {}
     received = {}
     hop_others(facts, 0, 2)
+    step(0, state[0][1][1])
+    hop_others(facts, 0, 3)
     if two:
-        step(1, state[0][1][1], token)
-    step(0, state[0][1][1], token)
+        step(1, state[0][1][1])
+    hop_others(facts, 0, 4)
+    new_cache, token = weave(fresh_keys, fresh_values, state[0][1][0])
     if two:
-        hop_others(facts, 1, 2)
-        facts = (after(tail_len, state[1][1][1]), shared_len, table)
-    hop_others(facts, 0, 3)
-    hop_others(facts, 0, 4)
+        hop_others((after(tail_len, token), shared_len, table), 1, 2)
     received[0] = [swap(state[0][shift][0], "seq", shift) for shift in others]
     if two:
-        step(1, state[0][1][0])
+        step(1, state[1][1][1])
         hop_others(facts, 1, 3)
         facts = (after(tail_len, received[0][0]), shared_len, table)
         hop_others(facts, 1, 4)

time: 70.1 us -> 67.8 us (0.967)
  waiting for transfers between devices: 10.2 us -> 8.18 us
    ppermute x14, waiting for transfers between devices: 8.21 us -> 6.99 us  [turn(): return lax.ppermute(value, 'seq', pairs)]
    ppermute x5, waiting for transfers between devices: 2.02 us -> 1.18 us  [swap(): return lax.ppermute(value, axis, pairs)]
  transfers between devices with their start and end apart: 19 -> 19, of which waited for: 8 -> 7; matrix products, arithmetic and copies ran while one was open for 1% -> 1% of each run, Pallas kernels for 46% -> 50%
where the time goes in v13:
time: 67.8 us; the launch traced here: 67.6 us
  Pallas kernels  36.3 us (54%)
  starting transfers between devices  19.9 us (29%)
  waiting for transfers between devices  8.18 us (12%)
  between operations  1.61 us (2%)
  other arithmetic  1.43 us (2%)
    pallas_call x9, Pallas kernels, attend(): pl.pallas_call(functools.partial(attend_kernel, (group, shifts, rings, sl...  20.8 us
    ppermute x14, starting transfers between devices, turn(): return lax.ppermute(value, 'seq', pairs)  15.5 us
    ppermute x14, waiting for transfers between devices, turn(): return lax.ppermute(value, 'seq', pairs)  6.99 us
    pallas_call x1, Pallas kernels, part_weights(): pl.pallas_call(weight_kernel, in_specs=[HBM], out_specs=VMEM, out_shape=j...  5.5 us
    ppermute x5, starting transfers between devices, swap(): return lax.ppermute(value, axis, pairs)  4.4 us
    pallas_call x1, Pallas kernels, project_keyval(): pl.pallas_call(keyval_kernel, in_specs=[VMEM] * 4, out_specs=[VMEM] * 3,...  2.53 us
    pallas_call x1, Pallas kernels, project_query(): pl.pallas_call(query_kernel, in_specs=[VMEM] * (len(pieces) + 3), out_spe...  2.02 us
    pallas_call x2, Pallas kernels, part_keyval(): pl.pallas_call(part_kernel, in_specs=[VMEM] * len(blocks), out_specs=[VME...  1.72 us
  transfers between devices with their start and end apart: 19, of which 7 were waited for; matrix products, arithmetic and copies ran while one was open for 1% of the time, Pallas kernels for 50%

profile of v13, /device:TPU:0, one launch (start us, length us, event | category | flops | bytes accessed | tf_op | source)
XLA Modules:
  0.0 67.6 jit_solution(4548798381561935850)
XLA Ops:
  0.6 3.0 %collective-permute-start.4 = (bf16[2048,128]{1,0:T(8,128)(2,1)}, bf16[2048,128]{1,0:T(8,128)(2,1)S(1)}, u32[]{:S(2)}, u32[]{:S(2)}) collective-permute-start(bf16[2048,128]{1,0:T(8,128)(2,1)} %bitcast.43), channel_id=1, source_target_pairs={{0,4},{2,6},{8,0},{10,2},{16,8},{18,10},{24,16},{26,18},{28,24},{3... | collective-permute-start | bytes 1572872 | tf_op jit(solution)/shard_map/ppermute | solution.py:50
  3.8 5.5 %part_weights.1.weight = bf16[2,2048,1024]{2,1,0:T(8,128)(2,1)S(1)} custom-call(bf16[32768,128]{1,0:T(8,128)(2,1)} %bitcast.56), custom_call_target="tpu_custom_call" | custom-call | flops 2147483648 | bytes 16777216 | tf_op jit(solution)/shard_map/part_weights/pallas_call | solution.py:251
  11.1 2.0 %project_query.1 = (bf16[256,1024]{1,0:T(8,128)(2,1)S(1)}, bf16[256,2048]{1,0:T(8,128)(2,1)S(1)}) custom-call(bf16[256,1024]{1,0:T(8,128)(2,1)S(1)} %copy-done.2, bf16[256,1024]{1,0:T(8,128)(2,1)S(1)} %collective-permute-done.refs_1_, bf16[2048,1024]{1,0:T(8,128)(2,1)S(1)} %copy-done.1, f32[256,128]{1,0:T(8,128)S(1)} %get-tuple-element.67.refs_3_.cosine, ...), custom_call_target="tpu_custom_call" | custom-call | flops 1073741824 | bytes 4194304 | tf_op jit(solution)/shard_map/project_query/pallas_call | solution.py:212
  13.1 1.9 %collective-permute-start.1 = (bf16[256,1024]{1,0:T(8,128)(2,1)S(1)}, bf16[256,1024]{1,0:T(8,128)(2,1)S(1)}, u32[]{:S(2)}, u32[]{:S(2)}) collective-permute-start(bf16[256,1024]{1,0:T(8,128)(2,1)S(1)} %get-tuple-element.64.refs_3_), channel_id=1, source_target_pairs={{0,2},{2,0},{4,6},{6,4},{8,10},{10,8},{12,14},{14,12},{16,18},{18,... | collective-permute-start | bytes 1572872 | tf_op jit(solution)/shard_map/ppermute | solution.py:41
  15.9 1.4 %collective-permute-done.2.refs_0_ = bf16[2048,128]{1,0:T(8,128)(2,1)S(1)} collective-permute-done((bf16[2048,128]{1,0:T(8,128)(2,1)}, bf16[2048,128]{1,0:T(8,128)(2,1)S(1)}, u32[]{:S(2)}, u32[]{:S(2)}) %collective-permute-start.2) | collective-permute-done | bytes 524320 | tf_op jit(solution)/shard_map/ppermute | solution.py:50
  17.7 1.6 %collective-permute-start.6 = (bf16[1024,128]{1,0:T(8,128)(2,1)S(1)}, bf16[1024,128]{1,0:T(8,128)(2,1)S(1)}, u32[]{:S(2)}, u32[]{:S(2)}) collective-permute-start(bf16[1024,128]{1,0:T(8,128)(2,1)S(1)} %get-tuple-element.123), channel_id=1, source_target_pairs={{0,4},{2,6},{8,0},{10,2},{16,8},{18,10},{24,16},{26,18},{28,24},{3... | collective-permute-start | bytes 786440 | tf_op jit(solution)/shard_map/ppermute | solution.py:50
  19.4 2.5 %project_keyval.1 = (bf16[256,1024]{1,0:T(8,128)(2,1)S(1)}, bf16[256,1024]{1,0:T(8,128)(2,1)S(1)}, bf16[1024,256]{1,0:T(8,128)(2,1)S(1)}) custom-call(bf16[256,2048]{1,0:T(8,128)(2,1)S(1)} %get-tuple-element.66.normed, bf16[2,2048,1024]{2,1,0:T(8,128)(2,1)S(1)} %part_weights.1.weight, f32[256,128]{1,0:T(8,128)S(1)} %get-tuple-element.67.refs_3_.cosine, ...), custom_call_target="tpu_custom_call" | custom-call | flops 2147483648 | bytes 8388608 | tf_op jit(solution)/shard_map/project_keyval/pallas_call | solution.py:284
  23.7 1.3 %collective-permute-done.6.refs_5_ = bf16[1024,128]{1,0:T(8,128)(2,1)S(1)} collective-permute-done((bf16[1024,128]{1,0:T(8,128)(2,1)S(1)}, bf16[1024,128]{1,0:T(8,128)(2,1)S(1)}, u32[]{:S(2)}, u32[]{:S(2)}) %collective-permute-start.6) | collective-permute-done | bytes 262176 | tf_op jit(solution)/shard_map/ppermute | solution.py:50
  24.9 1.0 %collective-permute-start.8 = (bf16[1024,128]{1,0:T(8,128)(2,1)S(1)}, bf16[1024,128]{1,0:T(8,128)(2,1)S(1)}, u32[]{:S(2)}, u32[]{:S(2)}) collective-permute-start(bf16[1024,128]{1,0:T(8,128)(2,1)S(1)} %collective-permute-done.6.refs_5_), channel_id=1, source_target_pairs={{0,4},{2,6},{8,0},{10,2},{16,8},{18,10},{24,16},{26,18},{28,24},{3... | collective-permute-start | bytes 786440 | tf_op jit(solution)/shard_map/ppermute | solution.py:50
  25.9 1.0 %collective-permute-start.5 = (bf16[1024,128]{1,0:T(8,128)(2,1)S(1)}, bf16[1024,128]{1,0:T(8,128)(2,1)S(1)}, u32[]{:S(2)}, u32[]{:S(2)}) collective-permute-start(bf16[1024,128]{1,0:T(8,128)(2,1)S(1)} %collective-permute-done.3.refs_4_), channel_id=1, source_target_pairs={{0,8},{2,10},{8,16},{10,18},{16,24},{18,26},{24,28},{26,30},{28,20... | collective-permute-start | bytes 786440 | tf_op jit(solution)/shard_map/ppermute | solution.py:50
  27.0 1.0 %collective-permute-start.13 = (bf16[1024,128]{1,0:T(8,128)(2,1)S(1)}, bf16[1024,128]{1,0:T(8,128)(2,1)S(1)}, u32[]{:S(2)}, u32[]{:S(2)}) collective-permute-start(bf16[1024,128]{1,0:T(8,128)(2,1)S(1)} %get-tuple-element.93), channel_id=1, source_target_pairs={{0,4},{2,6},{8,0},{10,2},{16,8},{18,10},{24,16},{26,18},{28,24},{3... | collective-permute-start | bytes 786440 | tf_op jit(solution)/shard_map/ppermute | solution.py:50
  28.0 1.0 %collective-permute-start.11 = (bf16[1024,128]{1,0:T(8,128)(2,1)S(1)}, bf16[1024,128]{1,0:T(8,128)(2,1)S(1)}, u32[]{:S(2)}, u32[]{:S(2)}) collective-permute-start(bf16[1024,128]{1,0:T(8,128)(2,1)S(1)} %get-tuple-element.88), channel_id=1, source_target_pairs={{0,8},{2,10},{8,16},{10,18},{16,24},{18,26},{24,28},{26,30},{28,20... | collective-permute-start | bytes 786440 | tf_op jit(solution)/shard_map/ppermute | solution.py:50
  29.0 4.3 %attend_near_others.1 = (f32[1024,256]{1,0:T(8,128)S(1)}, f32[8,256]{1,0:T(8,128)S(1)}) custom-call(s32[8]{0:T(128)S(1)} %copy-done.6, s32[1]{0:T(128)S(6)} %copy.23.shared.refs_1_, s32[4,8]{1,0:T(4,128)S(1)} %bitcast.46, bf16[256,1024]{1,0:T(8,128)(2,1)S(1)} %collective-permute-done.1.refs_3_, bf16[384,1024]{1,0:T(8,128)(2,1)S(1)} %get-tuple-element.70.refs_4_, ...), custom_call_target="tpu_custom_call" | custom-call | flops 939524096 | bytes 3670016 | tf_op jit(solution)/shard_map/attend_near_others/pallas_call | solution.py:553
  33.3 1.6 %attend_hop2_part0.1 = (f32[512,256]{1,0:T(8,128)S(1)}, f32[8,256]{1,0:T(8,128)S(1)}, bf16[256,512]{1,0:T(8,128)(2,1)S(1)}, bf16[512,256]{1,0:T(8,128)(2,1)S(1)}) custom-call(s32[8]{0:T(128)S(1)} %copy-done.6, s32[1]{0:T(128)S(6)} %copy.23.shared.refs_1_, s32[4,8]{1,0:T(4,128)S(1)} %bitcast.47, bf16[256,1024]{1,0:T(8,128)(2,1)S(1)} %collective-permute-done.1.refs_3_, ...), custom_call_target="tpu_custom_call" | custom-call | flops 134217728 | bytes 1048576 | tf_op jit(solution)/shard_map/attend_hop2_part0/pallas_call | solution.py:553
  35.0 1.0 %collective-permute-start.9 = (bf16[512,128]{1,0:T(8,128)(2,1)S(1)}, bf16[512,128]{1,0:T(8,128)(2,1)S(1)}, u32[]{:S(2)}, u32[]{:S(2)}) collective-permute-start(bf16[512,128]{1,0:T(8,128)(2,1)S(1)} %slice.27), channel_id=1, source_target_pairs={{0,4},{2,6},{8,0},{10,2},{16,8},{18,10},{24,16},{26,18},{28,24},{3... | collective-permute-start | bytes 393224 | tf_op jit(solution)/shard_map/ppermute | solution.py:50
  36.0 1.0 %collective-permute-start.7 = (bf16[512,128]{1,0:T(8,128)(2,1)S(1)}, bf16[512,128]{1,0:T(8,128)(2,1)S(1)}, u32[]{:S(2)}, u32[]{:S(2)}) collective-permute-start(bf16[512,128]{1,0:T(8,128)(2,1)S(1)} %slice.26), channel_id=1, source_target_pairs={{0,8},{2,10},{8,16},{10,18},{16,24},{18,26},{24,28},{26,30},{28,20... | collective-permute-start | bytes 393224 | tf_op jit(solution)/shard_map/ppermute | solution.py:50
  37.1 1.6 %attend_hop3_part0.1 = (f32[512,256]{1,0:T(8,128)S(1)}, f32[8,256]{1,0:T(8,128)S(1)}, bf16[256,512]{1,0:T(8,128)(2,1)S(1)}, bf16[512,256]{1,0:T(8,128)(2,1)S(1)}) custom-call(s32[8]{0:T(128)S(1)} %copy-done.6, s32[1]{0:T(128)S(6)} %copy.23.shared.refs_1_, s32[4,8]{1,0:T(4,128)S(1)} %bitcast.48, bf16[256,1024]{1,0:T(8,128)(2,1)S(1)} %collective-permute-done.1.refs_3_, ...), custom_call_target="tpu_custom_call" | custom-call | flops 134217728 | bytes 1048576 | tf_op jit(solution)/shard_map/attend_hop3_part0/pallas_call | solution.py:553
  38.7 1.0 %collective-permute-start.15 = (bf16[1024,128]{1,0:T(8,128)(2,1)S(1)}, bf16[1024,128]{1,0:T(8,128)(2,1)S(1)}, u32[]{:S(2)}, u32[]{:S(2)}) collective-permute-start(bf16[1024,128]{1,0:T(8,128)(2,1)S(1)} %collective-permute-done.13.refs_5_), channel_id=1, source_target_pairs={{0,4},{2,6},{8,0},{10,2},{16,8},{18,10},{24,16},{26,18},{28,24},{3... | collective-permute-start | bytes 786440 | tf_op jit(solution)/shard_map/ppermute | solution.py:50
  39.7 1.0 %collective-permute-start.12 = (bf16[1024,128]{1,0:T(8,128)(2,1)S(1)}, bf16[1024,128]{1,0:T(8,128)(2,1)S(1)}, u32[]{:S(2)}, u32[]{:S(2)}) collective-permute-start(bf16[1024,128]{1,0:T(8,128)(2,1)S(1)} %collective-permute-done.11.refs_4_), channel_id=1, source_target_pairs={{0,8},{2,10},{8,16},{10,18},{16,24},{18,26},{24,28},{26,30},{28,20... | collective-permute-start | bytes 786440 | tf_op jit(solution)/shard_map/ppermute | solution.py:50
  41.4 1.4 %attend_hop4_part0.1 = (bf16[528,256]{1,0:T(8,128)(2,1)S(1)}, bf16[128,512]{1,0:T(8,128)(2,1)S(1)}, bf16[512,128]{1,0:T(8,128)(2,1)S(1)}) custom-call(s32[8]{0:T(128)S(1)} %copy-done.6, s32[1]{0:T(128)S(6)} %copy.23.shared.refs_1_, s32[4,8]{1,0:T(4,128)S(1)} %bitcast.49, bf16[256,1024]{1,0:T(8,128)(2,1)S(1)} %collective-permute-done.1.refs_3_, ...), custom_call_target="tpu_custom_call" | custom-call | flops 67108864 | bytes 524288 | tf_op jit(solution)/shard_map/attend_hop4_part0/pallas_call | solution.py:553
  42.8 1.6 %collective-permute-start.10 = (bf16[528,256]{1,0:T(8,128)(2,1)S(1)}, bf16[528,256]{1,0:T(8,128)(2,1)S(1)}, u32[]{:S(2)}, u32[]{:S(2)}) collective-permute-start(bf16[528,256]{1,0:T(8,128)(2,1)S(1)} %get-tuple-element.86.refs_0_), channel_id=1, source_target_pairs={{0,2},{2,0},{4,6},{6,4},{8,10},{10,8},{12,14},{14,12},{16,18},{18,... | collective-permute-start | bytes 811016 | tf_op jit(solution)/shard_map/ppermute | solution.py:41
  44.3 1.4 %weave_cache.1 = (bf16[4096,128]{1,0:T(8,128)(2,1)}, f32[8,128]{1,0:T(8,128)S(1)}) custom-call(bf16[256,1024]{1,0:T(8,128)(2,1)S(1)} %get-tuple-element.68.refs_8_.keys.refs_14_, bf16[256,1024]{1,0:T(8,128)(2,1)S(1)} %get-tuple-element.90.values, bf16[528,256]{1,0:T(8,128)(2,1)S(1)} %get-tuple-element.86.refs_0_), custom_call_target="tpu_custom_call" | custom-call | flops 268435456 | bytes 2097152 | tf_op jit(solution)/shard_map/weave_cache/pallas_call | solution.py:323
  45.7 1.6 %attend_hop2_part1.1 = (f32[512,256]{1,0:T(8,128)S(1)}, f32[8,256]{1,0:T(8,128)S(1)}, bf16[256,512]{1,0:T(8,128)(2,1)S(1)}, bf16[512,256]{1,0:T(8,128)(2,1)S(1)}) custom-call(s32[8]{0:T(128)S(1)} %copy-done.6, s32[1]{0:T(128)S(6)} %copy.23.shared.refs_1_, s32[4,8]{1,0:T(4,128)S(1)} %bitcast.50, bf16[256,1024]{1,0:T(8,128)(2,1)S(1)} %collective-permute-done.1.refs_3_, ...), custom_call_target="tpu_custom_call" | custom-call | flops 134217728 | bytes 1048576 | tf_op jit(solution)/shard_map/attend_hop2_part1/pallas_call | solution.py:553
  47.4 1.6 %collective-permute-start.16 = (bf16[512,128]{1,0:T(8,128)(2,1)S(1)}, bf16[512,128]{1,0:T(8,128)(2,1)S(1)}, u32[]{:S(2)}, u32[]{:S(2)}) collective-permute-start(bf16[512,128]{1,0:T(8,128)(2,1)S(1)} %slice.31), channel_id=1, source_target_pairs={{0,4},{2,6},{8,0},{10,2},{16,8},{18,10},{24,16},{26,18},{28,24},{3... | collective-permute-start | bytes 393224 | tf_op jit(solution)/shard_map/ppermute | solution.py:50
  49.5 1.6 %attend_hop3_part1.1 = (f32[512,256]{1,0:T(8,128)S(1)}, f32[8,256]{1,0:T(8,128)S(1)}, bf16[256,512]{1,0:T(8,128)(2,1)S(1)}, bf16[512,256]{1,0:T(8,128)(2,1)S(1)}) custom-call(s32[8]{0:T(128)S(1)} %copy-done.6, s32[1]{0:T(128)S(6)} %copy.23.shared.refs_1_, s32[4,8]{1,0:T(4,128)S(1)} %bitcast.51, bf16[256,1024]{1,0:T(8,128)(2,1)S(1)} %collective-permute-done.1.refs_3_, ...), custom_call_target="tpu_custom_call" | custom-call | flops 134217728 | bytes 1048576 | tf_op jit(solution)/shard_map/attend_hop3_part1/pallas_call | solution.py:553
  51.1 1.3 %collective-permute-done.16.refs_5_ = bf16[512,128]{1,0:T(8,128)(2,1)S(1)} collective-permute-done((bf16[512,128]{1,0:T(8,128)(2,1)S(1)}, bf16[512,128]{1,0:T(8,128)(2,1)S(1)}, u32[]{:S(2)}, u32[]{:S(2)}) %collective-permute-start.16) | collective-permute-done | bytes 131104 | tf_op jit(solution)/shard_map/ppermute | solution.py:50
  52.4 1.6 %collective-permute-done.14.refs_4_ = bf16[512,128]{1,0:T(8,128)(2,1)S(1)} collective-permute-done((bf16[512,128]{1,0:T(8,128)(2,1)S(1)}, bf16[512,128]{1,0:T(8,128)(2,1)S(1)}, u32[]{:S(2)}, u32[]{:S(2)}) %collective-permute-start.14) | collective-permute-done | bytes 131104 | tf_op jit(solution)/shard_map/ppermute | solution.py:50
  54.0 1.4 %attend_hop4_part1.1 = (bf16[528,256]{1,0:T(8,128)(2,1)S(1)}, bf16[128,512]{1,0:T(8,128)(2,1)S(1)}, bf16[512,128]{1,0:T(8,128)(2,1)S(1)}) custom-call(s32[8]{0:T(128)S(1)} %copy-done.6, s32[1]{0:T(128)S(6)} %copy.23.shared.refs_1_, s32[4,8]{1,0:T(4,128)S(1)} %bitcast.52, bf16[256,1024]{1,0:T(8,128)(2,1)S(1)} %collective-permute-done.1.refs_3_, ...), custom_call_target="tpu_custom_call" | custom-call | flops 67108864 | bytes 524288 | tf_op jit(solution)/shard_map/attend_hop4_part1/pallas_call | solution.py:553
  56.2 3.7 %attend_own_part1.1 = (f32[512,256]{1,0:T(8,128)S(1)}, f32[8,256]{1,0:T(8,128)S(1)}) custom-call(s32[8]{0:T(128)S(1)} %copy-done.6, s32[1]{0:T(128)S(6)} %copy.23.shared.refs_1_, s32[4,8]{1,0:T(4,128)S(1)} %bitcast.53, bf16[256,1024]{1,0:T(8,128)(2,1)S(1)} %get-tuple-element.64.refs_3_, bf16[384,1024]{1,0:T(8,128)(2,1)S(1)} %get-tuple-element.70.refs_4_, ...), custom_call_target="tpu_custom_call" | custom-call | flops 805306368 | bytes 6291456 | tf_op jit(solution)/shard_map/attend_own_part1/pallas_call | solution.py:553
  59.9 3.7 %attend_own_part0.1 = (f32[512,256]{1,0:T(8,128)S(1)}, f32[8,256]{1,0:T(8,128)S(1)}) custom-call(s32[8]{0:T(128)S(1)} %copy-done.6, s32[1]{0:T(128)S(6)} %copy.23.shared.refs_1_, s32[4,8]{1,0:T(4,128)S(1)} %bitcast.54, bf16[256,1024]{1,0:T(8,128)(2,1)S(1)} %get-tuple-element.64.refs_3_, bf16[384,1024]{1,0:T(8,128)(2,1)S(1)} %get-tuple-element.70.refs_4_, ...), custom_call_target="tpu_custom_call" | custom-call | flops 805306368 | bytes 6291456 | tf_op jit(solution)/shard_map/attend_own_part0/pallas_call | solution.py:553
  63.6 1.0 %combine_send.1 = (bf16[256,1024]{1,0:T(8,128)(2,1)S(1)}, bf16[1,256,1024]{2,1,0:T(8,128)(2,1)S(1)}) custom-call(f32[512,256]{1,0:T(8,128)S(1)} %get-tuple-element.109.refs_0_, f32[512,256]{1,0:T(8,128)S(1)} %get-tuple-element.116.refs_1_, f32[8,256]{1,0:T(8,128)S(1)} %get-tuple-element.117.refs_2_, f32[8,256]{1,0:T(8,128)S(1)} %get-tuple-element.118.refs_3_, ...), custom_call_target="tpu_custom_call" | custom-call | flops 536870912 | bytes 4194304 | tf_op jit(solution)/shard_map/combine_send/pallas_call | solution.py:619
  65.5 1.2 %collective-permute-done.18 = bf16[256,1024]{1,0:T(8,128)(2,1)S(1)} collective-permute-done((bf16[256,1024]{1,0:T(8,128)(2,1)S(1)}, bf16[256,1024]{1,0:T(8,128)(2,1)S(1)}, u32[]{:S(2)}, u32[]{:S(2)}) %collective-permute-start.18) | collective-permute-done | bytes 524320 | tf_op jit(solution)/shard_map/ppermute | solution.py:41
  (47 shorter events, 7.9 us)
Async XLA Ops:
  0.6 15.2 %collective-permute-start.4 = (bf16[2048,128]{1,0:T(8,128)(2,1)}, bf16[2048,128]{1,0:T(8,128)(2,1)S(1)}, u32[]{:S(2)}, u32[]{:S(2)}) collective-permute-start(bf16[2048,128]{1,0:T(8,128)(2,1)} %bitcast.43), channel_id=1, source_target_pairs={{0,4},{2,6},{8,0},{10,2},{16,8},{18,10},{24,16},{26,18},{28,24},{3... | collective-permute-start | bytes 1572872 | tf_op jit(solution)/shard_map/ppermute | solution.py:50
  3.6 13.6 %collective-permute-start.2 = (bf16[2048,128]{1,0:T(8,128)(2,1)}, bf16[2048,128]{1,0:T(8,128)(2,1)S(1)}, u32[]{:S(2)}, u32[]{:S(2)}) collective-permute-start(bf16[2048,128]{1,0:T(8,128)(2,1)} %bitcast.44), channel_id=1, source_target_pairs={{0,8},{2,10},{8,16},{10,18},{16,24},{18,26},{24,28},{26,30},{28,20... | collective-permute-start | bytes 1572872 | tf_op jit(solution)/shard_map/ppermute | solution.py:50
  3.8 7.3 %collective-permute-start = (bf16[256,1024]{1,0:T(8,128)(2,1)}, bf16[256,1024]{1,0:T(8,128)(2,1)S(1)}, u32[]{:S(2)}, u32[]{:S(2)}) collective-permute-start(bf16[256,1024]{1,0:T(8,128)(2,1)} %hidden.1), channel_id=1, source_target_pairs={{0,1},{1,0},{2,3},{3,2},{4,5},{5,4},{6,7},{7,6},{8,9},{9,8},{10,11... | collective-permute-start | bytes 1572872 | tf_op jit(solution)/shard_map/ppermute | solution.py:41
  3.8 6.2 %copy-start.6 = (s32[8]{0:T(128)S(1)}, s32[8]{0:T(128)}, u32[]{:S(2)}) copy-start(s32[8]{0:T(128)} %refs_0_.14) | copy-start | bytes 100
  3.8 7.3 %copy-start.1 = (bf16[2048,1024]{1,0:T(8,128)(2,1)S(1)}, bf16[2048,1024]{1,0:T(8,128)(2,1)}, u32[]{:S(2)}) copy-start(bf16[2048,1024]{1,0:T(8,128)(2,1)} %refs_2_.1) | copy-start | bytes 12582916
  3.8 7.3 %copy-start.2 = (bf16[256,1024]{1,0:T(8,128)(2,1)S(1)}, bf16[256,1024]{1,0:T(8,128)(2,1)}, u32[]{:S(2)}) copy-start(bf16[256,1024]{1,0:T(8,128)(2,1)} %hidden.1) | copy-start | bytes 1572868
  11.1 11.6 %copy-start.3 = (bf16[2,128,2,1024]{3,2,1,0:T(2,128)(2,1)S(1)}, bf16[2,128,2,1024]{3,2,1,0:T(2,128)(2,1)}, u32[]{:S(2)}) copy-start(bf16[2,128,2,1024]{3,2,1,0:T(2,128)(2,1)} %param.14) | copy-start | bytes 3145732
  11.1 11.6 %copy-start.4 = (bf16[128,2,1024]{2,1,0:T(2,128)(2,1)S(1)}, bf16[128,2,1024]{2,1,0:T(2,128)(2,1)}, u32[]{:S(2)}) copy-start(bf16[128,2,1024]{2,1,0:T(2,128)(2,1)} %param.13) | copy-start | bytes 1572868
  13.1 15.9 %copy-start.5 = (s32[8,4]{0,1:T(4,128)S(1)}, s32[8,4]{0,1:T(4,128)}, u32[]{:S(2)}) copy-start(s32[8,4]{0,1:T(4,128)} %param.15) | copy-start | bytes 388
  13.1 15.9 %collective-permute-start.1 = (bf16[256,1024]{1,0:T(8,128)(2,1)S(1)}, bf16[256,1024]{1,0:T(8,128)(2,1)S(1)}, u32[]{:S(2)}, u32[]{:S(2)}) collective-permute-start(bf16[256,1024]{1,0:T(8,128)(2,1)S(1)} %get-tuple-element.64.refs_3_), channel_id=1, source_target_pairs={{0,2},{2,0},{4,6},{6,4},{8,10},{10,8},{12,14},{14,12},{16,18},{18,... | collective-permute-start | bytes 1572872 | tf_op jit(solution)/shard_map/ppermute | solution.py:41
  17.3 8.7 %collective-permute-start.3 = (bf16[1024,128]{1,0:T(8,128)(2,1)S(1)}, bf16[1024,128]{1,0:T(8,128)(2,1)S(1)}, u32[]{:S(2)}, u32[]{:S(2)}) collective-permute-start(bf16[1024,128]{1,0:T(8,128)(2,1)S(1)} %get-tuple-element.125), channel_id=1, source_target_pairs={{0,8},{2,10},{8,16},{10,18},{16,24},{18,26},{24,28},{26,30},{28,20... | collective-permute-start | bytes 786440 | tf_op jit(solution)/shard_map/ppermute | solution.py:50
  17.7 7.2 %collective-permute-start.6 = (bf16[1024,128]{1,0:T(8,128)(2,1)S(1)}, bf16[1024,128]{1,0:T(8,128)(2,1)S(1)}, u32[]{:S(2)}, u32[]{:S(2)}) collective-permute-start(bf16[1024,128]{1,0:T(8,128)(2,1)S(1)} %get-tuple-element.123), channel_id=1, source_target_pairs={{0,4},{2,6},{8,0},{10,2},{16,8},{18,10},{24,16},{26,18},{28,24},{3... | collective-permute-start | bytes 786440 | tf_op jit(solution)/shard_map/ppermute | solution.py:50
  24.9 10.0 %collective-permute-start.8 = (bf16[1024,128]{1,0:T(8,128)(2,1)S(1)}, bf16[1024,128]{1,0:T(8,128)(2,1)S(1)}, u32[]{:S(2)}, u32[]{:S(2)}) collective-permute-start(bf16[1024,128]{1,0:T(8,128)(2,1)S(1)} %collective-permute-done.6.refs_5_), channel_id=1, source_target_pairs={{0,4},{2,6},{8,0},{10,2},{16,8},{18,10},{24,16},{26,18},{28,24},{3... | collective-permute-start | bytes 786440 | tf_op jit(solution)/shard_map/ppermute | solution.py:50
  25.9 9.0 %collective-permute-start.5 = (bf16[1024,128]{1,0:T(8,128)(2,1)S(1)}, bf16[1024,128]{1,0:T(8,128)(2,1)S(1)}, u32[]{:S(2)}, u32[]{:S(2)}) collective-permute-start(bf16[1024,128]{1,0:T(8,128)(2,1)S(1)} %collective-permute-done.3.refs_4_), channel_id=1, source_target_pairs={{0,8},{2,10},{8,16},{10,18},{16,24},{18,26},{24,28},{26,30},{28,20... | collective-permute-start | bytes 786440 | tf_op jit(solution)/shard_map/ppermute | solution.py:50
  27.0 11.7 %collective-permute-start.13 = (bf16[1024,128]{1,0:T(8,128)(2,1)S(1)}, bf16[1024,128]{1,0:T(8,128)(2,1)S(1)}, u32[]{:S(2)}, u32[]{:S(2)}) collective-permute-start(bf16[1024,128]{1,0:T(8,128)(2,1)S(1)} %get-tuple-element.93), channel_id=1, source_target_pairs={{0,4},{2,6},{8,0},{10,2},{16,8},{18,10},{24,16},{26,18},{28,24},{3... | collective-permute-start | bytes 786440 | tf_op jit(solution)/shard_map/ppermute | solution.py:50
  28.0 11.8 %collective-permute-start.11 = (bf16[1024,128]{1,0:T(8,128)(2,1)S(1)}, bf16[1024,128]{1,0:T(8,128)(2,1)S(1)}, u32[]{:S(2)}, u32[]{:S(2)}) collective-permute-start(bf16[1024,128]{1,0:T(8,128)(2,1)S(1)} %get-tuple-element.88), channel_id=1, source_target_pairs={{0,8},{2,10},{8,16},{10,18},{16,24},{18,26},{24,28},{26,30},{28,20... | collective-permute-start | bytes 786440 | tf_op jit(solution)/shard_map/ppermute | solution.py:50
  35.0 5.8 %collective-permute-start.9 = (bf16[512,128]{1,0:T(8,128)(2,1)S(1)}, bf16[512,128]{1,0:T(8,128)(2,1)S(1)}, u32[]{:S(2)}, u32[]{:S(2)}) collective-permute-start(bf16[512,128]{1,0:T(8,128)(2,1)S(1)} %slice.27), channel_id=1, source_target_pairs={{0,4},{2,6},{8,0},{10,2},{16,8},{18,10},{24,16},{26,18},{28,24},{3... | collective-permute-start | bytes 393224 | tf_op jit(solution)/shard_map/ppermute | solution.py:50
  36.0 5.3 %collective-permute-start.7 = (bf16[512,128]{1,0:T(8,128)(2,1)S(1)}, bf16[512,128]{1,0:T(8,128)(2,1)S(1)}, u32[]{:S(2)}, u32[]{:S(2)}) collective-permute-start(bf16[512,128]{1,0:T(8,128)(2,1)S(1)} %slice.26), channel_id=1, source_target_pairs={{0,8},{2,10},{8,16},{10,18},{16,24},{18,26},{24,28},{26,30},{28,20... | collective-permute-start | bytes 393224 | tf_op jit(solution)/shard_map/ppermute | solution.py:50
  38.7 8.7 %collective-permute-start.15 = (bf16[1024,128]{1,0:T(8,128)(2,1)S(1)}, bf16[1024,128]{1,0:T(8,128)(2,1)S(1)}, u32[]{:S(2)}, u32[]{:S(2)}) collective-permute-start(bf16[1024,128]{1,0:T(8,128)(2,1)S(1)} %collective-permute-done.13.refs_5_), channel_id=1, source_target_pairs={{0,4},{2,6},{8,0},{10,2},{16,8},{18,10},{24,16},{26,18},{28,24},{3... | collective-permute-start | bytes 786440 | tf_op jit(solution)/shard_map/ppermute | solution.py:50
  39.7 7.6 %collective-permute-start.12 = (bf16[1024,128]{1,0:T(8,128)(2,1)S(1)}, bf16[1024,128]{1,0:T(8,128)(2,1)S(1)}, u32[]{:S(2)}, u32[]{:S(2)}) collective-permute-start(bf16[1024,128]{1,0:T(8,128)(2,1)S(1)} %collective-permute-done.11.refs_4_), channel_id=1, source_target_pairs={{0,8},{2,10},{8,16},{10,18},{16,24},{18,26},{24,28},{26,30},{28,20... | collective-permute-start | bytes 786440 | tf_op jit(solution)/shard_map/ppermute | solution.py:50
  42.8 8.3 %collective-permute-start.10 = (bf16[528,256]{1,0:T(8,128)(2,1)S(1)}, bf16[528,256]{1,0:T(8,128)(2,1)S(1)}, u32[]{:S(2)}, u32[]{:S(2)}) collective-permute-start(bf16[528,256]{1,0:T(8,128)(2,1)S(1)} %get-tuple-element.86.refs_0_), channel_id=1, source_target_pairs={{0,2},{2,0},{4,6},{6,4},{8,10},{10,8},{12,14},{14,12},{16,18},{18,... | collective-permute-start | bytes 811016 | tf_op jit(solution)/shard_map/ppermute | solution.py:41
  45.7 17.9 %copy-start = (bf16[1024,2048]{1,0:T(8,128)(2,1)S(1)}, bf16[1024,2048]{1,0:T(8,128)(2,1)}, u32[]{:S(2)}) copy-start(bf16[1024,2048]{1,0:T(8,128)(2,1)} %weight.1) | copy-start | bytes 12582916
  47.4 5.0 %collective-permute-start.16 = (bf16[512,128]{1,0:T(8,128)(2,1)S(1)}, bf16[512,128]{1,0:T(8,128)(2,1)S(1)}, u32[]{:S(2)}, u32[]{:S(2)}) collective-permute-start(bf16[512,128]{1,0:T(8,128)(2,1)S(1)} %slice.31), channel_id=1, source_target_pairs={{0,4},{2,6},{8,0},{10,2},{16,8},{18,10},{24,16},{26,18},{28,24},{3... | collective-permute-start | bytes 393224 | tf_op jit(solution)/shard_map/ppermute | solution.py:50
  49.0 5.0 %collective-permute-start.14 = (bf16[512,128]{1,0:T(8,128)(2,1)S(1)}, bf16[512,128]{1,0:T(8,128)(2,1)S(1)}, u32[]{:S(2)}, u32[]{:S(2)}) collective-permute-start(bf16[512,128]{1,0:T(8,128)(2,1)S(1)} %slice.30), channel_id=1, source_target_pairs={{0,8},{2,10},{8,16},{10,18},{16,24},{18,26},{24,28},{26,30},{28,20... | collective-permute-start | bytes 393224 | tf_op jit(solution)/shard_map/ppermute | solution.py:50
  55.4 8.3 %collective-permute-start.17 = (bf16[528,256]{1,0:T(8,128)(2,1)S(1)}, bf16[528,256]{1,0:T(8,128)(2,1)S(1)}, u32[]{:S(2)}, u32[]{:S(2)}) collective-permute-start(bf16[528,256]{1,0:T(8,128)(2,1)S(1)} %get-tuple-element.101), channel_id=1, source_target_pairs={{0,2},{2,0},{4,6},{6,4},{8,10},{10,8},{12,14},{14,12},{16,18},{18,... | collective-permute-start | bytes 811016 | tf_op jit(solution)/shard_map/ppermute | solution.py:41
  64.7 2.0 %collective-permute-start.18 = (bf16[256,1024]{1,0:T(8,128)(2,1)S(1)}, bf16[256,1024]{1,0:T(8,128)(2,1)S(1)}, u32[]{:S(2)}, u32[]{:S(2)}) collective-permute-start(bf16[256,1024]{1,0:T(8,128)(2,1)S(1)} %bitcast.55), channel_id=1, source_target_pairs={{0,1},{1,0},{2,3},{3,2},{4,5},{5,4},{6,7},{7,6},{8,9},{9,8},{10,11... | collective-permute-start | bytes 1572872 | tf_op jit(solution)/shard_map/ppermute | solution.py:41

commit v14 on v10

--- a/solution.py
+++ b/solution.py
@@ -337,7 +337,7 @@
 
 
 def attend_kernel(spec, *refs):
-    group, shifts, rings, slots, piece, parted, first, last = spec
+    group, shifts, rings, slots, piece, parted, first, last, lowest, heads = spec
     fresh = slots > 0
     refs = list(refs)
     take = lambda count: [refs.pop(0) for _ in range(count)]
@@ -362,7 +362,7 @@
         values_here = take(1)[0]
         keys_here, turned_here = sources[0]
     rows, width = queries[0].shape
-    heads = width // HD
+    stride = 2 * width // HD
     cycle = cycle_of(group)
     seq = lax.axis_index("seq")
     request, member = seq // group, seq % group
@@ -394,10 +394,10 @@
             causal[:, i * rows : (i + 1) * rows] = jnp.where(theirs <= mine, 0.0, NEGATIVE)
     if not parted:
         offset = 0
-        order = order_rows(2 * heads, False)
+        order = order_rows(stride, False)
         for block in raw:
             take_apart(block, order, keys_here, values_here, offset)
-            offset += block.shape[0] // (2 * heads)
+            offset += block.shape[0] // stride
         turn_heads(values_here, turned_here)
     many = len(shifts) * rows
     unit = jnp.where(lax.broadcasted_iota(jnp.int32, (many, HD), 1) == 0, 1.0, 0.0)
@@ -415,11 +415,11 @@
         return values[0] if len(values) == 1 else jnp.concatenate(values, axis=axis)
 
     def query_of(head):
-        return jnp.concatenate([beside([q[:, lanes(head * HD)] for q in queries], 0), unit], axis=1)
+        return jnp.concatenate([beside([q[:, lanes((lowest + head) * HD)] for q in queries], 0), unit], axis=1)
 
     def score(head, query, chunk, scores, top):
         (keys, _), start, size, at, masked = chunk
-        keys = keys[start : start + size, lanes(head * HD)]
+        keys = keys[start : start + size, lanes((lowest + head) * HD)]
         keys = jnp.concatenate([keys, bias[at : at + size, :]], axis=1)
         part = lax.dot_general(keys, query, ACROSS, preferred_element_type=jnp.float32)
         if masked:
@@ -433,7 +433,7 @@
         weights = jnp.exp2((scores[at : at + size, :] - top) * SCALE)
         here = jnp.sum(weights, axis=0, keepdims=True)
         product = jnp.dot(
-            turned[lanes(head * HD), start : start + size],
+            turned[lanes((lowest + head) * HD), start : start + size],
             weights.astype(jnp.bfloat16),
             preferred_element_type=jnp.float32,
         )
@@ -446,7 +446,7 @@
         line = lambda k: pl.ds(base + k, 1)
         each = range(together)
         if not first:
-            olds = [beside([extent[line(k), :] for extent in old_extents], 1) for k in each]
+            olds = [beside([extent[line(lowest + k), :] for extent in old_extents], 1) for k in each]
             tops = [jnp.maximum(top, old * (1.0 / SCALE)) for top, old in zip(tops, olds)]
         next_tops = [None] * together
         sums = [None] * together
@@ -464,7 +464,7 @@
             if not first:
                 factor = jnp.exp2(olds[k] - tops[k] * SCALE)
                 summed = summed + factor
-                old_mix = beside([old_mix[span(k), :] for old_mix in old_mixes], 1)
+                old_mix = beside([old_mix[span(lowest + k), :] for old_mix in old_mixes], 1)
                 mixed = mixed + old_mix * factor
             mixed = mixed * (1.0 / summed)
             extent = tops[k] * SCALE + jnp.log2(summed)
@@ -502,18 +502,18 @@
             gap = stat_rows(heads) - 3 * heads
             if gap:
                 packed.append(jnp.zeros((gap, rows), jnp.float32))
-            results[i][width:, :] = jnp.concatenate(packed, axis=0).astype(jnp.bfloat16)
+            results[i][heads * HD :, :] = jnp.concatenate(packed, axis=0).astype(jnp.bfloat16)
 
 
 def stat_rows(heads):
     return -(-3 * heads // 16) * 16
 
 
-def attend(facts, queries, shifts, rings, slots, piece, blocks, parted, old, last, name):
+def attend(facts, queries, shifts, rings, slots, piece, blocks, parted, old, last, name, within=None):
     group = len(queries)
     queries = [queries[shift] for shift in shifts]
     rows, width = queries[0].shape
-    heads = width // HD
+    lowest, heads = within or (0, width // HD)
     parted = len(blocks) // 2 if parted else 0
     operands = [*facts, *queries, *blocks]
     if old:
@@ -530,9 +530,9 @@
     if not parted:
         scratch.append(pltpu.VMEM((count, width), jnp.bfloat16))
     mixes = [
-        jax.ShapeDtypeStruct((width + stat_rows(heads), rows), jnp.bfloat16)
+        jax.ShapeDtypeStruct((heads * HD + stat_rows(heads), rows), jnp.bfloat16)
         if last and shift
-        else jax.ShapeDtypeStruct((width, rows), jnp.float32)
+        else jax.ShapeDtypeStruct((heads * HD, rows), jnp.float32)
         for shift in shifts
     ]
     extents = [
@@ -547,7 +547,8 @@
         ]
     results = pl.pallas_call(
         functools.partial(
-            attend_kernel, (group, shifts, rings, slots, piece, parted, not old, last)
+            attend_kernel,
+            (group, shifts, rings, slots, piece, parted, not old, last, lowest, heads),
         ),
         in_specs=[SMEM] * 3 + [VMEM] * (len(operands) - 3),
         out_specs=[VMEM] * len(shapes),
@@ -565,14 +566,19 @@
     return state, results[len(results) - 2 :]
 
 
-def combine_kernel(*refs):
-    result, extent, *parts, weight, _, attended, sent = refs
+def combine_kernel(pieces, *refs):
+    result, extent, *pairs, weight, _, attended, sent = refs
     width, rows = result.shape
     heads = width // HD
     extents = [extent[:heads, :]]
+    few = heads // pieces
+    parts = [pairs[start : start + pieces] for start in range(0, len(pairs), pieces)]
     for part in parts:
-        lines = part[width:, :].astype(jnp.float32)
-        extents.append(sum(lines[i * heads : (i + 1) * heads] for i in range(3)))
+        here = []
+        for half in part:
+            lines = half[few * HD :, :].astype(jnp.float32)
+            here.append(sum(lines[i * few : (i + 1) * few] for i in range(3)))
+        extents.append(here[0] if pieces == 1 else jnp.concatenate(here, axis=0))
     top = functools.reduce(jnp.maximum, extents)
     shares = [jnp.exp2(extent - top) for extent in extents]
     whole = sum(shares)
@@ -580,7 +586,10 @@
     unit = unit_matrix(rows)
     for head in range(heads):
         span = slice(head * HD, (head + 1) * HD)
-        mixes = [result[span, :]] + [part[span, :].astype(jnp.float32) for part in parts]
+        line = head % few * HD
+        mixes = [result[span, :]] + [
+            part[head // few][line : line + HD, :].astype(jnp.float32) for part in parts
+        ]
         mixed = sum(mix * share[head : head + 1] for mix, share in zip(mixes, shares))
         attended[:, span] = turned_over(unit, mixed.astype(jnp.bfloat16))
     index = lax.axis_index("tp")
@@ -594,11 +603,11 @@
         ).astype(jnp.bfloat16)
 
 
-def combine(result, extent, parts, w_out, token, ways):
+def combine(result, extent, parts, pieces, w_out, token, ways):
     width, rows = result.shape
     columns = w_out.shape[1] // ways
     return pl.pallas_call(
-        combine_kernel,
+        functools.partial(combine_kernel, pieces),
         in_specs=[VMEM] * (4 + len(parts)),
         out_specs=[VMEM] * 2,
         out_shape=[
@@ -718,12 +727,32 @@
         rest_rings += rings
     rings = [(-half, 0, middle), (half, middle, piece - middle)]
     blocks = [ahead[0][half], behind[1][half]]
-    theirs, parted = attend(
-        facts, queries, others, rings, 0, piece, blocks, False, theirs, True, "attend_far_others"
-    )
+    heads = width // HD
+    pieces_out = 2 if heads >= 4 else 1
+    few = heads // pieces_out
+    sending = []
+    parted = False
+    for lowest in range(0, heads, few):
+        name = f"attend_far_others{lowest}"
+        last, made = attend(
+            facts,
+            queries,
+            others,
+            rings,
+            0,
+            piece,
+            parted or blocks,
+            bool(parted),
+            theirs,
+            True,
+            name,
+            (lowest, few),
+        )
+        parted = parted or made
+        sending.append([last[shift][0] for shift in others])
+        facts = (after(tail_len, sending[-1][0]), shared_len, table)
     rest += parted
     rest_rings += rings
-    facts = (after(tail_len, theirs[1][0]), shared_len, table)
     own, _ = attend(
         facts,
         queries,
@@ -737,9 +766,12 @@
         True,
         "attend_own",
     )
-    new_cache, token = weave(fresh_keys, fresh_values, theirs[1][0])
-    parts = [swap(theirs[shift][0], "seq", shift) for shift in others]
-    attended, sent = combine(*own[0], parts, w_out, token, ways)
+    arrivals = [
+        [swap(part[i], "seq", shift) for i, shift in enumerate(others)] for part in sending
+    ]
+    parts = [part[i] for i in range(len(others)) for part in arrivals]
+    new_cache, token = weave(fresh_keys, fresh_values, own[0][1], arrivals[0][0])
+    attended, sent = combine(*own[0], parts, pieces_out, w_out, token, ways)
     received = [swap(sent[shift - 1], "tp", shift) for shift in range(1, ways)]
     total = keep(attended, w_out, hidden_in)
     for part in received:

time: 65.6 us -> 65.4 us (level)
  waiting for transfers between devices: 13.3 us -> 11.3 us
  starting transfers between devices: 16.7 us -> 17.6 us
  Pallas kernels: 32.5 us -> 33.3 us
    ppermute x4 -> x5, waiting for transfers between devices: 4.48 us -> 2.42 us  [swap(): return lax.ppermute(value, axis, pairs)]
    ppermute x4 -> x5, starting transfers between devices: 3.24 us -> 4.16 us  [swap(): return lax.ppermute(value, axis, pairs)]
    pallas_call x5 -> x6, Pallas kernels: 17 us -> 17.8 us  [attend(): pl.pallas_call(functools.partial(attend_kernel, (group, shifts, rings, sl...]
  transfers between devices with their start and end apart: 16 -> 17, of which waited for: 8 -> 8; matrix products, arithmetic and copies ran while one was open for 1% -> 1% of each run, Pallas kernels for 45% -> 47%
where the time goes in v14:
time: 65.4 us; the launch traced here: 65.2 us
  Pallas kernels  33.3 us (51%)
  starting transfers between devices  17.6 us (27%)
  waiting for transfers between devices  11.3 us (17%)
  between operations  1.5 us (2%)
  other arithmetic  1.42 us (2%)
    pallas_call x6, Pallas kernels, attend(): pl.pallas_call(functools.partial(attend_kernel, (group, shifts, rings, sl...  17.8 us
    ppermute x12, starting transfers between devices, turn(): return lax.ppermute(value, 'seq', pairs)  13.4 us
    ppermute x12, waiting for transfers between devices, turn(): return lax.ppermute(value, 'seq', pairs)  8.87 us
    pallas_call x1, Pallas kernels, part_weights(): pl.pallas_call(weight_kernel, in_specs=[HBM], out_specs=VMEM, out_shape=j...  5.5 us
    ppermute x5, starting transfers between devices, swap(): return lax.ppermute(value, axis, pairs)  4.16 us
    pallas_call x1, Pallas kernels, project_keyval(): pl.pallas_call(keyval_kernel, in_specs=[VMEM] * 4, out_specs=[VMEM] * 3,...  2.54 us
    ppermute x5, waiting for transfers between devices, swap(): return lax.ppermute(value, axis, pairs)  2.42 us
    pallas_call x1, Pallas kernels, project_query(): pl.pallas_call(query_kernel, in_specs=[VMEM] * (len(pieces) + 3), out_spe...  2.02 us
  transfers between devices with their start and end apart: 17, of which 8 were waited for; matrix products, arithmetic and copies ran while one was open for 1% of the time, Pallas kernels for 47%

profile of v14, /device:TPU:0, one launch (start us, length us, event | category | flops | bytes accessed | tf_op | source)
XLA Modules:
  0.0 65.2 jit_solution(4065694974465572108)
XLA Ops:
  0.6 3.0 %collective-permute-start.4 = (bf16[2048,128]{1,0:T(8,128)(2,1)}, bf16[2048,128]{1,0:T(8,128)(2,1)S(1)}, u32[]{:S(2)}, u32[]{:S(2)}) collective-permute-start(bf16[2048,128]{1,0:T(8,128)(2,1)} %bitcast.23), channel_id=1, source_target_pairs={{0,4},{2,6},{8,0},{10,2},{16,8},{18,10},{24,16},{26,18},{28,24},{3... | collective-permute-start | bytes 1572872 | tf_op jit(solution)/shard_map/ppermute | solution.py:50
  3.8 5.5 %part_weights.1.weight = bf16[2,2048,1024]{2,1,0:T(8,128)(2,1)S(1)} custom-call(bf16[32768,128]{1,0:T(8,128)(2,1)} %bitcast.33), custom_call_target="tpu_custom_call" | custom-call | flops 2147483648 | bytes 16777216 | tf_op jit(solution)/shard_map/part_weights/pallas_call | solution.py:251
  10.0 0.6 positions.1
  11.1 2.0 %project_query.1 = (bf16[256,1024]{1,0:T(8,128)(2,1)S(1)}, bf16[256,2048]{1,0:T(8,128)(2,1)S(1)}) custom-call(bf16[256,1024]{1,0:T(8,128)(2,1)S(1)} %copy-done.2, bf16[256,1024]{1,0:T(8,128)(2,1)S(1)} %collective-permute-done.refs_1_, bf16[2048,1024]{1,0:T(8,128)(2,1)S(1)} %copy-done.1, f32[256,128]{1,0:T(8,128)S(1)} %get-tuple-element.50.refs_3_.cosine, ...), custom_call_target="tpu_custom_call" | custom-call | flops 1073741824 | bytes 4194304 | tf_op jit(solution)/shard_map/project_query/pallas_call | solution.py:212
  13.1 1.9 %collective-permute-start.1 = (bf16[256,1024]{1,0:T(8,128)(2,1)S(1)}, bf16[256,1024]{1,0:T(8,128)(2,1)S(1)}, u32[]{:S(2)}, u32[]{:S(2)}) collective-permute-start(bf16[256,1024]{1,0:T(8,128)(2,1)S(1)} %get-tuple-element.47.refs_3_), channel_id=1, source_target_pairs={{0,2},{2,0},{4,6},{6,4},{8,10},{10,8},{12,14},{14,12},{16,18},{18,... | collective-permute-start | bytes 1572872 | tf_op jit(solution)/shard_map/ppermute | solution.py:41
  15.1 0.8 %collective-permute-done.4.refs_1_ = bf16[2048,128]{1,0:T(8,128)(2,1)S(1)} collective-permute-done((bf16[2048,128]{1,0:T(8,128)(2,1)}, bf16[2048,128]{1,0:T(8,128)(2,1)S(1)}, u32[]{:S(2)}, u32[]{:S(2)}) %collective-permute-start.4) | collective-permute-done | bytes 524320 | tf_op jit(solution)/shard_map/ppermute | solution.py:50
  15.9 1.7 %collective-permute-start.7 = (bf16[1024,128]{1,0:T(8,128)(2,1)S(1)}, bf16[1024,128]{1,0:T(8,128)(2,1)S(1)}, u32[]{:S(2)}, u32[]{:S(2)}) collective-permute-start(bf16[1024,128]{1,0:T(8,128)(2,1)S(1)} %get-tuple-element.60), channel_id=1, source_target_pairs={{0,4},{2,6},{8,0},{10,2},{16,8},{18,10},{24,16},{26,18},{28,24},{3... | collective-permute-start | bytes 786440 | tf_op jit(solution)/shard_map/ppermute | solution.py:50
  18.1 1.7 %collective-permute-start.10 = (bf16[1024,128]{1,0:T(8,128)(2,1)S(1)}, bf16[1024,128]{1,0:T(8,128)(2,1)S(1)}, u32[]{:S(2)}, u32[]{:S(2)}) collective-permute-start(bf16[1024,128]{1,0:T(8,128)(2,1)S(1)} %get-tuple-element.63), channel_id=1, source_target_pairs={{0,8},{2,10},{8,16},{10,18},{16,24},{18,26},{24,28},{26,30},{28,20... | collective-permute-start | bytes 786440 | tf_op jit(solution)/shard_map/ppermute | solution.py:50
  20.1 2.5 %project_keyval.1 = (bf16[256,1024]{1,0:T(8,128)(2,1)S(1)}, bf16[256,1024]{1,0:T(8,128)(2,1)S(1)}, bf16[1024,256]{1,0:T(8,128)(2,1)S(1)}) custom-call(bf16[256,2048]{1,0:T(8,128)(2,1)S(1)} %get-tuple-element.49.normed, bf16[2,2048,1024]{2,1,0:T(8,128)(2,1)S(1)} %part_weights.1.weight, f32[256,128]{1,0:T(8,128)S(1)} %get-tuple-element.50.refs_3_.cosine, ...), custom_call_target="tpu_custom_call" | custom-call | flops 2147483648 | bytes 8388608 | tf_op jit(solution)/shard_map/project_keyval/pallas_call | solution.py:284
  22.6 2.6 %collective-permute-done.7.refs_7_ = bf16[1024,128]{1,0:T(8,128)(2,1)S(1)} collective-permute-done((bf16[1024,128]{1,0:T(8,128)(2,1)S(1)}, bf16[1024,128]{1,0:T(8,128)(2,1)S(1)}, u32[]{:S(2)}, u32[]{:S(2)}) %collective-permute-start.7) | collective-permute-done | bytes 262176 | tf_op jit(solution)/shard_map/ppermute | solution.py:50
  25.2 1.7 %collective-permute-start.8 = (bf16[1024,128]{1,0:T(8,128)(2,1)S(1)}, bf16[1024,128]{1,0:T(8,128)(2,1)S(1)}, u32[]{:S(2)}, u32[]{:S(2)}) collective-permute-start(bf16[1024,128]{1,0:T(8,128)(2,1)S(1)} %collective-permute-done.7.refs_7_), channel_id=1, source_target_pairs={{0,4},{2,6},{8,0},{10,2},{16,8},{18,10},{24,16},{26,18},{28,24},{3... | collective-permute-start | bytes 786440 | tf_op jit(solution)/shard_map/ppermute | solution.py:50
  27.3 1.0 %part_own.1 = (bf16[384,1024]{1,0:T(8,128)(2,1)S(1)}, bf16[1024,384]{1,0:T(8,128)(2,1)S(1)}) custom-call(bf16[4096,128]{1,0:T(8,128)(2,1)S(1)} %bitcast.22, bf16[2048,128]{1,0:T(8,128)(2,1)S(1)} %bitcast.25), custom_call_target="tpu_custom_call" | custom-call | flops 402653184 | bytes 3145728 | tf_op jit(solution)/shard_map/part_own/pallas_call | solution.py:170
  28.3 0.7 %part_near.1 = (bf16[256,1024]{1,0:T(8,128)(2,1)S(1)}, bf16[1024,256]{1,0:T(8,128)(2,1)S(1)}) custom-call(bf16[2048,128]{1,0:T(8,128)(2,1)S(1)} %collective-permute-done.2.refs_0_, bf16[2048,128]{1,0:T(8,128)(2,1)S(1)} %collective-permute-done.4.refs_1_), custom_call_target="tpu_custom_call" | custom-call | flops 268435456 | bytes 2097152 | tf_op jit(solution)/shard_map/part_near/pallas_call | solution.py:170
  29.0 3.5 %collective-permute-done.10.refs_5_ = bf16[1024,128]{1,0:T(8,128)(2,1)S(1)} collective-permute-done((bf16[1024,128]{1,0:T(8,128)(2,1)S(1)}, bf16[1024,128]{1,0:T(8,128)(2,1)S(1)}, u32[]{:S(2)}, u32[]{:S(2)}) %collective-permute-start.10) | collective-permute-done | bytes 262176 | tf_op jit(solution)/shard_map/ppermute | solution.py:50
  32.9 1.7 %collective-permute-start.13 = (bf16[1024,128]{1,0:T(8,128)(2,1)S(1)}, bf16[1024,128]{1,0:T(8,128)(2,1)S(1)}, u32[]{:S(2)}, u32[]{:S(2)}) collective-permute-start(bf16[1024,128]{1,0:T(8,128)(2,1)S(1)} %collective-permute-done.12.refs_6_), channel_id=1, source_target_pairs={{0,4},{2,6},{8,0},{10,2},{16,8},{18,10},{24,16},{26,18},{28,24},{3... | collective-permute-start | bytes 786440 | tf_op jit(solution)/shard_map/ppermute | solution.py:50
  34.6 4.3 %attend_near_others.1 = (f32[1024,256]{1,0:T(8,128)S(1)}, f32[8,256]{1,0:T(8,128)S(1)}) custom-call(s32[8]{0:T(128)S(1)} %copy-done.6, s32[1]{0:T(128)S(6)} %copy.15.shared.refs_1_, s32[4,8]{1,0:T(4,128)S(1)} %bitcast.26, bf16[256,1024]{1,0:T(8,128)(2,1)S(1)} %collective-permute-done.1.refs_3_, bf16[384,1024]{1,0:T(8,128)(2,1)S(1)} %get-tuple-element.53.refs_4_, ...), custom_call_target="tpu_custom_call" | custom-call | flops 939524096 | bytes 3670016 | tf_op jit(solution)/shard_map/attend_near_others/pallas_call | solution.py:548
  39.4 1.7 %collective-permute-start.9 = (bf16[1024,128]{1,0:T(8,128)(2,1)S(1)}, bf16[1024,128]{1,0:T(8,128)(2,1)S(1)}, u32[]{:S(2)}, u32[]{:S(2)}) collective-permute-start(bf16[1024,128]{1,0:T(8,128)(2,1)S(1)} %collective-permute-done.8.refs_7_), channel_id=1, source_target_pairs={{0,4},{2,6},{8,0},{10,2},{16,8},{18,10},{24,16},{26,18},{28,24},{3... | collective-permute-start | bytes 786440 | tf_op jit(solution)/shard_map/ppermute | solution.py:50
  41.0 2.2 %attend_hop2_others.1 = (f32[1024,256]{1,0:T(8,128)S(1)}, f32[8,256]{1,0:T(8,128)S(1)}, bf16[256,1024]{1,0:T(8,128)(2,1)S(1)}, bf16[1024,256]{1,0:T(8,128)(2,1)S(1)}) custom-call(s32[8]{0:T(128)S(1)} %copy-done.6, s32[1]{0:T(128)S(6)} %copy.15.shared.refs_1_, s32[4,8]{1,0:T(4,128)S(1)} %bitcast.27, bf16[256,1024]{1,0:T(8,128)(2,1)S(1)} %collective-permute-done.1.refs_3_, ...), custom_call_target="tpu_custom_call" | custom-call | flops 268435456 | bytes 1048576 | tf_op jit(solution)/shard_map/attend_hop2_others/pallas_call | solution.py:548
  43.3 0.6 collective-permute-done.11.refs_5_
  43.8 2.2 %attend_hop3_others.1 = (f32[1024,256]{1,0:T(8,128)S(1)}, f32[8,256]{1,0:T(8,128)S(1)}, bf16[256,1024]{1,0:T(8,128)(2,1)S(1)}, bf16[1024,256]{1,0:T(8,128)(2,1)S(1)}) custom-call(s32[8]{0:T(128)S(1)} %copy-done.6, s32[1]{0:T(128)S(6)} %copy.15.shared.refs_1_, s32[4,8]{1,0:T(4,128)S(1)} %bitcast.28, bf16[256,1024]{1,0:T(8,128)(2,1)S(1)} %collective-permute-done.1.refs_3_, ...), custom_call_target="tpu_custom_call" | custom-call | flops 268435456 | bytes 1048576 | tf_op jit(solution)/shard_map/attend_hop3_others/pallas_call | solution.py:548
  46.1 1.3 %collective-permute-done.6.refs_4_ = bf16[1024,128]{1,0:T(8,128)(2,1)S(1)} collective-permute-done((bf16[1024,128]{1,0:T(8,128)(2,1)S(1)}, bf16[1024,128]{1,0:T(8,128)(2,1)S(1)}, u32[]{:S(2)}, u32[]{:S(2)}) %collective-permute-start.6) | collective-permute-done | bytes 262176 | tf_op jit(solution)/shard_map/ppermute | solution.py:50
  47.4 1.6 %attend_far_others0.1 = (bf16[528,256]{1,0:T(8,128)(2,1)S(1)}, bf16[128,1024]{1,0:T(8,128)(2,1)S(1)}, bf16[1024,128]{1,0:T(8,128)(2,1)S(1)}) custom-call(s32[8]{0:T(128)S(1)} %copy-done.6, s32[1]{0:T(128)S(6)} %copy.15.shared.refs_1_, s32[4,8]{1,0:T(4,128)S(1)} %bitcast.29, bf16[256,1024]{1,0:T(8,128)(2,1)S(1)} %collective-permute-done.1.refs_3_, ...), custom_call_target="tpu_custom_call" | custom-call | flops 67108864 | bytes 524288 | tf_op jit(solution)/shard_map/attend_far_others0/pallas_call | solution.py:548
  49.0 1.2 %collective-permute-start.14 = (bf16[528,256]{1,0:T(8,128)(2,1)S(1)}, bf16[528,256]{1,0:T(8,128)(2,1)S(1)}, u32[]{:S(2)}, u32[]{:S(2)}) collective-permute-start(bf16[528,256]{1,0:T(8,128)(2,1)S(1)} %get-tuple-element.72), channel_id=1, source_target_pairs={{0,2},{2,0},{4,6},{6,4},{8,10},{10,8},{12,14},{14,12},{16,18},{18,... | collective-permute-start | bytes 811016 | tf_op jit(solution)/shard_map/ppermute | solution.py:41
  50.2 1.1 %attend_far_others4.1 = bf16[528,256]{1,0:T(8,128)(2,1)S(1)} custom-call(s32[8]{0:T(128)S(1)} %copy-done.6, s32[1]{0:T(128)S(6)} %copy.15.shared.refs_1_, s32[4,8]{1,0:T(4,128)S(1)} %bitcast.30, bf16[256,1024]{1,0:T(8,128)(2,1)S(1)} %collective-permute-done.1.refs_3_, bf16[128,1024]{1,0:T(8,128)(2,1)S(1)} %get-tuple-element.74.refs_4_.refs_12_, ...), custom_call_target="tpu_custom_call" | custom-call | flops 67108864 | bytes 524288 | tf_op jit(solution)/shard_map/attend_far_others4/pallas_call | solution.py:548
  51.3 0.9 %collective-permute-start.15 = (bf16[528,256]{1,0:T(8,128)(2,1)S(1)}, bf16[528,256]{1,0:T(8,128)(2,1)S(1)}, u32[]{:S(2)}, u32[]{:S(2)}) collective-permute-start(bf16[528,256]{1,0:T(8,128)(2,1)S(1)} %attend_far_others4.1), channel_id=1, source_target_pairs={{0,2},{2,0},{4,6},{6,4},{8,10},{10,8},{12,14},{14,12},{16,18},{18,... | collective-permute-start | bytes 811016 | tf_op jit(solution)/shard_map/ppermute | solution.py:41
  52.2 6.4 %attend_own.1 = (f32[1024,256]{1,0:T(8,128)S(1)}, f32[8,256]{1,0:T(8,128)S(1)}) custom-call(s32[8]{0:T(128)S(1)} %copy-done.6, s32[1]{0:T(128)S(6)} %copy.15.shared.refs_1_, s32[4,8]{1,0:T(4,128)S(1)} %bitcast.31, bf16[256,1024]{1,0:T(8,128)(2,1)S(1)} %get-tuple-element.47.refs_3_, bf16[384,1024]{1,0:T(8,128)(2,1)S(1)} %get-tuple-element.53.refs_4_, ...), custom_call_target="tpu_custom_call" | custom-call | flops 1610612736 | bytes 6291456 | tf_op jit(solution)/shard_map/attend_own/pallas_call | solution.py:548
  58.6 1.4 %weave_cache.1 = (bf16[4096,128]{1,0:T(8,128)(2,1)}, f32[8,128]{1,0:T(8,128)S(1)}) custom-call(bf16[256,1024]{1,0:T(8,128)(2,1)S(1)} %get-tuple-element.51.refs_8_.refs_14_.keys, bf16[256,1024]{1,0:T(8,128)(2,1)S(1)} %get-tuple-element.83.values, f32[8,256]{1,0:T(8,128)S(1)} %get-tuple-element.82.refs_0_.refs_1_, ...), custom_call_target="tpu_custom_call" | custom-call | flops 268435456 | bytes 2097152 | tf_op jit(solution)/shard_map/weave_cache/pallas_call | solution.py:323
  60.0 1.2 %collective-permute-done.15.refs_3_ = bf16[528,256]{1,0:T(8,128)(2,1)S(1)} collective-permute-done((bf16[528,256]{1,0:T(8,128)(2,1)S(1)}, bf16[528,256]{1,0:T(8,128)(2,1)S(1)}, u32[]{:S(2)}, u32[]{:S(2)}) %collective-permute-start.15) | collective-permute-done | bytes 270368 | tf_op jit(solution)/shard_map/ppermute | solution.py:41
  61.3 1.0 %combine_send.1 = (bf16[256,1024]{1,0:T(8,128)(2,1)S(1)}, bf16[1,256,1024]{2,1,0:T(8,128)(2,1)S(1)}) custom-call(f32[1024,256]{1,0:T(8,128)S(1)} %get-tuple-element.81.refs_0_, f32[8,256]{1,0:T(8,128)S(1)} %get-tuple-element.82.refs_0_.refs_1_, bf16[528,256]{1,0:T(8,128)(2,1)S(1)} %collective-permute-done.14.refs_1_.refs_2_, ...), custom_call_target="tpu_custom_call" | custom-call | flops 536870912 | bytes 4194304 | tf_op jit(solution)/shard_map/combine_send/pallas_call | solution.py:609
  62.4 0.7 %keep_own.1 = f32[256,1024]{1,0:T(8,128)S(1)} custom-call(bf16[256,1024]{1,0:T(8,128)(2,1)S(1)} %get-tuple-element.85.attended, bf16[1024,2048]{1,0:T(8,128)(2,1)S(1)} %copy-done, bf16[256,1024]{1,0:T(8,128)(2,1)S(1)} %copy-done.2), custom_call_target="tpu_custom_call" | custom-call | flops 536870912 | bytes 4194304 | tf_op jit(solution)/shard_map/keep_own/pallas_call | solution.py:635
  63.1 1.2 %collective-permute-done.16 = bf16[256,1024]{1,0:T(8,128)(2,1)S(1)} collective-permute-done((bf16[256,1024]{1,0:T(8,128)(2,1)S(1)}, bf16[256,1024]{1,0:T(8,128)(2,1)S(1)}, u32[]{:S(2)}, u32[]{:S(2)}) %collective-permute-start.16) | collective-permute-done | bytes 524320 | tf_op jit(solution)/shard_map/ppermute | solution.py:41
  64.3 0.9 %add_convert_fusion = bf16[256,1024]{1,0:T(8,128)(2,1)} fusion(f32[256,1024]{1,0:T(8,128)S(1)} %keep_own.1, bf16[256,1024]{1,0:T(8,128)(2,1)S(1)} %collective-permute-done.16), kind=kLoop, calls=%fused_computation | loop fusion | flops 786432 | bytes 2097152 | tf_op jit(solution)/shard_map/convert_element_type | solution.py:779
  (36 shorter events, 2.7 us)
Async XLA Ops:
  0.6 15.2 %collective-permute-start.4 = (bf16[2048,128]{1,0:T(8,128)(2,1)}, bf16[2048,128]{1,0:T(8,128)(2,1)S(1)}, u32[]{:S(2)}, u32[]{:S(2)}) collective-permute-start(bf16[2048,128]{1,0:T(8,128)(2,1)} %bitcast.23), channel_id=1, source_target_pairs={{0,4},{2,6},{8,0},{10,2},{16,8},{18,10},{24,16},{26,18},{28,24},{3... | collective-permute-start | bytes 1572872 | tf_op jit(solution)/shard_map/ppermute | solution.py:50
  3.6 14.0 %collective-permute-start.2 = (bf16[2048,128]{1,0:T(8,128)(2,1)}, bf16[2048,128]{1,0:T(8,128)(2,1)S(1)}, u32[]{:S(2)}, u32[]{:S(2)}) collective-permute-start(bf16[2048,128]{1,0:T(8,128)(2,1)} %bitcast.24), channel_id=1, source_target_pairs={{0,8},{2,10},{8,16},{10,18},{16,24},{18,26},{24,28},{26,30},{28,20... | collective-permute-start | bytes 1572872 | tf_op jit(solution)/shard_map/ppermute | solution.py:50
  3.8 7.3 %collective-permute-start = (bf16[256,1024]{1,0:T(8,128)(2,1)}, bf16[256,1024]{1,0:T(8,128)(2,1)S(1)}, u32[]{:S(2)}, u32[]{:S(2)}) collective-permute-start(bf16[256,1024]{1,0:T(8,128)(2,1)} %hidden.1), channel_id=1, source_target_pairs={{0,1},{1,0},{2,3},{3,2},{4,5},{5,4},{6,7},{7,6},{8,9},{9,8},{10,11... | collective-permute-start | bytes 1572872 | tf_op jit(solution)/shard_map/ppermute | solution.py:41
  3.8 6.2 %copy-start.6 = (s32[8]{0:T(128)S(1)}, s32[8]{0:T(128)}, u32[]{:S(2)}) copy-start(s32[8]{0:T(128)} %refs_0_.10) | copy-start | bytes 100
  3.8 7.3 %copy-start.1 = (bf16[2048,1024]{1,0:T(8,128)(2,1)S(1)}, bf16[2048,1024]{1,0:T(8,128)(2,1)}, u32[]{:S(2)}) copy-start(bf16[2048,1024]{1,0:T(8,128)(2,1)} %refs_2_.1) | copy-start | bytes 12582916
  3.8 7.3 %copy-start.2 = (bf16[256,1024]{1,0:T(8,128)(2,1)S(1)}, bf16[256,1024]{1,0:T(8,128)(2,1)}, u32[]{:S(2)}) copy-start(bf16[256,1024]{1,0:T(8,128)(2,1)} %hidden.1) | copy-start | bytes 1572868
  11.1 16.2 %copy-start.3 = (bf16[2,128,2,1024]{3,2,1,0:T(2,128)(2,1)S(1)}, bf16[2,128,2,1024]{3,2,1,0:T(2,128)(2,1)}, u32[]{:S(2)}) copy-start(bf16[2,128,2,1024]{3,2,1,0:T(2,128)(2,1)} %param.14) | copy-start | bytes 3145732
  11.1 16.2 %copy-start.4 = (bf16[128,2,1024]{2,1,0:T(2,128)(2,1)S(1)}, bf16[128,2,1024]{2,1,0:T(2,128)(2,1)}, u32[]{:S(2)}) copy-start(bf16[128,2,1024]{2,1,0:T(2,128)(2,1)} %param.13) | copy-start | bytes 1572868
  13.1 21.5 %copy-start.5 = (s32[8,4]{0,1:T(4,128)S(1)}, s32[8,4]{0,1:T(4,128)}, u32[]{:S(2)}) copy-start(s32[8,4]{0,1:T(4,128)} %param.15) | copy-start | bytes 388
  13.1 21.5 %collective-permute-start.1 = (bf16[256,1024]{1,0:T(8,128)(2,1)S(1)}, bf16[256,1024]{1,0:T(8,128)(2,1)S(1)}, u32[]{:S(2)}, u32[]{:S(2)}) collective-permute-start(bf16[256,1024]{1,0:T(8,128)(2,1)S(1)} %get-tuple-element.47.refs_3_), channel_id=1, source_target_pairs={{0,2},{2,0},{4,6},{6,4},{8,10},{10,8},{12,14},{14,12},{16,18},{18,... | collective-permute-start | bytes 1572872 | tf_op jit(solution)/shard_map/ppermute | solution.py:41
  15.9 9.3 %collective-permute-start.7 = (bf16[1024,128]{1,0:T(8,128)(2,1)S(1)}, bf16[1024,128]{1,0:T(8,128)(2,1)S(1)}, u32[]{:S(2)}, u32[]{:S(2)}) collective-permute-start(bf16[1024,128]{1,0:T(8,128)(2,1)S(1)} %get-tuple-element.60), channel_id=1, source_target_pairs={{0,4},{2,6},{8,0},{10,2},{16,8},{18,10},{24,16},{26,18},{28,24},{3... | collective-permute-start | bytes 786440 | tf_op jit(solution)/shard_map/ppermute | solution.py:50
  17.7 9.3 %collective-permute-start.3 = (bf16[1024,128]{1,0:T(8,128)(2,1)S(1)}, bf16[1024,128]{1,0:T(8,128)(2,1)S(1)}, u32[]{:S(2)}, u32[]{:S(2)}) collective-permute-start(bf16[1024,128]{1,0:T(8,128)(2,1)S(1)} %get-tuple-element.48), channel_id=1, source_target_pairs={{0,8},{2,10},{8,16},{10,18},{16,24},{18,26},{24,28},{26,30},{28,20... | collective-permute-start | bytes 786440 | tf_op jit(solution)/shard_map/ppermute | solution.py:50
  18.1 14.5 %collective-permute-start.10 = (bf16[1024,128]{1,0:T(8,128)(2,1)S(1)}, bf16[1024,128]{1,0:T(8,128)(2,1)S(1)}, u32[]{:S(2)}, u32[]{:S(2)}) collective-permute-start(bf16[1024,128]{1,0:T(8,128)(2,1)S(1)} %get-tuple-element.63), channel_id=1, source_target_pairs={{0,8},{2,10},{8,16},{10,18},{16,24},{18,26},{24,28},{26,30},{28,20... | collective-permute-start | bytes 786440 | tf_op jit(solution)/shard_map/ppermute | solution.py:50
  19.8 13.1 %collective-permute-start.12 = (bf16[1024,128]{1,0:T(8,128)(2,1)S(1)}, bf16[1024,128]{1,0:T(8,128)(2,1)S(1)}, u32[]{:S(2)}, u32[]{:S(2)}) collective-permute-start(bf16[1024,128]{1,0:T(8,128)(2,1)S(1)} %get-tuple-element.65), channel_id=1, source_target_pairs={{0,4},{2,6},{8,0},{10,2},{16,8},{18,10},{24,16},{26,18},{28,24},{3... | collective-permute-start | bytes 786440 | tf_op jit(solution)/shard_map/ppermute | solution.py:50
  25.2 13.8 %collective-permute-start.8 = (bf16[1024,128]{1,0:T(8,128)(2,1)S(1)}, bf16[1024,128]{1,0:T(8,128)(2,1)S(1)}, u32[]{:S(2)}, u32[]{:S(2)}) collective-permute-start(bf16[1024,128]{1,0:T(8,128)(2,1)S(1)} %collective-permute-done.7.refs_7_), channel_id=1, source_target_pairs={{0,4},{2,6},{8,0},{10,2},{16,8},{18,10},{24,16},{26,18},{28,24},{3... | collective-permute-start | bytes 786440 | tf_op jit(solution)/shard_map/ppermute | solution.py:50
  27.0 12.0 %collective-permute-start.5 = (bf16[1024,128]{1,0:T(8,128)(2,1)S(1)}, bf16[1024,128]{1,0:T(8,128)(2,1)S(1)}, u32[]{:S(2)}, u32[]{:S(2)}) collective-permute-start(bf16[1024,128]{1,0:T(8,128)(2,1)S(1)} %collective-permute-done.3.refs_4_), channel_id=1, source_target_pairs={{0,8},{2,10},{8,16},{10,18},{16,24},{18,26},{24,28},{26,30},{28,20... | collective-permute-start | bytes 786440 | tf_op jit(solution)/shard_map/ppermute | solution.py:50
  32.6 11.2 %collective-permute-start.11 = (bf16[1024,128]{1,0:T(8,128)(2,1)S(1)}, bf16[1024,128]{1,0:T(8,128)(2,1)S(1)}, u32[]{:S(2)}, u32[]{:S(2)}) collective-permute-start(bf16[1024,128]{1,0:T(8,128)(2,1)S(1)} %collective-permute-done.10.refs_5_), channel_id=1, source_target_pairs={{0,8},{2,10},{8,16},{10,18},{16,24},{18,26},{24,28},{26,30},{28,20... | collective-permute-start | bytes 786440 | tf_op jit(solution)/shard_map/ppermute | solution.py:50
  32.9 10.9 %collective-permute-start.13 = (bf16[1024,128]{1,0:T(8,128)(2,1)S(1)}, bf16[1024,128]{1,0:T(8,128)(2,1)S(1)}, u32[]{:S(2)}, u32[]{:S(2)}) collective-permute-start(bf16[1024,128]{1,0:T(8,128)(2,1)S(1)} %collective-permute-done.12.refs_6_), channel_id=1, source_target_pairs={{0,4},{2,6},{8,0},{10,2},{16,8},{18,10},{24,16},{26,18},{28,24},{3... | collective-permute-start | bytes 786440 | tf_op jit(solution)/shard_map/ppermute | solution.py:50
  39.0 8.4 %collective-permute-start.6 = (bf16[1024,128]{1,0:T(8,128)(2,1)S(1)}, bf16[1024,128]{1,0:T(8,128)(2,1)S(1)}, u32[]{:S(2)}, u32[]{:S(2)}) collective-permute-start(bf16[1024,128]{1,0:T(8,128)(2,1)S(1)} %collective-permute-done.5.refs_4_), channel_id=1, source_target_pairs={{0,8},{2,10},{8,16},{10,18},{16,24},{18,26},{24,28},{26,30},{28,20... | collective-permute-start | bytes 786440 | tf_op jit(solution)/shard_map/ppermute | solution.py:50
  39.4 8.0 %collective-permute-start.9 = (bf16[1024,128]{1,0:T(8,128)(2,1)S(1)}, bf16[1024,128]{1,0:T(8,128)(2,1)S(1)}, u32[]{:S(2)}, u32[]{:S(2)}) collective-permute-start(bf16[1024,128]{1,0:T(8,128)(2,1)S(1)} %collective-permute-done.8.refs_7_), channel_id=1, source_target_pairs={{0,4},{2,6},{8,0},{10,2},{16,8},{18,10},{24,16},{26,18},{28,24},{3... | collective-permute-start | bytes 786440 | tf_op jit(solution)/shard_map/ppermute | solution.py:50
  41.0 20.2 %copy-start = (bf16[1024,2048]{1,0:T(8,128)(2,1)S(1)}, bf16[1024,2048]{1,0:T(8,128)(2,1)}, u32[]{:S(2)}) copy-start(bf16[1024,2048]{1,0:T(8,128)(2,1)} %weight.1) | copy-start | bytes 12582916
  49.0 9.7 %collective-permute-start.14 = (bf16[528,256]{1,0:T(8,128)(2,1)S(1)}, bf16[528,256]{1,0:T(8,128)(2,1)S(1)}, u32[]{:S(2)}, u32[]{:S(2)}) collective-permute-start(bf16[528,256]{1,0:T(8,128)(2,1)S(1)} %get-tuple-element.72), channel_id=1, source_target_pairs={{0,2},{2,0},{4,6},{6,4},{8,10},{10,8},{12,14},{14,12},{16,18},{18,... | collective-permute-start | bytes 811016 | tf_op jit(solution)/shard_map/ppermute | solution.py:41
  51.3 9.9 %collective-permute-start.15 = (bf16[528,256]{1,0:T(8,128)(2,1)S(1)}, bf16[528,256]{1,0:T(8,128)(2,1)S(1)}, u32[]{:S(2)}, u32[]{:S(2)}) collective-permute-start(bf16[528,256]{1,0:T(8,128)(2,1)S(1)} %attend_far_others4.1), channel_id=1, source_target_pairs={{0,2},{2,0},{4,6},{6,4},{8,10},{10,8},{12,14},{14,12},{16,18},{18,... | collective-permute-start | bytes 811016 | tf_op jit(solution)/shard_map/ppermute | solution.py:41
  62.3 2.0 %collective-permute-start.16 = (bf16[256,1024]{1,0:T(8,128)(2,1)S(1)}, bf16[256,1024]{1,0:T(8,128)(2,1)S(1)}, u32[]{:S(2)}, u32[]{:S(2)}) collective-permute-start(bf16[256,1024]{1,0:T(8,128)(2,1)S(1)} %bitcast.32), channel_id=1, source_target_pairs={{0,1},{1,0},{2,3},{3,2},{4,5},{5,4},{6,7},{7,6},{8,9},{9,8},{10,11... | collective-permute-start | bytes 1572872 | tf_op jit(solution)/shard_map/ppermute | solution.py:41

commit v15 on v14

--- a/solution.py
+++ b/solution.py
@@ -566,64 +566,67 @@
     return state, results[len(results) - 2 :]
 
 
-def combine_kernel(pieces, *refs):
-    result, extent, *pairs, weight, _, attended, sent = refs
-    width, rows = result.shape
-    heads = width // HD
-    extents = [extent[:heads, :]]
-    few = heads // pieces
-    parts = [pairs[start : start + pieces] for start in range(0, len(pairs), pieces)]
+def combine_kernel(lowest, last, earlier, *refs):
+    result, extent, *refs = refs
+    *parts, weight = refs[: len(refs) - 2 - earlier]
+    before = refs[len(refs) - 2 - earlier : len(refs) - 2]
+    attended, sent = refs[-2:]
+    rows, width = attended.shape
+    few = width // HD
+    extents = [extent[lowest : lowest + few, :]]
     for part in parts:
-        here = []
-        for half in part:
-            lines = half[few * HD :, :].astype(jnp.float32)
-            here.append(sum(lines[i * few : (i + 1) * few] for i in range(3)))
-        extents.append(here[0] if pieces == 1 else jnp.concatenate(here, axis=0))
+        lines = part[width:, :].astype(jnp.float32)
+        extents.append(sum(lines[i * few : (i + 1) * few] for i in range(3)))
     top = functools.reduce(jnp.maximum, extents)
     shares = [jnp.exp2(extent - top) for extent in extents]
     whole = sum(shares)
     shares = [share / whole for share in shares]
     unit = unit_matrix(rows)
-    for head in range(heads):
+    for head in range(few):
         span = slice(head * HD, (head + 1) * HD)
-        line = head % few * HD
-        mixes = [result[span, :]] + [
-            part[head // few][line : line + HD, :].astype(jnp.float32) for part in parts
-        ]
+        start = (lowest + head) * HD
+        mixes = [result[start : start + HD, :]]
+        mixes += [part[span, :].astype(jnp.float32) for part in parts]
         mixed = sum(mix * share[head : head + 1] for mix, share in zip(mixes, shares))
         attended[:, span] = turned_over(unit, mixed.astype(jnp.bfloat16))
     index = lax.axis_index("tp")
     ways = sent.shape[0] + 1
     columns = weight.shape[1] // ways
     for shift in range(1, ways):
-        sent[shift - 1] = jnp.dot(
+        product = jnp.dot(
             attended[...],
-            weight[:, lanes((index ^ shift) * columns, columns)],
+            weight[lowest * HD : lowest * HD + width, lanes((index ^ shift) * columns, columns)],
             preferred_element_type=jnp.float32,
-        ).astype(jnp.bfloat16)
-
-
-def combine(result, extent, parts, pieces, w_out, token, ways):
-    width, rows = result.shape
+        )
+        if len(before) > 1:
+            product += before[0][shift - 1]
+        sent[shift - 1] = product.astype(sent.dtype)
+
+
+def combine(own, parts, lowest, few, w_out, earlier, last, ways):
+    rows = own[0].shape[1]
     columns = w_out.shape[1] // ways
+    kind = jnp.bfloat16 if last else jnp.float32
     return pl.pallas_call(
-        functools.partial(combine_kernel, pieces),
-        in_specs=[VMEM] * (4 + len(parts)),
+        functools.partial(combine_kernel, lowest, last, len(earlier)),
+        in_specs=[VMEM] * (3 + len(parts) + len(earlier)),
         out_specs=[VMEM] * 2,
         out_shape=[
-            jax.ShapeDtypeStruct((rows, width), jnp.bfloat16),
-            jax.ShapeDtypeStruct((ways - 1, rows, columns), jnp.bfloat16),
+            jax.ShapeDtypeStruct((rows, few * HD), jnp.bfloat16),
+            jax.ShapeDtypeStruct((ways - 1, rows, columns), kind),
         ],
         compiler_params=params(20),
-        cost_estimate=cost(2 * rows * width * columns * (ways - 1), 2 * width * w_out.shape[1]),
-        name="combine_send",
-    )(result, extent, *parts, w_out, token)
-
-
-def keep_kernel(attended, weight, hidden, kept):
+        cost_estimate=cost(2 * rows * few * HD * columns * (ways - 1), 2 * few * HD * columns),
+        name=f"combine_send{lowest}",
+    )(*own, *parts, w_out, *earlier)
+
+
+def keep_kernel(*refs):
+    *pieces, weight, hidden, kept = refs
     columns = hidden.shape[1]
+    attended = [piece[...] for piece in pieces]
     product = jnp.dot(
-        attended[...],
+        attended[0] if len(pieces) == 1 else jnp.concatenate(attended, axis=1),
         weight[:, lanes(lax.axis_index("tp") * columns, columns)],
         preferred_element_type=jnp.float32,
     )
@@ -631,16 +634,16 @@
 
 
 def keep(attended, w_out, hidden):
-    rows, width = attended.shape
+    rows, width = hidden.shape[0], w_out.shape[0]
     return pl.pallas_call(
         keep_kernel,
-        in_specs=[VMEM] * 3,
+        in_specs=[VMEM] * (2 + len(attended)),
         out_specs=VMEM,
         out_shape=jax.ShapeDtypeStruct(hidden.shape, jnp.float32),
         compiler_params=params(20),
         cost_estimate=cost(2 * rows * width * hidden.shape[1], 2 * width * w_out.shape[1]),
         name="keep_own",
-    )(attended, w_out, hidden)
+    )(*attended, w_out, hidden)
 
 
 def local(
@@ -769,9 +772,14 @@
     arrivals = [
         [swap(part[i], "seq", shift) for i, shift in enumerate(others)] for part in sending
     ]
-    parts = [part[i] for i in range(len(others)) for part in arrivals]
     new_cache, token = weave(fresh_keys, fresh_values, own[0][1], arrivals[0][0])
-    attended, sent = combine(*own[0], parts, pieces_out, w_out, token, ways)
+    attended = []
+    earlier = [token]
+    for piece_out, part in enumerate(arrivals):
+        last = piece_out == pieces_out - 1
+        made, sent = combine(own[0], part, piece_out * few, few, w_out, earlier, last, ways)
+        attended.append(made)
+        earlier = [sent, token]
     received = [swap(sent[shift - 1], "tp", shift) for shift in range(1, ways)]
     total = keep(attended, w_out, hidden_in)
     for part in received:

time: 65.4 us -> 65 us (level)
  waiting for transfers between devices: 11.3 us -> 10.6 us
    ppermute x5, waiting for transfers between devices: 2.42 us -> 1.73 us  [swap(): return lax.ppermute(value, axis, pairs)]
    pallas_call x2 -> x3, Pallas kernels: 1.76 us -> 2.06 us  [the longest x2 1.33 us: combine(): pl.pallas_call(functools.partial(combine_kernel, lowest, last, len(earlie...]
  transfers between devices with their start and end apart: 17 -> 17, of which waited for: 8 -> 8; matrix products, arithmetic and copies ran while one was open for 1% -> 1% of each run, Pallas kernels for 47% -> 48%
where the time goes in v15:
time: 65 us; the launch traced here: 64.9 us
  Pallas kernels  33.6 us (52%)
  starting transfers between devices  17.6 us (27%)
  waiting for transfers between devices  10.6 us (16%)
  between operations  1.51 us (2%)
  other arithmetic  1.42 us (2%)
    pallas_call x6, Pallas kernels, attend(): pl.pallas_call(functools.partial(attend_kernel, (group, shifts, rings, sl...  17.8 us
    ppermute x12, starting transfers between devices, turn(): return lax.ppermute(value, 'seq', pairs)  13.4 us
    ppermute x12, waiting for transfers between devices, turn(): return lax.ppermute(value, 'seq', pairs)  8.87 us
    pallas_call x1, Pallas kernels, part_weights(): pl.pallas_call(weight_kernel, in_specs=[HBM], out_specs=VMEM, out_shape=j...  5.5 us
    ppermute x5, starting transfers between devices, swap(): return lax.ppermute(value, axis, pairs)  4.16 us
    pallas_call x1, Pallas kernels, project_keyval(): pl.pallas_call(keyval_kernel, in_specs=[VMEM] * 4, out_specs=[VMEM] * 3,...  2.54 us
    pallas_call x1, Pallas kernels, project_query(): pl.pallas_call(query_kernel, in_specs=[VMEM] * (len(pieces) + 3), out_spe...  2.02 us
    ppermute x5, waiting for transfers between devices, swap(): return lax.ppermute(value, axis, pairs)  1.73 us
  transfers between devices with their start and end apart: 17, of which 8 were waited for; matrix products, arithmetic and copies ran while one was open for 1% of the time, Pallas kernels for 48%

profile of v15, /device:TPU:0, one launch (start us, length us, event | category | flops | bytes accessed | tf_op | source)
XLA Modules:
  0.0 64.9 jit_solution(14403887347816866711)
XLA Ops:
  0.6 3.0 %collective-permute-start.4 = (bf16[2048,128]{1,0:T(8,128)(2,1)}, bf16[2048,128]{1,0:T(8,128)(2,1)S(1)}, u32[]{:S(2)}, u32[]{:S(2)}) collective-permute-start(bf16[2048,128]{1,0:T(8,128)(2,1)} %bitcast.23), channel_id=1, source_target_pairs={{0,4},{2,6},{8,0},{10,2},{16,8},{18,10},{24,16},{26,18},{28,24},{3... | collective-permute-start | bytes 1572872 | tf_op jit(solution)/shard_map/ppermute | solution.py:50
  3.8 5.5 %part_weights.1.weight = bf16[2,2048,1024]{2,1,0:T(8,128)(2,1)S(1)} custom-call(bf16[32768,128]{1,0:T(8,128)(2,1)} %bitcast.33), custom_call_target="tpu_custom_call" | custom-call | flops 2147483648 | bytes 16777216 | tf_op jit(solution)/shard_map/part_weights/pallas_call | solution.py:251
  10.0 0.6 positions.1
  11.1 2.0 %project_query.1 = (bf16[256,1024]{1,0:T(8,128)(2,1)S(1)}, bf16[256,2048]{1,0:T(8,128)(2,1)S(1)}) custom-call(bf16[256,1024]{1,0:T(8,128)(2,1)S(1)} %copy-done.2, bf16[256,1024]{1,0:T(8,128)(2,1)S(1)} %collective-permute-done.refs_1_, bf16[2048,1024]{1,0:T(8,128)(2,1)S(1)} %copy-done.1, f32[256,128]{1,0:T(8,128)S(1)} %get-tuple-element.52.refs_3_.cosine, ...), custom_call_target="tpu_custom_call" | custom-call | flops 1073741824 | bytes 4194304 | tf_op jit(solution)/shard_map/project_query/pallas_call | solution.py:212
  13.1 1.9 %collective-permute-start.1 = (bf16[256,1024]{1,0:T(8,128)(2,1)S(1)}, bf16[256,1024]{1,0:T(8,128)(2,1)S(1)}, u32[]{:S(2)}, u32[]{:S(2)}) collective-permute-start(bf16[256,1024]{1,0:T(8,128)(2,1)S(1)} %get-tuple-element.49.refs_3_), channel_id=1, source_target_pairs={{0,2},{2,0},{4,6},{6,4},{8,10},{10,8},{12,14},{14,12},{16,18},{18,... | collective-permute-start | bytes 1572872 | tf_op jit(solution)/shard_map/ppermute | solution.py:41
  15.1 0.8 %collective-permute-done.4.refs_1_ = bf16[2048,128]{1,0:T(8,128)(2,1)S(1)} collective-permute-done((bf16[2048,128]{1,0:T(8,128)(2,1)}, bf16[2048,128]{1,0:T(8,128)(2,1)S(1)}, u32[]{:S(2)}, u32[]{:S(2)}) %collective-permute-start.4) | collective-permute-done | bytes 524320 | tf_op jit(solution)/shard_map/ppermute | solution.py:50
  15.9 1.7 %collective-permute-start.7 = (bf16[1024,128]{1,0:T(8,128)(2,1)S(1)}, bf16[1024,128]{1,0:T(8,128)(2,1)S(1)}, u32[]{:S(2)}, u32[]{:S(2)}) collective-permute-start(bf16[1024,128]{1,0:T(8,128)(2,1)S(1)} %get-tuple-element.62), channel_id=1, source_target_pairs={{0,4},{2,6},{8,0},{10,2},{16,8},{18,10},{24,16},{26,18},{28,24},{3... | collective-permute-start | bytes 786440 | tf_op jit(solution)/shard_map/ppermute | solution.py:50
  18.1 1.7 %collective-permute-start.10 = (bf16[1024,128]{1,0:T(8,128)(2,1)S(1)}, bf16[1024,128]{1,0:T(8,128)(2,1)S(1)}, u32[]{:S(2)}, u32[]{:S(2)}) collective-permute-start(bf16[1024,128]{1,0:T(8,128)(2,1)S(1)} %get-tuple-element.65), channel_id=1, source_target_pairs={{0,8},{2,10},{8,16},{10,18},{16,24},{18,26},{24,28},{26,30},{28,20... | collective-permute-start | bytes 786440 | tf_op jit(solution)/shard_map/ppermute | solution.py:50
  20.1 2.5 %project_keyval.1 = (bf16[256,1024]{1,0:T(8,128)(2,1)S(1)}, bf16[256,1024]{1,0:T(8,128)(2,1)S(1)}, bf16[1024,256]{1,0:T(8,128)(2,1)S(1)}) custom-call(bf16[256,2048]{1,0:T(8,128)(2,1)S(1)} %get-tuple-element.51.normed, bf16[2,2048,1024]{2,1,0:T(8,128)(2,1)S(1)} %part_weights.1.weight, f32[256,128]{1,0:T(8,128)S(1)} %get-tuple-element.52.refs_3_.cosine, ...), custom_call_target="tpu_custom_call" | custom-call | flops 2147483648 | bytes 8388608 | tf_op jit(solution)/shard_map/project_keyval/pallas_call | solution.py:284
  22.6 2.6 %collective-permute-done.7.refs_7_ = bf16[1024,128]{1,0:T(8,128)(2,1)S(1)} collective-permute-done((bf16[1024,128]{1,0:T(8,128)(2,1)S(1)}, bf16[1024,128]{1,0:T(8,128)(2,1)S(1)}, u32[]{:S(2)}, u32[]{:S(2)}) %collective-permute-start.7) | collective-permute-done | bytes 262176 | tf_op jit(solution)/shard_map/ppermute | solution.py:50
  25.2 1.7 %collective-permute-start.8 = (bf16[1024,128]{1,0:T(8,128)(2,1)S(1)}, bf16[1024,128]{1,0:T(8,128)(2,1)S(1)}, u32[]{:S(2)}, u32[]{:S(2)}) collective-permute-start(bf16[1024,128]{1,0:T(8,128)(2,1)S(1)} %collective-permute-done.7.refs_7_), channel_id=1, source_target_pairs={{0,4},{2,6},{8,0},{10,2},{16,8},{18,10},{24,16},{26,18},{28,24},{3... | collective-permute-start | bytes 786440 | tf_op jit(solution)/shard_map/ppermute | solution.py:50
  27.3 1.0 %part_own.1 = (bf16[384,1024]{1,0:T(8,128)(2,1)S(1)}, bf16[1024,384]{1,0:T(8,128)(2,1)S(1)}) custom-call(bf16[4096,128]{1,0:T(8,128)(2,1)S(1)} %bitcast.22, bf16[2048,128]{1,0:T(8,128)(2,1)S(1)} %bitcast.25), custom_call_target="tpu_custom_call" | custom-call | flops 402653184 | bytes 3145728 | tf_op jit(solution)/shard_map/part_own/pallas_call | solution.py:170
  28.3 0.7 %part_near.1 = (bf16[256,1024]{1,0:T(8,128)(2,1)S(1)}, bf16[1024,256]{1,0:T(8,128)(2,1)S(1)}) custom-call(bf16[2048,128]{1,0:T(8,128)(2,1)S(1)} %collective-permute-done.2.refs_0_, bf16[2048,128]{1,0:T(8,128)(2,1)S(1)} %collective-permute-done.4.refs_1_), custom_call_target="tpu_custom_call" | custom-call | flops 268435456 | bytes 2097152 | tf_op jit(solution)/shard_map/part_near/pallas_call | solution.py:170
  29.0 3.5 %collective-permute-done.10.refs_5_ = bf16[1024,128]{1,0:T(8,128)(2,1)S(1)} collective-permute-done((bf16[1024,128]{1,0:T(8,128)(2,1)S(1)}, bf16[1024,128]{1,0:T(8,128)(2,1)S(1)}, u32[]{:S(2)}, u32[]{:S(2)}) %collective-permute-start.10) | collective-permute-done | bytes 262176 | tf_op jit(solution)/shard_map/ppermute | solution.py:50
  32.9 1.7 %collective-permute-start.13 = (bf16[1024,128]{1,0:T(8,128)(2,1)S(1)}, bf16[1024,128]{1,0:T(8,128)(2,1)S(1)}, u32[]{:S(2)}, u32[]{:S(2)}) collective-permute-start(bf16[1024,128]{1,0:T(8,128)(2,1)S(1)} %collective-permute-done.12.refs_6_), channel_id=1, source_target_pairs={{0,4},{2,6},{8,0},{10,2},{16,8},{18,10},{24,16},{26,18},{28,24},{3... | collective-permute-start | bytes 786440 | tf_op jit(solution)/shard_map/ppermute | solution.py:50
  34.6 4.3 %attend_near_others.1 = (f32[1024,256]{1,0:T(8,128)S(1)}, f32[8,256]{1,0:T(8,128)S(1)}) custom-call(s32[8]{0:T(128)S(1)} %copy-done.6, s32[1]{0:T(128)S(6)} %copy.15.shared.refs_1_, s32[4,8]{1,0:T(4,128)S(1)} %bitcast.26, bf16[256,1024]{1,0:T(8,128)(2,1)S(1)} %collective-permute-done.1.refs_3_, bf16[384,1024]{1,0:T(8,128)(2,1)S(1)} %get-tuple-element.55.refs_4_, ...), custom_call_target="tpu_custom_call" | custom-call | flops 939524096 | bytes 3670016 | tf_op jit(solution)/shard_map/attend_near_others/pallas_call | solution.py:548
  39.4 1.7 %collective-permute-start.9 = (bf16[1024,128]{1,0:T(8,128)(2,1)S(1)}, bf16[1024,128]{1,0:T(8,128)(2,1)S(1)}, u32[]{:S(2)}, u32[]{:S(2)}) collective-permute-start(bf16[1024,128]{1,0:T(8,128)(2,1)S(1)} %collective-permute-done.8.refs_7_), channel_id=1, source_target_pairs={{0,4},{2,6},{8,0},{10,2},{16,8},{18,10},{24,16},{26,18},{28,24},{3... | collective-permute-start | bytes 786440 | tf_op jit(solution)/shard_map/ppermute | solution.py:50
  41.0 2.2 %attend_hop2_others.1 = (f32[1024,256]{1,0:T(8,128)S(1)}, f32[8,256]{1,0:T(8,128)S(1)}, bf16[256,1024]{1,0:T(8,128)(2,1)S(1)}, bf16[1024,256]{1,0:T(8,128)(2,1)S(1)}) custom-call(s32[8]{0:T(128)S(1)} %copy-done.6, s32[1]{0:T(128)S(6)} %copy.15.shared.refs_1_, s32[4,8]{1,0:T(4,128)S(1)} %bitcast.27, bf16[256,1024]{1,0:T(8,128)(2,1)S(1)} %collective-permute-done.1.refs_3_, ...), custom_call_target="tpu_custom_call" | custom-call | flops 268435456 | bytes 1048576 | tf_op jit(solution)/shard_map/attend_hop2_others/pallas_call | solution.py:548
  43.8 2.2 %attend_hop3_others.1 = (f32[1024,256]{1,0:T(8,128)S(1)}, f32[8,256]{1,0:T(8,128)S(1)}, bf16[256,1024]{1,0:T(8,128)(2,1)S(1)}, bf16[1024,256]{1,0:T(8,128)(2,1)S(1)}) custom-call(s32[8]{0:T(128)S(1)} %copy-done.6, s32[1]{0:T(128)S(6)} %copy.15.shared.refs_1_, s32[4,8]{1,0:T(4,128)S(1)} %bitcast.28, bf16[256,1024]{1,0:T(8,128)(2,1)S(1)} %collective-permute-done.1.refs_3_, ...), custom_call_target="tpu_custom_call" | custom-call | flops 268435456 | bytes 1048576 | tf_op jit(solution)/shard_map/attend_hop3_others/pallas_call | solution.py:548
  46.1 1.3 %collective-permute-done.6.refs_4_ = bf16[1024,128]{1,0:T(8,128)(2,1)S(1)} collective-permute-done((bf16[1024,128]{1,0:T(8,128)(2,1)S(1)}, bf16[1024,128]{1,0:T(8,128)(2,1)S(1)}, u32[]{:S(2)}, u32[]{:S(2)}) %collective-permute-start.6) | collective-permute-done | bytes 262176 | tf_op jit(solution)/shard_map/ppermute | solution.py:50
  47.4 1.6 %attend_far_others0.1 = (bf16[528,256]{1,0:T(8,128)(2,1)S(1)}, bf16[128,1024]{1,0:T(8,128)(2,1)S(1)}, bf16[1024,128]{1,0:T(8,128)(2,1)S(1)}) custom-call(s32[8]{0:T(128)S(1)} %copy-done.6, s32[1]{0:T(128)S(6)} %copy.15.shared.refs_1_, s32[4,8]{1,0:T(4,128)S(1)} %bitcast.29, bf16[256,1024]{1,0:T(8,128)(2,1)S(1)} %collective-permute-done.1.refs_3_, ...), custom_call_target="tpu_custom_call" | custom-call | flops 67108864 | bytes 524288 | tf_op jit(solution)/shard_map/attend_far_others0/pallas_call | solution.py:548
  49.0 1.2 %collective-permute-start.14 = (bf16[528,256]{1,0:T(8,128)(2,1)S(1)}, bf16[528,256]{1,0:T(8,128)(2,1)S(1)}, u32[]{:S(2)}, u32[]{:S(2)}) collective-permute-start(bf16[528,256]{1,0:T(8,128)(2,1)S(1)} %get-tuple-element.74), channel_id=1, source_target_pairs={{0,2},{2,0},{4,6},{6,4},{8,10},{10,8},{12,14},{14,12},{16,18},{18,... | collective-permute-start | bytes 811016 | tf_op jit(solution)/shard_map/ppermute | solution.py:41
  50.2 1.1 %attend_far_others4.1 = bf16[528,256]{1,0:T(8,128)(2,1)S(1)} custom-call(s32[8]{0:T(128)S(1)} %copy-done.6, s32[1]{0:T(128)S(6)} %copy.15.shared.refs_1_, s32[4,8]{1,0:T(4,128)S(1)} %bitcast.30, bf16[256,1024]{1,0:T(8,128)(2,1)S(1)} %collective-permute-done.1.refs_3_, bf16[128,1024]{1,0:T(8,128)(2,1)S(1)} %get-tuple-element.76.refs_4_.refs_12_, ...), custom_call_target="tpu_custom_call" | custom-call | flops 67108864 | bytes 524288 | tf_op jit(solution)/shard_map/attend_far_others4/pallas_call | solution.py:548
  51.3 0.9 %collective-permute-start.15 = (bf16[528,256]{1,0:T(8,128)(2,1)S(1)}, bf16[528,256]{1,0:T(8,128)(2,1)S(1)}, u32[]{:S(2)}, u32[]{:S(2)}) collective-permute-start(bf16[528,256]{1,0:T(8,128)(2,1)S(1)} %attend_far_others4.1), channel_id=1, source_target_pairs={{0,2},{2,0},{4,6},{6,4},{8,10},{10,8},{12,14},{14,12},{16,18},{18,... | collective-permute-start | bytes 811016 | tf_op jit(solution)/shard_map/ppermute | solution.py:41
  52.2 6.4 %attend_own.1 = (f32[1024,256]{1,0:T(8,128)S(1)}, f32[8,256]{1,0:T(8,128)S(1)}) custom-call(s32[8]{0:T(128)S(1)} %copy-done.6, s32[1]{0:T(128)S(6)} %copy.15.shared.refs_1_, s32[4,8]{1,0:T(4,128)S(1)} %bitcast.31, bf16[256,1024]{1,0:T(8,128)(2,1)S(1)} %get-tuple-element.49.refs_3_, bf16[384,1024]{1,0:T(8,128)(2,1)S(1)} %get-tuple-element.55.refs_4_, ...), custom_call_target="tpu_custom_call" | custom-call | flops 1610612736 | bytes 6291456 | tf_op jit(solution)/shard_map/attend_own/pallas_call | solution.py:548
  58.6 1.4 %weave_cache.1 = (bf16[4096,128]{1,0:T(8,128)(2,1)}, f32[8,128]{1,0:T(8,128)S(1)}) custom-call(bf16[256,1024]{1,0:T(8,128)(2,1)S(1)} %get-tuple-element.53.refs_8_.refs_14_.keys, bf16[256,1024]{1,0:T(8,128)(2,1)S(1)} %get-tuple-element.85.values, f32[8,256]{1,0:T(8,128)S(1)} %get-tuple-element.84.refs_0_.refs_1_, ...), custom_call_target="tpu_custom_call" | custom-call | flops 268435456 | bytes 2097152 | tf_op jit(solution)/shard_map/weave_cache/pallas_call | solution.py:323
  60.0 0.7 %combine_send0.1 = (bf16[256,512]{1,0:T(8,128)(2,1)S(1)}, f32[1,256,1024]{2,1,0:T(8,128)S(1)}) custom-call(f32[1024,256]{1,0:T(8,128)S(1)} %get-tuple-element.83.refs_0_, f32[8,256]{1,0:T(8,128)S(1)} %get-tuple-element.84.refs_0_.refs_1_, bf16[528,256]{1,0:T(8,128)(2,1)S(1)} %collective-permute-done.14.refs_1_.refs_2_, bf16[1024,2048]{1,0:T(8,128)(2,1)S(1)} %copy-done, ...), custom_call_target="tpu_custom_call" | custom-call | flops 268435456 | bytes 1048576 | tf_op jit(solution)/shard_map/combine_send0/pallas_call | solution.py:610
  60.7 0.6 collective-permute-done.15.refs_2_
  61.3 0.7 %combine_send4.1 = (bf16[256,512]{1,0:T(8,128)(2,1)S(1)}, bf16[1,256,1024]{2,1,0:T(8,128)(2,1)S(1)}) custom-call(f32[1024,256]{1,0:T(8,128)S(1)} %get-tuple-element.83.refs_0_, f32[8,256]{1,0:T(8,128)S(1)} %get-tuple-element.84.refs_0_.refs_1_, bf16[528,256]{1,0:T(8,128)(2,1)S(1)} %collective-permute-done.15.refs_2_, bf16[1024,2048]{1,0:T(8,128)(2,1)S(1)} %copy-done, ...), custom_call_target="tpu_custom_call" | custom-call | flops 268435456 | bytes 1048576 | tf_op jit(solution)/shard_map/combine_send4/pallas_call | solution.py:610
  62.0 0.7 %keep_own.1 = f32[256,1024]{1,0:T(8,128)S(1)} custom-call(bf16[256,512]{1,0:T(8,128)(2,1)S(1)} %get-tuple-element.87.refs_0_, bf16[256,512]{1,0:T(8,128)(2,1)S(1)} %get-tuple-element.89.refs_1_, bf16[1024,2048]{1,0:T(8,128)(2,1)S(1)} %copy-done, bf16[256,1024]{1,0:T(8,128)(2,1)S(1)} %copy-done.2), custom_call_target="tpu_custom_call" | custom-call | flops 536870912 | bytes 4194304 | tf_op jit(solution)/shard_map/keep_own/pallas_call | solution.py:638
  62.8 1.2 %collective-permute-done.16 = bf16[256,1024]{1,0:T(8,128)(2,1)S(1)} collective-permute-done((bf16[256,1024]{1,0:T(8,128)(2,1)S(1)}, bf16[256,1024]{1,0:T(8,128)(2,1)S(1)}, u32[]{:S(2)}, u32[]{:S(2)}) %collective-permute-start.16) | collective-permute-done | bytes 524320 | tf_op jit(solution)/shard_map/ppermute | solution.py:41
  63.9 0.9 %add_convert_fusion = bf16[256,1024]{1,0:T(8,128)(2,1)} fusion(f32[256,1024]{1,0:T(8,128)S(1)} %keep_own.1, bf16[256,1024]{1,0:T(8,128)(2,1)S(1)} %collective-permute-done.16), kind=kLoop, calls=%fused_computation | loop fusion | flops 786432 | bytes 2097152 | tf_op jit(solution)/shard_map/convert_element_type | solution.py:787
  (37 shorter events, 3.2 us)
Async XLA Ops:
  0.6 15.2 %collective-permute-start.4 = (bf16[2048,128]{1,0:T(8,128)(2,1)}, bf16[2048,128]{1,0:T(8,128)(2,1)S(1)}, u32[]{:S(2)}, u32[]{:S(2)}) collective-permute-start(bf16[2048,128]{1,0:T(8,128)(2,1)} %bitcast.23), channel_id=1, source_target_pairs={{0,4},{2,6},{8,0},{10,2},{16,8},{18,10},{24,16},{26,18},{28,24},{3... | collective-permute-start | bytes 1572872 | tf_op jit(solution)/shard_map/ppermute | solution.py:50
  3.6 14.0 %collective-permute-start.2 = (bf16[2048,128]{1,0:T(8,128)(2,1)}, bf16[2048,128]{1,0:T(8,128)(2,1)S(1)}, u32[]{:S(2)}, u32[]{:S(2)}) collective-permute-start(bf16[2048,128]{1,0:T(8,128)(2,1)} %bitcast.24), channel_id=1, source_target_pairs={{0,8},{2,10},{8,16},{10,18},{16,24},{18,26},{24,28},{26,30},{28,20... | collective-permute-start | bytes 1572872 | tf_op jit(solution)/shard_map/ppermute | solution.py:50
  3.8 7.3 %collective-permute-start = (bf16[256,1024]{1,0:T(8,128)(2,1)}, bf16[256,1024]{1,0:T(8,128)(2,1)S(1)}, u32[]{:S(2)}, u32[]{:S(2)}) collective-permute-start(bf16[256,1024]{1,0:T(8,128)(2,1)} %refs_3_.5), channel_id=1, source_target_pairs={{0,1},{1,0},{2,3},{3,2},{4,5},{5,4},{6,7},{7,6},{8,9},{9,8},{10,11... | collective-permute-start | bytes 1572872 | tf_op jit(solution)/shard_map/ppermute | solution.py:41
  3.8 6.2 %copy-start.6 = (s32[8]{0:T(128)S(1)}, s32[8]{0:T(128)}, u32[]{:S(2)}) copy-start(s32[8]{0:T(128)} %refs_0_.10) | copy-start | bytes 100
  3.8 7.3 %copy-start.1 = (bf16[2048,1024]{1,0:T(8,128)(2,1)S(1)}, bf16[2048,1024]{1,0:T(8,128)(2,1)}, u32[]{:S(2)}) copy-start(bf16[2048,1024]{1,0:T(8,128)(2,1)} %refs_2_.2) | copy-start | bytes 12582916
  3.8 7.3 %copy-start.2 = (bf16[256,1024]{1,0:T(8,128)(2,1)S(1)}, bf16[256,1024]{1,0:T(8,128)(2,1)}, u32[]{:S(2)}) copy-start(bf16[256,1024]{1,0:T(8,128)(2,1)} %refs_3_.5) | copy-start | bytes 1572868
  11.1 16.2 %copy-start.3 = (bf16[2,128,2,1024]{3,2,1,0:T(2,128)(2,1)S(1)}, bf16[2,128,2,1024]{3,2,1,0:T(2,128)(2,1)}, u32[]{:S(2)}) copy-start(bf16[2,128,2,1024]{3,2,1,0:T(2,128)(2,1)} %param.14) | copy-start | bytes 3145732
  11.1 16.2 %copy-start.4 = (bf16[128,2,1024]{2,1,0:T(2,128)(2,1)S(1)}, bf16[128,2,1024]{2,1,0:T(2,128)(2,1)}, u32[]{:S(2)}) copy-start(bf16[128,2,1024]{2,1,0:T(2,128)(2,1)} %param.13) | copy-start | bytes 1572868
  13.1 21.5 %copy-start.5 = (s32[8,4]{0,1:T(4,128)S(1)}, s32[8,4]{0,1:T(4,128)}, u32[]{:S(2)}) copy-start(s32[8,4]{0,1:T(4,128)} %param.15) | copy-start | bytes 388
  13.1 21.5 %collective-permute-start.1 = (bf16[256,1024]{1,0:T(8,128)(2,1)S(1)}, bf16[256,1024]{1,0:T(8,128)(2,1)S(1)}, u32[]{:S(2)}, u32[]{:S(2)}) collective-permute-start(bf16[256,1024]{1,0:T(8,128)(2,1)S(1)} %get-tuple-element.49.refs_3_), channel_id=1, source_target_pairs={{0,2},{2,0},{4,6},{6,4},{8,10},{10,8},{12,14},{14,12},{16,18},{18,... | collective-permute-start | bytes 1572872 | tf_op jit(solution)/shard_map/ppermute | solution.py:41
  15.9 9.3 %collective-permute-start.7 = (bf16[1024,128]{1,0:T(8,128)(2,1)S(1)}, bf16[1024,128]{1,0:T(8,128)(2,1)S(1)}, u32[]{:S(2)}, u32[]{:S(2)}) collective-permute-start(bf16[1024,128]{1,0:T(8,128)(2,1)S(1)} %get-tuple-element.62), channel_id=1, source_target_pairs={{0,4},{2,6},{8,0},{10,2},{16,8},{18,10},{24,16},{26,18},{28,24},{3... | collective-permute-start | bytes 786440 | tf_op jit(solution)/shard_map/ppermute | solution.py:50
  17.7 9.3 %collective-permute-start.3 = (bf16[1024,128]{1,0:T(8,128)(2,1)S(1)}, bf16[1024,128]{1,0:T(8,128)(2,1)S(1)}, u32[]{:S(2)}, u32[]{:S(2)}) collective-permute-start(bf16[1024,128]{1,0:T(8,128)(2,1)S(1)} %get-tuple-element.50), channel_id=1, source_target_pairs={{0,8},{2,10},{8,16},{10,18},{16,24},{18,26},{24,28},{26,30},{28,20... | collective-permute-start | bytes 786440 | tf_op jit(solution)/shard_map/ppermute | solution.py:50
  18.1 14.5 %collective-permute-start.10 = (bf16[1024,128]{1,0:T(8,128)(2,1)S(1)}, bf16[1024,128]{1,0:T(8,128)(2,1)S(1)}, u32[]{:S(2)}, u32[]{:S(2)}) collective-permute-start(bf16[1024,128]{1,0:T(8,128)(2,1)S(1)} %get-tuple-element.65), channel_id=1, source_target_pairs={{0,8},{2,10},{8,16},{10,18},{16,24},{18,26},{24,28},{26,30},{28,20... | collective-permute-start | bytes 786440 | tf_op jit(solution)/shard_map/ppermute | solution.py:50
  19.8 13.1 %collective-permute-start.12 = (bf16[1024,128]{1,0:T(8,128)(2,1)S(1)}, bf16[1024,128]{1,0:T(8,128)(2,1)S(1)}, u32[]{:S(2)}, u32[]{:S(2)}) collective-permute-start(bf16[1024,128]{1,0:T(8,128)(2,1)S(1)} %get-tuple-element.67), channel_id=1, source_target_pairs={{0,4},{2,6},{8,0},{10,2},{16,8},{18,10},{24,16},{26,18},{28,24},{3... | collective-permute-start | bytes 786440 | tf_op jit(solution)/shard_map/ppermute | solution.py:50
  25.2 13.8 %collective-permute-start.8 = (bf16[1024,128]{1,0:T(8,128)(2,1)S(1)}, bf16[1024,128]{1,0:T(8,128)(2,1)S(1)}, u32[]{:S(2)}, u32[]{:S(2)}) collective-permute-start(bf16[1024,128]{1,0:T(8,128)(2,1)S(1)} %collective-permute-done.7.refs_7_), channel_id=1, source_target_pairs={{0,4},{2,6},{8,0},{10,2},{16,8},{18,10},{24,16},{26,18},{28,24},{3... | collective-permute-start | bytes 786440 | tf_op jit(solution)/shard_map/ppermute | solution.py:50
  27.0 12.0 %collective-permute-start.5 = (bf16[1024,128]{1,0:T(8,128)(2,1)S(1)}, bf16[1024,128]{1,0:T(8,128)(2,1)S(1)}, u32[]{:S(2)}, u32[]{:S(2)}) collective-permute-start(bf16[1024,128]{1,0:T(8,128)(2,1)S(1)} %collective-permute-done.3.refs_4_), channel_id=1, source_target_pairs={{0,8},{2,10},{8,16},{10,18},{16,24},{18,26},{24,28},{26,30},{28,20... | collective-permute-start | bytes 786440 | tf_op jit(solution)/shard_map/ppermute | solution.py:50
  32.6 11.2 %collective-permute-start.11 = (bf16[1024,128]{1,0:T(8,128)(2,1)S(1)}, bf16[1024,128]{1,0:T(8,128)(2,1)S(1)}, u32[]{:S(2)}, u32[]{:S(2)}) collective-permute-start(bf16[1024,128]{1,0:T(8,128)(2,1)S(1)} %collective-permute-done.10.refs_5_), channel_id=1, source_target_pairs={{0,8},{2,10},{8,16},{10,18},{16,24},{18,26},{24,28},{26,30},{28,20... | collective-permute-start | bytes 786440 | tf_op jit(solution)/shard_map/ppermute | solution.py:50
  32.9 10.9 %collective-permute-start.13 = (bf16[1024,128]{1,0:T(8,128)(2,1)S(1)}, bf16[1024,128]{1,0:T(8,128)(2,1)S(1)}, u32[]{:S(2)}, u32[]{:S(2)}) collective-permute-start(bf16[1024,128]{1,0:T(8,128)(2,1)S(1)} %collective-permute-done.12.refs_6_), channel_id=1, source_target_pairs={{0,4},{2,6},{8,0},{10,2},{16,8},{18,10},{24,16},{26,18},{28,24},{3... | collective-permute-start | bytes 786440 | tf_op jit(solution)/shard_map/ppermute | solution.py:50
  39.0 8.4 %collective-permute-start.6 = (bf16[1024,128]{1,0:T(8,128)(2,1)S(1)}, bf16[1024,128]{1,0:T(8,128)(2,1)S(1)}, u32[]{:S(2)}, u32[]{:S(2)}) collective-permute-start(bf16[1024,128]{1,0:T(8,128)(2,1)S(1)} %collective-permute-done.5.refs_4_), channel_id=1, source_target_pairs={{0,8},{2,10},{8,16},{10,18},{16,24},{18,26},{24,28},{26,30},{28,20... | collective-permute-start | bytes 786440 | tf_op jit(solution)/shard_map/ppermute | solution.py:50
  39.4 8.0 %collective-permute-start.9 = (bf16[1024,128]{1,0:T(8,128)(2,1)S(1)}, bf16[1024,128]{1,0:T(8,128)(2,1)S(1)}, u32[]{:S(2)}, u32[]{:S(2)}) collective-permute-start(bf16[1024,128]{1,0:T(8,128)(2,1)S(1)} %collective-permute-done.8.refs_7_), channel_id=1, source_target_pairs={{0,4},{2,6},{8,0},{10,2},{16,8},{18,10},{24,16},{26,18},{28,24},{3... | collective-permute-start | bytes 786440 | tf_op jit(solution)/shard_map/ppermute | solution.py:50
  41.0 19.0 %copy-start = (bf16[1024,2048]{1,0:T(8,128)(2,1)S(1)}, bf16[1024,2048]{1,0:T(8,128)(2,1)}, u32[]{:S(2)}) copy-start(bf16[1024,2048]{1,0:T(8,128)(2,1)} %refs_2_.3) | copy-start | bytes 12582916
  49.0 9.7 %collective-permute-start.14 = (bf16[528,256]{1,0:T(8,128)(2,1)S(1)}, bf16[528,256]{1,0:T(8,128)(2,1)S(1)}, u32[]{:S(2)}, u32[]{:S(2)}) collective-permute-start(bf16[528,256]{1,0:T(8,128)(2,1)S(1)} %get-tuple-element.74), channel_id=1, source_target_pairs={{0,2},{2,0},{4,6},{6,4},{8,10},{10,8},{12,14},{14,12},{16,18},{18,... | collective-permute-start | bytes 811016 | tf_op jit(solution)/shard_map/ppermute | solution.py:41
  51.3 9.9 %collective-permute-start.15 = (bf16[528,256]{1,0:T(8,128)(2,1)S(1)}, bf16[528,256]{1,0:T(8,128)(2,1)S(1)}, u32[]{:S(2)}, u32[]{:S(2)}) collective-permute-start(bf16[528,256]{1,0:T(8,128)(2,1)S(1)} %attend_far_others4.1), channel_id=1, source_target_pairs={{0,2},{2,0},{4,6},{6,4},{8,10},{10,8},{12,14},{14,12},{16,18},{18,... | collective-permute-start | bytes 811016 | tf_op jit(solution)/shard_map/ppermute | solution.py:41
  62.0 2.0 %collective-permute-start.16 = (bf16[256,1024]{1,0:T(8,128)(2,1)S(1)}, bf16[256,1024]{1,0:T(8,128)(2,1)S(1)}, u32[]{:S(2)}, u32[]{:S(2)}) collective-permute-start(bf16[256,1024]{1,0:T(8,128)(2,1)S(1)} %bitcast.32), channel_id=1, source_target_pairs={{0,1},{1,0},{2,3},{3,2},{4,5},{5,4},{6,7},{7,6},{8,9},{9,8},{10,11... | collective-permute-start | bytes 1572872 | tf_op jit(solution)/shard_map/ppermute | solution.py:41

commit v16 on v15

--- a/solution.py
+++ b/solution.py
@@ -644,6 +644,29 @@
         cost_estimate=cost(2 * rows * width * hidden.shape[1], 2 * width * w_out.shape[1]),
         name="keep_own",
     )(*attended, w_out, hidden)
+
+
+def finish_kernel(*refs):
+    kept, *received, result = refs
+    rows = 64 if kept.shape[0] % 64 == 0 else kept.shape[0]
+    for start in range(0, kept.shape[0], rows):
+        span = slice(start, start + rows)
+        total = kept[span, :]
+        for part in received:
+            total = total + part[span, :].astype(jnp.float32)
+        result[span, :] = total.astype(jnp.bfloat16)
+
+
+def finish(kept, received):
+    return pl.pallas_call(
+        finish_kernel,
+        in_specs=[VMEM] * (1 + len(received)),
+        out_specs=VMEM,
+        out_shape=jax.ShapeDtypeStruct(kept.shape, jnp.bfloat16),
+        compiler_params=params(16),
+        cost_estimate=cost(kept.size * len(received), 8 * kept.size),
+        name="finish",
+    )(kept, *received)
 
 
 def local(
@@ -781,10 +804,8 @@
         attended.append(made)
         earlier = [sent, token]
     received = [swap(sent[shift - 1], "tp", shift) for shift in range(1, ways)]
-    total = keep(attended, w_out, hidden_in)
-    for part in received:
-        total = total + part.astype(jnp.float32)
-    return (total.astype(jnp.bfloat16), new_cache)
+    hidden_out = finish(keep(attended, w_out, hidden_in), received)
+    return (hidden_out, new_cache)
 
 
 def solution(mesh):

time: 65 us -> 65 us (level)
  other arithmetic: 1.42 us -> 0.48 us
  Pallas kernels: 33.6 us -> 34.5 us
    convert_element_type x1 -> x0, other arithmetic: 0.94 us -> none  [local(): return (total.astype(jnp.bfloat16), new_cache)]
    pallas_call x0 -> x1, Pallas kernels: none -> 0.88 us  [finish(): pl.pallas_call(finish_kernel, in_specs=[VMEM] * (1 + len(received)), out_...]
where the time goes in v16:
time: 65 us; the launch traced here: 64.8 us
  Pallas kernels  34.5 us (53%)
  starting transfers between devices  17.6 us (27%)
  waiting for transfers between devices  10.6 us (16%)
  between operations  1.51 us (2%)
    pallas_call x6, Pallas kernels, attend(): pl.pallas_call(functools.partial(attend_kernel, (group, shifts, rings, sl...  17.8 us
    ppermute x12, starting transfers between devices, turn(): return lax.ppermute(value, 'seq', pairs)  13.4 us
    ppermute x12, waiting for transfers between devices, turn(): return lax.ppermute(value, 'seq', pairs)  8.87 us
    pallas_call x1, Pallas kernels, part_weights(): pl.pallas_call(weight_kernel, in_specs=[HBM], out_specs=VMEM, out_shape=j...  5.5 us
    ppermute x5, starting transfers between devices, swap(): return lax.ppermute(value, axis, pairs)  4.16 us
    pallas_call x1, Pallas kernels, project_keyval(): pl.pallas_call(keyval_kernel, in_specs=[VMEM] * 4, out_specs=[VMEM] * 3,...  2.54 us
    pallas_call x1, Pallas kernels, project_query(): pl.pallas_call(query_kernel, in_specs=[VMEM] * (len(pieces) + 3), out_spe...  2.02 us
    ppermute x5, waiting for transfers between devices, swap(): return lax.ppermute(value, axis, pairs)  1.73 us
  transfers between devices with their start and end apart: 17, of which 8 were waited for; matrix products, arithmetic and copies ran while one was open for 1% of the time, Pallas kernels for 48%

profile of v16, /device:TPU:0, one launch (start us, length us, event | category | flops | bytes accessed | tf_op | source)
XLA Modules:
  0.0 64.8 jit_solution(7547014690691198389)
XLA Ops:
  0.6 3.0 %collective-permute-start.4 = (bf16[2048,128]{1,0:T(8,128)(2,1)}, bf16[2048,128]{1,0:T(8,128)(2,1)S(1)}, u32[]{:S(2)}, u32[]{:S(2)}) collective-permute-start(bf16[2048,128]{1,0:T(8,128)(2,1)} %bitcast.23), channel_id=1, source_target_pairs={{0,4},{2,6},{8,0},{10,2},{16,8},{18,10},{24,16},{26,18},{28,24},{3... | collective-permute-start | bytes 1572872 | tf_op jit(solution)/shard_map/ppermute | solution.py:50
  3.8 5.5 %part_weights.1.weight = bf16[2,2048,1024]{2,1,0:T(8,128)(2,1)S(1)} custom-call(bf16[32768,128]{1,0:T(8,128)(2,1)} %bitcast.33), custom_call_target="tpu_custom_call" | custom-call | flops 2147483648 | bytes 16777216 | tf_op jit(solution)/shard_map/part_weights/pallas_call | solution.py:251
  10.0 0.6 positions.1
  11.1 2.0 %project_query.1 = (bf16[256,1024]{1,0:T(8,128)(2,1)S(1)}, bf16[256,2048]{1,0:T(8,128)(2,1)S(1)}) custom-call(bf16[256,1024]{1,0:T(8,128)(2,1)S(1)} %copy-done.2, bf16[256,1024]{1,0:T(8,128)(2,1)S(1)} %collective-permute-done.refs_1_, bf16[2048,1024]{1,0:T(8,128)(2,1)S(1)} %copy-done.1, f32[256,128]{1,0:T(8,128)S(1)} %get-tuple-element.52.refs_3_.cosine, ...), custom_call_target="tpu_custom_call" | custom-call | flops 1073741824 | bytes 4194304 | tf_op jit(solution)/shard_map/project_query/pallas_call | solution.py:212
  13.1 1.9 %collective-permute-start.1 = (bf16[256,1024]{1,0:T(8,128)(2,1)S(1)}, bf16[256,1024]{1,0:T(8,128)(2,1)S(1)}, u32[]{:S(2)}, u32[]{:S(2)}) collective-permute-start(bf16[256,1024]{1,0:T(8,128)(2,1)S(1)} %get-tuple-element.49.refs_3_), channel_id=1, source_target_pairs={{0,2},{2,0},{4,6},{6,4},{8,10},{10,8},{12,14},{14,12},{16,18},{18,... | collective-permute-start | bytes 1572872 | tf_op jit(solution)/shard_map/ppermute | solution.py:41
  15.1 0.8 %collective-permute-done.4.refs_1_ = bf16[2048,128]{1,0:T(8,128)(2,1)S(1)} collective-permute-done((bf16[2048,128]{1,0:T(8,128)(2,1)}, bf16[2048,128]{1,0:T(8,128)(2,1)S(1)}, u32[]{:S(2)}, u32[]{:S(2)}) %collective-permute-start.4) | collective-permute-done | bytes 524320 | tf_op jit(solution)/shard_map/ppermute | solution.py:50
  15.9 1.7 %collective-permute-start.7 = (bf16[1024,128]{1,0:T(8,128)(2,1)S(1)}, bf16[1024,128]{1,0:T(8,128)(2,1)S(1)}, u32[]{:S(2)}, u32[]{:S(2)}) collective-permute-start(bf16[1024,128]{1,0:T(8,128)(2,1)S(1)} %get-tuple-element.62), channel_id=1, source_target_pairs={{0,4},{2,6},{8,0},{10,2},{16,8},{18,10},{24,16},{26,18},{28,24},{3... | collective-permute-start | bytes 786440 | tf_op jit(solution)/shard_map/ppermute | solution.py:50
  18.1 1.7 %collective-permute-start.10 = (bf16[1024,128]{1,0:T(8,128)(2,1)S(1)}, bf16[1024,128]{1,0:T(8,128)(2,1)S(1)}, u32[]{:S(2)}, u32[]{:S(2)}) collective-permute-start(bf16[1024,128]{1,0:T(8,128)(2,1)S(1)} %get-tuple-element.65), channel_id=1, source_target_pairs={{0,8},{2,10},{8,16},{10,18},{16,24},{18,26},{24,28},{26,30},{28,20... | collective-permute-start | bytes 786440 | tf_op jit(solution)/shard_map/ppermute | solution.py:50
  20.1 2.5 %project_keyval.1 = (bf16[256,1024]{1,0:T(8,128)(2,1)S(1)}, bf16[256,1024]{1,0:T(8,128)(2,1)S(1)}, bf16[1024,256]{1,0:T(8,128)(2,1)S(1)}) custom-call(bf16[256,2048]{1,0:T(8,128)(2,1)S(1)} %get-tuple-element.51.normed, bf16[2,2048,1024]{2,1,0:T(8,128)(2,1)S(1)} %part_weights.1.weight, f32[256,128]{1,0:T(8,128)S(1)} %get-tuple-element.52.refs_3_.cosine, ...), custom_call_target="tpu_custom_call" | custom-call | flops 2147483648 | bytes 8388608 | tf_op jit(solution)/shard_map/project_keyval/pallas_call | solution.py:284
  22.6 2.6 %collective-permute-done.7.refs_7_ = bf16[1024,128]{1,0:T(8,128)(2,1)S(1)} collective-permute-done((bf16[1024,128]{1,0:T(8,128)(2,1)S(1)}, bf16[1024,128]{1,0:T(8,128)(2,1)S(1)}, u32[]{:S(2)}, u32[]{:S(2)}) %collective-permute-start.7) | collective-permute-done | bytes 262176 | tf_op jit(solution)/shard_map/ppermute | solution.py:50
  25.2 1.7 %collective-permute-start.8 = (bf16[1024,128]{1,0:T(8,128)(2,1)S(1)}, bf16[1024,128]{1,0:T(8,128)(2,1)S(1)}, u32[]{:S(2)}, u32[]{:S(2)}) collective-permute-start(bf16[1024,128]{1,0:T(8,128)(2,1)S(1)} %collective-permute-done.7.refs_7_), channel_id=1, source_target_pairs={{0,4},{2,6},{8,0},{10,2},{16,8},{18,10},{24,16},{26,18},{28,24},{3... | collective-permute-start | bytes 786440 | tf_op jit(solution)/shard_map/ppermute | solution.py:50
  27.3 1.0 %part_own.1 = (bf16[384,1024]{1,0:T(8,128)(2,1)S(1)}, bf16[1024,384]{1,0:T(8,128)(2,1)S(1)}) custom-call(bf16[4096,128]{1,0:T(8,128)(2,1)S(1)} %bitcast.22, bf16[2048,128]{1,0:T(8,128)(2,1)S(1)} %bitcast.25), custom_call_target="tpu_custom_call" | custom-call | flops 402653184 | bytes 3145728 | tf_op jit(solution)/shard_map/part_own/pallas_call | solution.py:170
  28.3 0.7 %part_near.1 = (bf16[256,1024]{1,0:T(8,128)(2,1)S(1)}, bf16[1024,256]{1,0:T(8,128)(2,1)S(1)}) custom-call(bf16[2048,128]{1,0:T(8,128)(2,1)S(1)} %collective-permute-done.2.refs_0_, bf16[2048,128]{1,0:T(8,128)(2,1)S(1)} %collective-permute-done.4.refs_1_), custom_call_target="tpu_custom_call" | custom-call | flops 268435456 | bytes 2097152 | tf_op jit(solution)/shard_map/part_near/pallas_call | solution.py:170
  29.0 3.5 %collective-permute-done.10.refs_5_ = bf16[1024,128]{1,0:T(8,128)(2,1)S(1)} collective-permute-done((bf16[1024,128]{1,0:T(8,128)(2,1)S(1)}, bf16[1024,128]{1,0:T(8,128)(2,1)S(1)}, u32[]{:S(2)}, u32[]{:S(2)}) %collective-permute-start.10) | collective-permute-done | bytes 262176 | tf_op jit(solution)/shard_map/ppermute | solution.py:50
  32.9 1.7 %collective-permute-start.13 = (bf16[1024,128]{1,0:T(8,128)(2,1)S(1)}, bf16[1024,128]{1,0:T(8,128)(2,1)S(1)}, u32[]{:S(2)}, u32[]{:S(2)}) collective-permute-start(bf16[1024,128]{1,0:T(8,128)(2,1)S(1)} %collective-permute-done.12.refs_6_), channel_id=1, source_target_pairs={{0,4},{2,6},{8,0},{10,2},{16,8},{18,10},{24,16},{26,18},{28,24},{3... | collective-permute-start | bytes 786440 | tf_op jit(solution)/shard_map/ppermute | solution.py:50
  34.6 4.3 %attend_near_others.1 = (f32[1024,256]{1,0:T(8,128)S(1)}, f32[8,256]{1,0:T(8,128)S(1)}) custom-call(s32[8]{0:T(128)S(1)} %copy-done.6, s32[1]{0:T(128)S(6)} %copy.15.shared.refs_1_, s32[4,8]{1,0:T(4,128)S(1)} %bitcast.26, bf16[256,1024]{1,0:T(8,128)(2,1)S(1)} %collective-permute-done.1.refs_3_, bf16[384,1024]{1,0:T(8,128)(2,1)S(1)} %get-tuple-element.55.refs_4_, ...), custom_call_target="tpu_custom_call" | custom-call | flops 939524096 | bytes 3670016 | tf_op jit(solution)/shard_map/attend_near_others/pallas_call | solution.py:548
  39.4 1.7 %collective-permute-start.9 = (bf16[1024,128]{1,0:T(8,128)(2,1)S(1)}, bf16[1024,128]{1,0:T(8,128)(2,1)S(1)}, u32[]{:S(2)}, u32[]{:S(2)}) collective-permute-start(bf16[1024,128]{1,0:T(8,128)(2,1)S(1)} %collective-permute-done.8.refs_7_), channel_id=1, source_target_pairs={{0,4},{2,6},{8,0},{10,2},{16,8},{18,10},{24,16},{26,18},{28,24},{3... | collective-permute-start | bytes 786440 | tf_op jit(solution)/shard_map/ppermute | solution.py:50
  41.0 2.2 %attend_hop2_others.1 = (f32[1024,256]{1,0:T(8,128)S(1)}, f32[8,256]{1,0:T(8,128)S(1)}, bf16[256,1024]{1,0:T(8,128)(2,1)S(1)}, bf16[1024,256]{1,0:T(8,128)(2,1)S(1)}) custom-call(s32[8]{0:T(128)S(1)} %copy-done.6, s32[1]{0:T(128)S(6)} %copy.15.shared.refs_1_, s32[4,8]{1,0:T(4,128)S(1)} %bitcast.27, bf16[256,1024]{1,0:T(8,128)(2,1)S(1)} %collective-permute-done.1.refs_3_, ...), custom_call_target="tpu_custom_call" | custom-call | flops 268435456 | bytes 1048576 | tf_op jit(solution)/shard_map/attend_hop2_others/pallas_call | solution.py:548
  43.8 2.2 %attend_hop3_others.1 = (f32[1024,256]{1,0:T(8,128)S(1)}, f32[8,256]{1,0:T(8,128)S(1)}, bf16[256,1024]{1,0:T(8,128)(2,1)S(1)}, bf16[1024,256]{1,0:T(8,128)(2,1)S(1)}) custom-call(s32[8]{0:T(128)S(1)} %copy-done.6, s32[1]{0:T(128)S(6)} %copy.15.shared.refs_1_, s32[4,8]{1,0:T(4,128)S(1)} %bitcast.28, bf16[256,1024]{1,0:T(8,128)(2,1)S(1)} %collective-permute-done.1.refs_3_, ...), custom_call_target="tpu_custom_call" | custom-call | flops 268435456 | bytes 1048576 | tf_op jit(solution)/shard_map/attend_hop3_others/pallas_call | solution.py:548
  46.1 1.3 %collective-permute-done.6.refs_4_ = bf16[1024,128]{1,0:T(8,128)(2,1)S(1)} collective-permute-done((bf16[1024,128]{1,0:T(8,128)(2,1)S(1)}, bf16[1024,128]{1,0:T(8,128)(2,1)S(1)}, u32[]{:S(2)}, u32[]{:S(2)}) %collective-permute-start.6) | collective-permute-done | bytes 262176 | tf_op jit(solution)/shard_map/ppermute | solution.py:50
  47.4 1.6 %attend_far_others0.1 = (bf16[528,256]{1,0:T(8,128)(2,1)S(1)}, bf16[128,1024]{1,0:T(8,128)(2,1)S(1)}, bf16[1024,128]{1,0:T(8,128)(2,1)S(1)}) custom-call(s32[8]{0:T(128)S(1)} %copy-done.6, s32[1]{0:T(128)S(6)} %copy.15.shared.refs_1_, s32[4,8]{1,0:T(4,128)S(1)} %bitcast.29, bf16[256,1024]{1,0:T(8,128)(2,1)S(1)} %collective-permute-done.1.refs_3_, ...), custom_call_target="tpu_custom_call" | custom-call | flops 67108864 | bytes 524288 | tf_op jit(solution)/shard_map/attend_far_others0/pallas_call | solution.py:548
  49.0 1.2 %collective-permute-start.14 = (bf16[528,256]{1,0:T(8,128)(2,1)S(1)}, bf16[528,256]{1,0:T(8,128)(2,1)S(1)}, u32[]{:S(2)}, u32[]{:S(2)}) collective-permute-start(bf16[528,256]{1,0:T(8,128)(2,1)S(1)} %get-tuple-element.74), channel_id=1, source_target_pairs={{0,2},{2,0},{4,6},{6,4},{8,10},{10,8},{12,14},{14,12},{16,18},{18,... | collective-permute-start | bytes 811016 | tf_op jit(solution)/shard_map/ppermute | solution.py:41
  50.2 1.1 %attend_far_others4.1 = bf16[528,256]{1,0:T(8,128)(2,1)S(1)} custom-call(s32[8]{0:T(128)S(1)} %copy-done.6, s32[1]{0:T(128)S(6)} %copy.15.shared.refs_1_, s32[4,8]{1,0:T(4,128)S(1)} %bitcast.30, bf16[256,1024]{1,0:T(8,128)(2,1)S(1)} %collective-permute-done.1.refs_3_, bf16[128,1024]{1,0:T(8,128)(2,1)S(1)} %get-tuple-element.76.refs_4_.refs_12_, ...), custom_call_target="tpu_custom_call" | custom-call | flops 67108864 | bytes 524288 | tf_op jit(solution)/shard_map/attend_far_others4/pallas_call | solution.py:548
  51.3 0.9 %collective-permute-start.15 = (bf16[528,256]{1,0:T(8,128)(2,1)S(1)}, bf16[528,256]{1,0:T(8,128)(2,1)S(1)}, u32[]{:S(2)}, u32[]{:S(2)}) collective-permute-start(bf16[528,256]{1,0:T(8,128)(2,1)S(1)} %attend_far_others4.1), channel_id=1, source_target_pairs={{0,2},{2,0},{4,6},{6,4},{8,10},{10,8},{12,14},{14,12},{16,18},{18,... | collective-permute-start | bytes 811016 | tf_op jit(solution)/shard_map/ppermute | solution.py:41
  52.2 6.4 %attend_own.1 = (f32[1024,256]{1,0:T(8,128)S(1)}, f32[8,256]{1,0:T(8,128)S(1)}) custom-call(s32[8]{0:T(128)S(1)} %copy-done.6, s32[1]{0:T(128)S(6)} %copy.15.shared.refs_1_, s32[4,8]{1,0:T(4,128)S(1)} %bitcast.31, bf16[256,1024]{1,0:T(8,128)(2,1)S(1)} %get-tuple-element.49.refs_3_, bf16[384,1024]{1,0:T(8,128)(2,1)S(1)} %get-tuple-element.55.refs_4_, ...), custom_call_target="tpu_custom_call" | custom-call | flops 1610612736 | bytes 6291456 | tf_op jit(solution)/shard_map/attend_own/pallas_call | solution.py:548
  58.6 1.4 %weave_cache.1 = (bf16[4096,128]{1,0:T(8,128)(2,1)}, f32[8,128]{1,0:T(8,128)S(1)}) custom-call(bf16[256,1024]{1,0:T(8,128)(2,1)S(1)} %get-tuple-element.53.refs_8_.refs_14_.keys, bf16[256,1024]{1,0:T(8,128)(2,1)S(1)} %get-tuple-element.85.values, f32[8,256]{1,0:T(8,128)S(1)} %get-tuple-element.84.refs_0_.refs_1_, ...), custom_call_target="tpu_custom_call" | custom-call | flops 268435456 | bytes 2097152 | tf_op jit(solution)/shard_map/weave_cache/pallas_call | solution.py:323
  60.0 0.7 %combine_send0.1 = (bf16[256,512]{1,0:T(8,128)(2,1)S(1)}, f32[1,256,1024]{2,1,0:T(8,128)S(1)}) custom-call(f32[1024,256]{1,0:T(8,128)S(1)} %get-tuple-element.83.refs_0_, f32[8,256]{1,0:T(8,128)S(1)} %get-tuple-element.84.refs_0_.refs_1_, bf16[528,256]{1,0:T(8,128)(2,1)S(1)} %collective-permute-done.14.refs_1_.refs_2_, bf16[1024,2048]{1,0:T(8,128)(2,1)S(1)} %copy-done, ...), custom_call_target="tpu_custom_call" | custom-call | flops 268435456 | bytes 1048576 | tf_op jit(solution)/shard_map/combine_send0/pallas_call | solution.py:610
  60.7 0.6 collective-permute-done.15.refs_2_
  61.3 0.7 %combine_send4.1 = (bf16[256,512]{1,0:T(8,128)(2,1)S(1)}, bf16[1,256,1024]{2,1,0:T(8,128)(2,1)S(1)}) custom-call(f32[1024,256]{1,0:T(8,128)S(1)} %get-tuple-element.83.refs_0_, f32[8,256]{1,0:T(8,128)S(1)} %get-tuple-element.84.refs_0_.refs_1_, bf16[528,256]{1,0:T(8,128)(2,1)S(1)} %collective-permute-done.15.refs_2_, bf16[1024,2048]{1,0:T(8,128)(2,1)S(1)} %copy-done, ...), custom_call_target="tpu_custom_call" | custom-call | flops 268435456 | bytes 1048576 | tf_op jit(solution)/shard_map/combine_send4/pallas_call | solution.py:610
  62.0 0.7 %keep_own.1.refs_0_ = f32[256,1024]{1,0:T(8,128)S(1)} custom-call(bf16[256,512]{1,0:T(8,128)(2,1)S(1)} %get-tuple-element.87.refs_0_, bf16[256,512]{1,0:T(8,128)(2,1)S(1)} %get-tuple-element.89.refs_1_, bf16[1024,2048]{1,0:T(8,128)(2,1)S(1)} %copy-done, bf16[256,1024]{1,0:T(8,128)(2,1)S(1)} %copy-done.2), custom_call_target="tpu_custom_call" | custom-call | flops 536870912 | bytes 4194304 | tf_op jit(solution)/shard_map/keep_own/pallas_call | solution.py:638
  62.8 1.2 %collective-permute-done.16.refs_1_ = bf16[256,1024]{1,0:T(8,128)(2,1)S(1)} collective-permute-done((bf16[256,1024]{1,0:T(8,128)(2,1)S(1)}, bf16[256,1024]{1,0:T(8,128)(2,1)S(1)}, u32[]{:S(2)}, u32[]{:S(2)}) %collective-permute-start.16) | collective-permute-done | bytes 524320 | tf_op jit(solution)/shard_map/ppermute | solution.py:41
  63.9 0.9 %finish.1 = bf16[256,1024]{1,0:T(8,128)(2,1)} custom-call(f32[256,1024]{1,0:T(8,128)S(1)} %keep_own.1.refs_0_, bf16[256,1024]{1,0:T(8,128)(2,1)S(1)} %collective-permute-done.16.refs_1_), custom_call_target="tpu_custom_call" | custom-call | flops 262144 | bytes 2097152 | tf_op jit(solution)/shard_map/finish/pallas_call | solution.py:661
  (37 shorter events, 3.2 us)
Async XLA Ops:
  0.6 15.2 %collective-permute-start.4 = (bf16[2048,128]{1,0:T(8,128)(2,1)}, bf16[2048,128]{1,0:T(8,128)(2,1)S(1)}, u32[]{:S(2)}, u32[]{:S(2)}) collective-permute-start(bf16[2048,128]{1,0:T(8,128)(2,1)} %bitcast.23), channel_id=1, source_target_pairs={{0,4},{2,6},{8,0},{10,2},{16,8},{18,10},{24,16},{26,18},{28,24},{3... | collective-permute-start | bytes 1572872 | tf_op jit(solution)/shard_map/ppermute | solution.py:50
  3.6 14.0 %collective-permute-start.2 = (bf16[2048,128]{1,0:T(8,128)(2,1)}, bf16[2048,128]{1,0:T(8,128)(2,1)S(1)}, u32[]{:S(2)}, u32[]{:S(2)}) collective-permute-start(bf16[2048,128]{1,0:T(8,128)(2,1)} %bitcast.24), channel_id=1, source_target_pairs={{0,8},{2,10},{8,16},{10,18},{16,24},{18,26},{24,28},{26,30},{28,20... | collective-permute-start | bytes 1572872 | tf_op jit(solution)/shard_map/ppermute | solution.py:50
  3.8 7.3 %collective-permute-start = (bf16[256,1024]{1,0:T(8,128)(2,1)}, bf16[256,1024]{1,0:T(8,128)(2,1)S(1)}, u32[]{:S(2)}, u32[]{:S(2)}) collective-permute-start(bf16[256,1024]{1,0:T(8,128)(2,1)} %refs_3_.5), channel_id=1, source_target_pairs={{0,1},{1,0},{2,3},{3,2},{4,5},{5,4},{6,7},{7,6},{8,9},{9,8},{10,11... | collective-permute-start | bytes 1572872 | tf_op jit(solution)/shard_map/ppermute | solution.py:41
  3.8 6.2 %copy-start.6 = (s32[8]{0:T(128)S(1)}, s32[8]{0:T(128)}, u32[]{:S(2)}) copy-start(s32[8]{0:T(128)} %refs_0_.10) | copy-start | bytes 100
  3.8 7.3 %copy-start.1 = (bf16[2048,1024]{1,0:T(8,128)(2,1)S(1)}, bf16[2048,1024]{1,0:T(8,128)(2,1)}, u32[]{:S(2)}) copy-start(bf16[2048,1024]{1,0:T(8,128)(2,1)} %refs_2_.2) | copy-start | bytes 12582916
  3.8 7.3 %copy-start.2 = (bf16[256,1024]{1,0:T(8,128)(2,1)S(1)}, bf16[256,1024]{1,0:T(8,128)(2,1)}, u32[]{:S(2)}) copy-start(bf16[256,1024]{1,0:T(8,128)(2,1)} %refs_3_.5) | copy-start | bytes 1572868
  11.1 16.2 %copy-start.3 = (bf16[2,128,2,1024]{3,2,1,0:T(2,128)(2,1)S(1)}, bf16[2,128,2,1024]{3,2,1,0:T(2,128)(2,1)}, u32[]{:S(2)}) copy-start(bf16[2,128,2,1024]{3,2,1,0:T(2,128)(2,1)} %param.14) | copy-start | bytes 3145732
  11.1 16.2 %copy-start.4 = (bf16[128,2,1024]{2,1,0:T(2,128)(2,1)S(1)}, bf16[128,2,1024]{2,1,0:T(2,128)(2,1)}, u32[]{:S(2)}) copy-start(bf16[128,2,1024]{2,1,0:T(2,128)(2,1)} %param.13) | copy-start | bytes 1572868
  13.1 21.5 %copy-start.5 = (s32[8,4]{0,1:T(4,128)S(1)}, s32[8,4]{0,1:T(4,128)}, u32[]{:S(2)}) copy-start(s32[8,4]{0,1:T(4,128)} %param.15) | copy-start | bytes 388
  13.1 21.5 %collective-permute-start.1 = (bf16[256,1024]{1,0:T(8,128)(2,1)S(1)}, bf16[256,1024]{1,0:T(8,128)(2,1)S(1)}, u32[]{:S(2)}, u32[]{:S(2)}) collective-permute-start(bf16[256,1024]{1,0:T(8,128)(2,1)S(1)} %get-tuple-element.49.refs_3_), channel_id=1, source_target_pairs={{0,2},{2,0},{4,6},{6,4},{8,10},{10,8},{12,14},{14,12},{16,18},{18,... | collective-permute-start | bytes 1572872 | tf_op jit(solution)/shard_map/ppermute | solution.py:41
  15.9 9.3 %collective-permute-start.7 = (bf16[1024,128]{1,0:T(8,128)(2,1)S(1)}, bf16[1024,128]{1,0:T(8,128)(2,1)S(1)}, u32[]{:S(2)}, u32[]{:S(2)}) collective-permute-start(bf16[1024,128]{1,0:T(8,128)(2,1)S(1)} %get-tuple-element.62), channel_id=1, source_target_pairs={{0,4},{2,6},{8,0},{10,2},{16,8},{18,10},{24,16},{26,18},{28,24},{3... | collective-permute-start | bytes 786440 | tf_op jit(solution)/shard_map/ppermute | solution.py:50
  17.7 9.3 %collective-permute-start.3 = (bf16[1024,128]{1,0:T(8,128)(2,1)S(1)}, bf16[1024,128]{1,0:T(8,128)(2,1)S(1)}, u32[]{:S(2)}, u32[]{:S(2)}) collective-permute-start(bf16[1024,128]{1,0:T(8,128)(2,1)S(1)} %get-tuple-element.50), channel_id=1, source_target_pairs={{0,8},{2,10},{8,16},{10,18},{16,24},{18,26},{24,28},{26,30},{28,20... | collective-permute-start | bytes 786440 | tf_op jit(solution)/shard_map/ppermute | solution.py:50
  18.1 14.5 %collective-permute-start.10 = (bf16[1024,128]{1,0:T(8,128)(2,1)S(1)}, bf16[1024,128]{1,0:T(8,128)(2,1)S(1)}, u32[]{:S(2)}, u32[]{:S(2)}) collective-permute-start(bf16[1024,128]{1,0:T(8,128)(2,1)S(1)} %get-tuple-element.65), channel_id=1, source_target_pairs={{0,8},{2,10},{8,16},{10,18},{16,24},{18,26},{24,28},{26,30},{28,20... | collective-permute-start | bytes 786440 | tf_op jit(solution)/shard_map/ppermute | solution.py:50
  19.8 13.1 %collective-permute-start.12 = (bf16[1024,128]{1,0:T(8,128)(2,1)S(1)}, bf16[1024,128]{1,0:T(8,128)(2,1)S(1)}, u32[]{:S(2)}, u32[]{:S(2)}) collective-permute-start(bf16[1024,128]{1,0:T(8,128)(2,1)S(1)} %get-tuple-element.67), channel_id=1, source_target_pairs={{0,4},{2,6},{8,0},{10,2},{16,8},{18,10},{24,16},{26,18},{28,24},{3... | collective-permute-start | bytes 786440 | tf_op jit(solution)/shard_map/ppermute | solution.py:50
  25.2 13.8 %collective-permute-start.8 = (bf16[1024,128]{1,0:T(8,128)(2,1)S(1)}, bf16[1024,128]{1,0:T(8,128)(2,1)S(1)}, u32[]{:S(2)}, u32[]{:S(2)}) collective-permute-start(bf16[1024,128]{1,0:T(8,128)(2,1)S(1)} %collective-permute-done.7.refs_7_), channel_id=1, source_target_pairs={{0,4},{2,6},{8,0},{10,2},{16,8},{18,10},{24,16},{26,18},{28,24},{3... | collective-permute-start | bytes 786440 | tf_op jit(solution)/shard_map/ppermute | solution.py:50
  27.0 12.0 %collective-permute-start.5 = (bf16[1024,128]{1,0:T(8,128)(2,1)S(1)}, bf16[1024,128]{1,0:T(8,128)(2,1)S(1)}, u32[]{:S(2)}, u32[]{:S(2)}) collective-permute-start(bf16[1024,128]{1,0:T(8,128)(2,1)S(1)} %collective-permute-done.3.refs_4_), channel_id=1, source_target_pairs={{0,8},{2,10},{8,16},{10,18},{16,24},{18,26},{24,28},{26,30},{28,20... | collective-permute-start | bytes 786440 | tf_op jit(solution)/shard_map/ppermute | solution.py:50
  32.6 11.2 %collective-permute-start.11 = (bf16[1024,128]{1,0:T(8,128)(2,1)S(1)}, bf16[1024,128]{1,0:T(8,128)(2,1)S(1)}, u32[]{:S(2)}, u32[]{:S(2)}) collective-permute-start(bf16[1024,128]{1,0:T(8,128)(2,1)S(1)} %collective-permute-done.10.refs_5_), channel_id=1, source_target_pairs={{0,8},{2,10},{8,16},{10,18},{16,24},{18,26},{24,28},{26,30},{28,20... | collective-permute-start | bytes 786440 | tf_op jit(solution)/shard_map/ppermute | solution.py:50
  32.9 10.9 %collective-permute-start.13 = (bf16[1024,128]{1,0:T(8,128)(2,1)S(1)}, bf16[1024,128]{1,0:T(8,128)(2,1)S(1)}, u32[]{:S(2)}, u32[]{:S(2)}) collective-permute-start(bf16[1024,128]{1,0:T(8,128)(2,1)S(1)} %collective-permute-done.12.refs_6_), channel_id=1, source_target_pairs={{0,4},{2,6},{8,0},{10,2},{16,8},{18,10},{24,16},{26,18},{28,24},{3... | collective-permute-start | bytes 786440 | tf_op jit(solution)/shard_map/ppermute | solution.py:50
  39.0 8.4 %collective-permute-start.6 = (bf16[1024,128]{1,0:T(8,128)(2,1)S(1)}, bf16[1024,128]{1,0:T(8,128)(2,1)S(1)}, u32[]{:S(2)}, u32[]{:S(2)}) collective-permute-start(bf16[1024,128]{1,0:T(8,128)(2,1)S(1)} %collective-permute-done.5.refs_4_), channel_id=1, source_target_pairs={{0,8},{2,10},{8,16},{10,18},{16,24},{18,26},{24,28},{26,30},{28,20... | collective-permute-start | bytes 786440 | tf_op jit(solution)/shard_map/ppermute | solution.py:50
  39.4 8.0 %collective-permute-start.9 = (bf16[1024,128]{1,0:T(8,128)(2,1)S(1)}, bf16[1024,128]{1,0:T(8,128)(2,1)S(1)}, u32[]{:S(2)}, u32[]{:S(2)}) collective-permute-start(bf16[1024,128]{1,0:T(8,128)(2,1)S(1)} %collective-permute-done.8.refs_7_), channel_id=1, source_target_pairs={{0,4},{2,6},{8,0},{10,2},{16,8},{18,10},{24,16},{26,18},{28,24},{3... | collective-permute-start | bytes 786440 | tf_op jit(solution)/shard_map/ppermute | solution.py:50
  41.0 19.0 %copy-start = (bf16[1024,2048]{1,0:T(8,128)(2,1)S(1)}, bf16[1024,2048]{1,0:T(8,128)(2,1)}, u32[]{:S(2)}) copy-start(bf16[1024,2048]{1,0:T(8,128)(2,1)} %refs_2_.3) | copy-start | bytes 12582916
  49.0 9.7 %collective-permute-start.14 = (bf16[528,256]{1,0:T(8,128)(2,1)S(1)}, bf16[528,256]{1,0:T(8,128)(2,1)S(1)}, u32[]{:S(2)}, u32[]{:S(2)}) collective-permute-start(bf16[528,256]{1,0:T(8,128)(2,1)S(1)} %get-tuple-element.74), channel_id=1, source_target_pairs={{0,2},{2,0},{4,6},{6,4},{8,10},{10,8},{12,14},{14,12},{16,18},{18,... | collective-permute-start | bytes 811016 | tf_op jit(solution)/shard_map/ppermute | solution.py:41
  51.3 9.9 %collective-permute-start.15 = (bf16[528,256]{1,0:T(8,128)(2,1)S(1)}, bf16[528,256]{1,0:T(8,128)(2,1)S(1)}, u32[]{:S(2)}, u32[]{:S(2)}) collective-permute-start(bf16[528,256]{1,0:T(8,128)(2,1)S(1)} %attend_far_others4.1), channel_id=1, source_target_pairs={{0,2},{2,0},{4,6},{6,4},{8,10},{10,8},{12,14},{14,12},{16,18},{18,... | collective-permute-start | bytes 811016 | tf_op jit(solution)/shard_map/ppermute | solution.py:41
  62.0 2.0 %collective-permute-start.16 = (bf16[256,1024]{1,0:T(8,128)(2,1)S(1)}, bf16[256,1024]{1,0:T(8,128)(2,1)S(1)}, u32[]{:S(2)}, u32[]{:S(2)}) collective-permute-start(bf16[256,1024]{1,0:T(8,128)(2,1)S(1)} %bitcast.32), channel_id=1, source_target_pairs={{0,1},{1,0},{2,3},{3,2},{4,5},{5,4},{6,7},{7,6},{8,9},{9,8},{10,11... | collective-permute-start | bytes 1572872 | tf_op jit(solution)/shard_map/ppermute | solution.py:41
